TPU v7x, 32 devices: a whole 2x2x4 slice. The times are simulated.
32 devices in a mesh: sect: 4 (over y, x), node: 8 (over z, core).
Axes of the slice: x: 2, y: 2, z: 4, core: 2. Of those that a mesh axis runs over, the one named last changes fastest.
Arguments:
- grid_feat: bfloat16 [8192, 512], P(('sect', 'node')), may hold values from -6 to 6
- edge_len: float32 [8192, 2], P(('sect', 'node')), may hold values from 0.2 to 1.5
- g2m_owner: int32 [8192, 2], P(('sect', 'node')), may hold values from 0 to 7, all different within a row; in each aligned block of 256 rows (0 to 255, 256 to 511, ...) at most 128 rows name the same one
- g2m_dst: int32 [8192, 2], P(('sect', 'node')), may hold values from 0 to 511
- enc_weight: bfloat16 [512, 512], replicated, may hold values from -0.25 to 0.25
- enc_vec: float32 [512], replicated, may hold values from -5 to 5
- mesh_init: bfloat16 [8, 512, 512], P('node', 'sect'), may hold values from -1.11 to 1.11
- mesh_weight: bfloat16 [512, 512], replicated, may hold values from -0.015625 to 0.015625
- halo_send: int32 [4, 8, 4, 8, 2], P('sect', 'node'), may hold values from 0 to 127
- mesh_src: int32 [8, 512, 8], P('node', 'sect'), may hold values from 0 to 191
- proc_weight: bfloat16 [2, 4, 512, 512], replicated, may hold values from -0.25 to 0.25
- cot: bfloat16 [8, 512, 512], P('node', 'sect'), may hold values from -16 to 16
Outputs:
- mesh_out: bfloat16 [8, 512, 512], P('node', 'sect')
- grid_grad: bfloat16 [8192, 512], P(('sect', 'node'))
Inputs may be any that keep to these rules, and one draw needn't show every extreme that they name: `g2m_owner`: within the 256 grid nodes of one device (aligned blocks), at most 128 edges name one mesh block, and some block is named by exactly 128 edges in some or all devices; the 2 edges of one grid node name different blocks. `mesh_src`: entries below 128 name own rows of the table, the others received rows.
All inputs are finite; a program needn't handle non-finite values.
Results may differ from a plain program's by a relative error of at most 0.009.
Values may be sent and summed in bfloat16 or wider, within the bound.
No kernel may reach another device: no remote copies, remote signals or barrier semaphores. Data moves between devices by JAX's collectives and lax.ppermute only.
A program may use at most 64 MiB of HBM per device.

v0:
```python
import functools
import math

import jax
import jax.numpy as jnp
from jax import lax
from jax.experimental import pallas as pl
from jax.experimental.pallas import tpu as pltpu
from jax.sharding import PartitionSpec as P

F32 = jnp.float32
BF16 = jnp.bfloat16
LANES = 128
META_ROWS = 16
MIB = 1024 * 1024


def sigmoid(value):
    return 0.5 * jnp.tanh(0.5 * value) + 0.5


def silu(value):
    return value * sigmoid(value)


def slope(value):
    sig = sigmoid(value)
    return sig * (1.0 + value * (1.0 - sig))


def dot(left, right):
    return jnp.dot(left, right, preferred_element_type=F32)


def dot_t(left, right):
    return lax.dot_general(left, right, (((1,), (1,)), ((), ())), preferred_element_type=F32)


def halves(value):
    high = value.astype(BF16)
    return high, (value - high.astype(F32)).astype(BF16)


def back_dot(grad, weight):
    rows = grad.shape[0]
    both = dot_t(jnp.concatenate(halves(grad), axis=0), weight)
    return both[:rows] + both[rows:]


def mark(equal):
    return jnp.where(equal, 1.0, 0.0).astype(BF16)


def iota(shape, axis):
    return lax.broadcasted_iota(jnp.int32, shape, axis)


def norm_parts(mixed):
    mean = jnp.mean(mixed, axis=-1, keepdims=True)
    centred = mixed - mean
    scale = lax.rsqrt(jnp.mean(centred * centred, axis=-1, keepdims=True) + 1e-05)
    return centred * scale, scale


def norm_back(grad, normed, scale):
    pull = grad * slope(normed)
    return scale * (
        pull
        - jnp.mean(pull, axis=-1, keepdims=True)
        - normed * jnp.mean(pull * normed, axis=-1, keepdims=True)
    )


def pack_kernel(block, feat, lens, owner, dst, *refs):
    *outs, held, own_held, dst_held, sems = refs
    rows = feat.shape[0] // len(outs)
    pairs = [(lens, held), (owner, own_held), (dst, dst_held)]
    pairs += [
        (feat.at[i * rows : (i + 1) * rows, :], out.at[:rows, :]) for i, out in enumerate(outs)
    ]
    copies = [
        pltpu.make_async_copy(source, target, sems.at[i])
        for i, (source, target) in enumerate(pairs)
    ]
    for copy in copies:
        copy.start()
    for copy in copies[:3]:
        copy.wait()
    high, middle = halves(held[...])
    low = (held[...] - high.astype(F32) - middle.astype(F32)).astype(BF16)
    far = dst_held[...]
    section = far // block
    found = [v.astype(F32) for v in (high, middle, low)]
    found += [v.astype(F32) for v in (own_held[...], section, far - section * block)]
    fill = META_ROWS - 6 * lens.shape[0]
    found.append(jnp.zeros((fill, feat.shape[0]), F32))
    meta = jnp.concatenate(found, axis=0).astype(BF16)
    rest = jnp.zeros((META_ROWS, feat.shape[1] - rows), BF16)
    for i, out in enumerate(outs):
        out[rows:, :] = jnp.concatenate([meta[:, i * rows : (i + 1) * rows], rest], axis=1)
    for copy in copies[3:]:
        copy.wait()


def index_kernel(block, parts, sends, src_row, pick, pick_t, source, source_t):
    sects, count, nodes = sends.shape
    pieces = pick.shape[0]
    at = iota((1, pieces), 1)
    part, row = at % parts, at // parts
    peer = row // count
    whose = mark(iota((nodes, pieces), 0) == peer % nodes)
    place = jnp.zeros((1, pieces), F32)
    for t in range(sects):
        found = dot(sends[t].astype(F32).astype(BF16), whose)
        for c in range(count):
            here = jnp.logical_and(peer // nodes == t, row % count == c)
            place = place + jnp.where(here, found[c : c + 1], 0.0)
    place = place + (part * block).astype(F32)
    pick_t[...] = mark(iota((parts * block, pieces), 0) == place.astype(jnp.int32))
    turned = jnp.broadcast_to(place, (8, pieces)).T[:, :1].astype(jnp.int32)
    pick[...] = mark(iota((pieces, parts * block), 1) == turned)
    table_len = source_t.shape[0]
    column = src_row[...].astype(F32).T.astype(jnp.int32)
    ids = iota((block, 2 * table_len), 1)
    ids = jnp.where(ids >= table_len, ids - table_len, ids)
    ids_t = iota((table_len, block), 0)
    for k in range(src_row.shape[0]):
        rows = slice(k * block, (k + 1) * block)
        source[rows, :] = mark(ids == column[:, k : k + 1])
        source_t[:, rows] = mark(ids_t == src_row[k : k + 1, :])


def edge_data(feat, at, rows):
    return feat[at + rows : at + rows + META_ROWS, :rows].astype(F32)


def edge_length(meta, fanout, k):
    high, middle, low = (meta[:, t * fanout + k : t * fanout + k + 1] for t in range(3))
    return high + middle + low


def spot_of(pick, fanout, k, section, node, nodes, block):
    owner, where, place = (pick((3 + t) * fanout + k).astype(jnp.int32) for t in range(3))
    apart = jnp.bitwise_xor(owner, node)
    order = lax.shift_right_logical(apart, 1) + jnp.bitwise_and(apart, 1) * (nodes // 2)
    return jnp.where(where == section, order * block + place, -1)


def add_rows(out, base, message, spots, before):
    step = min(out.shape[0], 512)

    def chunk(c, carry):
        start = pl.multiple_of(c * step, step)
        ids = iota((step, spots.shape[1]), 0) + (base + start)
        part = dot(mark(ids == spots[...]), message[...])
        for ref in before:
            part = part + ref[pl.ds(base + start, step), :]
        out[pl.ds(start, step), :] = part.astype(out.dtype)
        return carry

    lax.fori_loop(0, out.shape[0] // step, chunk, 0)


def encode_kernel(spans, nodes, block, fanout, rows, last, who, *refs):
    count = len(spans)
    feats = refs[:count]
    weight, vec = refs[count : count + 2]
    *before, out, message, spots = refs[count + 2 :]
    section, node = who[0], who[1]
    pre = 0.5 * dot(
        jnp.concatenate([feat[at : at + rows, :] for feat, at in zip(feats, spans)], axis=0),
        weight[...],
    )
    part = 0.5 * vec[...]
    for j in range(count):
        meta = edge_data(feats[j], spans[j], rows)
        turned = meta.T
        for k in range(fanout):
            at = (j * fanout + k) * rows
            act = pre[j * rows : (j + 1) * rows] + edge_length(turned, fanout, k) * part
            message[at : at + rows, :] = (act + act * jnp.tanh(act)).astype(BF16)
            spots[:, at : at + rows] = spot_of(
                lambda t, meta=meta: meta[t : t + 1], fanout, k, section, node, nodes, block
            )
    add_rows(out, nodes // 2 * block if last else 0, message, spots, before)


def keep_kernel(message, spots, before, out):
    add_rows(out, 0, message, spots, [before])


def slope_kernel(spans, fanout, rows, *refs):
    count = len(spans)
    feats = refs[:count]
    weight, vec = refs[count : count + 2]
    outs = refs[count + 2 :]
    for feat, at, out in zip(feats, spans, outs):
        pre = dot(feat[at : at + rows, :], weight[...])
        turned = edge_data(feat, at, rows).T
        for k in range(fanout):
            act = pre + edge_length(turned, fanout, k) * vec[...]
            out[k * rows : (k + 1) * rows, :] = slope(act).astype(BF16)


def halo_rows(state, pick, parts):
    stacked = jnp.concatenate(
        [state[:, i * LANES : (i + 1) * LANES] for i in range(parts)], axis=0
    )
    return dot(pick, stacked).astype(BF16)


def join_pieces(pieces, parts):
    count = pieces.shape[0]
    shape = (count // parts, count)
    return jnp.concatenate(
        [
            dot(mark(iota(shape, 1) == iota(shape, 0) * parts + i), pieces).astype(BF16)
            for i in range(parts)
        ],
        axis=1,
    )


def cut_pieces(rows, parts):
    count = rows.shape[0]
    shape = (count * parts, count)
    total = None
    for i in range(parts):
        onehot = mark(iota(shape, 0) == iota(shape, 1) * parts + i)
        piece = dot(onehot, rows[:, i * LANES : (i + 1) * LANES])
        total = piece if total is None else total + piece
    return total.astype(BF16)


def add_pieces(pieces, pick_t, block, parts):
    total = dot(pick_t, pieces)
    return jnp.concatenate([total[i * block : (i + 1) * block] for i in range(parts)], axis=1)


def start_kernel(parts, sums, *refs):
    received, (init, weight, pick, state, mesh_pre, halo) = refs[:-6], refs[-6:]
    agg = sums[...]
    for ref in received:
        agg = agg + ref[...].astype(F32)
    pre = dot(agg.astype(BF16), weight[...])
    mesh_pre[...] = pre
    new = (init[...].astype(F32) + silu(pre)).astype(BF16)
    state[...] = new
    halo[...] = halo_rows(new, pick[...], parts)


def layer_forward(state, pieces, source, weights, parts):
    block = state.shape[0]
    halo = join_pieces(pieces, parts)
    table = jnp.concatenate([state, halo], axis=0)
    from_src = 0.5 * dot(table, weights(0))
    to_dst = 0.5 * dot(state, weights(1))
    gathered = dot(source[...], jnp.concatenate(halves(from_src), axis=0))
    agg = jnp.zeros(state.shape, F32)
    slopes = []
    for k in range(source.shape[0] // block):
        joined = gathered[k * block : (k + 1) * block] + to_dst
        bend = jnp.tanh(joined)
        agg = agg + (joined + joined * bend)
        slopes.append((1.0 + bend + joined * (1.0 - bend * bend)).astype(BF16))
    mixed = dot(state, weights(2)) + dot(agg.astype(BF16), weights(3))
    return mixed, slopes


def layer_back(grad, mixed, slopes, source_t, weights):
    block = grad.shape[0]
    normed, scale = norm_parts(mixed)
    grad_mixed = norm_back(grad, normed, scale)
    grad_state = grad + back_dot(grad_mixed, weights(2))
    grad_agg = 0.5 * back_dot(grad_mixed, weights(3))
    total = jnp.zeros(grad.shape, F32)
    pieces = []
    for found in slopes:
        piece = grad_agg * found.astype(F32)
        total = total + piece
        pieces.append(piece.astype(BF16))
    grad_src = dot(source_t[...], jnp.concatenate(pieces, axis=0))
    grad_state = grad_state + back_dot(total, weights(1))
    grad_table = back_dot(grad_src, weights(0))
    return grad_state + grad_table[:block], grad_table[block:]


def layer_weights(weights, layer):
    return lambda i: weights[layer, i]


def first_kernel(
    layer, parts, state, pieces, source, weights, pick, new, mixed, slopes, halo
):
    block = state.shape[0]
    own = state[...]
    used = layer_weights(weights, layer)
    value, found = layer_forward(own, pieces[...], source, used, parts)
    mixed[...] = value
    for k, part in enumerate(found):
        slopes[k * block : (k + 1) * block, :] = part
    normed, _ = norm_parts(value)
    result = (own.astype(F32) + silu(normed)).astype(BF16)
    new[...] = result
    halo[...] = halo_rows(result, pick[...], parts)


def last_kernel(
    layer, parts, state, pieces, source, source_t, weights, cot, out, grad_own, grad_halo
):
    own = state[...]
    used = layer_weights(weights, layer)
    value, found = layer_forward(own, pieces[...], source, used, parts)
    normed, _ = norm_parts(value)
    out[...] = (own.astype(F32) + silu(normed)).astype(BF16)
    mine, sent = layer_back(cot[...].astype(F32), value, found, source_t, used)
    grad_own[...] = mine
    grad_halo[...] = cut_pieces(sent.astype(BF16), parts)


def back_kernel(
    layer,
    parts,
    mine,
    returned,
    pick_t,
    mixed,
    slopes,
    source_t,
    weights,
    grad_own,
    grad_halo,
):
    block = mine.shape[0]
    grad = mine[...] + add_pieces(returned[...], pick_t[...], block, parts)
    fan = slopes.shape[0] // block
    found = [slopes[k * block : (k + 1) * block, :] for k in range(fan)]
    used = layer_weights(weights, layer)
    own, sent = layer_back(grad, mixed[...], found, source_t, used)
    grad_own[...] = own
    grad_halo[...] = cut_pieces(sent.astype(BF16), parts)


def mesh_back_kernel(parts, mine, returned, pick_t, mesh_pre, weight, out):
    block = mine.shape[0]
    grad = mine[...] + add_pieces(returned[...], pick_t[...], block, parts)
    out[...] = back_dot(grad * slope(mesh_pre[...]), weight[...]).astype(BF16)


def edge_marks(feat, at, rows, nodes, block, fanout, who):
    turned = edge_data(feat, at, rows).T
    ids = iota((rows, nodes * block), 1)
    return [
        mark(
            ids
            == spot_of(
                lambda t: turned[:, t : t + 1], fanout, k, who[0], who[1], nodes, block
            )
        )
        for k in range(fanout)
    ]


def mark_kernel(spans, rows, nodes, block, fanout, who, *refs):
    feats, outs = refs[: len(spans)], refs[len(spans) :]
    for feat, at, out in zip(feats, spans, outs):
        for k, found in enumerate(edge_marks(feat, at, rows, nodes, block, fanout, who)):
            out[k * rows : (k + 1) * rows, :] = found


def message_back_kernel(spans, rows, ready, nodes, block, fanout, who, *refs):
    count = len(spans)
    feats, slopes = refs[:count], refs[count : 2 * count]
    outs = refs[2 * count :]
    grads, outs = outs[:nodes], outs[nodes:]
    marks = []
    for feat, at in zip(feats, spans):
        if ready:
            marks.append(feat[...])
        else:
            marks += edge_marks(feat, at, rows, nodes, block, fanout, who)
    picked = dot(
        jnp.concatenate(marks, axis=0), jnp.concatenate([ref[...] for ref in grads], axis=0)
    )
    per = count // len(outs)
    for i in range(count):
        total = jnp.zeros((rows, outs[0].shape[1]), F32)
        for k in range(fanout):
            at = (i * fanout + k) * rows
            part = slopes[i][k * rows : (k + 1) * rows, :].astype(F32)
            total = total + picked[at : at + rows] * part
        out, at = outs[i // per], i % per * rows
        out[at : at + rows, :] = total.astype(out.dtype)
    for out in outs:
        spare = out.shape[0] - per * rows
        if spare:
            out[per * rows :, :] = jnp.zeros((spare, out.shape[1]), out.dtype)


def grid_back_kernel(*refs):
    *parts, weight, out = refs
    rows = out.shape[0]
    total = parts[0][:rows, :].astype(F32)
    for ref in parts[1:]:
        total = total + ref[:rows, :].astype(F32)
    out[...] = back_dot(total, weight[...]).astype(BF16)


def call(kernel, outs, args, smem=0, scratch=(), space=pltpu.VMEM, aliases=None):
    specs = [pl.BlockSpec(memory_space=pltpu.SMEM)] * smem
    specs += [pl.BlockSpec(memory_space=space)] * (len(args) - smem)
    moved = sum(a.size * a.dtype.itemsize for a in list(args) + list(outs))
    held = sum(math.prod(a.shape) * 4 for a in scratch)
    limit = 2 * (moved + held) + 6 * MIB
    result = pl.pallas_call(
        kernel,
        out_shape=list(outs),
        in_specs=specs,
        out_specs=[pl.BlockSpec(memory_space=pltpu.VMEM)] * len(outs),
        scratch_shapes=list(scratch),
        input_output_aliases=aliases or {},
        compiler_params=pltpu.CompilerParams(vmem_limit_bytes=limit),
        cost_estimate=pl.CostEstimate(
            flops=0, bytes_accessed=moved, transcendentals=0
        ),
    )(*args)
    return result


def shape(dims, dtype):
    return jax.ShapeDtypeStruct(dims, dtype)


def swap(value, axis, apart):
    size = lax.axis_size(axis)
    return lax.ppermute(value, axis, [(i, i ^ apart) for i in range(size)])


def body(
    grid_feat,
    edge_len,
    g2m_owner,
    g2m_dst,
    enc_weight,
    enc_vec,
    mesh_init,
    mesh_weight,
    halo_send,
    mesh_src,
    proc_weight,
    cot,
):
    nodes = lax.axis_size("node")
    sects = lax.axis_size("sect")
    width = grid_feat.shape[1]
    grid_rows, fanout = edge_len.shape
    block = mesh_init.shape[1]
    parts = width // LANES
    both = ("sect", "node")
    who = jnp.stack([lax.axis_index("sect"), lax.axis_index("node")]).astype(jnp.int32)

    axes = [1 << i for i in range(sects.bit_length() - 1)]
    part_rows = grid_rows // len(axes)
    ends = pltpu.VMEM((fanout, grid_rows), jnp.int32)
    packed = call(
        functools.partial(pack_kernel, block),
        [shape((part_rows + META_ROWS, width), BF16)] * len(axes),
        [
            pltpu.with_memory_space_constraint(value, pltpu.HBM)
            for value in (grid_feat, edge_len.T, g2m_owner.T, g2m_dst.T)
        ],
        scratch=[
            pltpu.VMEM((fanout, grid_rows), F32),
            ends,
            ends,
            pltpu.SemaphoreType.DMA((3 + len(axes),)),
        ],
        space=pltpu.HBM,
    )
    where = {(0, p): (part, 0) for p, part in enumerate(packed)}
    steps = [[(0, p) for p in range(len(axes))]]
    held, names = list(packed), [[0] for _ in axes]
    for step in range(len(axes)):
        given = [
            swap(part, "sect", axes[(p + step) % len(axes)]) for p, part in enumerate(held)
        ]
        steps.append([])
        for p, part in enumerate(given):
            axis = axes[(p + step) % len(axes)]
            for i, j in enumerate(list(names[p])):
                where[j ^ axis, p] = (part, i * packed[0].shape[0])
                names[p].append(j ^ axis)
                steps[-1].append((j ^ axis, p))
        held = [jnp.concatenate(pair, axis=0) for pair in zip(held, given)]
    vec = enc_vec[None, :]
    half = nodes // 2
    sums_shape = shape((nodes * block, width), F32)

    def encode(units, last, before):
        edges = len(units) * part_rows * fanout
        used = [where[unit] for unit in units]
        args = [who, *(part for part, _ in used), enc_weight, vec, *before]
        outs = [
            shape((half * block, width), BF16) if last else sums_shape,
            shape((edges, width), BF16),
            shape((1, edges), jnp.int32),
        ]
        return call(
            functools.partial(
                encode_kernel,
                tuple(at for _, at in used),
                nodes,
                block,
                fanout,
                part_rows,
                last,
            ),
            outs if last else outs[:1],
            args,
            smem=1,
            scratch=() if last else [pltpu.VMEM(s.shape, s.dtype) for s in outs[1:]],
            aliases={len(args) - 1: 0} if before and not last else None,
        )

    before = []
    for units in steps[:-1]:
        before = encode(units, False, before)
    sends = halo_send[0, 0].transpose(0, 2, 1)
    src_row = mesh_src[0].T
    fan = src_row.shape[0]
    pieces = halo_send[0, 0].size * parts
    table_len = block + halo_send[0, 0].size
    found = call(
        functools.partial(index_kernel, block, parts),
        [
            shape((pieces, parts * block), BF16),
            shape((parts * block, pieces), BF16),
            shape((fan * block, 2 * table_len), BF16),
            shape((table_len, fan * block), BF16),
        ],
        [sends, src_row],
    )
    *before, pick, pick_t, source, source_t = lax.optimization_barrier((*before, *found))
    cross, message, spots = encode(steps[-1], True, before)
    (keep,) = call(
        keep_kernel, [shape((half * block, width), BF16)], [message, spots, *before]
    )

    pair = keep.astype(F32) + swap(cross, "node", 1).astype(F32)
    pair = pair.reshape(half, block, width)
    arrived = [swap(pair[q].astype(BF16), "node", 2 * q) for q in range(1, half)]

    units = [(j, p) for j in range(sects) for p in range(len(axes))]
    slopes = call(
        functools.partial(
            slope_kernel, tuple(where[unit][1] for unit in units), fanout, part_rows
        ),
        [shape((fanout * part_rows, width), BF16)] * len(units),
        [*(where[unit][0] for unit in units), enc_weight, vec],
    )
    tied = lax.optimization_barrier((*arrived, *slopes))
    arrived, slopes = tied[: half - 1], dict(zip(units, tied[half - 1 :]))

    halo_shape = shape((pieces, LANES), BF16)
    row_low, row_high = shape((block, width), BF16), shape((block, width), F32)

    def exchange(value):
        return lax.all_to_all(value, both, split_axis=0, concat_axis=0, tiled=True)

    state, mesh_pre, halo = call(
        functools.partial(start_kernel, parts),
        [row_low, row_high, halo_shape],
        [pair[0], *arrived, mesh_init[0], mesh_weight, pick],
    )
    assert proc_weight.shape[0] == 2
    state, mixed, slope_first, halo = call(
        functools.partial(first_kernel, 0, parts),
        [row_low, row_high, shape((fan * block, width), BF16), halo_shape],
        [state, exchange(halo), source, proc_weight, pick],
    )
    mesh_out, grad, halo = call(
        functools.partial(last_kernel, 1, parts),
        [row_low, row_high, halo_shape],
        [state, exchange(halo), source, source_t, proc_weight, cot[0]],
    )
    grad, halo = call(
        functools.partial(back_kernel, 0, parts),
        [row_high, halo_shape],
        [grad, exchange(halo), pick_t, mixed, slope_first, source_t, proc_weight],
    )
    (grad_sum,) = call(
        functools.partial(mesh_back_kernel, parts),
        [row_low],
        [grad, exchange(halo), pick_t, mesh_pre, mesh_weight],
    )

    same = [grad_sum] + [swap(grad_sum, "node", 2 * q) for q in range(1, half)]
    ready = nodes * block <= 8 * LANES
    picks_of = {unit: where[unit] for unit in units}
    if ready:
        seen, _ = lax.optimization_barrier((who, grad_sum))
        found = call(
            functools.partial(
                mark_kernel,
                tuple(where[unit][1] for unit in units),
                part_rows,
                nodes,
                block,
                fanout,
            ),
            [shape((fanout * part_rows, nodes * block), BF16)] * len(units),
            [seen, *(where[unit][0] for unit in units)],
            smem=1,
        )
        same[1] = lax.optimization_barrier((same[1], found[0]))[0]
        picks_of = {unit: (part, 0) for unit, part in zip(units, found)}
    other = [swap(rows, "node", 1) for rows in same]
    parts_of = {}
    ahead = []
    gathered = (*same, *other)
    near = [j for j in range(1, sects) if j.bit_count() < len(axes)]
    for group in (near, [sects - 1], [0]):
        if ahead:
            gathered = lax.optimization_barrier((*gathered, *ahead))[: len(gathered)]
        used = [(j, p) for j in group for p in range(len(axes))]
        spare = META_ROWS if group is near else 0
        found = call(
            functools.partial(
                message_back_kernel,
                tuple(picks_of[unit][1] for unit in used),
                part_rows,
                ready,
                nodes,
                block,
                fanout,
            ),
            [shape((grid_rows + spare, width), BF16)] * len(group),
            [
                who,
                *(picks_of[unit][0] for unit in used),
                *(slopes[unit] for unit in used),
                *gathered,
            ],
            smem=1,
        )
        ahead = found[:1]
        for j, grad_pre in zip(group, found):
            parts_of[j] = swap(grad_pre, "sect", j) if j else grad_pre
    mine, *sent = (parts_of[j] for j in range(sects))
    (grid_grad,) = call(
        grid_back_kernel,
        [shape((grid_rows, width), BF16)],
        [mine, *sent, enc_weight],
    )
    return (mesh_out[None], grid_grad)


def solution(mesh):
    return jax.shard_map(
        body,
        mesh=mesh,
        in_specs=(
            P(("sect", "node"), None),
            P(("sect", "node"), None),
            P(("sect", "node"), None),
            P(("sect", "node"), None),
            P(),
            P(),
            P("node", "sect", None),
            P(),
            P("sect", "node", None, None, None),
            P("node", "sect", None),
            P(),
            P("node", "sect", None),
        ),
        out_specs=(P("node", "sect", None), P(("sect", "node"), None)),
        check_vma=False,
    )
```

profile of v0, /device:TPU:0, one launch (start us, length us, event | category | flops | bytes accessed | tf_op | source)
XLA Modules:
  0.0 118.8 jit_solution(8295304881741977205)
XLA Ops:
  0.6 1.1 shard_map.131
  1.7 0.0 copy-start.2
  1.7 0.0 copy-start.7
  1.7 3.0 %collective-permute-start = (bf16[144,512]{1,0:T(8,128)(2,1)S(1)}, bf16[144,512]{1,0:T(8,128)(2,1)S(1)}, u32[]{:S(2)}, u32[]{:S(2)}) collective-permute-start(bf16[144,512]{1,0:T(8,128)(2,1)S(1)} %get-tuple-element.75.refs_0_), channel_id=1, source_target_pairs={{0,8},{8,0},{16,24},{24,16},{1,9},{9,1},{17,25},{25,17},{2,10},{10... | collective-permute-start | bytes 442376 | tf_op jit(solution)/shard_map/ppermute | solution.py:436
  4.7 1.5 %collective-permute-start.2 = (bf16[144,512]{1,0:T(8,128)(2,1)S(1)}, bf16[144,512]{1,0:T(8,128)(2,1)S(1)}, u32[]{:S(2)}, u32[]{:S(2)}) collective-permute-start(bf16[144,512]{1,0:T(8,128)(2,1)S(1)} %get-tuple-element.76.refs_1_), channel_id=1, source_target_pairs={{0,16},{8,24},{16,0},{24,8},{1,17},{9,25},{17,1},{25,9},{2,18},{10... | collective-permute-start | bytes 442376 | tf_op jit(solution)/shard_map/ppermute | solution.py:436
  6.2 2.3 %collective-permute-done.refs_0_.refs_2_ = bf16[144,512]{1,0:T(8,128)(2,1)S(1)} collective-permute-done((bf16[144,512]{1,0:T(8,128)(2,1)S(1)}, bf16[144,512]{1,0:T(8,128)(2,1)S(1)}, u32[]{:S(2)}, u32[]{:S(2)}) %collective-permute-start) | collective-permute-done | bytes 147488 | tf_op jit(solution)/shard_map/ppermute | solution.py:436
  8.6 1.8 %collective-permute-start.1 = (bf16[288,512]{1,0:T(8,128)(2,1)S(1)}, bf16[288,512]{1,0:T(8,128)(2,1)S(1)}, u32[]{:S(2)}, u32[]{:S(2)}) collective-permute-start(bf16[288,512]{1,0:T(8,128)(2,1)S(1)} %pad_maximum_fusion), channel_id=1, source_target_pairs={{0,16},{8,24},{16,0},{24,8},{1,17},{9,25},{17,1},{25,9},{2,18},{10... | collective-permute-start | bytes 884744 | tf_op jit(solution)/shard_map/ppermute | solution.py:436
  10.4 0.0 collective-permute-done.2.refs_1_.refs_5_
  10.5 1.6 %collective-permute-start.3 = (bf16[288,512]{1,0:T(8,128)(2,1)S(1)}, bf16[288,512]{1,0:T(8,128)(2,1)S(1)}, u32[]{:S(2)}, u32[]{:S(2)}) collective-permute-start(bf16[288,512]{1,0:T(8,128)(2,1)S(1)} %pad_maximum_fusion.1), channel_id=1, source_target_pairs={{0,8},{8,0},{16,24},{24,16},{1,9},{9,1},{17,25},{25,17},{2,10},{10... | collective-permute-start | bytes 884744 | tf_op jit(solution)/shard_map/ppermute | solution.py:436
  12.0 0.7 copy-done.8
  12.7 0.7 copy-done.9
  13.4 0.7 shard_map.134
  14.1 0.1 pad_add_fusion.who
  14.2 1.0 copy-done.1
  15.2 0.7 copy-done.6
  15.9 1.9 %shard_map.132.refs_4_ = f32[1024,512]{1,0:T(8,128)S(1)} custom-call(s32[2]{0:T(128)S(1)} %pad_add_fusion.who, bf16[144,512]{1,0:T(8,128)(2,1)S(1)} %get-tuple-element.75.refs_0_, bf16[144,512]{1,0:T(8,128)(2,1)S(1)} %get-tuple-element.76.refs_1_, bf16[512,512]{1,0:T(8,128)(2,1)S(1)} %copy-done.1, f32[1,512]{1,0:T(1,128)S(1)} %bitcast.33), custom_call_target="tpu_custom_call" | custom-call | bytes 2918408 | tf_op jit(solution)/shard_map/pallas_call | solution.py:415
  17.8 1.9 %shard_map.133.refs_6_.before = f32[1024,512]{1,0:T(8,128)S(1)} custom-call(s32[2]{0:T(128)S(1)} %pad_add_fusion.who, bf16[144,512]{1,0:T(8,128)(2,1)S(1)} %collective-permute-done.refs_0_.refs_2_, bf16[144,512]{1,0:T(8,128)(2,1)S(1)} %collective-permute-done.2.refs_1_.refs_5_, bf16[512,512]{1,0:T(8,128)(2,1)S(1)} %copy-done.2, ...), custom_call_target="tpu_custom_call", output_to_operand_aliasing={{}: (5, {})} | custom-call | bytes 5015560 | tf_op jit(solution)/shard_map/pallas_call | solution.py:415
  19.7 0.0 collective-permute-done.3.refs_2_.refs_3_.refs_7_
  19.7 2.0 %shard_map.135 = (bf16[512,512]{1,0:T(8,128)(2,1)S(1)}, bf16[1024,512]{1,0:T(8,128)(2,1)S(1)}, s32[1,1024]{1,0:T(1,128)S(1)}) custom-call(s32[2]{0:T(128)S(1)} %pad_add_fusion.who, bf16[288,512]{1,0:T(8,128)(2,1)S(1)} %collective-permute-done.1.refs_0_.refs_1_.refs_4_.refs_6_, bf16[288,512]{1,0:T(8,128)(2,1)S(1)} %collective-permute-done.1.refs_0_.refs_1_.refs_4_.refs_6_, ...), custom_call_target="tpu_custom_call" | custom-call | bytes 5380104 | tf_op jit(solution)/shard_map/pallas_call | solution.py:415
  21.8 0.1 collective-permute-start.4
  21.9 0.7 shard_map.136
  22.6 1.2 collective-permute-done.4
  23.7 0.2 fusion
  23.9 0.0 copy-start.3
  24.0 0.0 copy-start.4
  24.0 1.6 %collective-permute-start.5 = (bf16[128,512]{1,0:T(8,128)(2,1)S(1)}, bf16[128,512]{1,0:T(8,128)(2,1)S(1)}, u32[]{:S(2)}, u32[]{:S(2)}) collective-permute-start(bf16[128,512]{1,0:T(8,128)(2,1)S(1)} %get-tuple-element.152), channel_id=1, source_target_pairs={{0,2},{1,3},{2,0},{3,1},{4,6},{5,7},{6,4},{7,5},{8,10},{9,11},{10,... | collective-permute-start | bytes 393224 | tf_op jit(solution)/shard_map/ppermute | solution.py:436
  25.6 2.6 %collective-permute-start.6 = (bf16[128,512]{1,0:T(8,128)(2,1)S(1)}, bf16[128,512]{1,0:T(8,128)(2,1)S(1)}, u32[]{:S(2)}, u32[]{:S(2)}) collective-permute-start(bf16[128,512]{1,0:T(8,128)(2,1)S(1)} %get-tuple-element.151), channel_id=1, source_target_pairs={{0,4},{1,5},{2,6},{3,7},{4,0},{5,1},{6,2},{7,3},{8,12},{9,13},{10,... | collective-permute-start | bytes 393224 | tf_op jit(solution)/shard_map/ppermute | solution.py:436
  28.2 0.2 collective-permute-start.7
  28.5 2.2 %shard_map.137 = (bf16[256,512]{1,0:T(8,128)(2,1)S(1)}, bf16[256,512]{1,0:T(8,128)(2,1)S(1)}, bf16[256,512]{1,0:T(8,128)(2,1)S(1)}, bf16[256,512]{1,0:T(8,128)(2...) custom-call(bf16[144,512]{1,0:T(8,128)(2,1)S(1)} %get-tuple-element., ...), custom_call_target="tpu_custom_call" | custom-call | bytes 4392960 | tf_op jit(solution)/shard_map/pallas_call | solution.py:415
  30.7 0.8 collective-permute-done.5.refs_0_
  31.5 7.0 %collective-permute-done.6.refs_1_ = bf16[128,512]{1,0:T(8,128)(2,1)S(1)} collective-permute-done((bf16[128,512]{1,0:T(8,128)(2,1)S(1)}, bf16[128,512]{1,0:T(8,128)(2,1)S(1)}, u32[]{:S(2)}, u32[]{:S(2)}) %collective-permute-start.6) | collective-permute-done | bytes 131104 | tf_op jit(solution)/shard_map/ppermute | solution.py:436
  38.5 0.5 shard_map.138
  39.0 11.4 %all_to_all.44 = bf16[32,8,128]{2,1,0:T(8,128)(2,1)S(1)} all-to-all(bf16[32,8,128]{2,1,0:T(8,128)(2,1)S(1)} %bitcast.29), channel_id=1, replica_groups=mesh['sect'=4,'node'=8] {'sect','node'}, dimensions={0} | all-to-all | bytes 131072 | tf_op jit(solution)/shard_map/all_to_all | solution.py:568
  50.4 2.2 %shard_map.139 = (bf16[128,512]{1,0:T(8,128)(2,1)S(1)}, f32[128,512]{1,0:T(8,128)S(1)}, bf16[1024,512]{1,0:T(8,128)(2,1)S(1)}, bf16[256,128]{1,0:T(8,128)(2,1)S(1)}) custom-call(bf16[128,512]{1,0:T(8,128)(2,1)S(1)} %get-tuple-element.97.state, bf16[256,128]{1,0:T(8,128)(2,1)S(1)} %bitcast.24, bf16[1024,384]{1,0:T(8,128)(2,1)S(1)} %get-tuple-element.99.source, ...), custom_call_target="tpu_custom_call" | custom-call | bytes 6946816 | tf_op jit(solution)/shard_map/pallas_call | solution.py:415
  52.6 9.1 %all_to_all.45 = bf16[32,8,128]{2,1,0:T(8,128)(2,1)S(1)} all-to-all(bf16[32,8,128]{2,1,0:T(8,128)(2,1)S(1)} %bitcast.30), channel_id=1, replica_groups=mesh['sect'=4,'node'=8] {'sect','node'}, dimensions={0} | all-to-all | bytes 131072 | tf_op jit(solution)/shard_map/all_to_all | solution.py:568
  61.7 3.9 %shard_map.140 = (bf16[128,512]{1,0:T(8,128)(2,1)}, f32[128,512]{1,0:T(8,128)S(1)}, bf16[256,128]{1,0:T(8,128)(2,1)S(1)}) custom-call(bf16[128,512]{1,0:T(8,128)(2,1)S(1)} %get-tuple-element.100.state, bf16[256,128]{1,0:T(8,128)(2,1)S(1)} %bitcast.25, bf16[1024,384]{1,0:T(8,128)(2,1)S(1)} %get-tuple-element.99.source, ...), custom_call_target="tpu_custom_call" | custom-call | bytes 6160384 | tf_op jit(solution)/shard_map/pallas_call | solution.py:415
  65.6 9.1 %all_to_all.46 = bf16[32,8,128]{2,1,0:T(8,128)(2,1)S(1)} all-to-all(bf16[32,8,128]{2,1,0:T(8,128)(2,1)S(1)} %bitcast.32), channel_id=1, replica_groups=mesh['sect'=4,'node'=8] {'sect','node'}, dimensions={0} | all-to-all | bytes 131072 | tf_op jit(solution)/shard_map/all_to_all | solution.py:568
  74.7 1.9 %shard_map.141 = (f32[128,512]{1,0:T(8,128)S(1)}, bf16[256,128]{1,0:T(8,128)(2,1)S(1)}) custom-call(f32[128,512]{1,0:T(8,128)S(1)} %get-tuple-element.104.mine, bf16[256,128]{1,0:T(8,128)(2,1)S(1)} %bitcast.23, bf16[512,256]{1,0:T(8,128)(2,1)S(1)} %get-tuple-element.106.pick_t, f32[128,512]{1,0:T(8,128)S(1)} %get-tuple-element.107.mixed, ...), custom_call_target="tpu_custom_call" | custom-call | bytes 6815744 | tf_op jit(solution)/shard_map/pallas_call | solution.py:415
  76.6 9.1 %all_to_all.47 = bf16[32,8,128]{2,1,0:T(8,128)(2,1)S(1)} all-to-all(bf16[32,8,128]{2,1,0:T(8,128)(2,1)S(1)} %bitcast.31), channel_id=1, replica_groups=mesh['sect'=4,'node'=8] {'sect','node'}, dimensions={0} | all-to-all | bytes 131072 | tf_op jit(solution)/shard_map/all_to_all | solution.py:568
  85.7 0.5 shard_map.142.refs_8_.refs_4_
  86.2 0.5 collective-permute-start.8
  86.7 0.8 collective-permute-start.9
  87.5 3.1 %collective-permute-start.10 = (bf16[128,512]{1,0:T(8,128)(2,1)S(1)}, bf16[128,512]{1,0:T(8,128)(2,1)S(1)}, u32[]{:S(2)}, u32[]{:S(2)}) collective-permute-start(bf16[128,512]{1,0:T(8,128)(2,1)S(1)} %shard_map.142.refs_8_.refs_4_), channel_id=1, source_target_pairs={{0,6},{1,7},{2,4},{3,5},{4,2},{5,3},{6,0},{7,1},{8,14},{9,15},{10,... | collective-permute-start | bytes 393224 | tf_op jit(solution)/shard_map/ppermute | solution.py:436
  90.6 0.0 collective-permute-start.11
  90.6 2.6 %shard_map.143 = (bf16[256,1024]{1,0:T(8,128)(2,1)S(1)}, bf16[256,1024]{1,0:T(8,128)(2,1)S(1)}, bf16[256,1024]{1,0:T(8,128)(2,1)S(1)}, bf16[256,1024]{1,0:T(8,12...) custom-call(s32[2]{0:T(128)S(1)} %pad_add_fusion.who, ...), custom_call_target="tpu_custom_call" | custom-call | bytes 5963784 | tf_op jit(solution)/shard_map/pallas_call | solution.py:415
  93.2 0.1 collective-permute-done.8.refs_9_.refs_5_
  93.3 0.5 collective-permute-start.12
  93.8 5.7 %collective-permute-done.9.refs_10_.refs_6_ = bf16[128,512]{1,0:T(8,128)(2,1)S(1)} collective-permute-done((bf16[128,512]{1,0:T(8,128)(2,1)S(1)}, bf16[128,512]{1,0:T(8,128)(2,1)S(1)}, u32[]{:S(2)}, u32[]{:S(2)}) %collective-permute-start.9) | collective-permute-done | bytes 131104 | tf_op jit(solution)/shard_map/ppermute | solution.py:436
  99.6 0.0 collective-permute-start.13
  99.6 0.0 collective-permute-done.10.refs_11_.refs_7_
  99.6 0.5 collective-permute-start.14
  100.1 0.0 collective-permute-done.11.refs_12_.refs_8_
  100.1 0.0 collective-permute-done.12.refs_13_.refs_9_
  100.1 0.8 collective-permute-done.13.refs_14_.refs_10_
  100.9 0.2 collective-permute-done.14.refs_15_.refs_11_
  101.1 1.8 %shard_map.144 = (bf16[272,512]{1,0:T(8,128)(2,1)S(1)}, bf16[272,512]{1,0:T(8,128)(2,1)S(1)}) custom-call(s32[2]{0:T(128)S(1)} %pad_add_fusion.who, bf16[256,1024]{1,0:T(8,128)(2,1)S(1)} %get-tuple-element.118.refs_0_, bf16[256,1024]{1,0:T(8,128)(2,1)S(1)} %get-tuple-element.119.refs_1_, bf16[256,1024]{1,0:T(8,128)(2,1)S(1)} %get-tuple-element.120.refs_2_, ...), custom_call_target="tpu_custom_call" | custom-call | bytes 4751368 | tf_op jit(solution)/shard_map/pallas_call | solution.py:415
  102.9 0.5 collective-permute-start.15
  103.4 0.8 collective-permute-start.16
  104.2 1.3 %shard_map.145 = bf16[256,512]{1,0:T(8,128)(2,1)S(1)} custom-call(s32[2]{0:T(128)S(1)} %pad_add_fusion.who, bf16[256,1024]{1,0:T(8,128)(2,1)S(1)} %get-tuple-element.135.refs_0_, bf16[256,1024]{1,0:T(8,128)(2,1)S(1)} %get-tuple-element.136.refs_1_, bf16[256,512]{1,0:T(8,128)(2,1)S(1)} %get-tuple-element.137.refs_2_, ...), custom_call_target="tpu_custom_call" | custom-call | bytes 2883592 | tf_op jit(solution)/shard_map/pallas_call | solution.py:415
  105.5 2.3 %collective-permute-start.17 = (bf16[256,512]{1,0:T(8,128)(2,1)S(1)}, bf16[256,512]{1,0:T(8,128)(2,1)S(1)}, u32[]{:S(2)}, u32[]{:S(2)}) collective-permute-start(bf16[256,512]{1,0:T(8,128)(2,1)S(1)} %shard_map.145), channel_id=1, source_target_pairs={{0,24},{8,16},{16,8},{24,0},{1,25},{9,17},{17,9},{25,1},{2,26},{10... | collective-permute-start | bytes 786440 | tf_op jit(solution)/shard_map/ppermute | solution.py:436
  107.8 1.3 %shard_map.146.refs_0_ = bf16[256,512]{1,0:T(8,128)(2,1)S(1)} custom-call(s32[2]{0:T(128)S(1)} %pad_add_fusion.who, bf16[256,1024]{1,0:T(8,128)(2,1)S(1)} %get-tuple-element.113.refs_0_, bf16[256,1024]{1,0:T(8,128)(2,1)S(1)} %get-tuple-element.114.refs_1_, bf16[256,512]{1,0:T(8,128)(2,1)S(1)} %get-tuple-element.115.refs_2_, ...), custom_call_target="tpu_custom_call" | custom-call | bytes 2883592 | tf_op jit(solution)/shard_map/pallas_call | solution.py:415
  109.1 8.6 %collective-permute-done.17.refs_3_ = bf16[256,512]{1,0:T(8,128)(2,1)S(1)} collective-permute-done((bf16[256,512]{1,0:T(8,128)(2,1)S(1)}, bf16[256,512]{1,0:T(8,128)(2,1)S(1)}, u32[]{:S(2)}, u32[]{:S(2)}) %collective-permute-start.17) | collective-permute-done | bytes 262176 | tf_op jit(solution)/shard_map/ppermute | solution.py:436
  117.7 0.0 collective-permute-done.16.refs_2_
  117.7 1.2 shard_map.147
  (19 shorter events, 0.1 us)
Async XLA Ops:
  1.7 16.1 %copy-start.2 = (bf16[512,512]{1,0:T(8,128)(2,1)S(1)}, bf16[512,512]{1,0:T(8,128)(2,1)}, u32[]{:S(2)}) copy-start(bf16[512,512]{1,0:T(8,128)(2,1)} %refs_4_.5) | copy-start | bytes 1572868
  1.7 16.1 %copy-start.7 = (f32[512]{0:T(512)S(1)}, f32[512]{0:T(512)}, u32[]{:S(2)}) copy-start(f32[512]{0:T(512)} %param.17) | copy-start | bytes 6148
  1.7 6.9 %collective-permute-start = (bf16[144,512]{1,0:T(8,128)(2,1)S(1)}, bf16[144,512]{1,0:T(8,128)(2,1)S(1)}, u32[]{:S(2)}, u32[]{:S(2)}) collective-permute-start(bf16[144,512]{1,0:T(8,128)(2,1)S(1)} %get-tuple-element.75.refs_0_), channel_id=1, source_target_pairs={{0,8},{8,0},{16,24},{24,16},{1,9},{9,1},{17,25},{25,17},{2,10},{10... | collective-permute-start | bytes 442376 | tf_op jit(solution)/shard_map/ppermute | solution.py:436
  4.7 5.7 %collective-permute-start.2 = (bf16[144,512]{1,0:T(8,128)(2,1)S(1)}, bf16[144,512]{1,0:T(8,128)(2,1)S(1)}, u32[]{:S(2)}, u32[]{:S(2)}) collective-permute-start(bf16[144,512]{1,0:T(8,128)(2,1)S(1)} %get-tuple-element.76.refs_1_), channel_id=1, source_target_pairs={{0,16},{8,24},{16,0},{24,8},{1,17},{9,25},{17,1},{25,9},{2,18},{10... | collective-permute-start | bytes 442376 | tf_op jit(solution)/shard_map/ppermute | solution.py:436
  8.6 11.1 %collective-permute-start.1 = (bf16[288,512]{1,0:T(8,128)(2,1)S(1)}, bf16[288,512]{1,0:T(8,128)(2,1)S(1)}, u32[]{:S(2)}, u32[]{:S(2)}) collective-permute-start(bf16[288,512]{1,0:T(8,128)(2,1)S(1)} %pad_maximum_fusion), channel_id=1, source_target_pairs={{0,16},{8,24},{16,0},{24,8},{1,17},{9,25},{17,1},{25,9},{2,18},{10... | collective-permute-start | bytes 884744 | tf_op jit(solution)/shard_map/ppermute | solution.py:436
  10.5 9.3 %collective-permute-start.3 = (bf16[288,512]{1,0:T(8,128)(2,1)S(1)}, bf16[288,512]{1,0:T(8,128)(2,1)S(1)}, u32[]{:S(2)}, u32[]{:S(2)}) collective-permute-start(bf16[288,512]{1,0:T(8,128)(2,1)S(1)} %pad_maximum_fusion.1), channel_id=1, source_target_pairs={{0,8},{8,0},{16,24},{24,16},{1,9},{9,1},{17,25},{25,17},{2,10},{10... | collective-permute-start | bytes 884744 | tf_op jit(solution)/shard_map/ppermute | solution.py:436
  12.0 0.7 copy-start.8
  12.7 0.7 copy-start.9
  14.1 1.0 copy-start.1
  15.2 0.7 copy-start.6
  21.8 2.0 %collective-permute-start.4 = (bf16[512,512]{1,0:T(8,128)(2,1)S(1)}, bf16[512,512]{1,0:T(8,128)(2,1)S(1)}, u32[]{:S(2)}, u32[]{:S(2)}) collective-permute-start(bf16[512,512]{1,0:T(8,128)(2,1)S(1)} %get-tuple-element.84), channel_id=1, source_target_pairs={{0,1},{1,0},{2,3},{3,2},{4,5},{5,4},{6,7},{7,6},{8,9},{9,8},{10,11... | collective-permute-start | bytes 1572872 | tf_op jit(solution)/shard_map/ppermute | solution.py:436
  23.9 14.6 %copy-start.3 = (bf16[512,512]{1,0:T(8,128)(2,1)S(1)}, bf16[512,512]{1,0:T(8,128)(2,1)}, u32[]{:S(2)}) copy-start(bf16[512,512]{1,0:T(8,128)(2,1)} %weight.1) | copy-start | bytes 1572868
  24.0 14.6 %copy-start.4 = (bf16[1,128,512]{2,1,0:T(8,128)(2,1)S(1)}, bf16[1,128,512]{2,1,0:T(8,128)(2,1)}, u32[]{:S(2)}) copy-start(bf16[1,128,512]{2,1,0:T(8,128)(2,1)} %param.18) | copy-start | bytes 393220
  24.0 7.5 %collective-permute-start.5 = (bf16[128,512]{1,0:T(8,128)(2,1)S(1)}, bf16[128,512]{1,0:T(8,128)(2,1)S(1)}, u32[]{:S(2)}, u32[]{:S(2)}) collective-permute-start(bf16[128,512]{1,0:T(8,128)(2,1)S(1)} %get-tuple-element.152), channel_id=1, source_target_pairs={{0,2},{1,3},{2,0},{3,1},{4,6},{5,7},{6,4},{7,5},{8,10},{9,11},{10,... | collective-permute-start | bytes 393224 | tf_op jit(solution)/shard_map/ppermute | solution.py:436
  25.6 12.9 %collective-permute-start.6 = (bf16[128,512]{1,0:T(8,128)(2,1)S(1)}, bf16[128,512]{1,0:T(8,128)(2,1)S(1)}, u32[]{:S(2)}, u32[]{:S(2)}) collective-permute-start(bf16[128,512]{1,0:T(8,128)(2,1)S(1)} %get-tuple-element.151), channel_id=1, source_target_pairs={{0,4},{1,5},{2,6},{3,7},{4,0},{5,1},{6,2},{7,3},{8,12},{9,13},{10,... | collective-permute-start | bytes 393224 | tf_op jit(solution)/shard_map/ppermute | solution.py:436
  28.2 22.2 %copy-start = (bf16[2,4,512,512]{3,2,1,0:T(8,128)(2,1)S(1)}, bf16[2,4,512,512]{3,2,1,0:T(8,128)(2,1)}, u32[]{:S(2)}) copy-start(bf16[2,4,512,512]{3,2,1,0:T(8,128)(2,1)} %weights.5) | copy-start | bytes 12582916
  28.2 10.3 %collective-permute-start.7 = (bf16[128,512]{1,0:T(8,128)(2,1)S(1)}, bf16[128,512]{1,0:T(8,128)(2,1)S(1)}, u32[]{:S(2)}, u32[]{:S(2)}) collective-permute-start(bf16[128,512]{1,0:T(8,128)(2,1)S(1)} %get-tuple-element.150), channel_id=1, source_target_pairs={{0,6},{1,7},{2,4},{3,5},{4,2},{5,3},{6,0},{7,1},{8,14},{9,15},{10,... | collective-permute-start | bytes 393224 | tf_op jit(solution)/shard_map/ppermute | solution.py:436
  50.4 11.3 %copy-start.5 = (bf16[1,128,512]{2,1,0:T(8,128)(2,1)S(1)}, bf16[1,128,512]{2,1,0:T(8,128)(2,1)}, u32[]{:S(2)}) copy-start(bf16[1,128,512]{2,1,0:T(8,128)(2,1)} %param.23) | copy-start | bytes 393220
  86.2 7.2 %collective-permute-start.8 = (bf16[128,512]{1,0:T(8,128)(2,1)S(1)}, bf16[128,512]{1,0:T(8,128)(2,1)S(1)}, u32[]{:S(2)}, u32[]{:S(2)}) collective-permute-start(bf16[128,512]{1,0:T(8,128)(2,1)S(1)} %shard_map.142.refs_8_.refs_4_), channel_id=1, source_target_pairs={{0,2},{1,3},{2,0},{3,1},{4,6},{5,7},{6,4},{7,5},{8,10},{9,11},{10,... | collective-permute-start | bytes 393224 | tf_op jit(solution)/shard_map/ppermute | solution.py:436
  86.7 12.9 %collective-permute-start.9 = (bf16[128,512]{1,0:T(8,128)(2,1)S(1)}, bf16[128,512]{1,0:T(8,128)(2,1)S(1)}, u32[]{:S(2)}, u32[]{:S(2)}) collective-permute-start(bf16[128,512]{1,0:T(8,128)(2,1)S(1)} %shard_map.142.refs_8_.refs_4_), channel_id=1, source_target_pairs={{0,4},{1,5},{2,6},{3,7},{4,0},{5,1},{6,2},{7,3},{8,12},{9,13},{10,... | collective-permute-start | bytes 393224 | tf_op jit(solution)/shard_map/ppermute | solution.py:436
  87.5 12.1 %collective-permute-start.10 = (bf16[128,512]{1,0:T(8,128)(2,1)S(1)}, bf16[128,512]{1,0:T(8,128)(2,1)S(1)}, u32[]{:S(2)}, u32[]{:S(2)}) collective-permute-start(bf16[128,512]{1,0:T(8,128)(2,1)S(1)} %shard_map.142.refs_8_.refs_4_), channel_id=1, source_target_pairs={{0,6},{1,7},{2,4},{3,5},{4,2},{5,3},{6,0},{7,1},{8,14},{9,15},{10,... | collective-permute-start | bytes 393224 | tf_op jit(solution)/shard_map/ppermute | solution.py:436
  90.6 9.4 %collective-permute-start.11 = (bf16[128,512]{1,0:T(8,128)(2,1)S(1)}, bf16[128,512]{1,0:T(8,128)(2,1)S(1)}, u32[]{:S(2)}, u32[]{:S(2)}) collective-permute-start(bf16[128,512]{1,0:T(8,128)(2,1)S(1)} %shard_map.142.refs_8_.refs_4_), channel_id=1, source_target_pairs={{0,1},{1,0},{2,3},{3,2},{4,5},{5,4},{6,7},{7,6},{8,9},{9,8},{10,11... | collective-permute-start | bytes 393224 | tf_op jit(solution)/shard_map/ppermute | solution.py:436
  93.3 6.7 %collective-permute-start.12 = (bf16[128,512]{1,0:T(8,128)(2,1)S(1)}, bf16[128,512]{1,0:T(8,128)(2,1)S(1)}, u32[]{:S(2)}, u32[]{:S(2)}) collective-permute-start(bf16[128,512]{1,0:T(8,128)(2,1)S(1)} %collective-permute-done.8.refs_9_.refs_5_), channel_id=1, source_target_pairs={{0,1},{1,0},{2,3},{3,2},{4,5},{5,4},{6,7},{7,6},{8,9},{9,8},{10,11... | collective-permute-start | bytes 393224 | tf_op jit(solution)/shard_map/ppermute | solution.py:436
  99.6 1.3 %collective-permute-start.13 = (bf16[128,512]{1,0:T(8,128)(2,1)S(1)}, bf16[128,512]{1,0:T(8,128)(2,1)S(1)}, u32[]{:S(2)}, u32[]{:S(2)}) collective-permute-start(bf16[128,512]{1,0:T(8,128)(2,1)S(1)} %collective-permute-done.9.refs_10_.refs_6_), channel_id=1, source_target_pairs={{0,1},{1,0},{2,3},{3,2},{4,5},{5,4},{6,7},{7,6},{8,9},{9,8},{10,11... | collective-permute-start | bytes 393224 | tf_op jit(solution)/shard_map/ppermute | solution.py:436
  99.6 1.5 %collective-permute-start.14 = (bf16[128,512]{1,0:T(8,128)(2,1)S(1)}, bf16[128,512]{1,0:T(8,128)(2,1)S(1)}, u32[]{:S(2)}, u32[]{:S(2)}) collective-permute-start(bf16[128,512]{1,0:T(8,128)(2,1)S(1)} %collective-permute-done.10.refs_11_.refs_7_), channel_id=1, source_target_pairs={{0,1},{1,0},{2,3},{3,2},{4,5},{5,4},{6,7},{7,6},{8,9},{9,8},{10,11... | collective-permute-start | bytes 393224 | tf_op jit(solution)/shard_map/ppermute | solution.py:436
  102.9 14.7 %collective-permute-start.15 = (bf16[272,512]{1,0:T(8,128)(2,1)S(1)}, bf16[272,512]{1,0:T(8,128)(2,1)S(1)}, u32[]{:S(2)}, u32[]{:S(2)}) collective-permute-start(bf16[272,512]{1,0:T(8,128)(2,1)S(1)} %get-tuple-element.126), channel_id=1, source_target_pairs={{0,8},{8,0},{16,24},{24,16},{1,9},{9,1},{17,25},{25,17},{2,10},{10... | collective-permute-start | bytes 835592 | tf_op jit(solution)/shard_map/ppermute | solution.py:436
  103.4 14.2 %collective-permute-start.16 = (bf16[272,512]{1,0:T(8,128)(2,1)S(1)}, bf16[272,512]{1,0:T(8,128)(2,1)S(1)}, u32[]{:S(2)}, u32[]{:S(2)}) collective-permute-start(bf16[272,512]{1,0:T(8,128)(2,1)S(1)} %get-tuple-element.147), channel_id=1, source_target_pairs={{0,16},{8,24},{16,0},{24,8},{1,17},{9,25},{17,1},{25,9},{2,18},{10... | collective-permute-start | bytes 835592 | tf_op jit(solution)/shard_map/ppermute | solution.py:436
  105.5 12.1 %collective-permute-start.17 = (bf16[256,512]{1,0:T(8,128)(2,1)S(1)}, bf16[256,512]{1,0:T(8,128)(2,1)S(1)}, u32[]{:S(2)}, u32[]{:S(2)}) collective-permute-start(bf16[256,512]{1,0:T(8,128)(2,1)S(1)} %shard_map.145), channel_id=1, source_target_pairs={{0,24},{8,16},{16,8},{24,0},{1,25},{9,17},{17,9},{25,1},{2,26},{10... | collective-permute-start | bytes 786440 | tf_op jit(solution)/shard_map/ppermute | solution.py:436
where the time goes:
time: 119 us
  blocking collectives  38.6 us (32%)
  Pallas kernels  27.6 us (23%)
  waiting for transfers between devices  26.8 us (23%)
  starting transfers between devices  21.5 us (18%)
  local copies, waits for them, and re-layouts  3.17 us (3%)
    all_to_all x4, blocking collectives, exchange(): return lax.all_to_all(value, both, split_axis=0, concat_axis=0, tiled=True)  38.6 us
    pallas_call x17, Pallas kernels, call(): pl.pallas_call(kernel, out_shape=list(outs), in_specs=specs, out_specs=[p...  27.6 us
    ppermute x18, waiting for transfers between devices, swap(): return lax.ppermute(value, axis, [(i, i ^ apart) for i in range(size)])  26.8 us
    ppermute x18, starting transfers between devices, swap(): return lax.ppermute(value, axis, [(i, i ^ apart) for i in range(size)])  21.5 us
    unnamed x20, local copies, waits for them, and re-layouts  3.13 us
  transfers between devices with their start and end apart: 18, of which 9 were waited for; matrix products, arithmetic and copies ran while one was open for 0% of the time, Pallas kernels for 11%

commit v1 on v0

--- a/solution.py
+++ b/solution.py
@@ -102,7 +102,18 @@
         copy.wait()
 
 
-def index_kernel(block, parts, sends, src_row, pick, pick_t, source, source_t):
+def index_kernel(block, parts, *refs):
+    wanted, far_weight, far_vec = refs[:2], refs[2], refs[3]
+    pick, pick_t, source, source_t, weight, vec, sends, src_row, sems = refs[4:]
+    pairs = ((wanted[0], sends), (wanted[1], src_row), (far_vec, vec), (far_weight, weight))
+    copies = [
+        pltpu.make_async_copy(start, target, sems.at[i])
+        for i, (start, target) in enumerate(pairs)
+    ]
+    for copy in copies:
+        copy.start()
+    for copy in copies[:2]:
+        copy.wait()
     sects, count, nodes = sends.shape
     pieces = pick.shape[0]
     at = iota((1, pieces), 1)
@@ -121,13 +132,14 @@
     pick[...] = mark(iota((pieces, parts * block), 1) == turned)
     table_len = source_t.shape[0]
     column = src_row[...].astype(F32).T.astype(jnp.int32)
-    ids = iota((block, 2 * table_len), 1)
-    ids = jnp.where(ids >= table_len, ids - table_len, ids)
+    ids = iota((block, table_len), 1)
     ids_t = iota((table_len, block), 0)
     for k in range(src_row.shape[0]):
         rows = slice(k * block, (k + 1) * block)
         source[rows, :] = mark(ids == column[:, k : k + 1])
         source_t[:, rows] = mark(ids_t == src_row[k : k + 1, :])
+    for copy in copies[2:]:
+        copy.wait()
 
 
 def edge_data(feat, at, rows):
@@ -255,7 +267,7 @@
     table = jnp.concatenate([state, halo], axis=0)
     from_src = 0.5 * dot(table, weights(0))
     to_dst = 0.5 * dot(state, weights(1))
-    gathered = dot(source[...], jnp.concatenate(halves(from_src), axis=0))
+    gathered = dot(source[...], from_src.astype(BF16))
     agg = jnp.zeros(state.shape, F32)
     slopes = []
     for k in range(source.shape[0] // block):
@@ -391,19 +403,15 @@
             total = total + picked[at : at + rows] * part
         out, at = outs[i // per], i % per * rows
         out[at : at + rows, :] = total.astype(out.dtype)
-    for out in outs:
-        spare = out.shape[0] - per * rows
-        if spare:
-            out[per * rows :, :] = jnp.zeros((spare, out.shape[1]), out.dtype)
 
 
 def grid_back_kernel(*refs):
     *parts, weight, out = refs
-    rows = out.shape[0]
-    total = parts[0][:rows, :].astype(F32)
-    for ref in parts[1:]:
-        total = total + ref[:rows, :].astype(F32)
-    out[...] = back_dot(total, weight[...]).astype(BF16)
+    count = len(parts) // 2
+    total = [
+        mine[...] + given[...].astype(F32) for mine, given in zip(parts[:count], parts[count:])
+    ]
+    out[...] = back_dot(jnp.concatenate(total, axis=0), weight[...]).astype(BF16)
 
 
 def call(kernel, outs, args, smem=0, scratch=(), space=pltpu.VMEM, aliases=None):
@@ -492,14 +500,40 @@
                 names[p].append(j ^ axis)
                 steps[-1].append((j ^ axis, p))
         held = [jnp.concatenate(pair, axis=0) for pair in zip(held, given)]
-    vec = enc_vec[None, :]
+    sends = halo_send[0, 0].transpose(0, 2, 1)
+    src_row = mesh_src[0].T
+    fan = src_row.shape[0]
+    pieces = sends.size * parts
+    table_len = block + sends.size
+    pick, pick_t, source, source_t, weight, vec = call(
+        functools.partial(index_kernel, block, parts),
+        [
+            shape((pieces, parts * block), BF16),
+            shape((parts * block, pieces), BF16),
+            shape((fan * block, table_len), BF16),
+            shape((table_len, fan * block), BF16),
+            shape(enc_weight.shape, BF16),
+            shape((1, width), F32),
+        ],
+        [
+            pltpu.with_memory_space_constraint(value, pltpu.HBM)
+            for value in (sends, src_row, enc_weight, enc_vec[None, :])
+        ],
+        scratch=[
+            pltpu.VMEM(sends.shape, jnp.int32),
+            pltpu.VMEM(src_row.shape, jnp.int32),
+            pltpu.SemaphoreType.DMA((4,)),
+        ],
+        space=pltpu.HBM,
+    )
+
     half = nodes // 2
     sums_shape = shape((nodes * block, width), F32)
 
     def encode(units, last, before):
         edges = len(units) * part_rows * fanout
         used = [where[unit] for unit in units]
-        args = [who, *(part for part, _ in used), enc_weight, vec, *before]
+        args = [who, *(part for part, _ in used), weight, vec, *before]
         outs = [
             shape((half * block, width), BF16) if last else sums_shape,
             shape((edges, width), BF16),
@@ -525,22 +559,6 @@
     before = []
     for units in steps[:-1]:
         before = encode(units, False, before)
-    sends = halo_send[0, 0].transpose(0, 2, 1)
-    src_row = mesh_src[0].T
-    fan = src_row.shape[0]
-    pieces = halo_send[0, 0].size * parts
-    table_len = block + halo_send[0, 0].size
-    found = call(
-        functools.partial(index_kernel, block, parts),
-        [
-            shape((pieces, parts * block), BF16),
-            shape((parts * block, pieces), BF16),
-            shape((fan * block, 2 * table_len), BF16),
-            shape((table_len, fan * block), BF16),
-        ],
-        [sends, src_row],
-    )
-    *before, pick, pick_t, source, source_t = lax.optimization_barrier((*before, *found))
     cross, message, spots = encode(steps[-1], True, before)
     (keep,) = call(
         keep_kernel, [shape((half * block, width), BF16)], [message, spots, *before]
@@ -556,7 +574,7 @@
             slope_kernel, tuple(where[unit][1] for unit in units), fanout, part_rows
         ),
         [shape((fanout * part_rows, width), BF16)] * len(units),
-        [*(where[unit][0] for unit in units), enc_weight, vec],
+        [*(where[unit][0] for unit in units), weight, vec],
     )
     tied = lax.optimization_barrier((*arrived, *slopes))
     arrived, slopes = tied[: half - 1], dict(zip(units, tied[half - 1 :]))
@@ -615,16 +633,11 @@
         same[1] = lax.optimization_barrier((same[1], found[0]))[0]
         picks_of = {unit: (part, 0) for unit, part in zip(units, found)}
     other = [swap(rows, "node", 1) for rows in same]
-    parts_of = {}
-    ahead = []
     gathered = (*same, *other)
-    near = [j for j in range(1, sects) if j.bit_count() < len(axes)]
-    for group in (near, [sects - 1], [0]):
-        if ahead:
-            gathered = lax.optimization_barrier((*gathered, *ahead))[: len(gathered)]
-        used = [(j, p) for j in group for p in range(len(axes))]
-        spare = META_ROWS if group is near else 0
-        found = call(
+
+    def message_back(groups, dtype):
+        used = [unit for group in groups for unit in group]
+        return call(
             functools.partial(
                 message_back_kernel,
                 tuple(picks_of[unit][1] for unit in used),
@@ -634,7 +647,7 @@
                 block,
                 fanout,
             ),
-            [shape((grid_rows + spare, width), BF16)] * len(group),
+            [shape((len(group) * part_rows, width), dtype) for group in groups],
             [
                 who,
                 *(picks_of[unit][0] for unit in used),
@@ -643,14 +656,33 @@
             ],
             smem=1,
         )
-        ahead = found[:1]
-        for j, grad_pre in zip(group, found):
-            parts_of[j] = swap(grad_pre, "sect", j) if j else grad_pre
-    mine, *sent = (parts_of[j] for j in range(sects))
+
+    first = [axes[p] for p in range(len(axes))]
+    stay = [[j for j in range(sects) if not j & axis] for axis in first]
+    given = message_back(
+        [[(j ^ axis, p) for j in stay[p]] for p, axis in enumerate(first)], BF16
+    )
+    gathered = lax.optimization_barrier((*gathered, given[0]))[:-1]
+    kept = message_back([[(j, p) for j in stay[p]] for p in range(len(axes))], F32)
+    for step in range(len(axes)):
+        order = [axes[(p + step) % len(axes)] for p in range(len(axes))]
+        given = [swap(part, "sect", axis) for part, axis in zip(given, order)]
+        if step + 1 == len(axes):
+            break
+        kept = [mine + part.astype(F32) for mine, part in zip(kept, given)]
+        given = []
+        for p, axis in enumerate(axes[(p + step + 1) % len(axes)] for p in range(len(axes))):
+            rows = kept[p].reshape(len(stay[p]), part_rows, width)
+            left = [j for j in stay[p] if not j & axis]
+            given.append(
+                jnp.concatenate([rows[stay[p].index(j ^ axis)] for j in left]).astype(BF16)
+            )
+            kept[p] = jnp.concatenate([rows[stay[p].index(j)] for j in left])
+            stay[p] = left
     (grid_grad,) = call(
         grid_back_kernel,
         [shape((grid_rows, width), BF16)],
-        [mine, *sent, enc_weight],
+        [*kept, *given, enc_weight],
     )
     return (mesh_out[None], grid_grad)
 

time: 119 us -> 117 us (0.983)
  local copies, waits for them, and re-layouts: 3.17 us -> 0.15 us
  waiting for transfers between devices: 26.8 us -> 28.3 us
    unnamed x20 -> x10, local copies, waits for them, and re-layouts: 3.13 us -> 0.02 us
    ppermute x18 -> x19, waiting for transfers between devices: 26.8 us -> 28.3 us  [swap(): return lax.ppermute(value, axis, [(i, i ^ apart) for i in range(size)])]
    ppermute x18 -> x19, starting transfers between devices: 21.5 us -> 20.9 us  [swap(): return lax.ppermute(value, axis, [(i, i ^ apart) for i in range(size)])]
    pallas_call x17 -> x16, Pallas kernels: 27.6 us -> 27.2 us  [call(): pl.pallas_call(kernel, out_shape=list(outs), in_specs=specs, out_specs=[p...]
  transfers between devices with their start and end apart: 18 -> 19, of which waited for: 9 -> 12; matrix products, arithmetic and copies ran while one was open for 0% -> 0% of each run, Pallas kernels for 11% -> 11%
where the time goes in v1:
time: 117 us
  blocking collectives  39 us (33%)
  waiting for transfers between devices  28.3 us (24%)
  Pallas kernels  27.2 us (23%)
  starting transfers between devices  20.9 us (18%)
    all_to_all x4, blocking collectives, exchange(): return lax.all_to_all(value, both, split_axis=0, concat_axis=0, tiled=True)  39 us
    ppermute x19, waiting for transfers between devices, swap(): return lax.ppermute(value, axis, [(i, i ^ apart) for i in range(size)])  28.3 us
    pallas_call x16, Pallas kernels, call(): pl.pallas_call(kernel, out_shape=list(outs), in_specs=specs, out_specs=[p...  27.2 us
    ppermute x19, starting transfers between devices, swap(): return lax.ppermute(value, axis, [(i, i ^ apart) for i in range(size)])  20.9 us
  transfers between devices with their start and end apart: 19, of which 12 were waited for; matrix products, arithmetic and copies ran while one was open for 0% of the time, Pallas kernels for 11%

profile of v1, /device:TPU:0, one launch (start us, length us, event | category | flops | bytes accessed | tf_op | source)
XLA Modules:
  0.0 116.9 jit_solution(10604085069630949252)
XLA Ops:
  0.6 1.1 shard_map.131
  1.7 3.0 %collective-permute-start = (bf16[144,512]{1,0:T(8,128)(2,1)S(1)}, bf16[144,512]{1,0:T(8,128)(2,1)S(1)}, u32[]{:S(2)}, u32[]{:S(2)}) collective-permute-start(bf16[144,512]{1,0:T(8,128)(2,1)S(1)} %get-tuple-element.66.refs_0_), channel_id=1, source_target_pairs={{0,8},{8,0},{16,24},{24,16},{1,9},{9,1},{17,25},{25,17},{2,10},{10... | collective-permute-start | bytes 442376 | tf_op jit(solution)/shard_map/ppermute | solution.py:444
  4.7 1.5 %collective-permute-start.2 = (bf16[144,512]{1,0:T(8,128)(2,1)S(1)}, bf16[144,512]{1,0:T(8,128)(2,1)S(1)}, u32[]{:S(2)}, u32[]{:S(2)}) collective-permute-start(bf16[144,512]{1,0:T(8,128)(2,1)S(1)} %get-tuple-element.67.refs_1_), channel_id=1, source_target_pairs={{0,16},{8,24},{16,0},{24,8},{1,17},{9,25},{17,1},{25,9},{2,18},{10... | collective-permute-start | bytes 442376 | tf_op jit(solution)/shard_map/ppermute | solution.py:444
  6.2 2.3 %collective-permute-done.refs_0_.refs_2_ = bf16[144,512]{1,0:T(8,128)(2,1)S(1)} collective-permute-done((bf16[144,512]{1,0:T(8,128)(2,1)S(1)}, bf16[144,512]{1,0:T(8,128)(2,1)S(1)}, u32[]{:S(2)}, u32[]{:S(2)}) %collective-permute-start) | collective-permute-done | bytes 147488 | tf_op jit(solution)/shard_map/ppermute | solution.py:444
  8.6 1.8 %collective-permute-start.1 = (bf16[288,512]{1,0:T(8,128)(2,1)S(1)}, bf16[288,512]{1,0:T(8,128)(2,1)S(1)}, u32[]{:S(2)}, u32[]{:S(2)}) collective-permute-start(bf16[288,512]{1,0:T(8,128)(2,1)S(1)} %pad_maximum_fusion), channel_id=1, source_target_pairs={{0,16},{8,24},{16,0},{24,8},{1,17},{9,25},{17,1},{25,9},{2,18},{10... | collective-permute-start | bytes 884744 | tf_op jit(solution)/shard_map/ppermute | solution.py:444
  10.4 0.0 collective-permute-done.2.refs_1_.refs_5_
  10.4 1.6 %collective-permute-start.3 = (bf16[288,512]{1,0:T(8,128)(2,1)S(1)}, bf16[288,512]{1,0:T(8,128)(2,1)S(1)}, u32[]{:S(2)}, u32[]{:S(2)}) collective-permute-start(bf16[288,512]{1,0:T(8,128)(2,1)S(1)} %pad_maximum_fusion.1), channel_id=1, source_target_pairs={{0,8},{8,0},{16,24},{24,16},{1,9},{9,1},{17,25},{25,17},{2,10},{10... | collective-permute-start | bytes 884744 | tf_op jit(solution)/shard_map/ppermute | solution.py:444
  12.0 1.5 %shard_map.132 = (bf16[256,512]{1,0:T(8,128)(2,1)S(1)}, bf16[512,256]{1,0:T(8,128)(2,1)S(1)}, bf16[1024,192]{1,0:T(8,128)(2,1)S(1)}, bf16[192,1024]{1,0:T(8,128)...) custom-call(s32[4,2,8]{2,1,0:T(2,128)} %bitcast.33, s32[8,128]{1,0:T(8,128)} %bitcast.34, ...), custom_call_target="tpu_custom_call" | custom-call | bytes 2367744 | tf_op jit(solution)/shard_map/pallas_call | solution.py:423
  13.5 0.1 pad_add_fusion.who
  13.6 1.9 %shard_map.133.refs_4_ = f32[1024,512]{1,0:T(8,128)S(1)} custom-call(s32[2]{0:T(128)S(1)} %pad_add_fusion.who, bf16[144,512]{1,0:T(8,128)(2,1)S(1)} %get-tuple-element.66.refs_0_, bf16[144,512]{1,0:T(8,128)(2,1)S(1)} %get-tuple-element.67.refs_1_, bf16[512,512]{1,0:T(8,128)(2,1)S(1)} %get-tuple-element.68.refs_2_.refs_4_.refs_8_, ...), custom_call_target="tpu_custom_call" | custom-call | bytes 2918408 | tf_op jit(solution)/shard_map/pallas_call | solution.py:423
  15.5 1.9 %shard_map.134.refs_6_.before = f32[1024,512]{1,0:T(8,128)S(1)} custom-call(s32[2]{0:T(128)S(1)} %pad_add_fusion.who, bf16[144,512]{1,0:T(8,128)(2,1)S(1)} %collective-permute-done.refs_0_.refs_2_, bf16[144,512]{1,0:T(8,128)(2,1)S(1)} %collective-permute-done.2.refs_1_.refs_5_, ...), custom_call_target="tpu_custom_call", output_to_operand_aliasing={{}: (5, {})} | custom-call | bytes 5015560 | tf_op jit(solution)/shard_map/pallas_call | solution.py:423
  17.4 0.0 collective-permute-done.1.refs_0_.refs_1_.refs_4_.refs_6_
  17.4 0.7 collective-permute-done.3.refs_2_.refs_3_.refs_7_
  18.1 2.0 %shard_map.135 = (bf16[512,512]{1,0:T(8,128)(2,1)S(1)}, bf16[1024,512]{1,0:T(8,128)(2,1)S(1)}, s32[1,1024]{1,0:T(1,128)S(1)}) custom-call(s32[2]{0:T(128)S(1)} %pad_add_fusion.who, bf16[288,512]{1,0:T(8,128)(2,1)S(1)} %collective-permute-done.1.refs_0_.refs_1_.refs_4_.refs_6_, bf16[288,512]{1,0:T(8,128)(2,1)S(1)} %collective-permute-done.1.refs_0_.refs_1_.refs_4_.refs_6_, ...), custom_call_target="tpu_custom_call" | custom-call | bytes 5380104 | tf_op jit(solution)/shard_map/pallas_call | solution.py:423
  20.1 0.1 collective-permute-start.4
  20.2 0.7 shard_map.136
  20.9 1.2 %collective-permute-done.4 = bf16[512,512]{1,0:T(8,128)(2,1)S(1)} collective-permute-done((bf16[512,512]{1,0:T(8,128)(2,1)S(1)}, bf16[512,512]{1,0:T(8,128)(2,1)S(1)}, u32[]{:S(2)}, u32[]{:S(2)}) %collective-permute-start.4) | collective-permute-done | bytes 524320 | tf_op jit(solution)/shard_map/ppermute | solution.py:444
  22.1 0.2 fusion
  22.3 0.0 copy-start.1
  22.3 0.0 copy-start.3
  22.3 1.6 %collective-permute-start.5 = (bf16[128,512]{1,0:T(8,128)(2,1)S(1)}, bf16[128,512]{1,0:T(8,128)(2,1)S(1)}, u32[]{:S(2)}, u32[]{:S(2)}) collective-permute-start(bf16[128,512]{1,0:T(8,128)(2,1)S(1)} %get-tuple-element.134), channel_id=1, source_target_pairs={{0,2},{1,3},{2,0},{3,1},{4,6},{5,7},{6,4},{7,5},{8,10},{9,11},{10,... | collective-permute-start | bytes 393224 | tf_op jit(solution)/shard_map/ppermute | solution.py:444
  24.0 2.6 %collective-permute-start.6 = (bf16[128,512]{1,0:T(8,128)(2,1)S(1)}, bf16[128,512]{1,0:T(8,128)(2,1)S(1)}, u32[]{:S(2)}, u32[]{:S(2)}) collective-permute-start(bf16[128,512]{1,0:T(8,128)(2,1)S(1)} %get-tuple-element.133), channel_id=1, source_target_pairs={{0,4},{1,5},{2,6},{3,7},{4,0},{5,1},{6,2},{7,3},{8,12},{9,13},{10,... | collective-permute-start | bytes 393224 | tf_op jit(solution)/shard_map/ppermute | solution.py:444
  26.6 0.2 collective-permute-start.7
  26.8 2.3 %shard_map.137 = (bf16[256,512]{1,0:T(8,128)(2,1)S(1)}, bf16[256,512]{1,0:T(8,128)(2,1)S(1)}, bf16[256,512]{1,0:T(8,128)(2,1)S(1)}, bf16[256,512]{1,0:T(8,128)(2...) custom-call(bf16[144,512]{1,0:T(8,128)(2,1)S(1)} %get-tuple-element., ...), custom_call_target="tpu_custom_call" | custom-call | bytes 4392960 | tf_op jit(solution)/shard_map/pallas_call | solution.py:423
  29.1 0.8 collective-permute-done.5.refs_0_
  29.9 7.0 %collective-permute-done.6.refs_1_ = bf16[128,512]{1,0:T(8,128)(2,1)S(1)} collective-permute-done((bf16[128,512]{1,0:T(8,128)(2,1)S(1)}, bf16[128,512]{1,0:T(8,128)(2,1)S(1)}, u32[]{:S(2)}, u32[]{:S(2)}) %collective-permute-start.6) | collective-permute-done | bytes 131104 | tf_op jit(solution)/shard_map/ppermute | solution.py:444
  36.9 0.0 collective-permute-done.7.refs_2_
  36.9 0.5 shard_map.138
  37.4 11.8 %all_to_all.44 = bf16[32,8,128]{2,1,0:T(8,128)(2,1)S(1)} all-to-all(bf16[32,8,128]{2,1,0:T(8,128)(2,1)S(1)} %bitcast.29), channel_id=1, replica_groups=mesh['sect'=4,'node'=8] {'sect','node'}, dimensions={0} | all-to-all | bytes 131072 | tf_op jit(solution)/shard_map/all_to_all | solution.py:586
  49.2 1.9 %shard_map.139 = (bf16[128,512]{1,0:T(8,128)(2,1)S(1)}, f32[128,512]{1,0:T(8,128)S(1)}, bf16[1024,512]{1,0:T(8,128)(2,1)S(1)}, bf16[256,128]{1,0:T(8,128)(2,1)S(1)}) custom-call(bf16[128,512]{1,0:T(8,128)(2,1)S(1)} %get-tuple-element.85.state, bf16[256,128]{1,0:T(8,128)(2,1)S(1)} %bitcast.24, bf16[1024,192]{1,0:T(8,128)(2,1)S(1)} %get-tuple-element.87.source, ...), custom_call_target="tpu_custom_call" | custom-call | bytes 6553600 | tf_op jit(solution)/shard_map/pallas_call | solution.py:423
  51.1 9.1 %all_to_all.45 = bf16[32,8,128]{2,1,0:T(8,128)(2,1)S(1)} all-to-all(bf16[32,8,128]{2,1,0:T(8,128)(2,1)S(1)} %bitcast.30), channel_id=1, replica_groups=mesh['sect'=4,'node'=8] {'sect','node'}, dimensions={0} | all-to-all | bytes 131072 | tf_op jit(solution)/shard_map/all_to_all | solution.py:586
  60.2 3.7 %shard_map.140 = (bf16[128,512]{1,0:T(8,128)(2,1)}, f32[128,512]{1,0:T(8,128)S(1)}, bf16[256,128]{1,0:T(8,128)(2,1)S(1)}) custom-call(bf16[128,512]{1,0:T(8,128)(2,1)S(1)} %get-tuple-element.88.state, bf16[256,128]{1,0:T(8,128)(2,1)S(1)} %bitcast.25, bf16[1024,192]{1,0:T(8,128)(2,1)S(1)} %get-tuple-element.87.source, ...), custom_call_target="tpu_custom_call" | custom-call | bytes 5767168 | tf_op jit(solution)/shard_map/pallas_call | solution.py:423
  63.9 9.1 %all_to_all.46 = bf16[32,8,128]{2,1,0:T(8,128)(2,1)S(1)} all-to-all(bf16[32,8,128]{2,1,0:T(8,128)(2,1)S(1)} %bitcast.32), channel_id=1, replica_groups=mesh['sect'=4,'node'=8] {'sect','node'}, dimensions={0} | all-to-all | bytes 131072 | tf_op jit(solution)/shard_map/all_to_all | solution.py:586
  72.9 1.9 %shard_map.141 = (f32[128,512]{1,0:T(8,128)S(1)}, bf16[256,128]{1,0:T(8,128)(2,1)S(1)}) custom-call(f32[128,512]{1,0:T(8,128)S(1)} %get-tuple-element.92.mine, bf16[256,128]{1,0:T(8,128)(2,1)S(1)} %bitcast.23, bf16[512,256]{1,0:T(8,128)(2,1)S(1)} %get-tuple-element.94.pick_t, f32[128,512]{1,0:T(8,128)S(1)} %get-tuple-element.95.mixed, ...), custom_call_target="tpu_custom_call" | custom-call | bytes 6815744 | tf_op jit(solution)/shard_map/pallas_call | solution.py:423
  74.8 9.1 %all_to_all.47 = bf16[32,8,128]{2,1,0:T(8,128)(2,1)S(1)} all-to-all(bf16[32,8,128]{2,1,0:T(8,128)(2,1)S(1)} %bitcast.31), channel_id=1, replica_groups=mesh['sect'=4,'node'=8] {'sect','node'}, dimensions={0} | all-to-all | bytes 131072 | tf_op jit(solution)/shard_map/all_to_all | solution.py:586
  83.9 0.5 shard_map.142.refs_8_
  84.4 0.5 collective-permute-start.8
  84.9 0.8 collective-permute-start.9
  85.7 3.1 %collective-permute-start.10 = (bf16[128,512]{1,0:T(8,128)(2,1)S(1)}, bf16[128,512]{1,0:T(8,128)(2,1)S(1)}, u32[]{:S(2)}, u32[]{:S(2)}) collective-permute-start(bf16[128,512]{1,0:T(8,128)(2,1)S(1)} %shard_map.142.refs_8_), channel_id=1, source_target_pairs={{0,6},{1,7},{2,4},{3,5},{4,2},{5,3},{6,0},{7,1},{8,14},{9,15},{10,... | collective-permute-start | bytes 393224 | tf_op jit(solution)/shard_map/ppermute | solution.py:444
  88.9 0.0 collective-permute-start.11
  88.9 2.6 %shard_map.143 = (bf16[256,1024]{1,0:T(8,128)(2,1)S(1)}, bf16[256,1024]{1,0:T(8,128)(2,1)S(1)}, bf16[256,1024]{1,0:T(8,128)(2,1)S(1)}, bf16[256,1024]{1,0:T(8,12...) custom-call(s32[2]{0:T(128)S(1)} %pad_add_fusion.who, ...), custom_call_target="tpu_custom_call" | custom-call | bytes 5963784 | tf_op jit(solution)/shard_map/pallas_call | solution.py:423
  91.5 0.1 collective-permute-done.8.refs_9_
  91.6 0.5 collective-permute-start.12
  92.1 5.7 %collective-permute-done.9.refs_10_ = bf16[128,512]{1,0:T(8,128)(2,1)S(1)} collective-permute-done((bf16[128,512]{1,0:T(8,128)(2,1)S(1)}, bf16[128,512]{1,0:T(8,128)(2,1)S(1)}, u32[]{:S(2)}, u32[]{:S(2)}) %collective-permute-start.9) | collective-permute-done | bytes 131104 | tf_op jit(solution)/shard_map/ppermute | solution.py:444
  97.8 0.0 collective-permute-start.13
  97.8 0.0 collective-permute-done.10.refs_11_
  97.8 0.5 collective-permute-start.14
  98.3 0.0 collective-permute-done.11.refs_12_
  98.3 0.0 collective-permute-done.12.refs_13_
  98.3 0.8 collective-permute-done.13.refs_14_
  99.1 0.2 collective-permute-done.14.refs_15_
  99.3 1.8 %shard_map.144 = (bf16[256,512]{1,0:T(8,128)(2,1)S(1)}, bf16[256,512]{1,0:T(8,128)(2,1)S(1)}) custom-call(s32[2]{0:T(128)S(1)} %pad_add_fusion.who, bf16[256,1024]{1,0:T(8,128)(2,1)S(1)} %get-tuple-element.110.refs_0_, bf16[256,1024]{1,0:T(8,128)(2,1)S(1)} %get-tuple-element.111.refs_1_, bf16[256,1024]{1,0:T(8,128)(2,1)S(1)} %get-tuple-element.112.refs_2_, ...), custom_call_target="tpu_custom_call" | custom-call | bytes 4718600 | tf_op jit(solution)/shard_map/pallas_call | solution.py:423
  101.2 0.5 collective-permute-start.15
  101.7 0.8 collective-permute-start.16
  102.5 1.8 %shard_map.145 = (f32[256,512]{1,0:T(8,128)S(1)}, f32[256,512]{1,0:T(8,128)S(1)}) custom-call(s32[2]{0:T(128)S(1)} %pad_add_fusion.who, bf16[256,1024]{1,0:T(8,128)(2,1)S(1)} %get-tuple-element.101.refs_0_, bf16[256,1024]{1,0:T(8,128)(2,1)S(1)} %get-tuple-element.102.refs_1_, bf16[256,1024]{1,0:T(8,128)(2,1)S(1)} %get-tuple-element.103.refs_2_, ...), custom_call_target="tpu_custom_call" | custom-call | bytes 5242888 | tf_op jit(solution)/shard_map/pallas_call | solution.py:423
  104.3 5.5 %collective-permute-done.15 = bf16[256,512]{1,0:T(8,128)(2,1)S(1)} collective-permute-done((bf16[256,512]{1,0:T(8,128)(2,1)S(1)}, bf16[256,512]{1,0:T(8,128)(2,1)S(1)}, u32[]{:S(2)}, u32[]{:S(2)}) %collective-permute-start.15) | collective-permute-done | bytes 262176 | tf_op jit(solution)/shard_map/ppermute | solution.py:444
  109.8 0.1 convert_add_fusion.2
  109.9 0.7 collective-permute-start.17
  110.6 0.0 collective-permute-done.16
  110.6 0.1 convert_add_fusion.1
  110.7 1.0 collective-permute-start.18
  111.7 3.2 %collective-permute-done.17.refs_2_ = bf16[128,512]{1,0:T(8,128)(2,1)S(1)} collective-permute-done((bf16[128,512]{1,0:T(8,128)(2,1)S(1)}, bf16[128,512]{1,0:T(8,128)(2,1)S(1)}, u32[]{:S(2)}, u32[]{:S(2)}) %collective-permute-start.17) | collective-permute-done | bytes 131104 | tf_op jit(solution)/shard_map/ppermute | solution.py:444
  114.9 0.8 collective-permute-done.18.refs_3_
  115.7 1.2 %shard_map.146 = bf16[256,512]{1,0:T(8,128)(2,1)} custom-call(f32[128,512]{1,0:T(8,128)S(1)} %slice.49.refs_0_, f32[128,512]{1,0:T(8,128)S(1)} %slice.50.refs_1_, bf16[128,512]{1,0:T(8,128)(2,1)S(1)} %collective-permute-done.17.refs_2_, bf16[128,512]{1,0:T(8,128)(2,1)S(1)} %collective-permute-done.18.refs_3_, bf16[512,512]{1,0:T(8,128)(2,1)S(1)} %copy-done.2), custom_call_target="tpu_custom_call" | custom-call | bytes 1572864 | tf_op jit(solution)/shard_map/pallas_call | solution.py:423
  (16 shorter events, 0.2 us)
Async XLA Ops:
  1.7 6.9 %collective-permute-start = (bf16[144,512]{1,0:T(8,128)(2,1)S(1)}, bf16[144,512]{1,0:T(8,128)(2,1)S(1)}, u32[]{:S(2)}, u32[]{:S(2)}) collective-permute-start(bf16[144,512]{1,0:T(8,128)(2,1)S(1)} %get-tuple-element.66.refs_0_), channel_id=1, source_target_pairs={{0,8},{8,0},{16,24},{24,16},{1,9},{9,1},{17,25},{25,17},{2,10},{10... | collective-permute-start | bytes 442376 | tf_op jit(solution)/shard_map/ppermute | solution.py:444
  4.7 5.7 %collective-permute-start.2 = (bf16[144,512]{1,0:T(8,128)(2,1)S(1)}, bf16[144,512]{1,0:T(8,128)(2,1)S(1)}, u32[]{:S(2)}, u32[]{:S(2)}) collective-permute-start(bf16[144,512]{1,0:T(8,128)(2,1)S(1)} %get-tuple-element.67.refs_1_), channel_id=1, source_target_pairs={{0,16},{8,24},{16,0},{24,8},{1,17},{9,25},{17,1},{25,9},{2,18},{10... | collective-permute-start | bytes 442376 | tf_op jit(solution)/shard_map/ppermute | solution.py:444
  8.6 8.8 %collective-permute-start.1 = (bf16[288,512]{1,0:T(8,128)(2,1)S(1)}, bf16[288,512]{1,0:T(8,128)(2,1)S(1)}, u32[]{:S(2)}, u32[]{:S(2)}) collective-permute-start(bf16[288,512]{1,0:T(8,128)(2,1)S(1)} %pad_maximum_fusion), channel_id=1, source_target_pairs={{0,16},{8,24},{16,0},{24,8},{1,17},{9,25},{17,1},{25,9},{2,18},{10... | collective-permute-start | bytes 884744 | tf_op jit(solution)/shard_map/ppermute | solution.py:444
  10.4 7.7 %collective-permute-start.3 = (bf16[288,512]{1,0:T(8,128)(2,1)S(1)}, bf16[288,512]{1,0:T(8,128)(2,1)S(1)}, u32[]{:S(2)}, u32[]{:S(2)}) collective-permute-start(bf16[288,512]{1,0:T(8,128)(2,1)S(1)} %pad_maximum_fusion.1), channel_id=1, source_target_pairs={{0,8},{8,0},{16,24},{24,16},{1,9},{9,1},{17,25},{25,17},{2,10},{10... | collective-permute-start | bytes 884744 | tf_op jit(solution)/shard_map/ppermute | solution.py:444
  20.1 2.0 %collective-permute-start.4 = (bf16[512,512]{1,0:T(8,128)(2,1)S(1)}, bf16[512,512]{1,0:T(8,128)(2,1)S(1)}, u32[]{:S(2)}, u32[]{:S(2)}) collective-permute-start(bf16[512,512]{1,0:T(8,128)(2,1)S(1)} %get-tuple-element.72), channel_id=1, source_target_pairs={{0,1},{1,0},{2,3},{3,2},{4,5},{5,4},{6,7},{7,6},{8,9},{9,8},{10,11... | collective-permute-start | bytes 1572872 | tf_op jit(solution)/shard_map/ppermute | solution.py:444
  22.3 14.6 %copy-start.1 = (bf16[512,512]{1,0:T(8,128)(2,1)S(1)}, bf16[512,512]{1,0:T(8,128)(2,1)}, u32[]{:S(2)}) copy-start(bf16[512,512]{1,0:T(8,128)(2,1)} %weight.1) | copy-start | bytes 1572868
  22.3 14.6 %copy-start.3 = (bf16[1,128,512]{2,1,0:T(8,128)(2,1)S(1)}, bf16[1,128,512]{2,1,0:T(8,128)(2,1)}, u32[]{:S(2)}) copy-start(bf16[1,128,512]{2,1,0:T(8,128)(2,1)} %param.18) | copy-start | bytes 393220
  22.3 7.5 %collective-permute-start.5 = (bf16[128,512]{1,0:T(8,128)(2,1)S(1)}, bf16[128,512]{1,0:T(8,128)(2,1)S(1)}, u32[]{:S(2)}, u32[]{:S(2)}) collective-permute-start(bf16[128,512]{1,0:T(8,128)(2,1)S(1)} %get-tuple-element.134), channel_id=1, source_target_pairs={{0,2},{1,3},{2,0},{3,1},{4,6},{5,7},{6,4},{7,5},{8,10},{9,11},{10,... | collective-permute-start | bytes 393224 | tf_op jit(solution)/shard_map/ppermute | solution.py:444
  24.0 12.9 %collective-permute-start.6 = (bf16[128,512]{1,0:T(8,128)(2,1)S(1)}, bf16[128,512]{1,0:T(8,128)(2,1)S(1)}, u32[]{:S(2)}, u32[]{:S(2)}) collective-permute-start(bf16[128,512]{1,0:T(8,128)(2,1)S(1)} %get-tuple-element.133), channel_id=1, source_target_pairs={{0,4},{1,5},{2,6},{3,7},{4,0},{5,1},{6,2},{7,3},{8,12},{9,13},{10,... | collective-permute-start | bytes 393224 | tf_op jit(solution)/shard_map/ppermute | solution.py:444
  26.6 22.6 %copy-start = (bf16[2,4,512,512]{3,2,1,0:T(8,128)(2,1)S(1)}, bf16[2,4,512,512]{3,2,1,0:T(8,128)(2,1)}, u32[]{:S(2)}) copy-start(bf16[2,4,512,512]{3,2,1,0:T(8,128)(2,1)} %weights.5) | copy-start | bytes 12582916
  26.6 10.3 %collective-permute-start.7 = (bf16[128,512]{1,0:T(8,128)(2,1)S(1)}, bf16[128,512]{1,0:T(8,128)(2,1)S(1)}, u32[]{:S(2)}, u32[]{:S(2)}) collective-permute-start(bf16[128,512]{1,0:T(8,128)(2,1)S(1)} %get-tuple-element.132), channel_id=1, source_target_pairs={{0,6},{1,7},{2,4},{3,5},{4,2},{5,3},{6,0},{7,1},{8,14},{9,15},{10,... | collective-permute-start | bytes 393224 | tf_op jit(solution)/shard_map/ppermute | solution.py:444
  49.2 11.0 %copy-start.4 = (bf16[1,128,512]{2,1,0:T(8,128)(2,1)S(1)}, bf16[1,128,512]{2,1,0:T(8,128)(2,1)}, u32[]{:S(2)}) copy-start(bf16[1,128,512]{2,1,0:T(8,128)(2,1)} %param.23) | copy-start | bytes 393220
  84.4 7.2 %collective-permute-start.8 = (bf16[128,512]{1,0:T(8,128)(2,1)S(1)}, bf16[128,512]{1,0:T(8,128)(2,1)S(1)}, u32[]{:S(2)}, u32[]{:S(2)}) collective-permute-start(bf16[128,512]{1,0:T(8,128)(2,1)S(1)} %shard_map.142.refs_8_), channel_id=1, source_target_pairs={{0,2},{1,3},{2,0},{3,1},{4,6},{5,7},{6,4},{7,5},{8,10},{9,11},{10,... | collective-permute-start | bytes 393224 | tf_op jit(solution)/shard_map/ppermute | solution.py:444
  84.9 12.9 %collective-permute-start.9 = (bf16[128,512]{1,0:T(8,128)(2,1)S(1)}, bf16[128,512]{1,0:T(8,128)(2,1)S(1)}, u32[]{:S(2)}, u32[]{:S(2)}) collective-permute-start(bf16[128,512]{1,0:T(8,128)(2,1)S(1)} %shard_map.142.refs_8_), channel_id=1, source_target_pairs={{0,4},{1,5},{2,6},{3,7},{4,0},{5,1},{6,2},{7,3},{8,12},{9,13},{10,... | collective-permute-start | bytes 393224 | tf_op jit(solution)/shard_map/ppermute | solution.py:444
  85.7 12.1 %collective-permute-start.10 = (bf16[128,512]{1,0:T(8,128)(2,1)S(1)}, bf16[128,512]{1,0:T(8,128)(2,1)S(1)}, u32[]{:S(2)}, u32[]{:S(2)}) collective-permute-start(bf16[128,512]{1,0:T(8,128)(2,1)S(1)} %shard_map.142.refs_8_), channel_id=1, source_target_pairs={{0,6},{1,7},{2,4},{3,5},{4,2},{5,3},{6,0},{7,1},{8,14},{9,15},{10,... | collective-permute-start | bytes 393224 | tf_op jit(solution)/shard_map/ppermute | solution.py:444
  88.9 9.5 %collective-permute-start.11 = (bf16[128,512]{1,0:T(8,128)(2,1)S(1)}, bf16[128,512]{1,0:T(8,128)(2,1)S(1)}, u32[]{:S(2)}, u32[]{:S(2)}) collective-permute-start(bf16[128,512]{1,0:T(8,128)(2,1)S(1)} %shard_map.142.refs_8_), channel_id=1, source_target_pairs={{0,1},{1,0},{2,3},{3,2},{4,5},{5,4},{6,7},{7,6},{8,9},{9,8},{10,11... | collective-permute-start | bytes 393224 | tf_op jit(solution)/shard_map/ppermute | solution.py:444
  91.6 6.8 %collective-permute-start.12 = (bf16[128,512]{1,0:T(8,128)(2,1)S(1)}, bf16[128,512]{1,0:T(8,128)(2,1)S(1)}, u32[]{:S(2)}, u32[]{:S(2)}) collective-permute-start(bf16[128,512]{1,0:T(8,128)(2,1)S(1)} %collective-permute-done.8.refs_9_), channel_id=1, source_target_pairs={{0,1},{1,0},{2,3},{3,2},{4,5},{5,4},{6,7},{7,6},{8,9},{9,8},{10,11... | collective-permute-start | bytes 393224 | tf_op jit(solution)/shard_map/ppermute | solution.py:444
  97.8 1.3 %collective-permute-start.13 = (bf16[128,512]{1,0:T(8,128)(2,1)S(1)}, bf16[128,512]{1,0:T(8,128)(2,1)S(1)}, u32[]{:S(2)}, u32[]{:S(2)}) collective-permute-start(bf16[128,512]{1,0:T(8,128)(2,1)S(1)} %collective-permute-done.9.refs_10_), channel_id=1, source_target_pairs={{0,1},{1,0},{2,3},{3,2},{4,5},{5,4},{6,7},{7,6},{8,9},{9,8},{10,11... | collective-permute-start | bytes 393224 | tf_op jit(solution)/shard_map/ppermute | solution.py:444
  97.8 1.5 %collective-permute-start.14 = (bf16[128,512]{1,0:T(8,128)(2,1)S(1)}, bf16[128,512]{1,0:T(8,128)(2,1)S(1)}, u32[]{:S(2)}, u32[]{:S(2)}) collective-permute-start(bf16[128,512]{1,0:T(8,128)(2,1)S(1)} %collective-permute-done.10.refs_11_), channel_id=1, source_target_pairs={{0,1},{1,0},{2,3},{3,2},{4,5},{5,4},{6,7},{7,6},{8,9},{9,8},{10,11... | collective-permute-start | bytes 393224 | tf_op jit(solution)/shard_map/ppermute | solution.py:444
  101.2 8.6 %collective-permute-start.15 = (bf16[256,512]{1,0:T(8,128)(2,1)S(1)}, bf16[256,512]{1,0:T(8,128)(2,1)S(1)}, u32[]{:S(2)}, u32[]{:S(2)}) collective-permute-start(bf16[256,512]{1,0:T(8,128)(2,1)S(1)} %get-tuple-element.118), channel_id=1, source_target_pairs={{0,8},{8,0},{16,24},{24,16},{1,9},{9,1},{17,25},{25,17},{2,10},{10... | collective-permute-start | bytes 786440 | tf_op jit(solution)/shard_map/ppermute | solution.py:444
  101.7 8.9 %collective-permute-start.16 = (bf16[256,512]{1,0:T(8,128)(2,1)S(1)}, bf16[256,512]{1,0:T(8,128)(2,1)S(1)}, u32[]{:S(2)}, u32[]{:S(2)}) collective-permute-start(bf16[256,512]{1,0:T(8,128)(2,1)S(1)} %get-tuple-element.129), channel_id=1, source_target_pairs={{0,16},{8,24},{16,0},{24,8},{1,17},{9,25},{17,1},{25,9},{2,18},{10... | collective-permute-start | bytes 786440 | tf_op jit(solution)/shard_map/ppermute | solution.py:444
  109.8 5.9 %copy-start.2 = (bf16[512,512]{1,0:T(8,128)(2,1)S(1)}, bf16[512,512]{1,0:T(8,128)(2,1)}, u32[]{:S(2)}) copy-start(bf16[512,512]{1,0:T(8,128)(2,1)} %refs_4_.3) | copy-start | bytes 1572868
  109.9 5.0 %collective-permute-start.17 = (bf16[128,512]{1,0:T(8,128)(2,1)S(1)}, bf16[128,512]{1,0:T(8,128)(2,1)S(1)}, u32[]{:S(2)}, u32[]{:S(2)}) collective-permute-start(bf16[128,512]{1,0:T(8,128)(2,1)S(1)} %slice.56), channel_id=1, source_target_pairs={{0,16},{8,24},{16,0},{24,8},{1,17},{9,25},{17,1},{25,9},{2,18},{10... | collective-permute-start | bytes 393224 | tf_op jit(solution)/shard_map/ppermute | solution.py:444
  110.7 5.0 %collective-permute-start.18 = (bf16[128,512]{1,0:T(8,128)(2,1)S(1)}, bf16[128,512]{1,0:T(8,128)(2,1)S(1)}, u32[]{:S(2)}, u32[]{:S(2)}) collective-permute-start(bf16[128,512]{1,0:T(8,128)(2,1)S(1)} %slice.55), channel_id=1, source_target_pairs={{0,8},{8,0},{16,24},{24,16},{1,9},{9,1},{17,25},{25,17},{2,10},{10... | collective-permute-start | bytes 393224 | tf_op jit(solution)/shard_map/ppermute | solution.py:444

commit v2 on v1

--- a/solution.py
+++ b/solution.py
@@ -223,25 +223,21 @@
 
 def join_pieces(pieces, parts):
     count = pieces.shape[0]
-    shape = (count // parts, count)
-    return jnp.concatenate(
-        [
-            dot(mark(iota(shape, 1) == iota(shape, 0) * parts + i), pieces).astype(BF16)
-            for i in range(parts)
-        ],
-        axis=1,
-    )
+    rows = count // parts
+    at = iota((count, count), 0)
+    onehot = mark(iota((count, count), 1) == at % rows * parts + at // rows)
+    found = dot(onehot, pieces).astype(BF16)
+    return jnp.concatenate([found[i * rows : (i + 1) * rows] for i in range(parts)], axis=1)
 
 
 def cut_pieces(rows, parts):
-    count = rows.shape[0]
-    shape = (count * parts, count)
-    total = None
-    for i in range(parts):
-        onehot = mark(iota(shape, 0) == iota(shape, 1) * parts + i)
-        piece = dot(onehot, rows[:, i * LANES : (i + 1) * LANES])
-        total = piece if total is None else total + piece
-    return total.astype(BF16)
+    each, count = rows.shape[0], rows.shape[0] * parts
+    at = iota((count, count), 0)
+    onehot = mark(iota((count, count), 1) == at % parts * each + at // parts)
+    stacked = jnp.concatenate(
+        [rows[:, i * LANES : (i + 1) * LANES] for i in range(parts)], axis=0
+    )
+    return dot(onehot, stacked).astype(BF16)
 
 
 def add_pieces(pieces, pick_t, block, parts):
@@ -274,7 +270,8 @@
         joined = gathered[k * block : (k + 1) * block] + to_dst
         bend = jnp.tanh(joined)
         agg = agg + (joined + joined * bend)
-        slopes.append((1.0 + bend + joined * (1.0 - bend * bend)).astype(BF16))
+        joined, bend = joined.astype(BF16), bend.astype(BF16)
+        slopes.append(1 + bend + joined * (1 - bend * bend))
     mixed = dot(state, weights(2)) + dot(agg.astype(BF16), weights(3))
     return mixed, slopes
 
@@ -285,12 +282,12 @@
     grad_mixed = norm_back(grad, normed, scale)
     grad_state = grad + back_dot(grad_mixed, weights(2))
     grad_agg = 0.5 * back_dot(grad_mixed, weights(3))
+    low = grad_agg.astype(BF16)
     total = jnp.zeros(grad.shape, F32)
-    pieces = []
     for found in slopes:
-        piece = grad_agg * found.astype(F32)
-        total = total + piece
-        pieces.append(piece.astype(BF16))
+        total = total + found.astype(F32)
+    total = grad_agg * total
+    pieces = [low * found for found in slopes]
     grad_src = dot(source_t[...], jnp.concatenate(pieces, axis=0))
     grad_state = grad_state + back_dot(total, weights(1))
     grad_table = back_dot(grad_src, weights(0))
@@ -374,7 +371,9 @@
 
 
 def mark_kernel(spans, rows, nodes, block, fanout, who, *refs):
-    feats, outs = refs[: len(spans)], refs[len(spans) :]
+    feats, state = refs[: len(spans)], refs[len(spans)]
+    *outs, final = refs[len(spans) + 1 :]
+    final[...] = state[...]
     for feat, at, out in zip(feats, spans, outs):
         for k, found in enumerate(edge_marks(feat, at, rows, nodes, block, fanout, who)):
             out[k * rows : (k + 1) * rows, :] = found
@@ -566,7 +565,9 @@
 
     pair = keep.astype(F32) + swap(cross, "node", 1).astype(F32)
     pair = pair.reshape(half, block, width)
-    arrived = [swap(pair[q].astype(BF16), "node", 2 * q) for q in range(1, half)]
+    arrived = [
+        swap(pair[q].astype(BF16), "node", 2 * q) for q in reversed(range(1, half))
+    ]
 
     units = [(j, p) for j in range(sects) for p in range(len(axes))]
     slopes = call(
@@ -617,7 +618,7 @@
     picks_of = {unit: where[unit] for unit in units}
     if ready:
         seen, _ = lax.optimization_barrier((who, grad_sum))
-        found = call(
+        *found, mesh_out = call(
             functools.partial(
                 mark_kernel,
                 tuple(where[unit][1] for unit in units),
@@ -626,8 +627,8 @@
                 block,
                 fanout,
             ),
-            [shape((fanout * part_rows, nodes * block), BF16)] * len(units),
-            [seen, *(where[unit][0] for unit in units)],
+            [shape((fanout * part_rows, nodes * block), BF16)] * len(units) + [row_low],
+            [seen, *(where[unit][0] for unit in units), mesh_out],
             smem=1,
         )
         same[1] = lax.optimization_barrier((same[1], found[0]))[0]
@@ -659,9 +660,8 @@
 
     first = [axes[p] for p in range(len(axes))]
     stay = [[j for j in range(sects) if not j & axis] for axis in first]
-    given = message_back(
-        [[(j ^ axis, p) for j in stay[p]] for p, axis in enumerate(first)], BF16
-    )
+    sent = [[(j ^ axis, p) for j in stay[p]] for p, axis in enumerate(first)]
+    given = message_back(sent, BF16)
     gathered = lax.optimization_barrier((*gathered, given[0]))[:-1]
     kept = message_back([[(j, p) for j in stay[p]] for p in range(len(axes))], F32)
     for step in range(len(axes)):

time: 117 us -> 116 us (level)
  transfers between devices with their start and end apart: 19 -> 19, of which waited for: 12 -> 11; matrix products, arithmetic and copies ran while one was open for 0% -> 0% of each run, Pallas kernels for 11% -> 11%
where the time goes in v2:
time: 116 us
  blocking collectives  38.2 us (33%)
  waiting for transfers between devices  28.2 us (24%)
  Pallas kernels  27 us (23%)
  starting transfers between devices  20.9 us (18%)
    all_to_all x4, blocking collectives, exchange(): return lax.all_to_all(value, both, split_axis=0, concat_axis=0, tiled=True)  38.2 us
    ppermute x19, waiting for transfers between devices, swap(): return lax.ppermute(value, axis, [(i, i ^ apart) for i in range(size)])  28.2 us
    pallas_call x16, Pallas kernels, call(): pl.pallas_call(kernel, out_shape=list(outs), in_specs=specs, out_specs=[p...  27 us
    ppermute x19, starting transfers between devices, swap(): return lax.ppermute(value, axis, [(i, i ^ apart) for i in range(size)])  20.9 us
  transfers between devices with their start and end apart: 19, of which 11 were waited for; matrix products, arithmetic and copies ran while one was open for 0% of the time, Pallas kernels for 11%

profile of v2, /device:TPU:0, one launch (start us, length us, event | category | flops | bytes accessed | tf_op | source)
XLA Modules:
  0.0 115.8 jit_solution(12954075305246871158)
XLA Ops:
  0.6 1.1 shard_map.131
  1.7 3.0 %collective-permute-start = (bf16[144,512]{1,0:T(8,128)(2,1)S(1)}, bf16[144,512]{1,0:T(8,128)(2,1)S(1)}, u32[]{:S(2)}, u32[]{:S(2)}) collective-permute-start(bf16[144,512]{1,0:T(8,128)(2,1)S(1)} %get-tuple-element.67.refs_0_), channel_id=1, source_target_pairs={{0,8},{8,0},{16,24},{24,16},{1,9},{9,1},{17,25},{25,17},{2,10},{10... | collective-permute-start | bytes 442376 | tf_op jit(solution)/shard_map/ppermute | solution.py:443
  4.7 1.5 %collective-permute-start.2 = (bf16[144,512]{1,0:T(8,128)(2,1)S(1)}, bf16[144,512]{1,0:T(8,128)(2,1)S(1)}, u32[]{:S(2)}, u32[]{:S(2)}) collective-permute-start(bf16[144,512]{1,0:T(8,128)(2,1)S(1)} %get-tuple-element.68.refs_1_), channel_id=1, source_target_pairs={{0,16},{8,24},{16,0},{24,8},{1,17},{9,25},{17,1},{25,9},{2,18},{10... | collective-permute-start | bytes 442376 | tf_op jit(solution)/shard_map/ppermute | solution.py:443
  6.2 2.3 %collective-permute-done.refs_0_.refs_2_ = bf16[144,512]{1,0:T(8,128)(2,1)S(1)} collective-permute-done((bf16[144,512]{1,0:T(8,128)(2,1)S(1)}, bf16[144,512]{1,0:T(8,128)(2,1)S(1)}, u32[]{:S(2)}, u32[]{:S(2)}) %collective-permute-start) | collective-permute-done | bytes 147488 | tf_op jit(solution)/shard_map/ppermute | solution.py:443
  8.6 1.8 %collective-permute-start.1 = (bf16[288,512]{1,0:T(8,128)(2,1)S(1)}, bf16[288,512]{1,0:T(8,128)(2,1)S(1)}, u32[]{:S(2)}, u32[]{:S(2)}) collective-permute-start(bf16[288,512]{1,0:T(8,128)(2,1)S(1)} %pad_maximum_fusion), channel_id=1, source_target_pairs={{0,16},{8,24},{16,0},{24,8},{1,17},{9,25},{17,1},{25,9},{2,18},{10... | collective-permute-start | bytes 884744 | tf_op jit(solution)/shard_map/ppermute | solution.py:443
  10.4 0.0 collective-permute-done.2.refs_1_.refs_5_
  10.4 1.6 %collective-permute-start.3 = (bf16[288,512]{1,0:T(8,128)(2,1)S(1)}, bf16[288,512]{1,0:T(8,128)(2,1)S(1)}, u32[]{:S(2)}, u32[]{:S(2)}) collective-permute-start(bf16[288,512]{1,0:T(8,128)(2,1)S(1)} %pad_maximum_fusion.1), channel_id=1, source_target_pairs={{0,8},{8,0},{16,24},{24,16},{1,9},{9,1},{17,25},{25,17},{2,10},{10... | collective-permute-start | bytes 884744 | tf_op jit(solution)/shard_map/ppermute | solution.py:443
  12.0 1.5 %shard_map.132 = (bf16[256,512]{1,0:T(8,128)(2,1)S(1)}, bf16[512,256]{1,0:T(8,128)(2,1)S(1)}, bf16[1024,192]{1,0:T(8,128)(2,1)S(1)}, bf16[192,1024]{1,0:T(8,128)...) custom-call(s32[4,2,8]{2,1,0:T(2,128)} %bitcast.33, s32[8,128]{1,0:T(8,128)} %bitcast.34, ...), custom_call_target="tpu_custom_call" | custom-call | bytes 2367744 | tf_op jit(solution)/shard_map/pallas_call | solution.py:422
  13.5 0.1 pad_add_fusion.who
  13.6 1.9 %shard_map.133.refs_4_ = f32[1024,512]{1,0:T(8,128)S(1)} custom-call(s32[2]{0:T(128)S(1)} %pad_add_fusion.who, bf16[144,512]{1,0:T(8,128)(2,1)S(1)} %get-tuple-element.67.refs_0_, bf16[144,512]{1,0:T(8,128)(2,1)S(1)} %get-tuple-element.68.refs_1_, bf16[512,512]{1,0:T(8,128)(2,1)S(1)} %get-tuple-element.69.refs_2_.refs_4_.refs_8_, ...), custom_call_target="tpu_custom_call" | custom-call | bytes 2918408 | tf_op jit(solution)/shard_map/pallas_call | solution.py:422
  15.5 1.9 %shard_map.134.refs_6_.before = f32[1024,512]{1,0:T(8,128)S(1)} custom-call(s32[2]{0:T(128)S(1)} %pad_add_fusion.who, bf16[144,512]{1,0:T(8,128)(2,1)S(1)} %collective-permute-done.refs_0_.refs_2_, bf16[144,512]{1,0:T(8,128)(2,1)S(1)} %collective-permute-done.2.refs_1_.refs_5_, ...), custom_call_target="tpu_custom_call", output_to_operand_aliasing={{}: (5, {})} | custom-call | bytes 5015560 | tf_op jit(solution)/shard_map/pallas_call | solution.py:422
  17.4 0.0 collective-permute-done.1.refs_0_.refs_1_.refs_4_.refs_6_
  17.4 0.7 collective-permute-done.3.refs_2_.refs_3_.refs_7_
  18.1 2.0 %shard_map.135 = (bf16[512,512]{1,0:T(8,128)(2,1)S(1)}, bf16[1024,512]{1,0:T(8,128)(2,1)S(1)}, s32[1,1024]{1,0:T(1,128)S(1)}) custom-call(s32[2]{0:T(128)S(1)} %pad_add_fusion.who, bf16[288,512]{1,0:T(8,128)(2,1)S(1)} %collective-permute-done.1.refs_0_.refs_1_.refs_4_.refs_6_, bf16[288,512]{1,0:T(8,128)(2,1)S(1)} %collective-permute-done.1.refs_0_.refs_1_.refs_4_.refs_6_, ...), custom_call_target="tpu_custom_call" | custom-call | bytes 5380104 | tf_op jit(solution)/shard_map/pallas_call | solution.py:422
  20.1 0.1 collective-permute-start.4
  20.2 0.7 shard_map.136
  20.9 1.2 %collective-permute-done.4 = bf16[512,512]{1,0:T(8,128)(2,1)S(1)} collective-permute-done((bf16[512,512]{1,0:T(8,128)(2,1)S(1)}, bf16[512,512]{1,0:T(8,128)(2,1)S(1)}, u32[]{:S(2)}, u32[]{:S(2)}) %collective-permute-start.4) | collective-permute-done | bytes 524320 | tf_op jit(solution)/shard_map/ppermute | solution.py:443
  22.1 0.2 fusion
  22.3 0.0 copy-start.1
  22.3 0.0 copy-start.3
  22.3 3.7 %collective-permute-start.5 = (bf16[128,512]{1,0:T(8,128)(2,1)S(1)}, bf16[128,512]{1,0:T(8,128)(2,1)S(1)}, u32[]{:S(2)}, u32[]{:S(2)}) collective-permute-start(bf16[128,512]{1,0:T(8,128)(2,1)S(1)} %get-tuple-element.136), channel_id=1, source_target_pairs={{0,6},{1,7},{2,4},{3,5},{4,2},{5,3},{6,0},{7,1},{8,14},{9,15},{10,... | collective-permute-start | bytes 393224 | tf_op jit(solution)/shard_map/ppermute | solution.py:443
  26.0 0.0 collective-permute-start.6
  26.0 0.8 collective-permute-start.7
  26.8 2.3 %shard_map.137 = (bf16[256,512]{1,0:T(8,128)(2,1)S(1)}, bf16[256,512]{1,0:T(8,128)(2,1)S(1)}, bf16[256,512]{1,0:T(8,128)(2,1)S(1)}, bf16[256,512]{1,0:T(8,128)(2...) custom-call(bf16[144,512]{1,0:T(8,128)(2,1)S(1)} %get-tuple-element., ...), custom_call_target="tpu_custom_call" | custom-call | bytes 4392960 | tf_op jit(solution)/shard_map/pallas_call | solution.py:422
  29.1 1.5 %collective-permute-done.5.refs_0_ = bf16[128,512]{1,0:T(8,128)(2,1)S(1)} collective-permute-done((bf16[128,512]{1,0:T(8,128)(2,1)S(1)}, bf16[128,512]{1,0:T(8,128)(2,1)S(1)}, u32[]{:S(2)}, u32[]{:S(2)}) %collective-permute-start.5) | collective-permute-done | bytes 131104 | tf_op jit(solution)/shard_map/ppermute | solution.py:443
  30.6 6.7 %collective-permute-done.6.refs_1_ = bf16[128,512]{1,0:T(8,128)(2,1)S(1)} collective-permute-done((bf16[128,512]{1,0:T(8,128)(2,1)S(1)}, bf16[128,512]{1,0:T(8,128)(2,1)S(1)}, u32[]{:S(2)}, u32[]{:S(2)}) %collective-permute-start.6) | collective-permute-done | bytes 131104 | tf_op jit(solution)/shard_map/ppermute | solution.py:443
  37.4 0.0 collective-permute-done.7.refs_2_
  37.4 0.5 shard_map.138
  37.9 11.0 %all_to_all.44 = bf16[32,8,128]{2,1,0:T(8,128)(2,1)S(1)} all-to-all(bf16[32,8,128]{2,1,0:T(8,128)(2,1)S(1)} %bitcast.29), channel_id=1, replica_groups=mesh['sect'=4,'node'=8] {'sect','node'}, dimensions={0} | all-to-all | bytes 131072 | tf_op jit(solution)/shard_map/all_to_all | solution.py:587
  48.9 1.9 %shard_map.139 = (bf16[128,512]{1,0:T(8,128)(2,1)S(1)}, f32[128,512]{1,0:T(8,128)S(1)}, bf16[1024,512]{1,0:T(8,128)(2,1)S(1)}, bf16[256,128]{1,0:T(8,128)(2,1)S(1)}) custom-call(bf16[128,512]{1,0:T(8,128)(2,1)S(1)} %get-tuple-element.86.state, bf16[256,128]{1,0:T(8,128)(2,1)S(1)} %bitcast.24, bf16[1024,192]{1,0:T(8,128)(2,1)S(1)} %get-tuple-element.88.source, ...), custom_call_target="tpu_custom_call" | custom-call | bytes 6553600 | tf_op jit(solution)/shard_map/pallas_call | solution.py:422
  50.8 9.1 %all_to_all.45 = bf16[32,8,128]{2,1,0:T(8,128)(2,1)S(1)} all-to-all(bf16[32,8,128]{2,1,0:T(8,128)(2,1)S(1)} %bitcast.30), channel_id=1, replica_groups=mesh['sect'=4,'node'=8] {'sect','node'}, dimensions={0} | all-to-all | bytes 131072 | tf_op jit(solution)/shard_map/all_to_all | solution.py:587
  59.8 3.0 %shard_map.140 = (bf16[128,512]{1,0:T(8,128)(2,1)S(1)}, f32[128,512]{1,0:T(8,128)S(1)}, bf16[256,128]{1,0:T(8,128)(2,1)S(1)}) custom-call(bf16[128,512]{1,0:T(8,128)(2,1)S(1)} %get-tuple-element.89.state, bf16[256,128]{1,0:T(8,128)(2,1)S(1)} %bitcast.25, bf16[1024,192]{1,0:T(8,128)(2,1)S(1)} %get-tuple-element.88.source, ...), custom_call_target="tpu_custom_call" | custom-call | bytes 5767168 | tf_op jit(solution)/shard_map/pallas_call | solution.py:422
  62.9 9.1 %all_to_all.46 = bf16[32,8,128]{2,1,0:T(8,128)(2,1)S(1)} all-to-all(bf16[32,8,128]{2,1,0:T(8,128)(2,1)S(1)} %bitcast.32), channel_id=1, replica_groups=mesh['sect'=4,'node'=8] {'sect','node'}, dimensions={0} | all-to-all | bytes 131072 | tf_op jit(solution)/shard_map/all_to_all | solution.py:587
  72.0 1.8 %shard_map.141 = (f32[128,512]{1,0:T(8,128)S(1)}, bf16[256,128]{1,0:T(8,128)(2,1)S(1)}) custom-call(f32[128,512]{1,0:T(8,128)S(1)} %get-tuple-element.92.mine, bf16[256,128]{1,0:T(8,128)(2,1)S(1)} %bitcast.23, bf16[512,256]{1,0:T(8,128)(2,1)S(1)} %get-tuple-element.94.pick_t, f32[128,512]{1,0:T(8,128)S(1)} %get-tuple-element.95.mixed, ...), custom_call_target="tpu_custom_call" | custom-call | bytes 6815744 | tf_op jit(solution)/shard_map/pallas_call | solution.py:422
  73.8 9.1 %all_to_all.47 = bf16[32,8,128]{2,1,0:T(8,128)(2,1)S(1)} all-to-all(bf16[32,8,128]{2,1,0:T(8,128)(2,1)S(1)} %bitcast.31), channel_id=1, replica_groups=mesh['sect'=4,'node'=8] {'sect','node'}, dimensions={0} | all-to-all | bytes 131072 | tf_op jit(solution)/shard_map/all_to_all | solution.py:587
  82.8 0.5 shard_map.142.refs_8_
  83.3 0.5 collective-permute-start.8
  83.8 0.8 collective-permute-start.9
  84.7 3.1 %collective-permute-start.10 = (bf16[128,512]{1,0:T(8,128)(2,1)S(1)}, bf16[128,512]{1,0:T(8,128)(2,1)S(1)}, u32[]{:S(2)}, u32[]{:S(2)}) collective-permute-start(bf16[128,512]{1,0:T(8,128)(2,1)S(1)} %shard_map.142.refs_8_), channel_id=1, source_target_pairs={{0,6},{1,7},{2,4},{3,5},{4,2},{5,3},{6,0},{7,1},{8,14},{9,15},{10,... | collective-permute-start | bytes 393224 | tf_op jit(solution)/shard_map/ppermute | solution.py:443
  87.8 0.0 collective-permute-start.11
  87.8 3.2 %shard_map.143 = (bf16[256,1024]{1,0:T(8,128)(2,1)S(1)}, bf16[256,1024]{1,0:T(8,128)(2,1)S(1)}, bf16[256,1024]{1,0:T(8,128)(2,1)S(1)}, bf16[256,1024]{1,0:T(8,12...) custom-call(s32[2]{0:T(128)S(1)} %pad_add_fusion.who, ...), custom_call_target="tpu_custom_call" | custom-call | bytes 6225928 | tf_op jit(solution)/shard_map/pallas_call | solution.py:422
  91.0 0.0 collective-permute-done.8.refs_9_
  91.0 0.5 collective-permute-start.12
  91.5 5.2 %collective-permute-done.9.refs_10_ = bf16[128,512]{1,0:T(8,128)(2,1)S(1)} collective-permute-done((bf16[128,512]{1,0:T(8,128)(2,1)S(1)}, bf16[128,512]{1,0:T(8,128)(2,1)S(1)}, u32[]{:S(2)}, u32[]{:S(2)}) %collective-permute-start.9) | collective-permute-done | bytes 131104 | tf_op jit(solution)/shard_map/ppermute | solution.py:443
  96.7 0.0 collective-permute-start.13
  96.7 0.0 collective-permute-done.10.refs_11_
  96.7 0.5 collective-permute-start.14
  97.2 0.0 collective-permute-done.11.refs_12_
  97.2 0.0 collective-permute-done.12.refs_13_
  97.2 0.8 collective-permute-done.13.refs_14_
  98.1 0.2 collective-permute-done.14.refs_15_
  98.2 1.8 %shard_map.144 = (bf16[256,512]{1,0:T(8,128)(2,1)S(1)}, bf16[256,512]{1,0:T(8,128)(2,1)S(1)}) custom-call(s32[2]{0:T(128)S(1)} %pad_add_fusion.who, bf16[256,1024]{1,0:T(8,128)(2,1)S(1)} %get-tuple-element.112.refs_0_, bf16[256,1024]{1,0:T(8,128)(2,1)S(1)} %get-tuple-element.113.refs_1_, bf16[256,1024]{1,0:T(8,128)(2,1)S(1)} %get-tuple-element.114.refs_2_, ...), custom_call_target="tpu_custom_call" | custom-call | bytes 4718600 | tf_op jit(solution)/shard_map/pallas_call | solution.py:422
  100.1 0.5 collective-permute-start.15
  100.6 0.8 collective-permute-start.16
  101.4 1.8 %shard_map.145 = (f32[256,512]{1,0:T(8,128)S(1)}, f32[256,512]{1,0:T(8,128)S(1)}) custom-call(s32[2]{0:T(128)S(1)} %pad_add_fusion.who, bf16[256,1024]{1,0:T(8,128)(2,1)S(1)} %get-tuple-element.103.refs_0_, bf16[256,1024]{1,0:T(8,128)(2,1)S(1)} %get-tuple-element.104.refs_1_, bf16[256,1024]{1,0:T(8,128)(2,1)S(1)} %get-tuple-element.105.refs_2_, ...), custom_call_target="tpu_custom_call" | custom-call | bytes 5242888 | tf_op jit(solution)/shard_map/pallas_call | solution.py:422
  103.2 5.5 %collective-permute-done.15 = bf16[256,512]{1,0:T(8,128)(2,1)S(1)} collective-permute-done((bf16[256,512]{1,0:T(8,128)(2,1)S(1)}, bf16[256,512]{1,0:T(8,128)(2,1)S(1)}, u32[]{:S(2)}, u32[]{:S(2)}) %collective-permute-start.15) | collective-permute-done | bytes 262176 | tf_op jit(solution)/shard_map/ppermute | solution.py:443
  108.7 0.1 convert_add_fusion.2
  108.8 0.7 collective-permute-start.17
  109.5 0.0 collective-permute-done.16
  109.5 0.1 convert_add_fusion.1
  109.6 1.0 collective-permute-start.18
  110.7 3.2 %collective-permute-done.17.refs_2_ = bf16[128,512]{1,0:T(8,128)(2,1)S(1)} collective-permute-done((bf16[128,512]{1,0:T(8,128)(2,1)S(1)}, bf16[128,512]{1,0:T(8,128)(2,1)S(1)}, u32[]{:S(2)}, u32[]{:S(2)}) %collective-permute-start.17) | collective-permute-done | bytes 131104 | tf_op jit(solution)/shard_map/ppermute | solution.py:443
  113.8 0.8 collective-permute-done.18.refs_3_
  114.6 1.2 %shard_map.146 = bf16[256,512]{1,0:T(8,128)(2,1)} custom-call(f32[128,512]{1,0:T(8,128)S(1)} %slice.49.refs_0_, f32[128,512]{1,0:T(8,128)S(1)} %slice.50.refs_1_, bf16[128,512]{1,0:T(8,128)(2,1)S(1)} %collective-permute-done.17.refs_2_, bf16[128,512]{1,0:T(8,128)(2,1)S(1)} %collective-permute-done.18.refs_3_, bf16[512,512]{1,0:T(8,128)(2,1)S(1)} %copy-done.2), custom_call_target="tpu_custom_call" | custom-call | bytes 1572864 | tf_op jit(solution)/shard_map/pallas_call | solution.py:422
  (16 shorter events, 0.2 us)
Async XLA Ops:
  1.7 6.9 %collective-permute-start = (bf16[144,512]{1,0:T(8,128)(2,1)S(1)}, bf16[144,512]{1,0:T(8,128)(2,1)S(1)}, u32[]{:S(2)}, u32[]{:S(2)}) collective-permute-start(bf16[144,512]{1,0:T(8,128)(2,1)S(1)} %get-tuple-element.67.refs_0_), channel_id=1, source_target_pairs={{0,8},{8,0},{16,24},{24,16},{1,9},{9,1},{17,25},{25,17},{2,10},{10... | collective-permute-start | bytes 442376 | tf_op jit(solution)/shard_map/ppermute | solution.py:443
  4.7 5.7 %collective-permute-start.2 = (bf16[144,512]{1,0:T(8,128)(2,1)S(1)}, bf16[144,512]{1,0:T(8,128)(2,1)S(1)}, u32[]{:S(2)}, u32[]{:S(2)}) collective-permute-start(bf16[144,512]{1,0:T(8,128)(2,1)S(1)} %get-tuple-element.68.refs_1_), channel_id=1, source_target_pairs={{0,16},{8,24},{16,0},{24,8},{1,17},{9,25},{17,1},{25,9},{2,18},{10... | collective-permute-start | bytes 442376 | tf_op jit(solution)/shard_map/ppermute | solution.py:443
  8.6 8.8 %collective-permute-start.1 = (bf16[288,512]{1,0:T(8,128)(2,1)S(1)}, bf16[288,512]{1,0:T(8,128)(2,1)S(1)}, u32[]{:S(2)}, u32[]{:S(2)}) collective-permute-start(bf16[288,512]{1,0:T(8,128)(2,1)S(1)} %pad_maximum_fusion), channel_id=1, source_target_pairs={{0,16},{8,24},{16,0},{24,8},{1,17},{9,25},{17,1},{25,9},{2,18},{10... | collective-permute-start | bytes 884744 | tf_op jit(solution)/shard_map/ppermute | solution.py:443
  10.4 7.7 %collective-permute-start.3 = (bf16[288,512]{1,0:T(8,128)(2,1)S(1)}, bf16[288,512]{1,0:T(8,128)(2,1)S(1)}, u32[]{:S(2)}, u32[]{:S(2)}) collective-permute-start(bf16[288,512]{1,0:T(8,128)(2,1)S(1)} %pad_maximum_fusion.1), channel_id=1, source_target_pairs={{0,8},{8,0},{16,24},{24,16},{1,9},{9,1},{17,25},{25,17},{2,10},{10... | collective-permute-start | bytes 884744 | tf_op jit(solution)/shard_map/ppermute | solution.py:443
  20.1 2.0 %collective-permute-start.4 = (bf16[512,512]{1,0:T(8,128)(2,1)S(1)}, bf16[512,512]{1,0:T(8,128)(2,1)S(1)}, u32[]{:S(2)}, u32[]{:S(2)}) collective-permute-start(bf16[512,512]{1,0:T(8,128)(2,1)S(1)} %get-tuple-element.73), channel_id=1, source_target_pairs={{0,1},{1,0},{2,3},{3,2},{4,5},{5,4},{6,7},{7,6},{8,9},{9,8},{10,11... | collective-permute-start | bytes 1572872 | tf_op jit(solution)/shard_map/ppermute | solution.py:443
  22.3 15.1 %copy-start.1 = (bf16[512,512]{1,0:T(8,128)(2,1)S(1)}, bf16[512,512]{1,0:T(8,128)(2,1)}, u32[]{:S(2)}) copy-start(bf16[512,512]{1,0:T(8,128)(2,1)} %weight.1) | copy-start | bytes 1572868
  22.3 15.1 %copy-start.3 = (bf16[1,128,512]{2,1,0:T(8,128)(2,1)S(1)}, bf16[1,128,512]{2,1,0:T(8,128)(2,1)}, u32[]{:S(2)}) copy-start(bf16[1,128,512]{2,1,0:T(8,128)(2,1)} %param.18) | copy-start | bytes 393220
  22.3 8.3 %collective-permute-start.5 = (bf16[128,512]{1,0:T(8,128)(2,1)S(1)}, bf16[128,512]{1,0:T(8,128)(2,1)S(1)}, u32[]{:S(2)}, u32[]{:S(2)}) collective-permute-start(bf16[128,512]{1,0:T(8,128)(2,1)S(1)} %get-tuple-element.136), channel_id=1, source_target_pairs={{0,6},{1,7},{2,4},{3,5},{4,2},{5,3},{6,0},{7,1},{8,14},{9,15},{10,... | collective-permute-start | bytes 393224 | tf_op jit(solution)/shard_map/ppermute | solution.py:443
  26.0 11.4 %collective-permute-start.6 = (bf16[128,512]{1,0:T(8,128)(2,1)S(1)}, bf16[128,512]{1,0:T(8,128)(2,1)S(1)}, u32[]{:S(2)}, u32[]{:S(2)}) collective-permute-start(bf16[128,512]{1,0:T(8,128)(2,1)S(1)} %get-tuple-element.135), channel_id=1, source_target_pairs={{0,4},{1,5},{2,6},{3,7},{4,0},{5,1},{6,2},{7,3},{8,12},{9,13},{10,... | collective-permute-start | bytes 393224 | tf_op jit(solution)/shard_map/ppermute | solution.py:443
  26.0 22.9 %copy-start = (bf16[2,4,512,512]{3,2,1,0:T(8,128)(2,1)S(1)}, bf16[2,4,512,512]{3,2,1,0:T(8,128)(2,1)}, u32[]{:S(2)}) copy-start(bf16[2,4,512,512]{3,2,1,0:T(8,128)(2,1)} %weights.5) | copy-start | bytes 12582916
  26.0 11.4 %collective-permute-start.7 = (bf16[128,512]{1,0:T(8,128)(2,1)S(1)}, bf16[128,512]{1,0:T(8,128)(2,1)S(1)}, u32[]{:S(2)}, u32[]{:S(2)}) collective-permute-start(bf16[128,512]{1,0:T(8,128)(2,1)S(1)} %get-tuple-element.134), channel_id=1, source_target_pairs={{0,2},{1,3},{2,0},{3,1},{4,6},{5,7},{6,4},{7,5},{8,10},{9,11},{10,... | collective-permute-start | bytes 393224 | tf_op jit(solution)/shard_map/ppermute | solution.py:443
  48.9 11.0 %copy-start.4 = (bf16[1,128,512]{2,1,0:T(8,128)(2,1)S(1)}, bf16[1,128,512]{2,1,0:T(8,128)(2,1)}, u32[]{:S(2)}) copy-start(bf16[1,128,512]{2,1,0:T(8,128)(2,1)} %param.23) | copy-start | bytes 393220
  83.3 7.6 %collective-permute-start.8 = (bf16[128,512]{1,0:T(8,128)(2,1)S(1)}, bf16[128,512]{1,0:T(8,128)(2,1)S(1)}, u32[]{:S(2)}, u32[]{:S(2)}) collective-permute-start(bf16[128,512]{1,0:T(8,128)(2,1)S(1)} %shard_map.142.refs_8_), channel_id=1, source_target_pairs={{0,2},{1,3},{2,0},{3,1},{4,6},{5,7},{6,4},{7,5},{8,10},{9,11},{10,... | collective-permute-start | bytes 393224 | tf_op jit(solution)/shard_map/ppermute | solution.py:443
  83.8 12.9 %collective-permute-start.9 = (bf16[128,512]{1,0:T(8,128)(2,1)S(1)}, bf16[128,512]{1,0:T(8,128)(2,1)S(1)}, u32[]{:S(2)}, u32[]{:S(2)}) collective-permute-start(bf16[128,512]{1,0:T(8,128)(2,1)S(1)} %shard_map.142.refs_8_), channel_id=1, source_target_pairs={{0,4},{1,5},{2,6},{3,7},{4,0},{5,1},{6,2},{7,3},{8,12},{9,13},{10,... | collective-permute-start | bytes 393224 | tf_op jit(solution)/shard_map/ppermute | solution.py:443
  84.7 12.1 %collective-permute-start.10 = (bf16[128,512]{1,0:T(8,128)(2,1)S(1)}, bf16[128,512]{1,0:T(8,128)(2,1)S(1)}, u32[]{:S(2)}, u32[]{:S(2)}) collective-permute-start(bf16[128,512]{1,0:T(8,128)(2,1)S(1)} %shard_map.142.refs_8_), channel_id=1, source_target_pairs={{0,6},{1,7},{2,4},{3,5},{4,2},{5,3},{6,0},{7,1},{8,14},{9,15},{10,... | collective-permute-start | bytes 393224 | tf_op jit(solution)/shard_map/ppermute | solution.py:443
  87.8 9.5 %collective-permute-start.11 = (bf16[128,512]{1,0:T(8,128)(2,1)S(1)}, bf16[128,512]{1,0:T(8,128)(2,1)S(1)}, u32[]{:S(2)}, u32[]{:S(2)}) collective-permute-start(bf16[128,512]{1,0:T(8,128)(2,1)S(1)} %shard_map.142.refs_8_), channel_id=1, source_target_pairs={{0,1},{1,0},{2,3},{3,2},{4,5},{5,4},{6,7},{7,6},{8,9},{9,8},{10,11... | collective-permute-start | bytes 393224 | tf_op jit(solution)/shard_map/ppermute | solution.py:443
  91.0 6.3 %collective-permute-start.12 = (bf16[128,512]{1,0:T(8,128)(2,1)S(1)}, bf16[128,512]{1,0:T(8,128)(2,1)S(1)}, u32[]{:S(2)}, u32[]{:S(2)}) collective-permute-start(bf16[128,512]{1,0:T(8,128)(2,1)S(1)} %collective-permute-done.8.refs_9_), channel_id=1, source_target_pairs={{0,1},{1,0},{2,3},{3,2},{4,5},{5,4},{6,7},{7,6},{8,9},{9,8},{10,11... | collective-permute-start | bytes 393224 | tf_op jit(solution)/shard_map/ppermute | solution.py:443
  96.7 1.3 %collective-permute-start.13 = (bf16[128,512]{1,0:T(8,128)(2,1)S(1)}, bf16[128,512]{1,0:T(8,128)(2,1)S(1)}, u32[]{:S(2)}, u32[]{:S(2)}) collective-permute-start(bf16[128,512]{1,0:T(8,128)(2,1)S(1)} %collective-permute-done.9.refs_10_), channel_id=1, source_target_pairs={{0,1},{1,0},{2,3},{3,2},{4,5},{5,4},{6,7},{7,6},{8,9},{9,8},{10,11... | collective-permute-start | bytes 393224 | tf_op jit(solution)/shard_map/ppermute | solution.py:443
  96.7 1.5 %collective-permute-start.14 = (bf16[128,512]{1,0:T(8,128)(2,1)S(1)}, bf16[128,512]{1,0:T(8,128)(2,1)S(1)}, u32[]{:S(2)}, u32[]{:S(2)}) collective-permute-start(bf16[128,512]{1,0:T(8,128)(2,1)S(1)} %collective-permute-done.10.refs_11_), channel_id=1, source_target_pairs={{0,1},{1,0},{2,3},{3,2},{4,5},{5,4},{6,7},{7,6},{8,9},{9,8},{10,11... | collective-permute-start | bytes 393224 | tf_op jit(solution)/shard_map/ppermute | solution.py:443
  100.1 8.6 %collective-permute-start.15 = (bf16[256,512]{1,0:T(8,128)(2,1)S(1)}, bf16[256,512]{1,0:T(8,128)(2,1)S(1)}, u32[]{:S(2)}, u32[]{:S(2)}) collective-permute-start(bf16[256,512]{1,0:T(8,128)(2,1)S(1)} %get-tuple-element.120), channel_id=1, source_target_pairs={{0,8},{8,0},{16,24},{24,16},{1,9},{9,1},{17,25},{25,17},{2,10},{10... | collective-permute-start | bytes 786440 | tf_op jit(solution)/shard_map/ppermute | solution.py:443
  100.6 8.9 %collective-permute-start.16 = (bf16[256,512]{1,0:T(8,128)(2,1)S(1)}, bf16[256,512]{1,0:T(8,128)(2,1)S(1)}, u32[]{:S(2)}, u32[]{:S(2)}) collective-permute-start(bf16[256,512]{1,0:T(8,128)(2,1)S(1)} %get-tuple-element.131), channel_id=1, source_target_pairs={{0,16},{8,24},{16,0},{24,8},{1,17},{9,25},{17,1},{25,9},{2,18},{10... | collective-permute-start | bytes 786440 | tf_op jit(solution)/shard_map/ppermute | solution.py:443
  108.7 5.9 %copy-start.2 = (bf16[512,512]{1,0:T(8,128)(2,1)S(1)}, bf16[512,512]{1,0:T(8,128)(2,1)}, u32[]{:S(2)}) copy-start(bf16[512,512]{1,0:T(8,128)(2,1)} %refs_4_.3) | copy-start | bytes 1572868
  108.8 5.0 %collective-permute-start.17 = (bf16[128,512]{1,0:T(8,128)(2,1)S(1)}, bf16[128,512]{1,0:T(8,128)(2,1)S(1)}, u32[]{:S(2)}, u32[]{:S(2)}) collective-permute-start(bf16[128,512]{1,0:T(8,128)(2,1)S(1)} %slice.56), channel_id=1, source_target_pairs={{0,16},{8,24},{16,0},{24,8},{1,17},{9,25},{17,1},{25,9},{2,18},{10... | collective-permute-start | bytes 393224 | tf_op jit(solution)/shard_map/ppermute | solution.py:443
  109.6 5.0 %collective-permute-start.18 = (bf16[128,512]{1,0:T(8,128)(2,1)S(1)}, bf16[128,512]{1,0:T(8,128)(2,1)S(1)}, u32[]{:S(2)}, u32[]{:S(2)}) collective-permute-start(bf16[128,512]{1,0:T(8,128)(2,1)S(1)} %slice.55), channel_id=1, source_target_pairs={{0,8},{8,0},{16,24},{24,16},{1,9},{9,1},{17,25},{25,17},{2,10},{10... | collective-permute-start | bytes 393224 | tf_op jit(solution)/shard_map/ppermute | solution.py:443

commit v3 on v2

--- a/solution.py
+++ b/solution.py
@@ -12,6 +12,7 @@
 BF16 = jnp.bfloat16
 LANES = 128
 META_ROWS = 16
+CHUNKS = 2
 MIB = 1024 * 1024
 
 
@@ -393,24 +394,31 @@
     picked = dot(
         jnp.concatenate(marks, axis=0), jnp.concatenate([ref[...] for ref in grads], axis=0)
     )
-    per = count // len(outs)
+    size = outs[0].shape[1]
+    chunks = slopes[0].shape[1] // size
+    per = count * chunks // len(outs)
     for i in range(count):
-        total = jnp.zeros((rows, outs[0].shape[1]), F32)
+        total = jnp.zeros((rows, slopes[0].shape[1]), F32)
         for k in range(fanout):
             at = (i * fanout + k) * rows
             part = slopes[i][k * rows : (k + 1) * rows, :].astype(F32)
             total = total + picked[at : at + rows] * part
-        out, at = outs[i // per], i % per * rows
-        out[at : at + rows, :] = total.astype(out.dtype)
-
-
-def grid_back_kernel(*refs):
+        at = i % per * rows
+        for c, out in enumerate(outs[i // per * chunks : (i // per + 1) * chunks]):
+            out[at : at + rows, :] = total[:, c * size : (c + 1) * size].astype(out.dtype)
+
+
+def grid_back_kernel(chunks, *refs):
     *parts, weight, out = refs
     count = len(parts) // 2
     total = [
         mine[...] + given[...].astype(F32) for mine, given in zip(parts[:count], parts[count:])
     ]
-    out[...] = back_dot(jnp.concatenate(total, axis=0), weight[...]).astype(BF16)
+    each = count // chunks
+    columns = [
+        jnp.concatenate(total[c * each : (c + 1) * each], axis=0) for c in range(chunks)
+    ]
+    out[...] = back_dot(jnp.concatenate(columns, axis=1), weight[...]).astype(BF16)
 
 
 def call(kernel, outs, args, smem=0, scratch=(), space=pltpu.VMEM, aliases=None):
@@ -648,7 +656,11 @@
                 block,
                 fanout,
             ),
-            [shape((len(group) * part_rows, width), dtype) for group in groups],
+            [
+                shape((len(group) * part_rows, width // CHUNKS), dtype)
+                for group in groups
+                for _ in range(CHUNKS)
+            ],
             [
                 who,
                 *(picks_of[unit][0] for unit in used),
@@ -664,23 +676,31 @@
     given = message_back(sent, BF16)
     gathered = lax.optimization_barrier((*gathered, given[0]))[:-1]
     kept = message_back([[(j, p) for j in stay[p]] for p in range(len(axes))], F32)
+    turns = [(p, c) for c in range(CHUNKS) for p in range(len(axes))]
+    given = [given[p * CHUNKS + c] for p, c in turns]
+    kept = [kept[p * CHUNKS + c] for p, c in turns]
     for step in range(len(axes)):
-        order = [axes[(p + step) % len(axes)] for p in range(len(axes))]
-        given = [swap(part, "sect", axis) for part, axis in zip(given, order)]
+        given = [
+            swap(part, "sect", axes[(p + step) % len(axes)])
+            for part, (p, _) in zip(given, turns)
+        ]
         if step + 1 == len(axes):
             break
         kept = [mine + part.astype(F32) for mine, part in zip(kept, given)]
-        given = []
-        for p, axis in enumerate(axes[(p + step + 1) % len(axes)] for p in range(len(axes))):
-            rows = kept[p].reshape(len(stay[p]), part_rows, width)
-            left = [j for j in stay[p] if not j & axis]
+        given, left = [], []
+        for p in range(len(axes)):
+            axis = axes[(p + step + 1) % len(axes)]
+            left.append([j for j in stay[p] if not j & axis])
+        for i, (p, _) in enumerate(turns):
+            axis = axes[(p + step + 1) % len(axes)]
+            rows = kept[i].reshape(len(stay[p]), part_rows, width // CHUNKS)
             given.append(
-                jnp.concatenate([rows[stay[p].index(j ^ axis)] for j in left]).astype(BF16)
+                jnp.concatenate([rows[stay[p].index(j ^ axis)] for j in left[p]]).astype(BF16)
             )
-            kept[p] = jnp.concatenate([rows[stay[p].index(j)] for j in left])
-            stay[p] = left
+            kept[i] = jnp.concatenate([rows[stay[p].index(j)] for j in left[p]])
+        stay = left
     (grid_grad,) = call(
-        grid_back_kernel,
+        functools.partial(grid_back_kernel, CHUNKS),
         [shape((grid_rows, width), BF16)],
         [*kept, *given, enc_weight],
     )

time: 116 us -> 115 us (level)
  waiting for transfers between devices: 28.2 us -> 22.1 us
  starting transfers between devices: 20.9 us -> 26.4 us
    ppermute x19 -> x23, waiting for transfers between devices: 28.2 us -> 22.1 us  [swap(): return lax.ppermute(value, axis, [(i, i ^ apart) for i in range(size)])]
    ppermute x19 -> x23, starting transfers between devices: 20.9 us -> 26.4 us  [swap(): return lax.ppermute(value, axis, [(i, i ^ apart) for i in range(size)])]
  transfers between devices with their start and end apart: 19 -> 23, of which waited for: 11 -> 14; matrix products, arithmetic and copies ran while one was open for 0% -> 0% of each run, Pallas kernels for 11% -> 12%
where the time goes in v3:
time: 115 us
  blocking collectives  38.2 us (33%)
  Pallas kernels  27 us (23%)
  starting transfers between devices  26.4 us (23%)
  waiting for transfers between devices  22.1 us (19%)
    all_to_all x4, blocking collectives, exchange(): return lax.all_to_all(value, both, split_axis=0, concat_axis=0, tiled=True)  38.2 us
    pallas_call x16, Pallas kernels, call(): pl.pallas_call(kernel, out_shape=list(outs), in_specs=specs, out_specs=[p...  27 us
    ppermute x23, starting transfers between devices, swap(): return lax.ppermute(value, axis, [(i, i ^ apart) for i in range(size)])  26.4 us
    ppermute x23, waiting for transfers between devices, swap(): return lax.ppermute(value, axis, [(i, i ^ apart) for i in range(size)])  22.1 us
  transfers between devices with their start and end apart: 23, of which 14 were waited for; matrix products, arithmetic and copies ran while one was open for 0% of the time, Pallas kernels for 12%

profile of v3, /device:TPU:0, one launch (start us, length us, event | category | flops | bytes accessed | tf_op | source)
XLA Modules:
  0.0 115.1 jit_solution(1747094143432506240)
XLA Ops:
  0.6 1.1 shard_map.131
  1.7 3.0 %collective-permute-start = (bf16[144,512]{1,0:T(8,128)(2,1)S(1)}, bf16[144,512]{1,0:T(8,128)(2,1)S(1)}, u32[]{:S(2)}, u32[]{:S(2)}) collective-permute-start(bf16[144,512]{1,0:T(8,128)(2,1)S(1)} %get-tuple-element.71.refs_0_), channel_id=1, source_target_pairs={{0,8},{8,0},{16,24},{24,16},{1,9},{9,1},{17,25},{25,17},{2,10},{10... | collective-permute-start | bytes 442376 | tf_op jit(solution)/shard_map/ppermute | solution.py:451
  4.7 1.5 %collective-permute-start.2 = (bf16[144,512]{1,0:T(8,128)(2,1)S(1)}, bf16[144,512]{1,0:T(8,128)(2,1)S(1)}, u32[]{:S(2)}, u32[]{:S(2)}) collective-permute-start(bf16[144,512]{1,0:T(8,128)(2,1)S(1)} %get-tuple-element.72.refs_1_), channel_id=1, source_target_pairs={{0,16},{8,24},{16,0},{24,8},{1,17},{9,25},{17,1},{25,9},{2,18},{10... | collective-permute-start | bytes 442376 | tf_op jit(solution)/shard_map/ppermute | solution.py:451
  6.2 2.3 %collective-permute-done.refs_0_.refs_2_ = bf16[144,512]{1,0:T(8,128)(2,1)S(1)} collective-permute-done((bf16[144,512]{1,0:T(8,128)(2,1)S(1)}, bf16[144,512]{1,0:T(8,128)(2,1)S(1)}, u32[]{:S(2)}, u32[]{:S(2)}) %collective-permute-start) | collective-permute-done | bytes 147488 | tf_op jit(solution)/shard_map/ppermute | solution.py:451
  8.6 1.8 %collective-permute-start.1 = (bf16[288,512]{1,0:T(8,128)(2,1)S(1)}, bf16[288,512]{1,0:T(8,128)(2,1)S(1)}, u32[]{:S(2)}, u32[]{:S(2)}) collective-permute-start(bf16[288,512]{1,0:T(8,128)(2,1)S(1)} %pad_maximum_fusion), channel_id=1, source_target_pairs={{0,16},{8,24},{16,0},{24,8},{1,17},{9,25},{17,1},{25,9},{2,18},{10... | collective-permute-start | bytes 884744 | tf_op jit(solution)/shard_map/ppermute | solution.py:451
  10.4 0.0 collective-permute-done.2.refs_1_.refs_5_
  10.4 1.6 %collective-permute-start.3 = (bf16[288,512]{1,0:T(8,128)(2,1)S(1)}, bf16[288,512]{1,0:T(8,128)(2,1)S(1)}, u32[]{:S(2)}, u32[]{:S(2)}) collective-permute-start(bf16[288,512]{1,0:T(8,128)(2,1)S(1)} %pad_maximum_fusion.1), channel_id=1, source_target_pairs={{0,8},{8,0},{16,24},{24,16},{1,9},{9,1},{17,25},{25,17},{2,10},{10... | collective-permute-start | bytes 884744 | tf_op jit(solution)/shard_map/ppermute | solution.py:451
  12.0 1.5 %shard_map.132 = (bf16[256,512]{1,0:T(8,128)(2,1)S(1)}, bf16[512,256]{1,0:T(8,128)(2,1)S(1)}, bf16[1024,192]{1,0:T(8,128)(2,1)S(1)}, bf16[192,1024]{1,0:T(8,128)...) custom-call(s32[4,2,8]{2,1,0:T(2,128)} %bitcast.33, s32[8,128]{1,0:T(8,128)} %bitcast.34, ...), custom_call_target="tpu_custom_call" | custom-call | bytes 2367744 | tf_op jit(solution)/shard_map/pallas_call | solution.py:430
  13.5 0.1 pad_add_fusion.who
  13.6 1.9 %shard_map.133.refs_4_ = f32[1024,512]{1,0:T(8,128)S(1)} custom-call(s32[2]{0:T(128)S(1)} %pad_add_fusion.who, bf16[144,512]{1,0:T(8,128)(2,1)S(1)} %get-tuple-element.71.refs_0_, bf16[144,512]{1,0:T(8,128)(2,1)S(1)} %get-tuple-element.72.refs_1_, bf16[512,512]{1,0:T(8,128)(2,1)S(1)} %get-tuple-element.73.refs_2_.refs_4_.refs_8_, ...), custom_call_target="tpu_custom_call" | custom-call | bytes 2918408 | tf_op jit(solution)/shard_map/pallas_call | solution.py:430
  15.5 1.9 %shard_map.134.refs_6_.before = f32[1024,512]{1,0:T(8,128)S(1)} custom-call(s32[2]{0:T(128)S(1)} %pad_add_fusion.who, bf16[144,512]{1,0:T(8,128)(2,1)S(1)} %collective-permute-done.refs_0_.refs_2_, bf16[144,512]{1,0:T(8,128)(2,1)S(1)} %collective-permute-done.2.refs_1_.refs_5_, ...), custom_call_target="tpu_custom_call", output_to_operand_aliasing={{}: (5, {})} | custom-call | bytes 5015560 | tf_op jit(solution)/shard_map/pallas_call | solution.py:430
  17.4 0.0 collective-permute-done.1.refs_0_.refs_1_.refs_4_.refs_6_
  17.4 0.7 collective-permute-done.3.refs_2_.refs_3_.refs_7_
  18.1 2.0 %shard_map.135 = (bf16[512,512]{1,0:T(8,128)(2,1)S(1)}, bf16[1024,512]{1,0:T(8,128)(2,1)S(1)}, s32[1,1024]{1,0:T(1,128)S(1)}) custom-call(s32[2]{0:T(128)S(1)} %pad_add_fusion.who, bf16[288,512]{1,0:T(8,128)(2,1)S(1)} %collective-permute-done.1.refs_0_.refs_1_.refs_4_.refs_6_, bf16[288,512]{1,0:T(8,128)(2,1)S(1)} %collective-permute-done.1.refs_0_.refs_1_.refs_4_.refs_6_, ...), custom_call_target="tpu_custom_call" | custom-call | bytes 5380104 | tf_op jit(solution)/shard_map/pallas_call | solution.py:430
  20.1 0.1 collective-permute-start.4
  20.2 0.7 shard_map.136
  20.9 1.2 %collective-permute-done.4 = bf16[512,512]{1,0:T(8,128)(2,1)S(1)} collective-permute-done((bf16[512,512]{1,0:T(8,128)(2,1)S(1)}, bf16[512,512]{1,0:T(8,128)(2,1)S(1)}, u32[]{:S(2)}, u32[]{:S(2)}) %collective-permute-start.4) | collective-permute-done | bytes 524320 | tf_op jit(solution)/shard_map/ppermute | solution.py:451
  22.1 0.2 fusion
  22.3 0.0 copy-start.1
  22.3 0.0 copy-start.3
  22.3 3.7 %collective-permute-start.5 = (bf16[128,512]{1,0:T(8,128)(2,1)S(1)}, bf16[128,512]{1,0:T(8,128)(2,1)S(1)}, u32[]{:S(2)}, u32[]{:S(2)}) collective-permute-start(bf16[128,512]{1,0:T(8,128)(2,1)S(1)} %get-tuple-element.144), channel_id=1, source_target_pairs={{0,6},{1,7},{2,4},{3,5},{4,2},{5,3},{6,0},{7,1},{8,14},{9,15},{10,... | collective-permute-start | bytes 393224 | tf_op jit(solution)/shard_map/ppermute | solution.py:451
  26.0 0.0 collective-permute-start.6
  26.0 0.8 collective-permute-start.7
  26.8 2.3 %shard_map.137 = (bf16[256,512]{1,0:T(8,128)(2,1)S(1)}, bf16[256,512]{1,0:T(8,128)(2,1)S(1)}, bf16[256,512]{1,0:T(8,128)(2,1)S(1)}, bf16[256,512]{1,0:T(8,128)(2...) custom-call(bf16[144,512]{1,0:T(8,128)(2,1)S(1)} %get-tuple-element., ...), custom_call_target="tpu_custom_call" | custom-call | bytes 4392960 | tf_op jit(solution)/shard_map/pallas_call | solution.py:430
  29.1 1.5 %collective-permute-done.5.refs_0_ = bf16[128,512]{1,0:T(8,128)(2,1)S(1)} collective-permute-done((bf16[128,512]{1,0:T(8,128)(2,1)S(1)}, bf16[128,512]{1,0:T(8,128)(2,1)S(1)}, u32[]{:S(2)}, u32[]{:S(2)}) %collective-permute-start.5) | collective-permute-done | bytes 131104 | tf_op jit(solution)/shard_map/ppermute | solution.py:451
  30.6 6.7 %collective-permute-done.6.refs_1_ = bf16[128,512]{1,0:T(8,128)(2,1)S(1)} collective-permute-done((bf16[128,512]{1,0:T(8,128)(2,1)S(1)}, bf16[128,512]{1,0:T(8,128)(2,1)S(1)}, u32[]{:S(2)}, u32[]{:S(2)}) %collective-permute-start.6) | collective-permute-done | bytes 131104 | tf_op jit(solution)/shard_map/ppermute | solution.py:451
  37.4 0.0 collective-permute-done.7.refs_2_
  37.4 0.5 shard_map.138
  37.9 11.0 %all_to_all.44 = bf16[32,8,128]{2,1,0:T(8,128)(2,1)S(1)} all-to-all(bf16[32,8,128]{2,1,0:T(8,128)(2,1)S(1)} %bitcast.29), channel_id=1, replica_groups=mesh['sect'=4,'node'=8] {'sect','node'}, dimensions={0} | all-to-all | bytes 131072 | tf_op jit(solution)/shard_map/all_to_all | solution.py:595
  48.9 1.9 %shard_map.139 = (bf16[128,512]{1,0:T(8,128)(2,1)S(1)}, f32[128,512]{1,0:T(8,128)S(1)}, bf16[1024,512]{1,0:T(8,128)(2,1)S(1)}, bf16[256,128]{1,0:T(8,128)(2,1)S(1)}) custom-call(bf16[128,512]{1,0:T(8,128)(2,1)S(1)} %get-tuple-element.90.state, bf16[256,128]{1,0:T(8,128)(2,1)S(1)} %bitcast.24, bf16[1024,192]{1,0:T(8,128)(2,1)S(1)} %get-tuple-element.92.source, ...), custom_call_target="tpu_custom_call" | custom-call | bytes 6553600 | tf_op jit(solution)/shard_map/pallas_call | solution.py:430
  50.8 9.1 %all_to_all.45 = bf16[32,8,128]{2,1,0:T(8,128)(2,1)S(1)} all-to-all(bf16[32,8,128]{2,1,0:T(8,128)(2,1)S(1)} %bitcast.30), channel_id=1, replica_groups=mesh['sect'=4,'node'=8] {'sect','node'}, dimensions={0} | all-to-all | bytes 131072 | tf_op jit(solution)/shard_map/all_to_all | solution.py:595
  59.8 3.0 %shard_map.140 = (bf16[128,512]{1,0:T(8,128)(2,1)S(1)}, f32[128,512]{1,0:T(8,128)S(1)}, bf16[256,128]{1,0:T(8,128)(2,1)S(1)}) custom-call(bf16[128,512]{1,0:T(8,128)(2,1)S(1)} %get-tuple-element.93.state, bf16[256,128]{1,0:T(8,128)(2,1)S(1)} %bitcast.25, bf16[1024,192]{1,0:T(8,128)(2,1)S(1)} %get-tuple-element.92.source, ...), custom_call_target="tpu_custom_call" | custom-call | bytes 5767168 | tf_op jit(solution)/shard_map/pallas_call | solution.py:430
  62.9 9.1 %all_to_all.46 = bf16[32,8,128]{2,1,0:T(8,128)(2,1)S(1)} all-to-all(bf16[32,8,128]{2,1,0:T(8,128)(2,1)S(1)} %bitcast.32), channel_id=1, replica_groups=mesh['sect'=4,'node'=8] {'sect','node'}, dimensions={0} | all-to-all | bytes 131072 | tf_op jit(solution)/shard_map/all_to_all | solution.py:595
  72.0 1.8 %shard_map.141 = (f32[128,512]{1,0:T(8,128)S(1)}, bf16[256,128]{1,0:T(8,128)(2,1)S(1)}) custom-call(f32[128,512]{1,0:T(8,128)S(1)} %get-tuple-element.96.mine, bf16[256,128]{1,0:T(8,128)(2,1)S(1)} %bitcast.23, bf16[512,256]{1,0:T(8,128)(2,1)S(1)} %get-tuple-element.98.pick_t, f32[128,512]{1,0:T(8,128)S(1)} %get-tuple-element.99.mixed, ...), custom_call_target="tpu_custom_call" | custom-call | bytes 6815744 | tf_op jit(solution)/shard_map/pallas_call | solution.py:430
  73.8 9.1 %all_to_all.47 = bf16[32,8,128]{2,1,0:T(8,128)(2,1)S(1)} all-to-all(bf16[32,8,128]{2,1,0:T(8,128)(2,1)S(1)} %bitcast.31), channel_id=1, replica_groups=mesh['sect'=4,'node'=8] {'sect','node'}, dimensions={0} | all-to-all | bytes 131072 | tf_op jit(solution)/shard_map/all_to_all | solution.py:595
  82.8 0.5 shard_map.142.refs_8_
  83.3 0.5 collective-permute-start.8
  83.8 0.8 collective-permute-start.9
  84.7 3.1 %collective-permute-start.10 = (bf16[128,512]{1,0:T(8,128)(2,1)S(1)}, bf16[128,512]{1,0:T(8,128)(2,1)S(1)}, u32[]{:S(2)}, u32[]{:S(2)}) collective-permute-start(bf16[128,512]{1,0:T(8,128)(2,1)S(1)} %shard_map.142.refs_8_), channel_id=1, source_target_pairs={{0,6},{1,7},{2,4},{3,5},{4,2},{5,3},{6,0},{7,1},{8,14},{9,15},{10,... | collective-permute-start | bytes 393224 | tf_op jit(solution)/shard_map/ppermute | solution.py:451
  87.8 0.0 collective-permute-start.11
  87.8 3.2 %shard_map.143 = (bf16[256,1024]{1,0:T(8,128)(2,1)S(1)}, bf16[256,1024]{1,0:T(8,128)(2,1)S(1)}, bf16[256,1024]{1,0:T(8,128)(2,1)S(1)}, bf16[256,1024]{1,0:T(8,12...) custom-call(s32[2]{0:T(128)S(1)} %pad_add_fusion.who, ...), custom_call_target="tpu_custom_call" | custom-call | bytes 6225928 | tf_op jit(solution)/shard_map/pallas_call | solution.py:430
  91.0 0.5 collective-permute-start.12
  91.5 5.2 %collective-permute-done.9.refs_10_ = bf16[128,512]{1,0:T(8,128)(2,1)S(1)} collective-permute-done((bf16[128,512]{1,0:T(8,128)(2,1)S(1)}, bf16[128,512]{1,0:T(8,128)(2,1)S(1)}, u32[]{:S(2)}, u32[]{:S(2)}) %collective-permute-start.9) | collective-permute-done | bytes 131104 | tf_op jit(solution)/shard_map/ppermute | solution.py:451
  96.7 0.5 collective-permute-start.14
  97.2 0.0 collective-permute-done.12.refs_13_
  97.2 0.8 collective-permute-done.13.refs_14_
  98.1 0.2 collective-permute-done.14.refs_15_
  98.2 1.8 %shard_map.144 = (bf16[256,256]{1,0:T(8,128)(2,1)S(1)}, bf16[256,256]{1,0:T(8,128)(2,1)S(1)}, bf16[256,256]{1,0:T(8,128)(2,1)S(1)}, bf16[256,256]{1,0:T(8,128)(2,1)S(1)}) custom-call(s32[2]{0:T(128)S(1)} %pad_add_fusion.who, bf16[256,1024]{1,0:T(8,128)(2,1)S(1)} %get-tuple-element.116.refs_0_, bf16[256,1024]{1,0:T(8,128)(2,1)S(1)} %get-tuple-element.117.refs_1_, ...), custom_call_target="tpu_custom_call" | custom-call | bytes 4718600 | tf_op jit(solution)/shard_map/pallas_call | solution.py:430
  100.1 0.5 collective-permute-start.15
  100.6 0.8 collective-permute-start.16
  101.4 1.4 %collective-permute-start.17 = (bf16[256,256]{1,0:T(8,128)(2,1)S(1)}, bf16[256,256]{1,0:T(8,128)(2,1)S(1)}, u32[]{:S(2)}, u32[]{:S(2)}) collective-permute-start(bf16[256,256]{1,0:T(8,128)(2,1)S(1)} %get-tuple-element.137), channel_id=1, source_target_pairs={{0,8},{8,0},{16,24},{24,16},{1,9},{9,1},{17,25},{25,17},{2,10},{10... | collective-permute-start | bytes 393224 | tf_op jit(solution)/shard_map/ppermute | solution.py:451
  102.8 1.4 %collective-permute-start.18 = (bf16[256,256]{1,0:T(8,128)(2,1)S(1)}, bf16[256,256]{1,0:T(8,128)(2,1)S(1)}, u32[]{:S(2)}, u32[]{:S(2)}) collective-permute-start(bf16[256,256]{1,0:T(8,128)(2,1)S(1)} %get-tuple-element.139), channel_id=1, source_target_pairs={{0,16},{8,24},{16,0},{24,8},{1,17},{9,25},{17,1},{25,9},{2,18},{10... | collective-permute-start | bytes 393224 | tf_op jit(solution)/shard_map/ppermute | solution.py:451
  104.2 1.8 %shard_map.145 = (f32[256,256]{1,0:T(8,128)S(1)}, f32[256,256]{1,0:T(8,128)S(1)}, f32[256,256]{1,0:T(8,128)S(1)}, f32[256,256]{1,0:T(8,128)S(1)}) custom-call(s32[2]{0:T(128)S(1)} %pad_add_fusion.who, bf16[256,1024]{1,0:T(8,128)(2,1)S(1)} %get-tuple-element.107.refs_0_, bf16[256,1024]{1,0:T(8,128)(2,1)S(1)} %get-tuple-element.108.refs_1_, ...), custom_call_target="tpu_custom_call" | custom-call | bytes 5242888 | tf_op jit(solution)/shard_map/pallas_call | solution.py:430
  106.0 0.4 collective-permute-done.15
  106.5 0.7 collective-permute-start.19
  107.2 1.4 %collective-permute-start.20 = (bf16[128,256]{1,0:T(8,128)(2,1)S(1)}, bf16[128,256]{1,0:T(8,128)(2,1)S(1)}, u32[]{:S(2)}, u32[]{:S(2)}) collective-permute-start(bf16[128,256]{1,0:T(8,128)(2,1)S(1)} %slice.85), channel_id=1, source_target_pairs={{0,8},{8,0},{16,24},{24,16},{1,9},{9,1},{17,25},{25,17},{2,10},{10... | collective-permute-start | bytes 196616 | tf_op jit(solution)/shard_map/ppermute | solution.py:451
  108.6 0.1 collective-permute-done.17
  108.8 0.6 collective-permute-start.21
  109.4 0.1 collective-permute-done.18
  109.6 1.6 %collective-permute-start.22 = (bf16[128,256]{1,0:T(8,128)(2,1)S(1)}, bf16[128,256]{1,0:T(8,128)(2,1)S(1)}, u32[]{:S(2)}, u32[]{:S(2)}) collective-permute-start(bf16[128,256]{1,0:T(8,128)(2,1)S(1)} %slice.83), channel_id=1, source_target_pairs={{0,8},{8,0},{16,24},{24,16},{1,9},{9,1},{17,25},{25,17},{2,10},{10... | collective-permute-start | bytes 196616 | tf_op jit(solution)/shard_map/ppermute | solution.py:451
  111.3 0.5 collective-permute-done.20.refs_5_
  111.9 1.3 %collective-permute-done.21.refs_6_ = bf16[128,256]{1,0:T(8,128)(2,1)S(1)} collective-permute-done((bf16[128,256]{1,0:T(8,128)(2,1)S(1)}, bf16[128,256]{1,0:T(8,128)(2,1)S(1)}, u32[]{:S(2)}, u32[]{:S(2)}) %collective-permute-start.21) | collective-permute-done | bytes 65568 | tf_op jit(solution)/shard_map/ppermute | solution.py:451
  113.1 0.8 collective-permute-done.22.refs_7_
  113.9 1.2 %shard_map.146 = bf16[256,512]{1,0:T(8,128)(2,1)} custom-call(f32[128,256]{1,0:T(8,128)S(1)} %slice.71.refs_0_, f32[128,256]{1,0:T(8,128)S(1)} %slice.72.refs_1_, f32[128,256]{1,0:T(8,128)S(1)} %slice.73.refs_2_, f32[128,256]{1,0:T(8,128)S(1)} %slice.74.refs_3_, bf16[128,256]{1,0:T(8,128)(2,1)S(1)} %collective-permute-done.19.refs_4_, ...), custom_call_target="tpu_custom_call" | custom-call | bytes 1572864 | tf_op jit(solution)/shard_map/pallas_call | solution.py:430
  (30 shorter events, 0.3 us)
Async XLA Ops:
  1.7 6.9 %collective-permute-start = (bf16[144,512]{1,0:T(8,128)(2,1)S(1)}, bf16[144,512]{1,0:T(8,128)(2,1)S(1)}, u32[]{:S(2)}, u32[]{:S(2)}) collective-permute-start(bf16[144,512]{1,0:T(8,128)(2,1)S(1)} %get-tuple-element.71.refs_0_), channel_id=1, source_target_pairs={{0,8},{8,0},{16,24},{24,16},{1,9},{9,1},{17,25},{25,17},{2,10},{10... | collective-permute-start | bytes 442376 | tf_op jit(solution)/shard_map/ppermute | solution.py:451
  4.7 5.7 %collective-permute-start.2 = (bf16[144,512]{1,0:T(8,128)(2,1)S(1)}, bf16[144,512]{1,0:T(8,128)(2,1)S(1)}, u32[]{:S(2)}, u32[]{:S(2)}) collective-permute-start(bf16[144,512]{1,0:T(8,128)(2,1)S(1)} %get-tuple-element.72.refs_1_), channel_id=1, source_target_pairs={{0,16},{8,24},{16,0},{24,8},{1,17},{9,25},{17,1},{25,9},{2,18},{10... | collective-permute-start | bytes 442376 | tf_op jit(solution)/shard_map/ppermute | solution.py:451
  8.6 8.8 %collective-permute-start.1 = (bf16[288,512]{1,0:T(8,128)(2,1)S(1)}, bf16[288,512]{1,0:T(8,128)(2,1)S(1)}, u32[]{:S(2)}, u32[]{:S(2)}) collective-permute-start(bf16[288,512]{1,0:T(8,128)(2,1)S(1)} %pad_maximum_fusion), channel_id=1, source_target_pairs={{0,16},{8,24},{16,0},{24,8},{1,17},{9,25},{17,1},{25,9},{2,18},{10... | collective-permute-start | bytes 884744 | tf_op jit(solution)/shard_map/ppermute | solution.py:451
  10.4 7.7 %collective-permute-start.3 = (bf16[288,512]{1,0:T(8,128)(2,1)S(1)}, bf16[288,512]{1,0:T(8,128)(2,1)S(1)}, u32[]{:S(2)}, u32[]{:S(2)}) collective-permute-start(bf16[288,512]{1,0:T(8,128)(2,1)S(1)} %pad_maximum_fusion.1), channel_id=1, source_target_pairs={{0,8},{8,0},{16,24},{24,16},{1,9},{9,1},{17,25},{25,17},{2,10},{10... | collective-permute-start | bytes 884744 | tf_op jit(solution)/shard_map/ppermute | solution.py:451
  20.1 2.0 %collective-permute-start.4 = (bf16[512,512]{1,0:T(8,128)(2,1)S(1)}, bf16[512,512]{1,0:T(8,128)(2,1)S(1)}, u32[]{:S(2)}, u32[]{:S(2)}) collective-permute-start(bf16[512,512]{1,0:T(8,128)(2,1)S(1)} %get-tuple-element.77), channel_id=1, source_target_pairs={{0,1},{1,0},{2,3},{3,2},{4,5},{5,4},{6,7},{7,6},{8,9},{9,8},{10,11... | collective-permute-start | bytes 1572872 | tf_op jit(solution)/shard_map/ppermute | solution.py:451
  22.3 15.1 %copy-start.1 = (bf16[512,512]{1,0:T(8,128)(2,1)S(1)}, bf16[512,512]{1,0:T(8,128)(2,1)}, u32[]{:S(2)}) copy-start(bf16[512,512]{1,0:T(8,128)(2,1)} %weight.1) | copy-start | bytes 1572868
  22.3 15.1 %copy-start.3 = (bf16[1,128,512]{2,1,0:T(8,128)(2,1)S(1)}, bf16[1,128,512]{2,1,0:T(8,128)(2,1)}, u32[]{:S(2)}) copy-start(bf16[1,128,512]{2,1,0:T(8,128)(2,1)} %param.18) | copy-start | bytes 393220
  22.3 8.3 %collective-permute-start.5 = (bf16[128,512]{1,0:T(8,128)(2,1)S(1)}, bf16[128,512]{1,0:T(8,128)(2,1)S(1)}, u32[]{:S(2)}, u32[]{:S(2)}) collective-permute-start(bf16[128,512]{1,0:T(8,128)(2,1)S(1)} %get-tuple-element.144), channel_id=1, source_target_pairs={{0,6},{1,7},{2,4},{3,5},{4,2},{5,3},{6,0},{7,1},{8,14},{9,15},{10,... | collective-permute-start | bytes 393224 | tf_op jit(solution)/shard_map/ppermute | solution.py:451
  26.0 11.4 %collective-permute-start.6 = (bf16[128,512]{1,0:T(8,128)(2,1)S(1)}, bf16[128,512]{1,0:T(8,128)(2,1)S(1)}, u32[]{:S(2)}, u32[]{:S(2)}) collective-permute-start(bf16[128,512]{1,0:T(8,128)(2,1)S(1)} %get-tuple-element.143), channel_id=1, source_target_pairs={{0,4},{1,5},{2,6},{3,7},{4,0},{5,1},{6,2},{7,3},{8,12},{9,13},{10,... | collective-permute-start | bytes 393224 | tf_op jit(solution)/shard_map/ppermute | solution.py:451
  26.0 22.9 %copy-start = (bf16[2,4,512,512]{3,2,1,0:T(8,128)(2,1)S(1)}, bf16[2,4,512,512]{3,2,1,0:T(8,128)(2,1)}, u32[]{:S(2)}) copy-start(bf16[2,4,512,512]{3,2,1,0:T(8,128)(2,1)} %weights.5) | copy-start | bytes 12582916
  26.0 11.4 %collective-permute-start.7 = (bf16[128,512]{1,0:T(8,128)(2,1)S(1)}, bf16[128,512]{1,0:T(8,128)(2,1)S(1)}, u32[]{:S(2)}, u32[]{:S(2)}) collective-permute-start(bf16[128,512]{1,0:T(8,128)(2,1)S(1)} %get-tuple-element.142), channel_id=1, source_target_pairs={{0,2},{1,3},{2,0},{3,1},{4,6},{5,7},{6,4},{7,5},{8,10},{9,11},{10,... | collective-permute-start | bytes 393224 | tf_op jit(solution)/shard_map/ppermute | solution.py:451
  48.9 11.0 %copy-start.4 = (bf16[1,128,512]{2,1,0:T(8,128)(2,1)S(1)}, bf16[1,128,512]{2,1,0:T(8,128)(2,1)}, u32[]{:S(2)}) copy-start(bf16[1,128,512]{2,1,0:T(8,128)(2,1)} %param.23) | copy-start | bytes 393220
  83.3 7.6 %collective-permute-start.8 = (bf16[128,512]{1,0:T(8,128)(2,1)S(1)}, bf16[128,512]{1,0:T(8,128)(2,1)S(1)}, u32[]{:S(2)}, u32[]{:S(2)}) collective-permute-start(bf16[128,512]{1,0:T(8,128)(2,1)S(1)} %shard_map.142.refs_8_), channel_id=1, source_target_pairs={{0,2},{1,3},{2,0},{3,1},{4,6},{5,7},{6,4},{7,5},{8,10},{9,11},{10,... | collective-permute-start | bytes 393224 | tf_op jit(solution)/shard_map/ppermute | solution.py:451
  83.8 12.9 %collective-permute-start.9 = (bf16[128,512]{1,0:T(8,128)(2,1)S(1)}, bf16[128,512]{1,0:T(8,128)(2,1)S(1)}, u32[]{:S(2)}, u32[]{:S(2)}) collective-permute-start(bf16[128,512]{1,0:T(8,128)(2,1)S(1)} %shard_map.142.refs_8_), channel_id=1, source_target_pairs={{0,4},{1,5},{2,6},{3,7},{4,0},{5,1},{6,2},{7,3},{8,12},{9,13},{10,... | collective-permute-start | bytes 393224 | tf_op jit(solution)/shard_map/ppermute | solution.py:451
  84.7 12.1 %collective-permute-start.10 = (bf16[128,512]{1,0:T(8,128)(2,1)S(1)}, bf16[128,512]{1,0:T(8,128)(2,1)S(1)}, u32[]{:S(2)}, u32[]{:S(2)}) collective-permute-start(bf16[128,512]{1,0:T(8,128)(2,1)S(1)} %shard_map.142.refs_8_), channel_id=1, source_target_pairs={{0,6},{1,7},{2,4},{3,5},{4,2},{5,3},{6,0},{7,1},{8,14},{9,15},{10,... | collective-permute-start | bytes 393224 | tf_op jit(solution)/shard_map/ppermute | solution.py:451
  87.8 9.5 %collective-permute-start.11 = (bf16[128,512]{1,0:T(8,128)(2,1)S(1)}, bf16[128,512]{1,0:T(8,128)(2,1)S(1)}, u32[]{:S(2)}, u32[]{:S(2)}) collective-permute-start(bf16[128,512]{1,0:T(8,128)(2,1)S(1)} %shard_map.142.refs_8_), channel_id=1, source_target_pairs={{0,1},{1,0},{2,3},{3,2},{4,5},{5,4},{6,7},{7,6},{8,9},{9,8},{10,11... | collective-permute-start | bytes 393224 | tf_op jit(solution)/shard_map/ppermute | solution.py:451
  91.0 6.3 %collective-permute-start.12 = (bf16[128,512]{1,0:T(8,128)(2,1)S(1)}, bf16[128,512]{1,0:T(8,128)(2,1)S(1)}, u32[]{:S(2)}, u32[]{:S(2)}) collective-permute-start(bf16[128,512]{1,0:T(8,128)(2,1)S(1)} %collective-permute-done.8.refs_9_), channel_id=1, source_target_pairs={{0,1},{1,0},{2,3},{3,2},{4,5},{5,4},{6,7},{7,6},{8,9},{9,8},{10,11... | collective-permute-start | bytes 393224 | tf_op jit(solution)/shard_map/ppermute | solution.py:451
  96.7 1.3 %collective-permute-start.13 = (bf16[128,512]{1,0:T(8,128)(2,1)S(1)}, bf16[128,512]{1,0:T(8,128)(2,1)S(1)}, u32[]{:S(2)}, u32[]{:S(2)}) collective-permute-start(bf16[128,512]{1,0:T(8,128)(2,1)S(1)} %collective-permute-done.9.refs_10_), channel_id=1, source_target_pairs={{0,1},{1,0},{2,3},{3,2},{4,5},{5,4},{6,7},{7,6},{8,9},{9,8},{10,11... | collective-permute-start | bytes 393224 | tf_op jit(solution)/shard_map/ppermute | solution.py:451
  96.7 1.5 %collective-permute-start.14 = (bf16[128,512]{1,0:T(8,128)(2,1)S(1)}, bf16[128,512]{1,0:T(8,128)(2,1)S(1)}, u32[]{:S(2)}, u32[]{:S(2)}) collective-permute-start(bf16[128,512]{1,0:T(8,128)(2,1)S(1)} %collective-permute-done.10.refs_11_), channel_id=1, source_target_pairs={{0,1},{1,0},{2,3},{3,2},{4,5},{5,4},{6,7},{7,6},{8,9},{9,8},{10,11... | collective-permute-start | bytes 393224 | tf_op jit(solution)/shard_map/ppermute | solution.py:451
  100.1 6.4 %collective-permute-start.15 = (bf16[256,256]{1,0:T(8,128)(2,1)S(1)}, bf16[256,256]{1,0:T(8,128)(2,1)S(1)}, u32[]{:S(2)}, u32[]{:S(2)}) collective-permute-start(bf16[256,256]{1,0:T(8,128)(2,1)S(1)} %get-tuple-element.124), channel_id=1, source_target_pairs={{0,8},{8,0},{16,24},{24,16},{1,9},{9,1},{17,25},{25,17},{2,10},{10... | collective-permute-start | bytes 393224 | tf_op jit(solution)/shard_map/ppermute | solution.py:451
  100.6 6.6 %collective-permute-start.16 = (bf16[256,256]{1,0:T(8,128)(2,1)S(1)}, bf16[256,256]{1,0:T(8,128)(2,1)S(1)}, u32[]{:S(2)}, u32[]{:S(2)}) collective-permute-start(bf16[256,256]{1,0:T(8,128)(2,1)S(1)} %get-tuple-element.135), channel_id=1, source_target_pairs={{0,16},{8,24},{16,0},{24,8},{1,17},{9,25},{17,1},{25,9},{2,18},{10... | collective-permute-start | bytes 393224 | tf_op jit(solution)/shard_map/ppermute | solution.py:451
  101.4 7.4 %collective-permute-start.17 = (bf16[256,256]{1,0:T(8,128)(2,1)S(1)}, bf16[256,256]{1,0:T(8,128)(2,1)S(1)}, u32[]{:S(2)}, u32[]{:S(2)}) collective-permute-start(bf16[256,256]{1,0:T(8,128)(2,1)S(1)} %get-tuple-element.137), channel_id=1, source_target_pairs={{0,8},{8,0},{16,24},{24,16},{1,9},{9,1},{17,25},{25,17},{2,10},{10... | collective-permute-start | bytes 393224 | tf_op jit(solution)/shard_map/ppermute | solution.py:451
  102.8 6.8 %collective-permute-start.18 = (bf16[256,256]{1,0:T(8,128)(2,1)S(1)}, bf16[256,256]{1,0:T(8,128)(2,1)S(1)}, u32[]{:S(2)}, u32[]{:S(2)}) collective-permute-start(bf16[256,256]{1,0:T(8,128)(2,1)S(1)} %get-tuple-element.139), channel_id=1, source_target_pairs={{0,16},{8,24},{16,0},{24,8},{1,17},{9,25},{17,1},{25,9},{2,18},{10... | collective-permute-start | bytes 393224 | tf_op jit(solution)/shard_map/ppermute | solution.py:451
  106.5 7.5 %copy-start.2 = (bf16[512,512]{1,0:T(8,128)(2,1)S(1)}, bf16[512,512]{1,0:T(8,128)(2,1)}, u32[]{:S(2)}) copy-start(bf16[512,512]{1,0:T(8,128)(2,1)} %refs_8_.1) | copy-start | bytes 1572868
  106.5 4.8 %collective-permute-start.19 = (bf16[128,256]{1,0:T(8,128)(2,1)S(1)}, bf16[128,256]{1,0:T(8,128)(2,1)S(1)}, u32[]{:S(2)}, u32[]{:S(2)}) collective-permute-start(bf16[128,256]{1,0:T(8,128)(2,1)S(1)} %slice.86), channel_id=1, source_target_pairs={{0,16},{8,24},{16,0},{24,8},{1,17},{9,25},{17,1},{25,9},{2,18},{10... | collective-permute-start | bytes 196616 | tf_op jit(solution)/shard_map/ppermute | solution.py:451
  107.2 4.6 %collective-permute-start.20 = (bf16[128,256]{1,0:T(8,128)(2,1)S(1)}, bf16[128,256]{1,0:T(8,128)(2,1)S(1)}, u32[]{:S(2)}, u32[]{:S(2)}) collective-permute-start(bf16[128,256]{1,0:T(8,128)(2,1)S(1)} %slice.85), channel_id=1, source_target_pairs={{0,8},{8,0},{16,24},{24,16},{1,9},{9,1},{17,25},{25,17},{2,10},{10... | collective-permute-start | bytes 196616 | tf_op jit(solution)/shard_map/ppermute | solution.py:451
  108.8 4.3 %collective-permute-start.21 = (bf16[128,256]{1,0:T(8,128)(2,1)S(1)}, bf16[128,256]{1,0:T(8,128)(2,1)S(1)}, u32[]{:S(2)}, u32[]{:S(2)}) collective-permute-start(bf16[128,256]{1,0:T(8,128)(2,1)S(1)} %slice.84), channel_id=1, source_target_pairs={{0,16},{8,24},{16,0},{24,8},{1,17},{9,25},{17,1},{25,9},{2,18},{10... | collective-permute-start | bytes 196616 | tf_op jit(solution)/shard_map/ppermute | solution.py:451
  109.6 4.3 %collective-permute-start.22 = (bf16[128,256]{1,0:T(8,128)(2,1)S(1)}, bf16[128,256]{1,0:T(8,128)(2,1)S(1)}, u32[]{:S(2)}, u32[]{:S(2)}) collective-permute-start(bf16[128,256]{1,0:T(8,128)(2,1)S(1)} %slice.83), channel_id=1, source_target_pairs={{0,8},{8,0},{16,24},{24,16},{1,9},{9,1},{17,25},{25,17},{2,10},{10... | collective-permute-start | bytes 196616 | tf_op jit(solution)/shard_map/ppermute | solution.py:451

commit v4 on v3

--- a/solution.py
+++ b/solution.py
@@ -410,9 +410,13 @@
 
 def grid_back_kernel(chunks, *refs):
     *parts, weight, out = refs
-    count = len(parts) // 2
+    count = len(parts) // 3
+    rows = parts[0].shape[0]
     total = [
-        mine[...] + given[...].astype(F32) for mine, given in zip(parts[:count], parts[count:])
+        parts[i][...]
+        + parts[count + i][:rows, :].astype(F32)
+        + parts[2 * count + i][...].astype(F32)
+        for i in range(count)
     ]
     each = count // chunks
     columns = [
@@ -476,6 +480,7 @@
 
     axes = [1 << i for i in range(sects.bit_length() - 1)]
     part_rows = grid_rows // len(axes)
+    assert len(axes) == 2
     ends = pltpu.VMEM((fanout, grid_rows), jnp.int32)
     packed = call(
         functools.partial(pack_kernel, block),
@@ -621,7 +626,8 @@
         [grad, exchange(halo), pick_t, mesh_pre, mesh_weight],
     )
 
-    same = [grad_sum] + [swap(grad_sum, "node", 2 * q) for q in range(1, half)]
+    same = [swap(grad_sum, "node", 2 * q) for q in reversed(range(1, half))]
+    same = [grad_sum, *same[::-1]]
     ready = nodes * block <= 8 * LANES
     picks_of = {unit: where[unit] for unit in units}
     if ready:
@@ -639,9 +645,9 @@
             [seen, *(where[unit][0] for unit in units), mesh_out],
             smem=1,
         )
-        same[1] = lax.optimization_barrier((same[1], found[0]))[0]
+        same[-1] = lax.optimization_barrier((same[-1], found[0]))[0]
         picks_of = {unit: (part, 0) for unit, part in zip(units, found)}
-    other = [swap(rows, "node", 1) for rows in same]
+    other = [swap(rows, "node", 1) for rows in same[::-1]][::-1]
     gathered = (*same, *other)
 
     def message_back(groups, dtype):
@@ -670,39 +676,31 @@
             smem=1,
         )
 
-    first = [axes[p] for p in range(len(axes))]
-    stay = [[j for j in range(sects) if not j & axis] for axis in first]
-    sent = [[(j ^ axis, p) for j in stay[p]] for p, axis in enumerate(first)]
-    given = message_back(sent, BF16)
-    gathered = lax.optimization_barrier((*gathered, given[0]))[:-1]
-    kept = message_back([[(j, p) for j in stay[p]] for p in range(len(axes))], F32)
-    turns = [(p, c) for c in range(CHUNKS) for p in range(len(axes))]
-    given = [given[p * CHUNKS + c] for p, c in turns]
-    kept = [kept[p * CHUNKS + c] for p, c in turns]
-    for step in range(len(axes)):
-        given = [
-            swap(part, "sect", axes[(p + step) % len(axes)])
-            for part, (p, _) in zip(given, turns)
-        ]
-        if step + 1 == len(axes):
-            break
-        kept = [mine + part.astype(F32) for mine, part in zip(kept, given)]
-        given, left = [], []
-        for p in range(len(axes)):
-            axis = axes[(p + step + 1) % len(axes)]
-            left.append([j for j in stay[p] if not j & axis])
-        for i, (p, _) in enumerate(turns):
-            axis = axes[(p + step + 1) % len(axes)]
-            rows = kept[i].reshape(len(stay[p]), part_rows, width // CHUNKS)
-            given.append(
-                jnp.concatenate([rows[stay[p].index(j ^ axis)] for j in left[p]]).astype(BF16)
-            )
-            kept[i] = jnp.concatenate([rows[stay[p].index(j)] for j in left[p]])
-        stay = left
+    first, then = axes, axes[::-1]
+    chunks = [(p, c) for c in range(CHUNKS) for p in range(len(axes))]
+
+    def ordered(found):
+        return [found[p * CHUNKS + c] for p, c in chunks]
+
+    given = ordered(
+        message_back(
+            [[(a, p), (a ^ b, p)] for p, (a, b) in enumerate(zip(first, then))], BF16
+        )
+    )
+    gathered = lax.optimization_barrier((*gathered, *given))[: len(gathered)]
+    passed = ordered(message_back([[(b, p)] for p, b in enumerate(then)], F32))
+    gathered = lax.optimization_barrier((*gathered, *passed))[: len(gathered)]
+    given = [swap(part, "sect", first[p]) for part, (p, _) in zip(given, chunks)]
+    passed = [
+        (mine + part[part_rows:].astype(F32)).astype(BF16)
+        for mine, part in zip(passed, given)
+    ]
+    kept = ordered(message_back([[(0, p)] for p in range(len(axes))], F32))
+    passed = [swap(part, "sect", then[p]) for part, (p, _) in zip(passed, chunks)]
     (grid_grad,) = call(
         functools.partial(grid_back_kernel, CHUNKS),
         [shape((grid_rows, width), BF16)],
-        [*kept, *given, enc_weight],
+        [*kept, *given, *passed, enc_weight],
     )
     return (mesh_out[None], grid_grad)
 

time: 115 us -> 116 us (level)
  starting transfers between devices: 26.4 us -> 25.1 us
    ppermute x23, starting transfers between devices: 26.4 us -> 25.1 us  [swap(): return lax.ppermute(value, axis, [(i, i ^ apart) for i in range(size)])]
    pallas_call x16 -> x17, Pallas kernels: 27 us -> 27.7 us  [call(): pl.pallas_call(kernel, out_shape=list(outs), in_specs=specs, out_specs=[p...]
where the time goes in v4:
time: 116 us; the launch traced here: 115 us
  blocking collectives  38.3 us (33%)
  Pallas kernels  27.7 us (24%)
  starting transfers between devices  25.1 us (22%)
  waiting for transfers between devices  23 us (20%)
    all_to_all x4, blocking collectives, exchange(): return lax.all_to_all(value, both, split_axis=0, concat_axis=0, tiled=True)  38.3 us
    pallas_call x17, Pallas kernels, call(): pl.pallas_call(kernel, out_shape=list(outs), in_specs=specs, out_specs=[p...  27.7 us
    ppermute x23, starting transfers between devices, swap(): return lax.ppermute(value, axis, [(i, i ^ apart) for i in range(size)])  25.1 us
    ppermute x23, waiting for transfers between devices, swap(): return lax.ppermute(value, axis, [(i, i ^ apart) for i in range(size)])  23 us
  transfers between devices with their start and end apart: 23, of which 14 were waited for; matrix products, arithmetic and copies ran while one was open for 0% of the time, Pallas kernels for 12%

profile of v4, /device:TPU:0, one launch (start us, length us, event | category | flops | bytes accessed | tf_op | source)
XLA Modules:
  0.0 115.4 jit_solution(8367922648839849553)
XLA Ops:
  0.6 1.1 shard_map.131
  1.7 3.0 %collective-permute-start.2 = (bf16[144,512]{1,0:T(8,128)(2,1)S(1)}, bf16[144,512]{1,0:T(8,128)(2,1)S(1)}, u32[]{:S(2)}, u32[]{:S(2)}) collective-permute-start(bf16[144,512]{1,0:T(8,128)(2,1)S(1)} %get-tuple-element.84.refs_1_), channel_id=1, source_target_pairs={{0,16},{8,24},{16,0},{24,8},{1,17},{9,25},{17,1},{25,9},{2,18},{10... | collective-permute-start | bytes 442376 | tf_op jit(solution)/shard_map/ppermute | solution.py:455
  4.7 1.5 %collective-permute-start = (bf16[144,512]{1,0:T(8,128)(2,1)S(1)}, bf16[144,512]{1,0:T(8,128)(2,1)S(1)}, u32[]{:S(2)}, u32[]{:S(2)}) collective-permute-start(bf16[144,512]{1,0:T(8,128)(2,1)S(1)} %get-tuple-element.83.refs_0_), channel_id=1, source_target_pairs={{0,8},{8,0},{16,24},{24,16},{1,9},{9,1},{17,25},{25,17},{2,10},{10... | collective-permute-start | bytes 442376 | tf_op jit(solution)/shard_map/ppermute | solution.py:455
  6.2 2.4 %collective-permute-done.2.refs_1_.refs_5_ = bf16[144,512]{1,0:T(8,128)(2,1)S(1)} collective-permute-done((bf16[144,512]{1,0:T(8,128)(2,1)S(1)}, bf16[144,512]{1,0:T(8,128)(2,1)S(1)}, u32[]{:S(2)}, u32[]{:S(2)}) %collective-permute-start.2) | collective-permute-done | bytes 147488 | tf_op jit(solution)/shard_map/ppermute | solution.py:455
  8.6 1.8 %collective-permute-start.3 = (bf16[288,512]{1,0:T(8,128)(2,1)S(1)}, bf16[288,512]{1,0:T(8,128)(2,1)S(1)}, u32[]{:S(2)}, u32[]{:S(2)}) collective-permute-start(bf16[288,512]{1,0:T(8,128)(2,1)S(1)} %pad_maximum_fusion.1), channel_id=1, source_target_pairs={{0,8},{8,0},{16,24},{24,16},{1,9},{9,1},{17,25},{25,17},{2,10},{10... | collective-permute-start | bytes 884744 | tf_op jit(solution)/shard_map/ppermute | solution.py:455
  10.4 0.0 collective-permute-done.refs_0_.refs_2_
  10.4 1.6 %collective-permute-start.1 = (bf16[288,512]{1,0:T(8,128)(2,1)S(1)}, bf16[288,512]{1,0:T(8,128)(2,1)S(1)}, u32[]{:S(2)}, u32[]{:S(2)}) collective-permute-start(bf16[288,512]{1,0:T(8,128)(2,1)S(1)} %pad_maximum_fusion), channel_id=1, source_target_pairs={{0,16},{8,24},{16,0},{24,8},{1,17},{9,25},{17,1},{25,9},{2,18},{10... | collective-permute-start | bytes 884744 | tf_op jit(solution)/shard_map/ppermute | solution.py:455
  12.0 1.5 %shard_map.132 = (bf16[256,512]{1,0:T(8,128)(2,1)S(1)}, bf16[512,256]{1,0:T(8,128)(2,1)S(1)}, bf16[1024,192]{1,0:T(8,128)(2,1)S(1)}, bf16[192,1024]{1,0:T(8,128)...) custom-call(s32[4,2,8]{2,1,0:T(2,128)} %bitcast.33, s32[8,128]{1,0:T(8,128)} %bitcast.34, ...), custom_call_target="tpu_custom_call" | custom-call | bytes 2367744 | tf_op jit(solution)/shard_map/pallas_call | solution.py:434
  13.5 0.1 pad_add_fusion.who
  13.6 1.9 %shard_map.133.refs_4_ = f32[1024,512]{1,0:T(8,128)S(1)} custom-call(s32[2]{0:T(128)S(1)} %pad_add_fusion.who, bf16[144,512]{1,0:T(8,128)(2,1)S(1)} %get-tuple-element.83.refs_0_, bf16[144,512]{1,0:T(8,128)(2,1)S(1)} %get-tuple-element.84.refs_1_, bf16[512,512]{1,0:T(8,128)(2,1)S(1)} %get-tuple-element.85.refs_2_.refs_4_.refs_8_, ...), custom_call_target="tpu_custom_call" | custom-call | bytes 2918408 | tf_op jit(solution)/shard_map/pallas_call | solution.py:434
  15.5 1.9 %shard_map.134.refs_6_.before = f32[1024,512]{1,0:T(8,128)S(1)} custom-call(s32[2]{0:T(128)S(1)} %pad_add_fusion.who, bf16[144,512]{1,0:T(8,128)(2,1)S(1)} %collective-permute-done.refs_0_.refs_2_, bf16[144,512]{1,0:T(8,128)(2,1)S(1)} %collective-permute-done.2.refs_1_.refs_5_, ...), custom_call_target="tpu_custom_call", output_to_operand_aliasing={{}: (5, {})} | custom-call | bytes 5015560 | tf_op jit(solution)/shard_map/pallas_call | solution.py:434
  17.4 0.7 collective-permute-done.1.refs_0_.refs_1_.refs_4_.refs_6_
  18.1 2.0 %shard_map.135 = (bf16[512,512]{1,0:T(8,128)(2,1)S(1)}, bf16[1024,512]{1,0:T(8,128)(2,1)S(1)}, s32[1,1024]{1,0:T(1,128)S(1)}) custom-call(s32[2]{0:T(128)S(1)} %pad_add_fusion.who, bf16[288,512]{1,0:T(8,128)(2,1)S(1)} %collective-permute-done.1.refs_0_.refs_1_.refs_4_.refs_6_, bf16[288,512]{1,0:T(8,128)(2,1)S(1)} %collective-permute-done.1.refs_0_.refs_1_.refs_4_.refs_6_, ...), custom_call_target="tpu_custom_call" | custom-call | bytes 5380104 | tf_op jit(solution)/shard_map/pallas_call | solution.py:434
  20.1 0.1 collective-permute-start.4
  20.2 0.7 shard_map.136
  20.9 1.2 %collective-permute-done.4 = bf16[512,512]{1,0:T(8,128)(2,1)S(1)} collective-permute-done((bf16[512,512]{1,0:T(8,128)(2,1)S(1)}, bf16[512,512]{1,0:T(8,128)(2,1)S(1)}, u32[]{:S(2)}, u32[]{:S(2)}) %collective-permute-start.4) | collective-permute-done | bytes 524320 | tf_op jit(solution)/shard_map/ppermute | solution.py:455
  22.1 0.2 fusion
  22.3 0.0 copy-start.1
  22.3 0.0 copy-start.3
  22.3 3.7 %collective-permute-start.5 = (bf16[128,512]{1,0:T(8,128)(2,1)S(1)}, bf16[128,512]{1,0:T(8,128)(2,1)S(1)}, u32[]{:S(2)}, u32[]{:S(2)}) collective-permute-start(bf16[128,512]{1,0:T(8,128)(2,1)S(1)} %get-tuple-element.168), channel_id=1, source_target_pairs={{0,6},{1,7},{2,4},{3,5},{4,2},{5,3},{6,0},{7,1},{8,14},{9,15},{10,... | collective-permute-start | bytes 393224 | tf_op jit(solution)/shard_map/ppermute | solution.py:455
  26.0 0.0 collective-permute-start.6
  26.0 0.8 collective-permute-start.7
  26.8 2.3 %shard_map.137 = (bf16[256,512]{1,0:T(8,128)(2,1)S(1)}, bf16[256,512]{1,0:T(8,128)(2,1)S(1)}, bf16[256,512]{1,0:T(8,128)(2,1)S(1)}, bf16[256,512]{1,0:T(8,128)(2...) custom-call(bf16[144,512]{1,0:T(8,128)(2,1)S(1)} %get-tuple-element., ...), custom_call_target="tpu_custom_call" | custom-call | bytes 4392960 | tf_op jit(solution)/shard_map/pallas_call | solution.py:434
  29.1 1.5 %collective-permute-done.5.refs_0_ = bf16[128,512]{1,0:T(8,128)(2,1)S(1)} collective-permute-done((bf16[128,512]{1,0:T(8,128)(2,1)S(1)}, bf16[128,512]{1,0:T(8,128)(2,1)S(1)}, u32[]{:S(2)}, u32[]{:S(2)}) %collective-permute-start.5) | collective-permute-done | bytes 131104 | tf_op jit(solution)/shard_map/ppermute | solution.py:455
  30.6 6.7 %collective-permute-done.6.refs_1_ = bf16[128,512]{1,0:T(8,128)(2,1)S(1)} collective-permute-done((bf16[128,512]{1,0:T(8,128)(2,1)S(1)}, bf16[128,512]{1,0:T(8,128)(2,1)S(1)}, u32[]{:S(2)}, u32[]{:S(2)}) %collective-permute-start.6) | collective-permute-done | bytes 131104 | tf_op jit(solution)/shard_map/ppermute | solution.py:455
  37.4 0.5 shard_map.138
  37.8 11.0 %all_to_all.44 = bf16[32,8,128]{2,1,0:T(8,128)(2,1)S(1)} all-to-all(bf16[32,8,128]{2,1,0:T(8,128)(2,1)S(1)} %bitcast.29), channel_id=1, replica_groups=mesh['sect'=4,'node'=8] {'sect','node'}, dimensions={0} | all-to-all | bytes 131072 | tf_op jit(solution)/shard_map/all_to_all | solution.py:600
  48.9 1.9 %shard_map.139 = (bf16[128,512]{1,0:T(8,128)(2,1)S(1)}, f32[128,512]{1,0:T(8,128)S(1)}, bf16[1024,512]{1,0:T(8,128)(2,1)S(1)}, bf16[256,128]{1,0:T(8,128)(2,1)S(1)}) custom-call(bf16[128,512]{1,0:T(8,128)(2,1)S(1)} %get-tuple-element.102.state, bf16[256,128]{1,0:T(8,128)(2,1)S(1)} %bitcast.24, bf16[1024,192]{1,0:T(8,128)(2,1)S(1)} %get-tuple-element.104.source, ...), custom_call_target="tpu_custom_call" | custom-call | bytes 6553600 | tf_op jit(solution)/shard_map/pallas_call | solution.py:434
  50.7 9.1 %all_to_all.45 = bf16[32,8,128]{2,1,0:T(8,128)(2,1)S(1)} all-to-all(bf16[32,8,128]{2,1,0:T(8,128)(2,1)S(1)} %bitcast.30), channel_id=1, replica_groups=mesh['sect'=4,'node'=8] {'sect','node'}, dimensions={0} | all-to-all | bytes 131072 | tf_op jit(solution)/shard_map/all_to_all | solution.py:600
  59.8 3.0 %shard_map.140 = (bf16[128,512]{1,0:T(8,128)(2,1)S(1)}, f32[128,512]{1,0:T(8,128)S(1)}, bf16[256,128]{1,0:T(8,128)(2,1)S(1)}) custom-call(bf16[128,512]{1,0:T(8,128)(2,1)S(1)} %get-tuple-element.105.state, bf16[256,128]{1,0:T(8,128)(2,1)S(1)} %bitcast.25, bf16[1024,192]{1,0:T(8,128)(2,1)S(1)} %get-tuple-element.104.source, ...), custom_call_target="tpu_custom_call" | custom-call | bytes 5767168 | tf_op jit(solution)/shard_map/pallas_call | solution.py:434
  62.9 9.1 %all_to_all.46 = bf16[32,8,128]{2,1,0:T(8,128)(2,1)S(1)} all-to-all(bf16[32,8,128]{2,1,0:T(8,128)(2,1)S(1)} %bitcast.32), channel_id=1, replica_groups=mesh['sect'=4,'node'=8] {'sect','node'}, dimensions={0} | all-to-all | bytes 131072 | tf_op jit(solution)/shard_map/all_to_all | solution.py:600
  72.0 1.8 %shard_map.141 = (f32[128,512]{1,0:T(8,128)S(1)}, bf16[256,128]{1,0:T(8,128)(2,1)S(1)}) custom-call(f32[128,512]{1,0:T(8,128)S(1)} %get-tuple-element.108.mine, bf16[256,128]{1,0:T(8,128)(2,1)S(1)} %bitcast.23, bf16[512,256]{1,0:T(8,128)(2,1)S(1)} %get-tuple-element.110.pick_t, f32[128,512]{1,0:T(8,128)S(1)} %get-tuple-element.111.mixed, ...), custom_call_target="tpu_custom_call" | custom-call | bytes 6815744 | tf_op jit(solution)/shard_map/pallas_call | solution.py:434
  73.7 9.1 %all_to_all.47 = bf16[32,8,128]{2,1,0:T(8,128)(2,1)S(1)} all-to-all(bf16[32,8,128]{2,1,0:T(8,128)(2,1)S(1)} %bitcast.31), channel_id=1, replica_groups=mesh['sect'=4,'node'=8] {'sect','node'}, dimensions={0} | all-to-all | bytes 131072 | tf_op jit(solution)/shard_map/all_to_all | solution.py:600
  82.8 0.5 shard_map.142.refs_8_.refs_4_
  83.3 0.8 collective-permute-start.10
  84.1 0.2 collective-permute-start.8
  84.3 3.5 %collective-permute-start.9 = (bf16[128,512]{1,0:T(8,128)(2,1)S(1)}, bf16[128,512]{1,0:T(8,128)(2,1)S(1)}, u32[]{:S(2)}, u32[]{:S(2)}) collective-permute-start(bf16[128,512]{1,0:T(8,128)(2,1)S(1)} %shard_map.142.refs_8_.refs_4_), channel_id=1, source_target_pairs={{0,4},{1,5},{2,6},{3,7},{4,0},{5,1},{6,2},{7,3},{8,12},{9,13},{10,... | collective-permute-start | bytes 393224 | tf_op jit(solution)/shard_map/ppermute | solution.py:455
  87.8 3.2 %shard_map.143 = (bf16[256,1024]{1,0:T(8,128)(2,1)S(1)}, bf16[256,1024]{1,0:T(8,128)(2,1)S(1)}, bf16[256,1024]{1,0:T(8,128)(2,1)S(1)}, bf16[256,1024]{1,0:T(8,12...) custom-call(s32[2]{0:T(128)S(1)} %pad_add_fusion.who, ...), custom_call_target="tpu_custom_call" | custom-call | bytes 6225928 | tf_op jit(solution)/shard_map/pallas_call | solution.py:434
  91.0 0.6 collective-permute-done.10.refs_11_.refs_7_
  91.6 0.0 collective-permute-start.14
  91.6 2.2 %collective-permute-done.8.refs_9_.refs_5_ = bf16[128,512]{1,0:T(8,128)(2,1)S(1)} collective-permute-done((bf16[128,512]{1,0:T(8,128)(2,1)S(1)}, bf16[128,512]{1,0:T(8,128)(2,1)S(1)}, u32[]{:S(2)}, u32[]{:S(2)}) %collective-permute-start.8) | collective-permute-done | bytes 131104 | tf_op jit(solution)/shard_map/ppermute | solution.py:455
  93.8 0.0 collective-permute-start.12
  93.8 3.4 %collective-permute-done.9.refs_10_.refs_6_ = bf16[128,512]{1,0:T(8,128)(2,1)S(1)} collective-permute-done((bf16[128,512]{1,0:T(8,128)(2,1)S(1)}, bf16[128,512]{1,0:T(8,128)(2,1)S(1)}, u32[]{:S(2)}, u32[]{:S(2)}) %collective-permute-start.9) | collective-permute-done | bytes 131104 | tf_op jit(solution)/shard_map/ppermute | solution.py:455
  97.2 0.0 collective-permute-start.13
  97.2 0.0 collective-permute-done.11.refs_12_.refs_8_
  97.2 1.3 %collective-permute-done.13.refs_14_.refs_10_ = bf16[128,512]{1,0:T(8,128)(2,1)S(1)} collective-permute-done((bf16[128,512]{1,0:T(8,128)(2,1)S(1)}, bf16[128,512]{1,0:T(8,128)(2,1)S(1)}, u32[]{:S(2)}, u32[]{:S(2)}) %collective-permute-start.13) | collective-permute-done | bytes 131104 | tf_op jit(solution)/shard_map/ppermute | solution.py:455
  98.6 1.8 %shard_map.144 = (bf16[256,256]{1,0:T(8,128)(2,1)S(1)}, bf16[256,256]{1,0:T(8,128)(2,1)S(1)}, bf16[256,256]{1,0:T(8,128)(2,1)S(1)}, bf16[256,256]{1,0:T(8,128)(2,1)S(1)}) custom-call(s32[2]{0:T(128)S(1)} %pad_add_fusion.who, bf16[256,1024]{1,0:T(8,128)(2,1)S(1)} %get-tuple-element.124.refs_0_, bf16[256,1024]{1,0:T(8,128)(2,1)S(1)} %get-tuple-element.125.refs_1_, ...), custom_call_target="tpu_custom_call" | custom-call | bytes 4718600 | tf_op jit(solution)/shard_map/pallas_call | solution.py:434
  100.4 0.7 collective-permute-start.18
  101.1 0.5 collective-permute-start.17
  101.6 1.5 %collective-permute-start.16 = (bf16[256,256]{1,0:T(8,128)(2,1)S(1)}, bf16[256,256]{1,0:T(8,128)(2,1)S(1)}, u32[]{:S(2)}, u32[]{:S(2)}) collective-permute-start(bf16[256,256]{1,0:T(8,128)(2,1)S(1)} %get-tuple-element.133), channel_id=1, source_target_pairs={{0,16},{8,24},{16,0},{24,8},{1,17},{9,25},{17,1},{25,9},{2,18},{10... | collective-permute-start | bytes 393224 | tf_op jit(solution)/shard_map/ppermute | solution.py:455
  103.1 1.4 %collective-permute-start.15 = (bf16[256,256]{1,0:T(8,128)(2,1)S(1)}, bf16[256,256]{1,0:T(8,128)(2,1)S(1)}, u32[]{:S(2)}, u32[]{:S(2)}) collective-permute-start(bf16[256,256]{1,0:T(8,128)(2,1)S(1)} %get-tuple-element.132), channel_id=1, source_target_pairs={{0,8},{8,0},{16,24},{24,16},{1,9},{9,1},{17,25},{25,17},{2,10},{10... | collective-permute-start | bytes 393224 | tf_op jit(solution)/shard_map/ppermute | solution.py:455
  104.5 1.3 %shard_map.145 = (f32[128,256]{1,0:T(8,128)S(1)}, f32[128,256]{1,0:T(8,128)S(1)}, f32[128,256]{1,0:T(8,128)S(1)}, f32[128,256]{1,0:T(8,128)S(1)}) custom-call(s32[2]{0:T(128)S(1)} %pad_add_fusion.who, bf16[256,1024]{1,0:T(8,128)(2,1)S(1)} %get-tuple-element.144.refs_0_, bf16[256,1024]{1,0:T(8,128)(2,1)S(1)} %get-tuple-element.145.refs_1_, ...), custom_call_target="tpu_custom_call" | custom-call | bytes 3145736 | tf_op jit(solution)/shard_map/pallas_call | solution.py:434
  105.8 0.0 copy-start.2
  105.8 1.0 collective-permute-done.18.refs_7_
  106.8 0.7 collective-permute-start.22
  107.5 1.4 %collective-permute-start.21 = (bf16[128,256]{1,0:T(8,128)(2,1)S(1)}, bf16[128,256]{1,0:T(8,128)(2,1)S(1)}, u32[]{:S(2)}, u32[]{:S(2)}) collective-permute-start(bf16[128,256]{1,0:T(8,128)(2,1)S(1)} %add_convert_fusion.1), channel_id=1, source_target_pairs={{0,16},{8,24},{16,0},{24,8},{1,17},{9,25},{17,1},{25,9},{2,18},{10... | collective-permute-start | bytes 196616 | tf_op jit(solution)/shard_map/ppermute | solution.py:455
  108.9 0.2 collective-permute-done.16.refs_5_
  109.1 0.6 collective-permute-start.20
  109.7 0.2 collective-permute-done.15.refs_4_
  109.9 1.4 %collective-permute-start.19 = (bf16[128,256]{1,0:T(8,128)(2,1)S(1)}, bf16[128,256]{1,0:T(8,128)(2,1)S(1)}, u32[]{:S(2)}, u32[]{:S(2)}) collective-permute-start(bf16[128,256]{1,0:T(8,128)(2,1)S(1)} %add_convert_fusion.3), channel_id=1, source_target_pairs={{0,16},{8,24},{16,0},{24,8},{1,17},{9,25},{17,1},{25,9},{2,18},{10... | collective-permute-start | bytes 196616 | tf_op jit(solution)/shard_map/ppermute | solution.py:455
  111.3 1.3 %shard_map.146 = (f32[128,256]{1,0:T(8,128)S(1)}, f32[128,256]{1,0:T(8,128)S(1)}, f32[128,256]{1,0:T(8,128)S(1)}, f32[128,256]{1,0:T(8,128)S(1)}) custom-call(s32[2]{0:T(128)S(1)} %pad_add_fusion.who, bf16[256,1024]{1,0:T(8,128)(2,1)S(1)} %get-tuple-element.119.refs_0_, bf16[256,1024]{1,0:T(8,128)(2,1)S(1)} %get-tuple-element.120.refs_1_, ...), custom_call_target="tpu_custom_call" | custom-call | bytes 3145736 | tf_op jit(solution)/shard_map/pallas_call | solution.py:434
  112.6 0.8 collective-permute-done.20.refs_9_
  113.5 0.8 collective-permute-done.19.refs_8_
  114.2 1.2 %shard_map.147 = bf16[256,512]{1,0:T(8,128)(2,1)} custom-call(f32[128,256]{1,0:T(8,128)S(1)} %get-tuple-element.160.refs_0_, f32[128,256]{1,0:T(8,128)S(1)} %get-tuple-element.161.refs_1_, f32[128,256]{1,0:T(8,128)S(1)} %get-tuple-element.162.refs_2_, f32[128,256]{1,0:T(8,128)S(1)} %get-tuple-element.163.refs_3_, ...), custom_call_target="tpu_custom_call" | custom-call | bytes 2097152 | tf_op jit(solution)/shard_map/pallas_call | solution.py:434
  (23 shorter events, 0.2 us)
Async XLA Ops:
  1.7 6.9 %collective-permute-start.2 = (bf16[144,512]{1,0:T(8,128)(2,1)S(1)}, bf16[144,512]{1,0:T(8,128)(2,1)S(1)}, u32[]{:S(2)}, u32[]{:S(2)}) collective-permute-start(bf16[144,512]{1,0:T(8,128)(2,1)S(1)} %get-tuple-element.84.refs_1_), channel_id=1, source_target_pairs={{0,16},{8,24},{16,0},{24,8},{1,17},{9,25},{17,1},{25,9},{2,18},{10... | collective-permute-start | bytes 442376 | tf_op jit(solution)/shard_map/ppermute | solution.py:455
  4.7 5.7 %collective-permute-start = (bf16[144,512]{1,0:T(8,128)(2,1)S(1)}, bf16[144,512]{1,0:T(8,128)(2,1)S(1)}, u32[]{:S(2)}, u32[]{:S(2)}) collective-permute-start(bf16[144,512]{1,0:T(8,128)(2,1)S(1)} %get-tuple-element.83.refs_0_), channel_id=1, source_target_pairs={{0,8},{8,0},{16,24},{24,16},{1,9},{9,1},{17,25},{25,17},{2,10},{10... | collective-permute-start | bytes 442376 | tf_op jit(solution)/shard_map/ppermute | solution.py:455
  8.6 8.8 %collective-permute-start.3 = (bf16[288,512]{1,0:T(8,128)(2,1)S(1)}, bf16[288,512]{1,0:T(8,128)(2,1)S(1)}, u32[]{:S(2)}, u32[]{:S(2)}) collective-permute-start(bf16[288,512]{1,0:T(8,128)(2,1)S(1)} %pad_maximum_fusion.1), channel_id=1, source_target_pairs={{0,8},{8,0},{16,24},{24,16},{1,9},{9,1},{17,25},{25,17},{2,10},{10... | collective-permute-start | bytes 884744 | tf_op jit(solution)/shard_map/ppermute | solution.py:455
  10.4 7.7 %collective-permute-start.1 = (bf16[288,512]{1,0:T(8,128)(2,1)S(1)}, bf16[288,512]{1,0:T(8,128)(2,1)S(1)}, u32[]{:S(2)}, u32[]{:S(2)}) collective-permute-start(bf16[288,512]{1,0:T(8,128)(2,1)S(1)} %pad_maximum_fusion), channel_id=1, source_target_pairs={{0,16},{8,24},{16,0},{24,8},{1,17},{9,25},{17,1},{25,9},{2,18},{10... | collective-permute-start | bytes 884744 | tf_op jit(solution)/shard_map/ppermute | solution.py:455
  20.1 2.0 %collective-permute-start.4 = (bf16[512,512]{1,0:T(8,128)(2,1)S(1)}, bf16[512,512]{1,0:T(8,128)(2,1)S(1)}, u32[]{:S(2)}, u32[]{:S(2)}) collective-permute-start(bf16[512,512]{1,0:T(8,128)(2,1)S(1)} %get-tuple-element.89), channel_id=1, source_target_pairs={{0,1},{1,0},{2,3},{3,2},{4,5},{5,4},{6,7},{7,6},{8,9},{9,8},{10,11... | collective-permute-start | bytes 1572872 | tf_op jit(solution)/shard_map/ppermute | solution.py:455
  22.3 15.1 %copy-start.1 = (bf16[512,512]{1,0:T(8,128)(2,1)S(1)}, bf16[512,512]{1,0:T(8,128)(2,1)}, u32[]{:S(2)}) copy-start(bf16[512,512]{1,0:T(8,128)(2,1)} %weight.1) | copy-start | bytes 1572868
  22.3 15.1 %copy-start.3 = (bf16[1,128,512]{2,1,0:T(8,128)(2,1)S(1)}, bf16[1,128,512]{2,1,0:T(8,128)(2,1)}, u32[]{:S(2)}) copy-start(bf16[1,128,512]{2,1,0:T(8,128)(2,1)} %param.18) | copy-start | bytes 393220
  22.3 8.3 %collective-permute-start.5 = (bf16[128,512]{1,0:T(8,128)(2,1)S(1)}, bf16[128,512]{1,0:T(8,128)(2,1)S(1)}, u32[]{:S(2)}, u32[]{:S(2)}) collective-permute-start(bf16[128,512]{1,0:T(8,128)(2,1)S(1)} %get-tuple-element.168), channel_id=1, source_target_pairs={{0,6},{1,7},{2,4},{3,5},{4,2},{5,3},{6,0},{7,1},{8,14},{9,15},{10,... | collective-permute-start | bytes 393224 | tf_op jit(solution)/shard_map/ppermute | solution.py:455
  26.0 11.4 %collective-permute-start.6 = (bf16[128,512]{1,0:T(8,128)(2,1)S(1)}, bf16[128,512]{1,0:T(8,128)(2,1)S(1)}, u32[]{:S(2)}, u32[]{:S(2)}) collective-permute-start(bf16[128,512]{1,0:T(8,128)(2,1)S(1)} %get-tuple-element.167), channel_id=1, source_target_pairs={{0,4},{1,5},{2,6},{3,7},{4,0},{5,1},{6,2},{7,3},{8,12},{9,13},{10,... | collective-permute-start | bytes 393224 | tf_op jit(solution)/shard_map/ppermute | solution.py:455
  26.0 22.9 %copy-start = (bf16[2,4,512,512]{3,2,1,0:T(8,128)(2,1)S(1)}, bf16[2,4,512,512]{3,2,1,0:T(8,128)(2,1)}, u32[]{:S(2)}) copy-start(bf16[2,4,512,512]{3,2,1,0:T(8,128)(2,1)} %weights.5) | copy-start | bytes 12582916
  26.0 11.4 %collective-permute-start.7 = (bf16[128,512]{1,0:T(8,128)(2,1)S(1)}, bf16[128,512]{1,0:T(8,128)(2,1)S(1)}, u32[]{:S(2)}, u32[]{:S(2)}) collective-permute-start(bf16[128,512]{1,0:T(8,128)(2,1)S(1)} %get-tuple-element.166), channel_id=1, source_target_pairs={{0,2},{1,3},{2,0},{3,1},{4,6},{5,7},{6,4},{7,5},{8,10},{9,11},{10,... | collective-permute-start | bytes 393224 | tf_op jit(solution)/shard_map/ppermute | solution.py:455
  48.9 11.0 %copy-start.4 = (bf16[1,128,512]{2,1,0:T(8,128)(2,1)S(1)}, bf16[1,128,512]{2,1,0:T(8,128)(2,1)}, u32[]{:S(2)}) copy-start(bf16[1,128,512]{2,1,0:T(8,128)(2,1)} %param.23) | copy-start | bytes 393220
  83.3 8.3 %collective-permute-start.10 = (bf16[128,512]{1,0:T(8,128)(2,1)S(1)}, bf16[128,512]{1,0:T(8,128)(2,1)S(1)}, u32[]{:S(2)}, u32[]{:S(2)}) collective-permute-start(bf16[128,512]{1,0:T(8,128)(2,1)S(1)} %shard_map.142.refs_8_.refs_4_), channel_id=1, source_target_pairs={{0,6},{1,7},{2,4},{3,5},{4,2},{5,3},{6,0},{7,1},{8,14},{9,15},{10,... | collective-permute-start | bytes 393224 | tf_op jit(solution)/shard_map/ppermute | solution.py:455
  84.1 9.7 %collective-permute-start.8 = (bf16[128,512]{1,0:T(8,128)(2,1)S(1)}, bf16[128,512]{1,0:T(8,128)(2,1)S(1)}, u32[]{:S(2)}, u32[]{:S(2)}) collective-permute-start(bf16[128,512]{1,0:T(8,128)(2,1)S(1)} %shard_map.142.refs_8_.refs_4_), channel_id=1, source_target_pairs={{0,2},{1,3},{2,0},{3,1},{4,6},{5,7},{6,4},{7,5},{8,10},{9,11},{10,... | collective-permute-start | bytes 393224 | tf_op jit(solution)/shard_map/ppermute | solution.py:455
  84.3 12.9 %collective-permute-start.9 = (bf16[128,512]{1,0:T(8,128)(2,1)S(1)}, bf16[128,512]{1,0:T(8,128)(2,1)S(1)}, u32[]{:S(2)}, u32[]{:S(2)}) collective-permute-start(bf16[128,512]{1,0:T(8,128)(2,1)S(1)} %shard_map.142.refs_8_.refs_4_), channel_id=1, source_target_pairs={{0,4},{1,5},{2,6},{3,7},{4,0},{5,1},{6,2},{7,3},{8,12},{9,13},{10,... | collective-permute-start | bytes 393224 | tf_op jit(solution)/shard_map/ppermute | solution.py:455
  87.8 9.5 %collective-permute-start.11 = (bf16[128,512]{1,0:T(8,128)(2,1)S(1)}, bf16[128,512]{1,0:T(8,128)(2,1)S(1)}, u32[]{:S(2)}, u32[]{:S(2)}) collective-permute-start(bf16[128,512]{1,0:T(8,128)(2,1)S(1)} %shard_map.142.refs_8_.refs_4_), channel_id=1, source_target_pairs={{0,1},{1,0},{2,3},{3,2},{4,5},{5,4},{6,7},{7,6},{8,9},{9,8},{10,11... | collective-permute-start | bytes 393224 | tf_op jit(solution)/shard_map/ppermute | solution.py:455
  91.6 5.7 %collective-permute-start.14 = (bf16[128,512]{1,0:T(8,128)(2,1)S(1)}, bf16[128,512]{1,0:T(8,128)(2,1)S(1)}, u32[]{:S(2)}, u32[]{:S(2)}) collective-permute-start(bf16[128,512]{1,0:T(8,128)(2,1)S(1)} %collective-permute-done.10.refs_11_.refs_7_), channel_id=1, source_target_pairs={{0,1},{1,0},{2,3},{3,2},{4,5},{5,4},{6,7},{7,6},{8,9},{9,8},{10,11... | collective-permute-start | bytes 393224 | tf_op jit(solution)/shard_map/ppermute | solution.py:455
  93.8 3.4 %collective-permute-start.12 = (bf16[128,512]{1,0:T(8,128)(2,1)S(1)}, bf16[128,512]{1,0:T(8,128)(2,1)S(1)}, u32[]{:S(2)}, u32[]{:S(2)}) collective-permute-start(bf16[128,512]{1,0:T(8,128)(2,1)S(1)} %collective-permute-done.8.refs_9_.refs_5_), channel_id=1, source_target_pairs={{0,1},{1,0},{2,3},{3,2},{4,5},{5,4},{6,7},{7,6},{8,9},{9,8},{10,11... | collective-permute-start | bytes 393224 | tf_op jit(solution)/shard_map/ppermute | solution.py:455
  97.2 1.3 %collective-permute-start.13 = (bf16[128,512]{1,0:T(8,128)(2,1)S(1)}, bf16[128,512]{1,0:T(8,128)(2,1)S(1)}, u32[]{:S(2)}, u32[]{:S(2)}) collective-permute-start(bf16[128,512]{1,0:T(8,128)(2,1)S(1)} %collective-permute-done.9.refs_10_.refs_6_), channel_id=1, source_target_pairs={{0,1},{1,0},{2,3},{3,2},{4,5},{5,4},{6,7},{7,6},{8,9},{9,8},{10,11... | collective-permute-start | bytes 393224 | tf_op jit(solution)/shard_map/ppermute | solution.py:455
  100.4 6.4 %collective-permute-start.18 = (bf16[256,256]{1,0:T(8,128)(2,1)S(1)}, bf16[256,256]{1,0:T(8,128)(2,1)S(1)}, u32[]{:S(2)}, u32[]{:S(2)}) collective-permute-start(bf16[256,256]{1,0:T(8,128)(2,1)S(1)} %get-tuple-element.135), channel_id=1, source_target_pairs={{0,16},{8,24},{16,0},{24,8},{1,17},{9,25},{17,1},{25,9},{2,18},{10... | collective-permute-start | bytes 393224 | tf_op jit(solution)/shard_map/ppermute | solution.py:455
  101.1 6.4 %collective-permute-start.17 = (bf16[256,256]{1,0:T(8,128)(2,1)S(1)}, bf16[256,256]{1,0:T(8,128)(2,1)S(1)}, u32[]{:S(2)}, u32[]{:S(2)}) collective-permute-start(bf16[256,256]{1,0:T(8,128)(2,1)S(1)} %get-tuple-element.134), channel_id=1, source_target_pairs={{0,8},{8,0},{16,24},{24,16},{1,9},{9,1},{17,25},{25,17},{2,10},{10... | collective-permute-start | bytes 393224 | tf_op jit(solution)/shard_map/ppermute | solution.py:455
  101.6 7.5 %collective-permute-start.16 = (bf16[256,256]{1,0:T(8,128)(2,1)S(1)}, bf16[256,256]{1,0:T(8,128)(2,1)S(1)}, u32[]{:S(2)}, u32[]{:S(2)}) collective-permute-start(bf16[256,256]{1,0:T(8,128)(2,1)S(1)} %get-tuple-element.133), channel_id=1, source_target_pairs={{0,16},{8,24},{16,0},{24,8},{1,17},{9,25},{17,1},{25,9},{2,18},{10... | collective-permute-start | bytes 393224 | tf_op jit(solution)/shard_map/ppermute | solution.py:455
  103.1 6.8 %collective-permute-start.15 = (bf16[256,256]{1,0:T(8,128)(2,1)S(1)}, bf16[256,256]{1,0:T(8,128)(2,1)S(1)}, u32[]{:S(2)}, u32[]{:S(2)}) collective-permute-start(bf16[256,256]{1,0:T(8,128)(2,1)S(1)} %get-tuple-element.132), channel_id=1, source_target_pairs={{0,8},{8,0},{16,24},{24,16},{1,9},{9,1},{17,25},{25,17},{2,10},{10... | collective-permute-start | bytes 393224 | tf_op jit(solution)/shard_map/ppermute | solution.py:455
  105.8 8.5 %copy-start.2 = (bf16[512,512]{1,0:T(8,128)(2,1)S(1)}, bf16[512,512]{1,0:T(8,128)(2,1)}, u32[]{:S(2)}) copy-start(bf16[512,512]{1,0:T(8,128)(2,1)} %refs_12_.1) | copy-start | bytes 1572868
  106.8 5.8 %collective-permute-start.22 = (bf16[128,256]{1,0:T(8,128)(2,1)S(1)}, bf16[128,256]{1,0:T(8,128)(2,1)S(1)}, u32[]{:S(2)}, u32[]{:S(2)}) collective-permute-start(bf16[128,256]{1,0:T(8,128)(2,1)S(1)} %add_convert_fusion), channel_id=1, source_target_pairs={{0,8},{8,0},{16,24},{24,16},{1,9},{9,1},{17,25},{25,17},{2,10},{10... | collective-permute-start | bytes 196616 | tf_op jit(solution)/shard_map/ppermute | solution.py:455
  107.5 5.1 %collective-permute-start.21 = (bf16[128,256]{1,0:T(8,128)(2,1)S(1)}, bf16[128,256]{1,0:T(8,128)(2,1)S(1)}, u32[]{:S(2)}, u32[]{:S(2)}) collective-permute-start(bf16[128,256]{1,0:T(8,128)(2,1)S(1)} %add_convert_fusion.1), channel_id=1, source_target_pairs={{0,16},{8,24},{16,0},{24,8},{1,17},{9,25},{17,1},{25,9},{2,18},{10... | collective-permute-start | bytes 196616 | tf_op jit(solution)/shard_map/ppermute | solution.py:455
  109.1 4.3 %collective-permute-start.20 = (bf16[128,256]{1,0:T(8,128)(2,1)S(1)}, bf16[128,256]{1,0:T(8,128)(2,1)S(1)}, u32[]{:S(2)}, u32[]{:S(2)}) collective-permute-start(bf16[128,256]{1,0:T(8,128)(2,1)S(1)} %add_convert_fusion.2), channel_id=1, source_target_pairs={{0,8},{8,0},{16,24},{24,16},{1,9},{9,1},{17,25},{25,17},{2,10},{10... | collective-permute-start | bytes 196616 | tf_op jit(solution)/shard_map/ppermute | solution.py:455
  109.9 4.3 %collective-permute-start.19 = (bf16[128,256]{1,0:T(8,128)(2,1)S(1)}, bf16[128,256]{1,0:T(8,128)(2,1)S(1)}, u32[]{:S(2)}, u32[]{:S(2)}) collective-permute-start(bf16[128,256]{1,0:T(8,128)(2,1)S(1)} %add_convert_fusion.3), channel_id=1, source_target_pairs={{0,16},{8,24},{16,0},{24,8},{1,17},{9,25},{17,1},{25,9},{2,18},{10... | collective-permute-start | bytes 196616 | tf_op jit(solution)/shard_map/ppermute | solution.py:455

commit v5 on v4

--- a/solution.py
+++ b/solution.py
@@ -282,7 +282,7 @@
     normed, scale = norm_parts(mixed)
     grad_mixed = norm_back(grad, normed, scale)
     grad_state = grad + back_dot(grad_mixed, weights(2))
-    grad_agg = 0.5 * back_dot(grad_mixed, weights(3))
+    grad_agg = 0.5 * dot_t(grad_mixed.astype(BF16), weights(3))
     low = grad_agg.astype(BF16)
     total = jnp.zeros(grad.shape, F32)
     for found in slopes:
@@ -291,7 +291,7 @@
     pieces = [low * found for found in slopes]
     grad_src = dot(source_t[...], jnp.concatenate(pieces, axis=0))
     grad_state = grad_state + back_dot(total, weights(1))
-    grad_table = back_dot(grad_src, weights(0))
+    grad_table = dot_t(grad_src.astype(BF16), weights(0))
     return grad_state + grad_table[:block], grad_table[block:]
 
 
@@ -391,8 +391,10 @@
             marks.append(feat[...])
         else:
             marks += edge_marks(feat, at, rows, nodes, block, fanout, who)
+    same, other = grads[: nodes // 2][::-1], grads[nodes // 2 :][::-1]
     picked = dot(
-        jnp.concatenate(marks, axis=0), jnp.concatenate([ref[...] for ref in grads], axis=0)
+        jnp.concatenate(marks, axis=0),
+        jnp.concatenate([ref[...] for ref in (*same, *other)], axis=0),
     )
     size = outs[0].shape[1]
     chunks = slopes[0].shape[1] // size
@@ -648,7 +650,7 @@
         same[-1] = lax.optimization_barrier((same[-1], found[0]))[0]
         picks_of = {unit: (part, 0) for unit, part in zip(units, found)}
     other = [swap(rows, "node", 1) for rows in same[::-1]][::-1]
-    gathered = (*same, *other)
+    gathered = (*same[::-1], *other[::-1])
 
     def message_back(groups, dtype):
         used = [unit for group in groups for unit in group]

time: 116 us -> 116 us (level)
  no operation moved by 1% of the time
where the time goes in v5:
time: 116 us
  blocking collectives  38.3 us (33%)
  Pallas kernels  27.5 us (24%)
  starting transfers between devices  25.6 us (22%)
  waiting for transfers between devices  22.9 us (20%)
    all_to_all x4, blocking collectives, exchange(): return lax.all_to_all(value, both, split_axis=0, concat_axis=0, tiled=True)  38.3 us
    pallas_call x17, Pallas kernels, call(): pl.pallas_call(kernel, out_shape=list(outs), in_specs=specs, out_specs=[p...  27.5 us
    ppermute x23, starting transfers between devices, swap(): return lax.ppermute(value, axis, [(i, i ^ apart) for i in range(size)])  25.6 us
    ppermute x23, waiting for transfers between devices, swap(): return lax.ppermute(value, axis, [(i, i ^ apart) for i in range(size)])  22.9 us
  transfers between devices with their start and end apart: 23, of which 14 were waited for; matrix products, arithmetic and copies ran while one was open for 0% of the time, Pallas kernels for 12%

profile of v5, /device:TPU:0, one launch (start us, length us, event | category | flops | bytes accessed | tf_op | source)
XLA Modules:
  0.0 115.6 jit_solution(15320532574212894054)
XLA Ops:
  0.6 1.1 shard_map.131
  1.7 3.0 %collective-permute-start.2 = (bf16[144,512]{1,0:T(8,128)(2,1)S(1)}, bf16[144,512]{1,0:T(8,128)(2,1)S(1)}, u32[]{:S(2)}, u32[]{:S(2)}) collective-permute-start(bf16[144,512]{1,0:T(8,128)(2,1)S(1)} %get-tuple-element.84.refs_1_), channel_id=1, source_target_pairs={{0,16},{8,24},{16,0},{24,8},{1,17},{9,25},{17,1},{25,9},{2,18},{10... | collective-permute-start | bytes 442376 | tf_op jit(solution)/shard_map/ppermute | solution.py:457
  4.7 1.5 %collective-permute-start = (bf16[144,512]{1,0:T(8,128)(2,1)S(1)}, bf16[144,512]{1,0:T(8,128)(2,1)S(1)}, u32[]{:S(2)}, u32[]{:S(2)}) collective-permute-start(bf16[144,512]{1,0:T(8,128)(2,1)S(1)} %get-tuple-element.83.refs_0_), channel_id=1, source_target_pairs={{0,8},{8,0},{16,24},{24,16},{1,9},{9,1},{17,25},{25,17},{2,10},{10... | collective-permute-start | bytes 442376 | tf_op jit(solution)/shard_map/ppermute | solution.py:457
  6.2 2.4 %collective-permute-done.2.refs_1_.refs_5_ = bf16[144,512]{1,0:T(8,128)(2,1)S(1)} collective-permute-done((bf16[144,512]{1,0:T(8,128)(2,1)S(1)}, bf16[144,512]{1,0:T(8,128)(2,1)S(1)}, u32[]{:S(2)}, u32[]{:S(2)}) %collective-permute-start.2) | collective-permute-done | bytes 147488 | tf_op jit(solution)/shard_map/ppermute | solution.py:457
  8.6 1.8 %collective-permute-start.3 = (bf16[288,512]{1,0:T(8,128)(2,1)S(1)}, bf16[288,512]{1,0:T(8,128)(2,1)S(1)}, u32[]{:S(2)}, u32[]{:S(2)}) collective-permute-start(bf16[288,512]{1,0:T(8,128)(2,1)S(1)} %pad_maximum_fusion.1), channel_id=1, source_target_pairs={{0,8},{8,0},{16,24},{24,16},{1,9},{9,1},{17,25},{25,17},{2,10},{10... | collective-permute-start | bytes 884744 | tf_op jit(solution)/shard_map/ppermute | solution.py:457
  10.4 1.6 %collective-permute-start.1 = (bf16[288,512]{1,0:T(8,128)(2,1)S(1)}, bf16[288,512]{1,0:T(8,128)(2,1)S(1)}, u32[]{:S(2)}, u32[]{:S(2)}) collective-permute-start(bf16[288,512]{1,0:T(8,128)(2,1)S(1)} %pad_maximum_fusion), channel_id=1, source_target_pairs={{0,16},{8,24},{16,0},{24,8},{1,17},{9,25},{17,1},{25,9},{2,18},{10... | collective-permute-start | bytes 884744 | tf_op jit(solution)/shard_map/ppermute | solution.py:457
  12.0 1.5 %shard_map.132 = (bf16[256,512]{1,0:T(8,128)(2,1)S(1)}, bf16[512,256]{1,0:T(8,128)(2,1)S(1)}, bf16[1024,192]{1,0:T(8,128)(2,1)S(1)}, bf16[192,1024]{1,0:T(8,128)...) custom-call(s32[4,2,8]{2,1,0:T(2,128)} %bitcast.33, s32[8,128]{1,0:T(8,128)} %bitcast.34, ...), custom_call_target="tpu_custom_call" | custom-call | bytes 2367744 | tf_op jit(solution)/shard_map/pallas_call | solution.py:436
  13.5 0.1 pad_add_fusion.who
  13.6 1.9 %shard_map.133.refs_4_ = f32[1024,512]{1,0:T(8,128)S(1)} custom-call(s32[2]{0:T(128)S(1)} %pad_add_fusion.who, bf16[144,512]{1,0:T(8,128)(2,1)S(1)} %get-tuple-element.83.refs_0_, bf16[144,512]{1,0:T(8,128)(2,1)S(1)} %get-tuple-element.84.refs_1_, bf16[512,512]{1,0:T(8,128)(2,1)S(1)} %get-tuple-element.85.refs_2_.refs_4_.refs_8_, ...), custom_call_target="tpu_custom_call" | custom-call | bytes 2918408 | tf_op jit(solution)/shard_map/pallas_call | solution.py:436
  15.5 1.9 %shard_map.134.refs_6_.before = f32[1024,512]{1,0:T(8,128)S(1)} custom-call(s32[2]{0:T(128)S(1)} %pad_add_fusion.who, bf16[144,512]{1,0:T(8,128)(2,1)S(1)} %collective-permute-done.refs_0_.refs_2_, bf16[144,512]{1,0:T(8,128)(2,1)S(1)} %collective-permute-done.2.refs_1_.refs_5_, ...), custom_call_target="tpu_custom_call", output_to_operand_aliasing={{}: (5, {})} | custom-call | bytes 5015560 | tf_op jit(solution)/shard_map/pallas_call | solution.py:436
  17.4 0.0 collective-permute-done.3.refs_2_.refs_3_.refs_7_
  17.4 0.7 collective-permute-done.1.refs_0_.refs_1_.refs_4_.refs_6_
  18.1 2.0 %shard_map.135 = (bf16[512,512]{1,0:T(8,128)(2,1)S(1)}, bf16[1024,512]{1,0:T(8,128)(2,1)S(1)}, s32[1,1024]{1,0:T(1,128)S(1)}) custom-call(s32[2]{0:T(128)S(1)} %pad_add_fusion.who, bf16[288,512]{1,0:T(8,128)(2,1)S(1)} %collective-permute-done.1.refs_0_.refs_1_.refs_4_.refs_6_, bf16[288,512]{1,0:T(8,128)(2,1)S(1)} %collective-permute-done.1.refs_0_.refs_1_.refs_4_.refs_6_, ...), custom_call_target="tpu_custom_call" | custom-call | bytes 5380104 | tf_op jit(solution)/shard_map/pallas_call | solution.py:436
  20.1 0.1 collective-permute-start.4
  20.2 0.7 shard_map.136
  20.9 1.2 %collective-permute-done.4 = bf16[512,512]{1,0:T(8,128)(2,1)S(1)} collective-permute-done((bf16[512,512]{1,0:T(8,128)(2,1)S(1)}, bf16[512,512]{1,0:T(8,128)(2,1)S(1)}, u32[]{:S(2)}, u32[]{:S(2)}) %collective-permute-start.4) | collective-permute-done | bytes 524320 | tf_op jit(solution)/shard_map/ppermute | solution.py:457
  22.1 0.2 fusion
  22.3 0.0 copy-start.1
  22.3 0.0 copy-start.3
  22.3 3.7 %collective-permute-start.5 = (bf16[128,512]{1,0:T(8,128)(2,1)S(1)}, bf16[128,512]{1,0:T(8,128)(2,1)S(1)}, u32[]{:S(2)}, u32[]{:S(2)}) collective-permute-start(bf16[128,512]{1,0:T(8,128)(2,1)S(1)} %get-tuple-element.168), channel_id=1, source_target_pairs={{0,6},{1,7},{2,4},{3,5},{4,2},{5,3},{6,0},{7,1},{8,14},{9,15},{10,... | collective-permute-start | bytes 393224 | tf_op jit(solution)/shard_map/ppermute | solution.py:457
  26.0 0.8 collective-permute-start.7
  26.8 2.3 %shard_map.137 = (bf16[256,512]{1,0:T(8,128)(2,1)S(1)}, bf16[256,512]{1,0:T(8,128)(2,1)S(1)}, bf16[256,512]{1,0:T(8,128)(2,1)S(1)}, bf16[256,512]{1,0:T(8,128)(2...) custom-call(bf16[144,512]{1,0:T(8,128)(2,1)S(1)} %get-tuple-element., ...), custom_call_target="tpu_custom_call" | custom-call | bytes 4392960 | tf_op jit(solution)/shard_map/pallas_call | solution.py:436
  29.1 1.5 %collective-permute-done.5.refs_0_ = bf16[128,512]{1,0:T(8,128)(2,1)S(1)} collective-permute-done((bf16[128,512]{1,0:T(8,128)(2,1)S(1)}, bf16[128,512]{1,0:T(8,128)(2,1)S(1)}, u32[]{:S(2)}, u32[]{:S(2)}) %collective-permute-start.5) | collective-permute-done | bytes 131104 | tf_op jit(solution)/shard_map/ppermute | solution.py:457
  30.6 6.7 %collective-permute-done.6.refs_1_ = bf16[128,512]{1,0:T(8,128)(2,1)S(1)} collective-permute-done((bf16[128,512]{1,0:T(8,128)(2,1)S(1)}, bf16[128,512]{1,0:T(8,128)(2,1)S(1)}, u32[]{:S(2)}, u32[]{:S(2)}) %collective-permute-start.6) | collective-permute-done | bytes 131104 | tf_op jit(solution)/shard_map/ppermute | solution.py:457
  37.4 0.5 shard_map.138
  37.8 11.0 %all_to_all.44 = bf16[32,8,128]{2,1,0:T(8,128)(2,1)S(1)} all-to-all(bf16[32,8,128]{2,1,0:T(8,128)(2,1)S(1)} %bitcast.29), channel_id=1, replica_groups=mesh['sect'=4,'node'=8] {'sect','node'}, dimensions={0} | all-to-all | bytes 131072 | tf_op jit(solution)/shard_map/all_to_all | solution.py:602
  48.9 1.9 %shard_map.139 = (bf16[128,512]{1,0:T(8,128)(2,1)S(1)}, f32[128,512]{1,0:T(8,128)S(1)}, bf16[1024,512]{1,0:T(8,128)(2,1)S(1)}, bf16[256,128]{1,0:T(8,128)(2,1)S(1)}) custom-call(bf16[128,512]{1,0:T(8,128)(2,1)S(1)} %get-tuple-element.102.state, bf16[256,128]{1,0:T(8,128)(2,1)S(1)} %bitcast.24, bf16[1024,192]{1,0:T(8,128)(2,1)S(1)} %get-tuple-element.104.source, ...), custom_call_target="tpu_custom_call" | custom-call | bytes 6553600 | tf_op jit(solution)/shard_map/pallas_call | solution.py:436
  50.7 9.1 %all_to_all.45 = bf16[32,8,128]{2,1,0:T(8,128)(2,1)S(1)} all-to-all(bf16[32,8,128]{2,1,0:T(8,128)(2,1)S(1)} %bitcast.30), channel_id=1, replica_groups=mesh['sect'=4,'node'=8] {'sect','node'}, dimensions={0} | all-to-all | bytes 131072 | tf_op jit(solution)/shard_map/all_to_all | solution.py:602
  59.8 3.0 %shard_map.140 = (bf16[128,512]{1,0:T(8,128)(2,1)S(1)}, f32[128,512]{1,0:T(8,128)S(1)}, bf16[256,128]{1,0:T(8,128)(2,1)S(1)}) custom-call(bf16[128,512]{1,0:T(8,128)(2,1)S(1)} %get-tuple-element.105.state, bf16[256,128]{1,0:T(8,128)(2,1)S(1)} %bitcast.25, bf16[1024,192]{1,0:T(8,128)(2,1)S(1)} %get-tuple-element.104.source, ...), custom_call_target="tpu_custom_call" | custom-call | bytes 5767168 | tf_op jit(solution)/shard_map/pallas_call | solution.py:436
  62.8 9.1 %all_to_all.46 = bf16[32,8,128]{2,1,0:T(8,128)(2,1)S(1)} all-to-all(bf16[32,8,128]{2,1,0:T(8,128)(2,1)S(1)} %bitcast.32), channel_id=1, replica_groups=mesh['sect'=4,'node'=8] {'sect','node'}, dimensions={0} | all-to-all | bytes 131072 | tf_op jit(solution)/shard_map/all_to_all | solution.py:602
  71.9 1.7 %shard_map.141 = (f32[128,512]{1,0:T(8,128)S(1)}, bf16[256,128]{1,0:T(8,128)(2,1)S(1)}) custom-call(f32[128,512]{1,0:T(8,128)S(1)} %get-tuple-element.108.mine, bf16[256,128]{1,0:T(8,128)(2,1)S(1)} %bitcast.23, bf16[512,256]{1,0:T(8,128)(2,1)S(1)} %get-tuple-element.110.pick_t, f32[128,512]{1,0:T(8,128)S(1)} %get-tuple-element.111.mixed, ...), custom_call_target="tpu_custom_call" | custom-call | bytes 6815744 | tf_op jit(solution)/shard_map/pallas_call | solution.py:436
  73.6 9.1 %all_to_all.47 = bf16[32,8,128]{2,1,0:T(8,128)(2,1)S(1)} all-to-all(bf16[32,8,128]{2,1,0:T(8,128)(2,1)S(1)} %bitcast.31), channel_id=1, replica_groups=mesh['sect'=4,'node'=8] {'sect','node'}, dimensions={0} | all-to-all | bytes 131072 | tf_op jit(solution)/shard_map/all_to_all | solution.py:602
  82.7 0.5 shard_map.142.refs_11_.refs_7_
  83.2 0.8 collective-permute-start.8
  83.9 1.2 %collective-permute-start.9 = (bf16[128,512]{1,0:T(8,128)(2,1)S(1)}, bf16[128,512]{1,0:T(8,128)(2,1)S(1)}, u32[]{:S(2)}, u32[]{:S(2)}) collective-permute-start(bf16[128,512]{1,0:T(8,128)(2,1)S(1)} %shard_map.142.refs_11_.refs_7_), channel_id=1, source_target_pairs={{0,4},{1,5},{2,6},{3,7},{4,0},{5,1},{6,2},{7,3},{8,12},{9,13},{10,... | collective-permute-start | bytes 393224 | tf_op jit(solution)/shard_map/ppermute | solution.py:457
  85.1 2.5 %collective-permute-start.10 = (bf16[128,512]{1,0:T(8,128)(2,1)S(1)}, bf16[128,512]{1,0:T(8,128)(2,1)S(1)}, u32[]{:S(2)}, u32[]{:S(2)}) collective-permute-start(bf16[128,512]{1,0:T(8,128)(2,1)S(1)} %shard_map.142.refs_11_.refs_7_), channel_id=1, source_target_pairs={{0,2},{1,3},{2,0},{3,1},{4,6},{5,7},{6,4},{7,5},{8,10},{9,11},{10,... | collective-permute-start | bytes 393224 | tf_op jit(solution)/shard_map/ppermute | solution.py:457
  87.6 0.0 collective-permute-start.14
  87.6 3.2 %shard_map.143 = (bf16[256,1024]{1,0:T(8,128)(2,1)S(1)}, bf16[256,1024]{1,0:T(8,128)(2,1)S(1)}, bf16[256,1024]{1,0:T(8,128)(2,1)S(1)}, bf16[256,1024]{1,0:T(8,12...) custom-call(s32[2]{0:T(128)S(1)} %pad_add_fusion.who, ...), custom_call_target="tpu_custom_call" | custom-call | bytes 6225928 | tf_op jit(solution)/shard_map/pallas_call | solution.py:436
  90.8 0.7 collective-permute-done.8.refs_8_.refs_4_
  91.5 0.0 collective-permute-start.11
  91.5 5.6 %collective-permute-done.9.refs_9_.refs_5_ = bf16[128,512]{1,0:T(8,128)(2,1)S(1)} collective-permute-done((bf16[128,512]{1,0:T(8,128)(2,1)S(1)}, bf16[128,512]{1,0:T(8,128)(2,1)S(1)}, u32[]{:S(2)}, u32[]{:S(2)}) %collective-permute-start.9) | collective-permute-done | bytes 131104 | tf_op jit(solution)/shard_map/ppermute | solution.py:457
  97.1 0.0 collective-permute-start.12
  97.1 0.0 collective-permute-done.10.refs_10_.refs_6_
  97.1 0.5 collective-permute-start.13
  97.6 0.8 collective-permute-done.12.refs_13_.refs_9_
  98.4 0.2 collective-permute-done.13.refs_14_.refs_10_
  98.6 1.8 %shard_map.144 = (bf16[256,256]{1,0:T(8,128)(2,1)S(1)}, bf16[256,256]{1,0:T(8,128)(2,1)S(1)}, bf16[256,256]{1,0:T(8,128)(2,1)S(1)}, bf16[256,256]{1,0:T(8,128)(2,1)S(1)}) custom-call(s32[2]{0:T(128)S(1)} %pad_add_fusion.who, bf16[256,1024]{1,0:T(8,128)(2,1)S(1)} %get-tuple-element.124.refs_0_, bf16[256,1024]{1,0:T(8,128)(2,1)S(1)} %get-tuple-element.125.refs_1_, ...), custom_call_target="tpu_custom_call" | custom-call | bytes 4718600 | tf_op jit(solution)/shard_map/pallas_call | solution.py:436
  100.5 0.7 collective-permute-start.18
  101.1 0.5 collective-permute-start.17
  101.7 1.5 %collective-permute-start.16 = (bf16[256,256]{1,0:T(8,128)(2,1)S(1)}, bf16[256,256]{1,0:T(8,128)(2,1)S(1)}, u32[]{:S(2)}, u32[]{:S(2)}) collective-permute-start(bf16[256,256]{1,0:T(8,128)(2,1)S(1)} %get-tuple-element.133), channel_id=1, source_target_pairs={{0,16},{8,24},{16,0},{24,8},{1,17},{9,25},{17,1},{25,9},{2,18},{10... | collective-permute-start | bytes 393224 | tf_op jit(solution)/shard_map/ppermute | solution.py:457
  103.1 1.4 %collective-permute-start.15 = (bf16[256,256]{1,0:T(8,128)(2,1)S(1)}, bf16[256,256]{1,0:T(8,128)(2,1)S(1)}, u32[]{:S(2)}, u32[]{:S(2)}) collective-permute-start(bf16[256,256]{1,0:T(8,128)(2,1)S(1)} %get-tuple-element.132), channel_id=1, source_target_pairs={{0,8},{8,0},{16,24},{24,16},{1,9},{9,1},{17,25},{25,17},{2,10},{10... | collective-permute-start | bytes 393224 | tf_op jit(solution)/shard_map/ppermute | solution.py:457
  104.6 1.3 %shard_map.145 = (f32[128,256]{1,0:T(8,128)S(1)}, f32[128,256]{1,0:T(8,128)S(1)}, f32[128,256]{1,0:T(8,128)S(1)}, f32[128,256]{1,0:T(8,128)S(1)}) custom-call(s32[2]{0:T(128)S(1)} %pad_add_fusion.who, bf16[256,1024]{1,0:T(8,128)(2,1)S(1)} %get-tuple-element.144.refs_0_, bf16[256,1024]{1,0:T(8,128)(2,1)S(1)} %get-tuple-element.145.refs_1_, ...), custom_call_target="tpu_custom_call" | custom-call | bytes 3145736 | tf_op jit(solution)/shard_map/pallas_call | solution.py:436
  105.8 0.0 copy-start.2
  105.8 1.0 collective-permute-done.18.refs_7_
  106.9 0.7 collective-permute-start.22
  107.5 1.4 %collective-permute-start.21 = (bf16[128,256]{1,0:T(8,128)(2,1)S(1)}, bf16[128,256]{1,0:T(8,128)(2,1)S(1)}, u32[]{:S(2)}, u32[]{:S(2)}) collective-permute-start(bf16[128,256]{1,0:T(8,128)(2,1)S(1)} %add_convert_fusion.1), channel_id=1, source_target_pairs={{0,16},{8,24},{16,0},{24,8},{1,17},{9,25},{17,1},{25,9},{2,18},{10... | collective-permute-start | bytes 196616 | tf_op jit(solution)/shard_map/ppermute | solution.py:457
  109.0 0.2 collective-permute-done.16.refs_5_
  109.2 0.6 collective-permute-start.20
  109.7 0.4 collective-permute-done.15.refs_4_
  110.1 1.5 %collective-permute-start.19 = (bf16[128,256]{1,0:T(8,128)(2,1)S(1)}, bf16[128,256]{1,0:T(8,128)(2,1)S(1)}, u32[]{:S(2)}, u32[]{:S(2)}) collective-permute-start(bf16[128,256]{1,0:T(8,128)(2,1)S(1)} %add_convert_fusion.3), channel_id=1, source_target_pairs={{0,16},{8,24},{16,0},{24,8},{1,17},{9,25},{17,1},{25,9},{2,18},{10... | collective-permute-start | bytes 196616 | tf_op jit(solution)/shard_map/ppermute | solution.py:457
  111.6 1.3 %shard_map.146 = (f32[128,256]{1,0:T(8,128)S(1)}, f32[128,256]{1,0:T(8,128)S(1)}, f32[128,256]{1,0:T(8,128)S(1)}, f32[128,256]{1,0:T(8,128)S(1)}) custom-call(s32[2]{0:T(128)S(1)} %pad_add_fusion.who, bf16[256,1024]{1,0:T(8,128)(2,1)S(1)} %get-tuple-element.119.refs_0_, bf16[256,1024]{1,0:T(8,128)(2,1)S(1)} %get-tuple-element.120.refs_1_, ...), custom_call_target="tpu_custom_call" | custom-call | bytes 3145736 | tf_op jit(solution)/shard_map/pallas_call | solution.py:436
  112.9 0.7 collective-permute-done.20.refs_9_
  113.5 0.9 collective-permute-done.19.refs_8_
  114.5 1.2 %shard_map.147 = bf16[256,512]{1,0:T(8,128)(2,1)} custom-call(f32[128,256]{1,0:T(8,128)S(1)} %get-tuple-element.160.refs_0_, f32[128,256]{1,0:T(8,128)S(1)} %get-tuple-element.161.refs_1_, f32[128,256]{1,0:T(8,128)S(1)} %get-tuple-element.162.refs_2_, f32[128,256]{1,0:T(8,128)S(1)} %get-tuple-element.163.refs_3_, ...), custom_call_target="tpu_custom_call" | custom-call | bytes 2097152 | tf_op jit(solution)/shard_map/pallas_call | solution.py:436
  (23 shorter events, 0.2 us)
Async XLA Ops:
  1.7 6.9 %collective-permute-start.2 = (bf16[144,512]{1,0:T(8,128)(2,1)S(1)}, bf16[144,512]{1,0:T(8,128)(2,1)S(1)}, u32[]{:S(2)}, u32[]{:S(2)}) collective-permute-start(bf16[144,512]{1,0:T(8,128)(2,1)S(1)} %get-tuple-element.84.refs_1_), channel_id=1, source_target_pairs={{0,16},{8,24},{16,0},{24,8},{1,17},{9,25},{17,1},{25,9},{2,18},{10... | collective-permute-start | bytes 442376 | tf_op jit(solution)/shard_map/ppermute | solution.py:457
  4.7 5.7 %collective-permute-start = (bf16[144,512]{1,0:T(8,128)(2,1)S(1)}, bf16[144,512]{1,0:T(8,128)(2,1)S(1)}, u32[]{:S(2)}, u32[]{:S(2)}) collective-permute-start(bf16[144,512]{1,0:T(8,128)(2,1)S(1)} %get-tuple-element.83.refs_0_), channel_id=1, source_target_pairs={{0,8},{8,0},{16,24},{24,16},{1,9},{9,1},{17,25},{25,17},{2,10},{10... | collective-permute-start | bytes 442376 | tf_op jit(solution)/shard_map/ppermute | solution.py:457
  8.6 8.8 %collective-permute-start.3 = (bf16[288,512]{1,0:T(8,128)(2,1)S(1)}, bf16[288,512]{1,0:T(8,128)(2,1)S(1)}, u32[]{:S(2)}, u32[]{:S(2)}) collective-permute-start(bf16[288,512]{1,0:T(8,128)(2,1)S(1)} %pad_maximum_fusion.1), channel_id=1, source_target_pairs={{0,8},{8,0},{16,24},{24,16},{1,9},{9,1},{17,25},{25,17},{2,10},{10... | collective-permute-start | bytes 884744 | tf_op jit(solution)/shard_map/ppermute | solution.py:457
  10.4 7.7 %collective-permute-start.1 = (bf16[288,512]{1,0:T(8,128)(2,1)S(1)}, bf16[288,512]{1,0:T(8,128)(2,1)S(1)}, u32[]{:S(2)}, u32[]{:S(2)}) collective-permute-start(bf16[288,512]{1,0:T(8,128)(2,1)S(1)} %pad_maximum_fusion), channel_id=1, source_target_pairs={{0,16},{8,24},{16,0},{24,8},{1,17},{9,25},{17,1},{25,9},{2,18},{10... | collective-permute-start | bytes 884744 | tf_op jit(solution)/shard_map/ppermute | solution.py:457
  20.1 2.0 %collective-permute-start.4 = (bf16[512,512]{1,0:T(8,128)(2,1)S(1)}, bf16[512,512]{1,0:T(8,128)(2,1)S(1)}, u32[]{:S(2)}, u32[]{:S(2)}) collective-permute-start(bf16[512,512]{1,0:T(8,128)(2,1)S(1)} %get-tuple-element.89), channel_id=1, source_target_pairs={{0,1},{1,0},{2,3},{3,2},{4,5},{5,4},{6,7},{7,6},{8,9},{9,8},{10,11... | collective-permute-start | bytes 1572872 | tf_op jit(solution)/shard_map/ppermute | solution.py:457
  22.3 15.1 %copy-start.1 = (bf16[512,512]{1,0:T(8,128)(2,1)S(1)}, bf16[512,512]{1,0:T(8,128)(2,1)}, u32[]{:S(2)}) copy-start(bf16[512,512]{1,0:T(8,128)(2,1)} %weight.1) | copy-start | bytes 1572868
  22.3 15.1 %copy-start.3 = (bf16[1,128,512]{2,1,0:T(8,128)(2,1)S(1)}, bf16[1,128,512]{2,1,0:T(8,128)(2,1)}, u32[]{:S(2)}) copy-start(bf16[1,128,512]{2,1,0:T(8,128)(2,1)} %param.18) | copy-start | bytes 393220
  22.3 8.3 %collective-permute-start.5 = (bf16[128,512]{1,0:T(8,128)(2,1)S(1)}, bf16[128,512]{1,0:T(8,128)(2,1)S(1)}, u32[]{:S(2)}, u32[]{:S(2)}) collective-permute-start(bf16[128,512]{1,0:T(8,128)(2,1)S(1)} %get-tuple-element.168), channel_id=1, source_target_pairs={{0,6},{1,7},{2,4},{3,5},{4,2},{5,3},{6,0},{7,1},{8,14},{9,15},{10,... | collective-permute-start | bytes 393224 | tf_op jit(solution)/shard_map/ppermute | solution.py:457
  26.0 11.4 %collective-permute-start.6 = (bf16[128,512]{1,0:T(8,128)(2,1)S(1)}, bf16[128,512]{1,0:T(8,128)(2,1)S(1)}, u32[]{:S(2)}, u32[]{:S(2)}) collective-permute-start(bf16[128,512]{1,0:T(8,128)(2,1)S(1)} %get-tuple-element.167), channel_id=1, source_target_pairs={{0,4},{1,5},{2,6},{3,7},{4,0},{5,1},{6,2},{7,3},{8,12},{9,13},{10,... | collective-permute-start | bytes 393224 | tf_op jit(solution)/shard_map/ppermute | solution.py:457
  26.0 22.9 %copy-start = (bf16[2,4,512,512]{3,2,1,0:T(8,128)(2,1)S(1)}, bf16[2,4,512,512]{3,2,1,0:T(8,128)(2,1)}, u32[]{:S(2)}) copy-start(bf16[2,4,512,512]{3,2,1,0:T(8,128)(2,1)} %weights.5) | copy-start | bytes 12582916
  26.0 11.4 %collective-permute-start.7 = (bf16[128,512]{1,0:T(8,128)(2,1)S(1)}, bf16[128,512]{1,0:T(8,128)(2,1)S(1)}, u32[]{:S(2)}, u32[]{:S(2)}) collective-permute-start(bf16[128,512]{1,0:T(8,128)(2,1)S(1)} %get-tuple-element.166), channel_id=1, source_target_pairs={{0,2},{1,3},{2,0},{3,1},{4,6},{5,7},{6,4},{7,5},{8,10},{9,11},{10,... | collective-permute-start | bytes 393224 | tf_op jit(solution)/shard_map/ppermute | solution.py:457
  48.9 11.0 %copy-start.4 = (bf16[1,128,512]{2,1,0:T(8,128)(2,1)S(1)}, bf16[1,128,512]{2,1,0:T(8,128)(2,1)}, u32[]{:S(2)}) copy-start(bf16[1,128,512]{2,1,0:T(8,128)(2,1)} %param.23) | copy-start | bytes 393220
  83.2 8.3 %collective-permute-start.8 = (bf16[128,512]{1,0:T(8,128)(2,1)S(1)}, bf16[128,512]{1,0:T(8,128)(2,1)S(1)}, u32[]{:S(2)}, u32[]{:S(2)}) collective-permute-start(bf16[128,512]{1,0:T(8,128)(2,1)S(1)} %shard_map.142.refs_11_.refs_7_), channel_id=1, source_target_pairs={{0,6},{1,7},{2,4},{3,5},{4,2},{5,3},{6,0},{7,1},{8,14},{9,15},{10,... | collective-permute-start | bytes 393224 | tf_op jit(solution)/shard_map/ppermute | solution.py:457
  83.9 13.2 %collective-permute-start.9 = (bf16[128,512]{1,0:T(8,128)(2,1)S(1)}, bf16[128,512]{1,0:T(8,128)(2,1)S(1)}, u32[]{:S(2)}, u32[]{:S(2)}) collective-permute-start(bf16[128,512]{1,0:T(8,128)(2,1)S(1)} %shard_map.142.refs_11_.refs_7_), channel_id=1, source_target_pairs={{0,4},{1,5},{2,6},{3,7},{4,0},{5,1},{6,2},{7,3},{8,12},{9,13},{10,... | collective-permute-start | bytes 393224 | tf_op jit(solution)/shard_map/ppermute | solution.py:457
  85.1 12.0 %collective-permute-start.10 = (bf16[128,512]{1,0:T(8,128)(2,1)S(1)}, bf16[128,512]{1,0:T(8,128)(2,1)S(1)}, u32[]{:S(2)}, u32[]{:S(2)}) collective-permute-start(bf16[128,512]{1,0:T(8,128)(2,1)S(1)} %shard_map.142.refs_11_.refs_7_), channel_id=1, source_target_pairs={{0,2},{1,3},{2,0},{3,1},{4,6},{5,7},{6,4},{7,5},{8,10},{9,11},{10,... | collective-permute-start | bytes 393224 | tf_op jit(solution)/shard_map/ppermute | solution.py:457
  87.6 10.0 %collective-permute-start.14 = (bf16[128,512]{1,0:T(8,128)(2,1)S(1)}, bf16[128,512]{1,0:T(8,128)(2,1)S(1)}, u32[]{:S(2)}, u32[]{:S(2)}) collective-permute-start(bf16[128,512]{1,0:T(8,128)(2,1)S(1)} %shard_map.142.refs_11_.refs_7_), channel_id=1, source_target_pairs={{0,1},{1,0},{2,3},{3,2},{4,5},{5,4},{6,7},{7,6},{8,9},{9,8},{10,11... | collective-permute-start | bytes 393224 | tf_op jit(solution)/shard_map/ppermute | solution.py:457
  91.5 6.1 %collective-permute-start.11 = (bf16[128,512]{1,0:T(8,128)(2,1)S(1)}, bf16[128,512]{1,0:T(8,128)(2,1)S(1)}, u32[]{:S(2)}, u32[]{:S(2)}) collective-permute-start(bf16[128,512]{1,0:T(8,128)(2,1)S(1)} %collective-permute-done.8.refs_8_.refs_4_), channel_id=1, source_target_pairs={{0,1},{1,0},{2,3},{3,2},{4,5},{5,4},{6,7},{7,6},{8,9},{9,8},{10,11... | collective-permute-start | bytes 393224 | tf_op jit(solution)/shard_map/ppermute | solution.py:457
  97.1 1.3 %collective-permute-start.12 = (bf16[128,512]{1,0:T(8,128)(2,1)S(1)}, bf16[128,512]{1,0:T(8,128)(2,1)S(1)}, u32[]{:S(2)}, u32[]{:S(2)}) collective-permute-start(bf16[128,512]{1,0:T(8,128)(2,1)S(1)} %collective-permute-done.9.refs_9_.refs_5_), channel_id=1, source_target_pairs={{0,1},{1,0},{2,3},{3,2},{4,5},{5,4},{6,7},{7,6},{8,9},{9,8},{10,11... | collective-permute-start | bytes 393224 | tf_op jit(solution)/shard_map/ppermute | solution.py:457
  97.1 1.5 %collective-permute-start.13 = (bf16[128,512]{1,0:T(8,128)(2,1)S(1)}, bf16[128,512]{1,0:T(8,128)(2,1)S(1)}, u32[]{:S(2)}, u32[]{:S(2)}) collective-permute-start(bf16[128,512]{1,0:T(8,128)(2,1)S(1)} %collective-permute-done.10.refs_10_.refs_6_), channel_id=1, source_target_pairs={{0,1},{1,0},{2,3},{3,2},{4,5},{5,4},{6,7},{7,6},{8,9},{9,8},{10,11... | collective-permute-start | bytes 393224 | tf_op jit(solution)/shard_map/ppermute | solution.py:457
  100.5 6.4 %collective-permute-start.18 = (bf16[256,256]{1,0:T(8,128)(2,1)S(1)}, bf16[256,256]{1,0:T(8,128)(2,1)S(1)}, u32[]{:S(2)}, u32[]{:S(2)}) collective-permute-start(bf16[256,256]{1,0:T(8,128)(2,1)S(1)} %get-tuple-element.135), channel_id=1, source_target_pairs={{0,16},{8,24},{16,0},{24,8},{1,17},{9,25},{17,1},{25,9},{2,18},{10... | collective-permute-start | bytes 393224 | tf_op jit(solution)/shard_map/ppermute | solution.py:457
  101.1 6.4 %collective-permute-start.17 = (bf16[256,256]{1,0:T(8,128)(2,1)S(1)}, bf16[256,256]{1,0:T(8,128)(2,1)S(1)}, u32[]{:S(2)}, u32[]{:S(2)}) collective-permute-start(bf16[256,256]{1,0:T(8,128)(2,1)S(1)} %get-tuple-element.134), channel_id=1, source_target_pairs={{0,8},{8,0},{16,24},{24,16},{1,9},{9,1},{17,25},{25,17},{2,10},{10... | collective-permute-start | bytes 393224 | tf_op jit(solution)/shard_map/ppermute | solution.py:457
  101.7 7.5 %collective-permute-start.16 = (bf16[256,256]{1,0:T(8,128)(2,1)S(1)}, bf16[256,256]{1,0:T(8,128)(2,1)S(1)}, u32[]{:S(2)}, u32[]{:S(2)}) collective-permute-start(bf16[256,256]{1,0:T(8,128)(2,1)S(1)} %get-tuple-element.133), channel_id=1, source_target_pairs={{0,16},{8,24},{16,0},{24,8},{1,17},{9,25},{17,1},{25,9},{2,18},{10... | collective-permute-start | bytes 393224 | tf_op jit(solution)/shard_map/ppermute | solution.py:457
  103.1 7.0 %collective-permute-start.15 = (bf16[256,256]{1,0:T(8,128)(2,1)S(1)}, bf16[256,256]{1,0:T(8,128)(2,1)S(1)}, u32[]{:S(2)}, u32[]{:S(2)}) collective-permute-start(bf16[256,256]{1,0:T(8,128)(2,1)S(1)} %get-tuple-element.132), channel_id=1, source_target_pairs={{0,8},{8,0},{16,24},{24,16},{1,9},{9,1},{17,25},{25,17},{2,10},{10... | collective-permute-start | bytes 393224 | tf_op jit(solution)/shard_map/ppermute | solution.py:457
  105.8 8.6 %copy-start.2 = (bf16[512,512]{1,0:T(8,128)(2,1)S(1)}, bf16[512,512]{1,0:T(8,128)(2,1)}, u32[]{:S(2)}) copy-start(bf16[512,512]{1,0:T(8,128)(2,1)} %refs_12_.1) | copy-start | bytes 1572868
  106.9 6.0 %collective-permute-start.22 = (bf16[128,256]{1,0:T(8,128)(2,1)S(1)}, bf16[128,256]{1,0:T(8,128)(2,1)S(1)}, u32[]{:S(2)}, u32[]{:S(2)}) collective-permute-start(bf16[128,256]{1,0:T(8,128)(2,1)S(1)} %add_convert_fusion), channel_id=1, source_target_pairs={{0,8},{8,0},{16,24},{24,16},{1,9},{9,1},{17,25},{25,17},{2,10},{10... | collective-permute-start | bytes 196616 | tf_op jit(solution)/shard_map/ppermute | solution.py:457
  107.5 5.3 %collective-permute-start.21 = (bf16[128,256]{1,0:T(8,128)(2,1)S(1)}, bf16[128,256]{1,0:T(8,128)(2,1)S(1)}, u32[]{:S(2)}, u32[]{:S(2)}) collective-permute-start(bf16[128,256]{1,0:T(8,128)(2,1)S(1)} %add_convert_fusion.1), channel_id=1, source_target_pairs={{0,16},{8,24},{16,0},{24,8},{1,17},{9,25},{17,1},{25,9},{2,18},{10... | collective-permute-start | bytes 196616 | tf_op jit(solution)/shard_map/ppermute | solution.py:457
  109.2 4.3 %collective-permute-start.20 = (bf16[128,256]{1,0:T(8,128)(2,1)S(1)}, bf16[128,256]{1,0:T(8,128)(2,1)S(1)}, u32[]{:S(2)}, u32[]{:S(2)}) collective-permute-start(bf16[128,256]{1,0:T(8,128)(2,1)S(1)} %add_convert_fusion.2), channel_id=1, source_target_pairs={{0,8},{8,0},{16,24},{24,16},{1,9},{9,1},{17,25},{25,17},{2,10},{10... | collective-permute-start | bytes 196616 | tf_op jit(solution)/shard_map/ppermute | solution.py:457
  110.1 4.3 %collective-permute-start.19 = (bf16[128,256]{1,0:T(8,128)(2,1)S(1)}, bf16[128,256]{1,0:T(8,128)(2,1)S(1)}, u32[]{:S(2)}, u32[]{:S(2)}) collective-permute-start(bf16[128,256]{1,0:T(8,128)(2,1)S(1)} %add_convert_fusion.3), channel_id=1, source_target_pairs={{0,16},{8,24},{16,0},{24,8},{1,17},{9,25},{17,1},{25,9},{2,18},{10... | collective-permute-start | bytes 196616 | tf_op jit(solution)/shard_map/ppermute | solution.py:457

commit v6 on v5

--- a/solution.py
+++ b/solution.py
@@ -103,18 +103,18 @@
         copy.wait()
 
 
-def index_kernel(block, parts, *refs):
-    wanted, far_weight, far_vec = refs[:2], refs[2], refs[3]
-    pick, pick_t, source, source_t, weight, vec, sends, src_row, sems = refs[4:]
-    pairs = ((wanted[0], sends), (wanted[1], src_row), (far_vec, vec), (far_weight, weight))
+def load_kernel(far_weight, far_vec, weight, vec, sems):
     copies = [
-        pltpu.make_async_copy(start, target, sems.at[i])
-        for i, (start, target) in enumerate(pairs)
+        pltpu.make_async_copy(far_vec, vec, sems.at[0]),
+        pltpu.make_async_copy(far_weight, weight, sems.at[1]),
     ]
     for copy in copies:
         copy.start()
-    for copy in copies[:2]:
+    for copy in copies:
         copy.wait()
+
+
+def index_kernel(block, parts, sends, src_row, pick, pick_t, source, source_t):
     sects, count, nodes = sends.shape
     pieces = pick.shape[0]
     at = iota((1, pieces), 1)
@@ -139,8 +139,6 @@
         rows = slice(k * block, (k + 1) * block)
         source[rows, :] = mark(ids == column[:, k : k + 1])
         source_t[:, rows] = mark(ids_t == src_row[k : k + 1, :])
-    for copy in copies[2:]:
-        copy.wait()
 
 
 def edge_data(feat, at, rows):
@@ -202,17 +200,18 @@
     add_rows(out, 0, message, spots, [before])
 
 
-def slope_kernel(spans, fanout, rows, *refs):
+def slope_kernel(spans, block, parts, fanout, rows, *refs):
     count = len(spans)
     feats = refs[:count]
-    weight, vec = refs[count : count + 2]
-    outs = refs[count + 2 :]
+    weight, vec, sends, src_row = refs[count : count + 4]
+    outs, found = refs[count + 4 : -4], refs[-4:]
     for feat, at, out in zip(feats, spans, outs):
         pre = dot(feat[at : at + rows, :], weight[...])
         turned = edge_data(feat, at, rows).T
         for k in range(fanout):
             act = pre + edge_length(turned, fanout, k) * vec[...]
             out[k * rows : (k + 1) * rows, :] = slope(act).astype(BF16)
+    index_kernel(block, parts, sends, src_row, *found)
 
 
 def halo_rows(state, pick, parts):
@@ -519,25 +518,14 @@
     fan = src_row.shape[0]
     pieces = sends.size * parts
     table_len = block + sends.size
-    pick, pick_t, source, source_t, weight, vec = call(
-        functools.partial(index_kernel, block, parts),
-        [
-            shape((pieces, parts * block), BF16),
-            shape((parts * block, pieces), BF16),
-            shape((fan * block, table_len), BF16),
-            shape((table_len, fan * block), BF16),
-            shape(enc_weight.shape, BF16),
-            shape((1, width), F32),
-        ],
+    weight, vec = call(
+        load_kernel,
+        [shape(enc_weight.shape, BF16), shape((1, width), F32)],
         [
             pltpu.with_memory_space_constraint(value, pltpu.HBM)
-            for value in (sends, src_row, enc_weight, enc_vec[None, :])
+            for value in (enc_weight, enc_vec[None, :])
         ],
-        scratch=[
-            pltpu.VMEM(sends.shape, jnp.int32),
-            pltpu.VMEM(src_row.shape, jnp.int32),
-            pltpu.SemaphoreType.DMA((4,)),
-        ],
+        scratch=[pltpu.SemaphoreType.DMA((2,))],
         space=pltpu.HBM,
     )
 
@@ -570,10 +558,12 @@
             aliases={len(args) - 1: 0} if before and not last else None,
         )
 
-    before = []
-    for units in steps[:-1]:
-        before = encode(units, False, before)
-    cross, message, spots = encode(steps[-1], True, before)
+    before = encode([unit for units in steps[:-1] for unit in units], False, [])
+    for p in range(len(axes) - 1):
+        before = encode([unit for unit in steps[-1] if unit[1] == p], False, before)
+    cross, message, spots = encode(
+        [unit for unit in steps[-1] if unit[1] == len(axes) - 1], True, before
+    )
     (keep,) = call(
         keep_kernel, [shape((half * block, width), BF16)], [message, spots, *before]
     )
@@ -585,15 +575,27 @@
     ]
 
     units = [(j, p) for j in range(sects) for p in range(len(axes))]
-    slopes = call(
+    found = call(
         functools.partial(
-            slope_kernel, tuple(where[unit][1] for unit in units), fanout, part_rows
+            slope_kernel,
+            tuple(where[unit][1] for unit in units),
+            block,
+            parts,
+            fanout,
+            part_rows,
         ),
-        [shape((fanout * part_rows, width), BF16)] * len(units),
-        [*(where[unit][0] for unit in units), weight, vec],
-    )
-    tied = lax.optimization_barrier((*arrived, *slopes))
-    arrived, slopes = tied[: half - 1], dict(zip(units, tied[half - 1 :]))
+        [shape((fanout * part_rows, width), BF16)] * len(units)
+        + [
+            shape((pieces, parts * block), BF16),
+            shape((parts * block, pieces), BF16),
+            shape((fan * block, table_len), BF16),
+            shape((table_len, fan * block), BF16),
+        ],
+        [*(where[unit][0] for unit in units), weight, vec, sends, src_row],
+    )
+    tied = lax.optimization_barrier((*arrived, *found))
+    arrived, slopes = tied[: half - 1], dict(zip(units, tied[half - 1 : -4]))
+    pick, pick_t, source, source_t = tied[-4:]
 
     halo_shape = shape((pieces, LANES), BF16)
     row_low, row_high = shape((block, width), BF16), shape((block, width), F32)

time: 116 us -> 117 us (level)
  no operation moved by 1% of the time
where the time goes in v6:
time: 117 us
  blocking collectives  39.2 us (34%)
  Pallas kernels  27.6 us (24%)
  starting transfers between devices  25.6 us (22%)
  waiting for transfers between devices  22.9 us (20%)
    all_to_all x4, blocking collectives, exchange(): return lax.all_to_all(value, both, split_axis=0, concat_axis=0, tiled=True)  39.2 us
    pallas_call x17, Pallas kernels, call(): pl.pallas_call(kernel, out_shape=list(outs), in_specs=specs, out_specs=[p...  27.6 us
    ppermute x23, starting transfers between devices, swap(): return lax.ppermute(value, axis, [(i, i ^ apart) for i in range(size)])  25.6 us
    ppermute x23, waiting for transfers between devices, swap(): return lax.ppermute(value, axis, [(i, i ^ apart) for i in range(size)])  22.9 us
  transfers between devices with their start and end apart: 23, of which 14 were waited for; matrix products, arithmetic and copies ran while one was open for 0% of the time, Pallas kernels for 12%

profile of v6, /device:TPU:0, one launch (start us, length us, event | category | flops | bytes accessed | tf_op | source)
XLA Modules:
  0.0 116.7 jit_solution(13992222867717369728)
XLA Ops:
  0.6 1.1 shard_map.131
  1.7 3.0 %collective-permute-start.2 = (bf16[144,512]{1,0:T(8,128)(2,1)S(1)}, bf16[144,512]{1,0:T(8,128)(2,1)S(1)}, u32[]{:S(2)}, u32[]{:S(2)}) collective-permute-start(bf16[144,512]{1,0:T(8,128)(2,1)S(1)} %get-tuple-element.90.refs_0_), channel_id=1, source_target_pairs={{0,8},{8,0},{16,24},{24,16},{1,9},{9,1},{17,25},{25,17},{2,10},{10... | collective-permute-start | bytes 442376 | tf_op jit(solution)/shard_map/ppermute | solution.py:456
  4.7 1.5 %collective-permute-start = (bf16[144,512]{1,0:T(8,128)(2,1)S(1)}, bf16[144,512]{1,0:T(8,128)(2,1)S(1)}, u32[]{:S(2)}, u32[]{:S(2)}) collective-permute-start(bf16[144,512]{1,0:T(8,128)(2,1)S(1)} %get-tuple-element.87.refs_1_), channel_id=1, source_target_pairs={{0,16},{8,24},{16,0},{24,8},{1,17},{9,25},{17,1},{25,9},{2,18},{10... | collective-permute-start | bytes 442376 | tf_op jit(solution)/shard_map/ppermute | solution.py:456
  6.2 2.3 %collective-permute-done.2.refs_2_ = bf16[144,512]{1,0:T(8,128)(2,1)S(1)} collective-permute-done((bf16[144,512]{1,0:T(8,128)(2,1)S(1)}, bf16[144,512]{1,0:T(8,128)(2,1)S(1)}, u32[]{:S(2)}, u32[]{:S(2)}) %collective-permute-start.2) | collective-permute-done | bytes 147488 | tf_op jit(solution)/shard_map/ppermute | solution.py:456
  8.6 1.8 %collective-permute-start.3 = (bf16[288,512]{1,0:T(8,128)(2,1)S(1)}, bf16[288,512]{1,0:T(8,128)(2,1)S(1)}, u32[]{:S(2)}, u32[]{:S(2)}) collective-permute-start(bf16[288,512]{1,0:T(8,128)(2,1)S(1)} %pad_maximum_fusion.1), channel_id=1, source_target_pairs={{0,16},{8,24},{16,0},{24,8},{1,17},{9,25},{17,1},{25,9},{2,18},{10... | collective-permute-start | bytes 884744 | tf_op jit(solution)/shard_map/ppermute | solution.py:456
  10.4 0.0 collective-permute-done.refs_3_.refs_5_
  10.4 1.6 %collective-permute-start.1 = (bf16[288,512]{1,0:T(8,128)(2,1)S(1)}, bf16[288,512]{1,0:T(8,128)(2,1)S(1)}, u32[]{:S(2)}, u32[]{:S(2)}) collective-permute-start(bf16[288,512]{1,0:T(8,128)(2,1)S(1)} %pad_maximum_fusion), channel_id=1, source_target_pairs={{0,8},{8,0},{16,24},{24,16},{1,9},{9,1},{17,25},{25,17},{2,10},{10... | collective-permute-start | bytes 884744 | tf_op jit(solution)/shard_map/ppermute | solution.py:456
  12.0 1.1 shard_map.132
  13.1 0.1 pad_add_fusion.who
  13.2 2.9 %shard_map.133.refs_4_ = f32[1024,512]{1,0:T(8,128)S(1)} custom-call(s32[2]{0:T(128)S(1)} %pad_add_fusion.who, bf16[144,512]{1,0:T(8,128)(2,1)S(1)} %get-tuple-element.90.refs_0_, bf16[144,512]{1,0:T(8,128)(2,1)S(1)} %get-tuple-element.87.refs_1_, bf16[144,512]{1,0:T(8,128)(2,1)S(1)} %collective-permute-done.2.refs_2_, ...), custom_call_target="tpu_custom_call" | custom-call | bytes 3213320 | tf_op jit(solution)/shard_map/pallas_call | solution.py:435
  16.0 0.8 collective-permute-done.3.refs_0_.refs_1_.refs_4_.refs_6_
  16.8 1.9 %shard_map.134.refs_4_.before = f32[1024,512]{1,0:T(8,128)S(1)} custom-call(s32[2]{0:T(128)S(1)} %pad_add_fusion.who, bf16[288,512]{1,0:T(8,128)(2,1)S(1)} %collective-permute-done.3.refs_0_.refs_1_.refs_4_.refs_6_, bf16[288,512]{1,0:T(8,128)(2,1)S(1)} %collective-permute-done.3.refs_0_.refs_1_.refs_4_.refs_6_, ...), custom_call_target="tpu_custom_call", output_to_operand_aliasing={{}: (5, {})} | custom-call | bytes 5310472 | tf_op jit(solution)/shard_map/pallas_call | solution.py:435
  18.8 0.0 collective-permute-done.1.refs_0_.refs_1_.refs_3_.refs_7_
  18.8 1.5 %shard_map.135 = (bf16[512,512]{1,0:T(8,128)(2,1)S(1)}, bf16[512,512]{1,0:T(8,128)(2,1)S(1)}, s32[1,512]{1,0:T(1,128)S(1)}) custom-call(s32[2]{0:T(128)S(1)} %pad_add_fusion.who, bf16[288,512]{1,0:T(8,128)(2,1)S(1)} %collective-permute-done.1.refs_0_.refs_1_.refs_3_.refs_7_, bf16[288,512]{1,0:T(8,128)(2,1)S(1)} %collective-permute-done.1.refs_0_.refs_1_.refs_3_.refs_7_, ...), custom_call_target="tpu_custom_call" | custom-call | bytes 4263944 | tf_op jit(solution)/shard_map/pallas_call | solution.py:435
  20.2 0.1 collective-permute-start.4
  20.3 0.4 shard_map.136
  20.8 0.0 copy-start.5
  20.8 0.0 copy-start.6
  20.8 1.4 %collective-permute-done.4 = bf16[512,512]{1,0:T(8,128)(2,1)S(1)} collective-permute-done((bf16[512,512]{1,0:T(8,128)(2,1)S(1)}, bf16[512,512]{1,0:T(8,128)(2,1)S(1)}, u32[]{:S(2)}, u32[]{:S(2)}) %collective-permute-start.4) | collective-permute-done | bytes 524320 | tf_op jit(solution)/shard_map/ppermute | solution.py:456
  22.2 0.2 fusion
  22.4 0.0 copy-start.1
  22.4 0.0 copy-start.3
  22.5 3.6 %collective-permute-start.5 = (bf16[128,512]{1,0:T(8,128)(2,1)S(1)}, bf16[128,512]{1,0:T(8,128)(2,1)S(1)}, u32[]{:S(2)}, u32[]{:S(2)}) collective-permute-start(bf16[128,512]{1,0:T(8,128)(2,1)S(1)} %get-tuple-element.176), channel_id=1, source_target_pairs={{0,6},{1,7},{2,4},{3,5},{4,2},{5,3},{6,0},{7,1},{8,14},{9,15},{10,... | collective-permute-start | bytes 393224 | tf_op jit(solution)/shard_map/ppermute | solution.py:456
  26.0 0.0 collective-permute-start.6
  26.1 0.9 collective-permute-start.7
  26.9 2.6 %shard_map.137 = (bf16[256,512]{1,0:T(8,128)(2,1)S(1)}, bf16[256,512]{1,0:T(8,128)(2,1)S(1)}, bf16[256,512]{1,0:T(8,128)(2,1)S(1)}, bf16[256,512]{1,0:T(8,128)(2...) custom-call(bf16[144,512]{1,0:T(8,128)(2,1)S(1)} %get-tuple-element., ...), custom_call_target="tpu_custom_call" | custom-call | bytes 5708032 | tf_op jit(solution)/shard_map/pallas_call | solution.py:435
  29.5 1.2 %collective-permute-done.5.refs_0_ = bf16[128,512]{1,0:T(8,128)(2,1)S(1)} collective-permute-done((bf16[128,512]{1,0:T(8,128)(2,1)S(1)}, bf16[128,512]{1,0:T(8,128)(2,1)S(1)}, u32[]{:S(2)}, u32[]{:S(2)}) %collective-permute-start.5) | collective-permute-done | bytes 131104 | tf_op jit(solution)/shard_map/ppermute | solution.py:456
  30.8 6.7 %collective-permute-done.6.refs_1_ = bf16[128,512]{1,0:T(8,128)(2,1)S(1)} collective-permute-done((bf16[128,512]{1,0:T(8,128)(2,1)S(1)}, bf16[128,512]{1,0:T(8,128)(2,1)S(1)}, u32[]{:S(2)}, u32[]{:S(2)}) %collective-permute-start.6) | collective-permute-done | bytes 131104 | tf_op jit(solution)/shard_map/ppermute | solution.py:456
  37.4 0.5 shard_map.138
  37.9 12.0 %all_to_all.44 = bf16[32,8,128]{2,1,0:T(8,128)(2,1)S(1)} all-to-all(bf16[32,8,128]{2,1,0:T(8,128)(2,1)S(1)} %bitcast.29), channel_id=1, replica_groups=mesh['sect'=4,'node'=8] {'sect','node'}, dimensions={0} | all-to-all | bytes 131072 | tf_op jit(solution)/shard_map/all_to_all | solution.py:604
  49.9 1.9 %shard_map.139 = (bf16[128,512]{1,0:T(8,128)(2,1)S(1)}, f32[128,512]{1,0:T(8,128)S(1)}, bf16[1024,512]{1,0:T(8,128)(2,1)S(1)}, bf16[256,128]{1,0:T(8,128)(2,1)S(1)}) custom-call(bf16[128,512]{1,0:T(8,128)(2,1)S(1)} %get-tuple-element.110.state, bf16[256,128]{1,0:T(8,128)(2,1)S(1)} %bitcast.24, bf16[1024,192]{1,0:T(8,128)(2,1)S(1)} %get-tuple-element.112.source, ...), custom_call_target="tpu_custom_call" | custom-call | bytes 6553600 | tf_op jit(solution)/shard_map/pallas_call | solution.py:435
  51.8 9.1 %all_to_all.45 = bf16[32,8,128]{2,1,0:T(8,128)(2,1)S(1)} all-to-all(bf16[32,8,128]{2,1,0:T(8,128)(2,1)S(1)} %bitcast.30), channel_id=1, replica_groups=mesh['sect'=4,'node'=8] {'sect','node'}, dimensions={0} | all-to-all | bytes 131072 | tf_op jit(solution)/shard_map/all_to_all | solution.py:604
  60.9 3.0 %shard_map.140 = (bf16[128,512]{1,0:T(8,128)(2,1)S(1)}, f32[128,512]{1,0:T(8,128)S(1)}, bf16[256,128]{1,0:T(8,128)(2,1)S(1)}) custom-call(bf16[128,512]{1,0:T(8,128)(2,1)S(1)} %get-tuple-element.113.state, bf16[256,128]{1,0:T(8,128)(2,1)S(1)} %bitcast.25, bf16[1024,192]{1,0:T(8,128)(2,1)S(1)} %get-tuple-element.112.source, ...), custom_call_target="tpu_custom_call" | custom-call | bytes 5767168 | tf_op jit(solution)/shard_map/pallas_call | solution.py:435
  63.9 9.1 %all_to_all.46 = bf16[32,8,128]{2,1,0:T(8,128)(2,1)S(1)} all-to-all(bf16[32,8,128]{2,1,0:T(8,128)(2,1)S(1)} %bitcast.32), channel_id=1, replica_groups=mesh['sect'=4,'node'=8] {'sect','node'}, dimensions={0} | all-to-all | bytes 131072 | tf_op jit(solution)/shard_map/all_to_all | solution.py:604
  73.0 1.7 %shard_map.141 = (f32[128,512]{1,0:T(8,128)S(1)}, bf16[256,128]{1,0:T(8,128)(2,1)S(1)}) custom-call(f32[128,512]{1,0:T(8,128)S(1)} %get-tuple-element.116.mine, bf16[256,128]{1,0:T(8,128)(2,1)S(1)} %bitcast.23, bf16[512,256]{1,0:T(8,128)(2,1)S(1)} %get-tuple-element.118.pick_t, f32[128,512]{1,0:T(8,128)S(1)} %get-tuple-element.119.mixed, ...), custom_call_target="tpu_custom_call" | custom-call | bytes 6815744 | tf_op jit(solution)/shard_map/pallas_call | solution.py:435
  74.6 9.1 %all_to_all.47 = bf16[32,8,128]{2,1,0:T(8,128)(2,1)S(1)} all-to-all(bf16[32,8,128]{2,1,0:T(8,128)(2,1)S(1)} %bitcast.31), channel_id=1, replica_groups=mesh['sect'=4,'node'=8] {'sect','node'}, dimensions={0} | all-to-all | bytes 131072 | tf_op jit(solution)/shard_map/all_to_all | solution.py:604
  83.7 0.5 shard_map.142.refs_11_.refs_7_
  84.2 0.8 collective-permute-start.8
  85.0 1.2 %collective-permute-start.9 = (bf16[128,512]{1,0:T(8,128)(2,1)S(1)}, bf16[128,512]{1,0:T(8,128)(2,1)S(1)}, u32[]{:S(2)}, u32[]{:S(2)}) collective-permute-start(bf16[128,512]{1,0:T(8,128)(2,1)S(1)} %shard_map.142.refs_11_.refs_7_), channel_id=1, source_target_pairs={{0,4},{1,5},{2,6},{3,7},{4,0},{5,1},{6,2},{7,3},{8,12},{9,13},{10,... | collective-permute-start | bytes 393224 | tf_op jit(solution)/shard_map/ppermute | solution.py:456
  86.2 2.5 %collective-permute-start.10 = (bf16[128,512]{1,0:T(8,128)(2,1)S(1)}, bf16[128,512]{1,0:T(8,128)(2,1)S(1)}, u32[]{:S(2)}, u32[]{:S(2)}) collective-permute-start(bf16[128,512]{1,0:T(8,128)(2,1)S(1)} %shard_map.142.refs_11_.refs_7_), channel_id=1, source_target_pairs={{0,2},{1,3},{2,0},{3,1},{4,6},{5,7},{6,4},{7,5},{8,10},{9,11},{10,... | collective-permute-start | bytes 393224 | tf_op jit(solution)/shard_map/ppermute | solution.py:456
  88.7 3.2 %shard_map.143 = (bf16[256,1024]{1,0:T(8,128)(2,1)S(1)}, bf16[256,1024]{1,0:T(8,128)(2,1)S(1)}, bf16[256,1024]{1,0:T(8,128)(2,1)S(1)}, bf16[256,1024]{1,0:T(8,12...) custom-call(s32[2]{0:T(128)S(1)} %pad_add_fusion.who, ...), custom_call_target="tpu_custom_call" | custom-call | bytes 6225928 | tf_op jit(solution)/shard_map/pallas_call | solution.py:435
  91.9 0.7 collective-permute-done.8.refs_8_.refs_4_
  92.6 5.6 %collective-permute-done.9.refs_9_.refs_5_ = bf16[128,512]{1,0:T(8,128)(2,1)S(1)} collective-permute-done((bf16[128,512]{1,0:T(8,128)(2,1)S(1)}, bf16[128,512]{1,0:T(8,128)(2,1)S(1)}, u32[]{:S(2)}, u32[]{:S(2)}) %collective-permute-start.9) | collective-permute-done | bytes 131104 | tf_op jit(solution)/shard_map/ppermute | solution.py:456
  98.1 0.5 collective-permute-start.13
  98.7 0.8 collective-permute-done.12.refs_13_.refs_9_
  99.5 0.2 collective-permute-done.13.refs_14_.refs_10_
  99.7 1.8 %shard_map.144 = (bf16[256,256]{1,0:T(8,128)(2,1)S(1)}, bf16[256,256]{1,0:T(8,128)(2,1)S(1)}, bf16[256,256]{1,0:T(8,128)(2,1)S(1)}, bf16[256,256]{1,0:T(8,128)(2,1)S(1)}) custom-call(s32[2]{0:T(128)S(1)} %pad_add_fusion.who, bf16[256,1024]{1,0:T(8,128)(2,1)S(1)} %get-tuple-element.132.refs_0_, bf16[256,1024]{1,0:T(8,128)(2,1)S(1)} %get-tuple-element.133.refs_1_, ...), custom_call_target="tpu_custom_call" | custom-call | bytes 4718600 | tf_op jit(solution)/shard_map/pallas_call | solution.py:435
  101.5 0.7 collective-permute-start.18
  102.2 0.5 collective-permute-start.17
  102.7 1.5 %collective-permute-start.16 = (bf16[256,256]{1,0:T(8,128)(2,1)S(1)}, bf16[256,256]{1,0:T(8,128)(2,1)S(1)}, u32[]{:S(2)}, u32[]{:S(2)}) collective-permute-start(bf16[256,256]{1,0:T(8,128)(2,1)S(1)} %get-tuple-element.141), channel_id=1, source_target_pairs={{0,16},{8,24},{16,0},{24,8},{1,17},{9,25},{17,1},{25,9},{2,18},{10... | collective-permute-start | bytes 393224 | tf_op jit(solution)/shard_map/ppermute | solution.py:456
  104.2 1.4 %collective-permute-start.15 = (bf16[256,256]{1,0:T(8,128)(2,1)S(1)}, bf16[256,256]{1,0:T(8,128)(2,1)S(1)}, u32[]{:S(2)}, u32[]{:S(2)}) collective-permute-start(bf16[256,256]{1,0:T(8,128)(2,1)S(1)} %get-tuple-element.140), channel_id=1, source_target_pairs={{0,8},{8,0},{16,24},{24,16},{1,9},{9,1},{17,25},{25,17},{2,10},{10... | collective-permute-start | bytes 393224 | tf_op jit(solution)/shard_map/ppermute | solution.py:456
  105.6 1.3 %shard_map.145 = (f32[128,256]{1,0:T(8,128)S(1)}, f32[128,256]{1,0:T(8,128)S(1)}, f32[128,256]{1,0:T(8,128)S(1)}, f32[128,256]{1,0:T(8,128)S(1)}) custom-call(s32[2]{0:T(128)S(1)} %pad_add_fusion.who, bf16[256,1024]{1,0:T(8,128)(2,1)S(1)} %get-tuple-element.152.refs_0_, bf16[256,1024]{1,0:T(8,128)(2,1)S(1)} %get-tuple-element.153.refs_1_, ...), custom_call_target="tpu_custom_call" | custom-call | bytes 3145736 | tf_op jit(solution)/shard_map/pallas_call | solution.py:435
  106.9 0.0 copy-start.2
  106.9 1.0 collective-permute-done.18.refs_7_
  107.9 0.7 collective-permute-start.22
  108.6 1.4 %collective-permute-start.21 = (bf16[128,256]{1,0:T(8,128)(2,1)S(1)}, bf16[128,256]{1,0:T(8,128)(2,1)S(1)}, u32[]{:S(2)}, u32[]{:S(2)}) collective-permute-start(bf16[128,256]{1,0:T(8,128)(2,1)S(1)} %add_convert_fusion.1), channel_id=1, source_target_pairs={{0,16},{8,24},{16,0},{24,8},{1,17},{9,25},{17,1},{25,9},{2,18},{10... | collective-permute-start | bytes 196616 | tf_op jit(solution)/shard_map/ppermute | solution.py:456
  110.0 0.2 collective-permute-done.16.refs_5_
  110.2 0.6 collective-permute-start.20
  110.8 0.4 collective-permute-done.15.refs_4_
  111.2 1.5 %collective-permute-start.19 = (bf16[128,256]{1,0:T(8,128)(2,1)S(1)}, bf16[128,256]{1,0:T(8,128)(2,1)S(1)}, u32[]{:S(2)}, u32[]{:S(2)}) collective-permute-start(bf16[128,256]{1,0:T(8,128)(2,1)S(1)} %add_convert_fusion.3), channel_id=1, source_target_pairs={{0,16},{8,24},{16,0},{24,8},{1,17},{9,25},{17,1},{25,9},{2,18},{10... | collective-permute-start | bytes 196616 | tf_op jit(solution)/shard_map/ppermute | solution.py:456
  112.6 1.3 %shard_map.146 = (f32[128,256]{1,0:T(8,128)S(1)}, f32[128,256]{1,0:T(8,128)S(1)}, f32[128,256]{1,0:T(8,128)S(1)}, f32[128,256]{1,0:T(8,128)S(1)}) custom-call(s32[2]{0:T(128)S(1)} %pad_add_fusion.who, bf16[256,1024]{1,0:T(8,128)(2,1)S(1)} %get-tuple-element.127.refs_0_, bf16[256,1024]{1,0:T(8,128)(2,1)S(1)} %get-tuple-element.128.refs_1_, ...), custom_call_target="tpu_custom_call" | custom-call | bytes 3145736 | tf_op jit(solution)/shard_map/pallas_call | solution.py:435
  113.9 0.7 collective-permute-done.20.refs_9_
  114.6 0.9 collective-permute-done.19.refs_8_
  115.5 1.2 %shard_map.147 = bf16[256,512]{1,0:T(8,128)(2,1)} custom-call(f32[128,256]{1,0:T(8,128)S(1)} %get-tuple-element.168.refs_0_, f32[128,256]{1,0:T(8,128)S(1)} %get-tuple-element.169.refs_1_, f32[128,256]{1,0:T(8,128)S(1)} %get-tuple-element.170.refs_2_, f32[128,256]{1,0:T(8,128)S(1)} %get-tuple-element.171.refs_3_, ...), custom_call_target="tpu_custom_call" | custom-call | bytes 2097152 | tf_op jit(solution)/shard_map/pallas_call | solution.py:435
  (27 shorter events, 0.2 us)
Async XLA Ops:
  1.7 6.9 %collective-permute-start.2 = (bf16[144,512]{1,0:T(8,128)(2,1)S(1)}, bf16[144,512]{1,0:T(8,128)(2,1)S(1)}, u32[]{:S(2)}, u32[]{:S(2)}) collective-permute-start(bf16[144,512]{1,0:T(8,128)(2,1)S(1)} %get-tuple-element.90.refs_0_), channel_id=1, source_target_pairs={{0,8},{8,0},{16,24},{24,16},{1,9},{9,1},{17,25},{25,17},{2,10},{10... | collective-permute-start | bytes 442376 | tf_op jit(solution)/shard_map/ppermute | solution.py:456
  4.7 5.7 %collective-permute-start = (bf16[144,512]{1,0:T(8,128)(2,1)S(1)}, bf16[144,512]{1,0:T(8,128)(2,1)S(1)}, u32[]{:S(2)}, u32[]{:S(2)}) collective-permute-start(bf16[144,512]{1,0:T(8,128)(2,1)S(1)} %get-tuple-element.87.refs_1_), channel_id=1, source_target_pairs={{0,16},{8,24},{16,0},{24,8},{1,17},{9,25},{17,1},{25,9},{2,18},{10... | collective-permute-start | bytes 442376 | tf_op jit(solution)/shard_map/ppermute | solution.py:456
  8.6 8.3 %collective-permute-start.3 = (bf16[288,512]{1,0:T(8,128)(2,1)S(1)}, bf16[288,512]{1,0:T(8,128)(2,1)S(1)}, u32[]{:S(2)}, u32[]{:S(2)}) collective-permute-start(bf16[288,512]{1,0:T(8,128)(2,1)S(1)} %pad_maximum_fusion.1), channel_id=1, source_target_pairs={{0,16},{8,24},{16,0},{24,8},{1,17},{9,25},{17,1},{25,9},{2,18},{10... | collective-permute-start | bytes 884744 | tf_op jit(solution)/shard_map/ppermute | solution.py:456
  10.4 8.3 %collective-permute-start.1 = (bf16[288,512]{1,0:T(8,128)(2,1)S(1)}, bf16[288,512]{1,0:T(8,128)(2,1)S(1)}, u32[]{:S(2)}, u32[]{:S(2)}) collective-permute-start(bf16[288,512]{1,0:T(8,128)(2,1)S(1)} %pad_maximum_fusion), channel_id=1, source_target_pairs={{0,8},{8,0},{16,24},{24,16},{1,9},{9,1},{17,25},{25,17},{2,10},{10... | collective-permute-start | bytes 884744 | tf_op jit(solution)/shard_map/ppermute | solution.py:456
  20.2 2.0 %collective-permute-start.4 = (bf16[512,512]{1,0:T(8,128)(2,1)S(1)}, bf16[512,512]{1,0:T(8,128)(2,1)S(1)}, u32[]{:S(2)}, u32[]{:S(2)}) collective-permute-start(bf16[512,512]{1,0:T(8,128)(2,1)S(1)} %get-tuple-element.93), channel_id=1, source_target_pairs={{0,1},{1,0},{2,3},{3,2},{4,5},{5,4},{6,7},{7,6},{8,9},{9,8},{10,11... | collective-permute-start | bytes 1572872 | tf_op jit(solution)/shard_map/ppermute | solution.py:456
  20.8 6.2 %copy-start.5 = (s32[1,1,4,8,2]{3,4,2,1,0:T(2,128)S(1)}, s32[1,1,4,8,2]{3,4,2,1,0:T(2,128)}, u32[]{:S(2)}) copy-start(s32[1,1,4,8,2]{3,4,2,1,0:T(2,128)} %param.20) | copy-start | bytes 772
  20.8 6.1 %copy-start.6 = (s32[1,128,8]{1,2,0:T(8,128)S(1)}, s32[1,128,8]{1,2,0:T(8,128)}, u32[]{:S(2)}) copy-start(s32[1,128,8]{1,2,0:T(8,128)} %param.21) | copy-start | bytes 12292
  22.4 15.1 %copy-start.1 = (bf16[512,512]{1,0:T(8,128)(2,1)S(1)}, bf16[512,512]{1,0:T(8,128)(2,1)}, u32[]{:S(2)}) copy-start(bf16[512,512]{1,0:T(8,128)(2,1)} %weight.1) | copy-start | bytes 1572868
  22.4 15.0 %copy-start.3 = (bf16[1,128,512]{2,1,0:T(8,128)(2,1)S(1)}, bf16[1,128,512]{2,1,0:T(8,128)(2,1)}, u32[]{:S(2)}) copy-start(bf16[1,128,512]{2,1,0:T(8,128)(2,1)} %param.18) | copy-start | bytes 393220
  22.5 8.3 %collective-permute-start.5 = (bf16[128,512]{1,0:T(8,128)(2,1)S(1)}, bf16[128,512]{1,0:T(8,128)(2,1)S(1)}, u32[]{:S(2)}, u32[]{:S(2)}) collective-permute-start(bf16[128,512]{1,0:T(8,128)(2,1)S(1)} %get-tuple-element.176), channel_id=1, source_target_pairs={{0,6},{1,7},{2,4},{3,5},{4,2},{5,3},{6,0},{7,1},{8,14},{9,15},{10,... | collective-permute-start | bytes 393224 | tf_op jit(solution)/shard_map/ppermute | solution.py:456
  26.0 11.4 %collective-permute-start.6 = (bf16[128,512]{1,0:T(8,128)(2,1)S(1)}, bf16[128,512]{1,0:T(8,128)(2,1)S(1)}, u32[]{:S(2)}, u32[]{:S(2)}) collective-permute-start(bf16[128,512]{1,0:T(8,128)(2,1)S(1)} %get-tuple-element.175), channel_id=1, source_target_pairs={{0,4},{1,5},{2,6},{3,7},{4,0},{5,1},{6,2},{7,3},{8,12},{9,13},{10,... | collective-permute-start | bytes 393224 | tf_op jit(solution)/shard_map/ppermute | solution.py:456
  26.1 11.4 %collective-permute-start.7 = (bf16[128,512]{1,0:T(8,128)(2,1)S(1)}, bf16[128,512]{1,0:T(8,128)(2,1)S(1)}, u32[]{:S(2)}, u32[]{:S(2)}) collective-permute-start(bf16[128,512]{1,0:T(8,128)(2,1)S(1)} %get-tuple-element.174), channel_id=1, source_target_pairs={{0,2},{1,3},{2,0},{3,1},{4,6},{5,7},{6,4},{7,5},{8,10},{9,11},{10,... | collective-permute-start | bytes 393224 | tf_op jit(solution)/shard_map/ppermute | solution.py:456
  26.9 23.0 %copy-start = (bf16[2,4,512,512]{3,2,1,0:T(8,128)(2,1)S(1)}, bf16[2,4,512,512]{3,2,1,0:T(8,128)(2,1)}, u32[]{:S(2)}) copy-start(bf16[2,4,512,512]{3,2,1,0:T(8,128)(2,1)} %weights.5) | copy-start | bytes 12582916
  49.9 11.0 %copy-start.4 = (bf16[1,128,512]{2,1,0:T(8,128)(2,1)S(1)}, bf16[1,128,512]{2,1,0:T(8,128)(2,1)}, u32[]{:S(2)}) copy-start(bf16[1,128,512]{2,1,0:T(8,128)(2,1)} %param.23) | copy-start | bytes 393220
  84.2 8.3 %collective-permute-start.8 = (bf16[128,512]{1,0:T(8,128)(2,1)S(1)}, bf16[128,512]{1,0:T(8,128)(2,1)S(1)}, u32[]{:S(2)}, u32[]{:S(2)}) collective-permute-start(bf16[128,512]{1,0:T(8,128)(2,1)S(1)} %shard_map.142.refs_11_.refs_7_), channel_id=1, source_target_pairs={{0,6},{1,7},{2,4},{3,5},{4,2},{5,3},{6,0},{7,1},{8,14},{9,15},{10,... | collective-permute-start | bytes 393224 | tf_op jit(solution)/shard_map/ppermute | solution.py:456
  85.0 13.2 %collective-permute-start.9 = (bf16[128,512]{1,0:T(8,128)(2,1)S(1)}, bf16[128,512]{1,0:T(8,128)(2,1)S(1)}, u32[]{:S(2)}, u32[]{:S(2)}) collective-permute-start(bf16[128,512]{1,0:T(8,128)(2,1)S(1)} %shard_map.142.refs_11_.refs_7_), channel_id=1, source_target_pairs={{0,4},{1,5},{2,6},{3,7},{4,0},{5,1},{6,2},{7,3},{8,12},{9,13},{10,... | collective-permute-start | bytes 393224 | tf_op jit(solution)/shard_map/ppermute | solution.py:456
  86.2 12.0 %collective-permute-start.10 = (bf16[128,512]{1,0:T(8,128)(2,1)S(1)}, bf16[128,512]{1,0:T(8,128)(2,1)S(1)}, u32[]{:S(2)}, u32[]{:S(2)}) collective-permute-start(bf16[128,512]{1,0:T(8,128)(2,1)S(1)} %shard_map.142.refs_11_.refs_7_), channel_id=1, source_target_pairs={{0,2},{1,3},{2,0},{3,1},{4,6},{5,7},{6,4},{7,5},{8,10},{9,11},{10,... | collective-permute-start | bytes 393224 | tf_op jit(solution)/shard_map/ppermute | solution.py:456
  88.7 10.0 %collective-permute-start.14 = (bf16[128,512]{1,0:T(8,128)(2,1)S(1)}, bf16[128,512]{1,0:T(8,128)(2,1)S(1)}, u32[]{:S(2)}, u32[]{:S(2)}) collective-permute-start(bf16[128,512]{1,0:T(8,128)(2,1)S(1)} %shard_map.142.refs_11_.refs_7_), channel_id=1, source_target_pairs={{0,1},{1,0},{2,3},{3,2},{4,5},{5,4},{6,7},{7,6},{8,9},{9,8},{10,11... | collective-permute-start | bytes 393224 | tf_op jit(solution)/shard_map/ppermute | solution.py:456
  92.6 6.1 %collective-permute-start.11 = (bf16[128,512]{1,0:T(8,128)(2,1)S(1)}, bf16[128,512]{1,0:T(8,128)(2,1)S(1)}, u32[]{:S(2)}, u32[]{:S(2)}) collective-permute-start(bf16[128,512]{1,0:T(8,128)(2,1)S(1)} %collective-permute-done.8.refs_8_.refs_4_), channel_id=1, source_target_pairs={{0,1},{1,0},{2,3},{3,2},{4,5},{5,4},{6,7},{7,6},{8,9},{9,8},{10,11... | collective-permute-start | bytes 393224 | tf_op jit(solution)/shard_map/ppermute | solution.py:456
  98.1 1.3 %collective-permute-start.12 = (bf16[128,512]{1,0:T(8,128)(2,1)S(1)}, bf16[128,512]{1,0:T(8,128)(2,1)S(1)}, u32[]{:S(2)}, u32[]{:S(2)}) collective-permute-start(bf16[128,512]{1,0:T(8,128)(2,1)S(1)} %collective-permute-done.9.refs_9_.refs_5_), channel_id=1, source_target_pairs={{0,1},{1,0},{2,3},{3,2},{4,5},{5,4},{6,7},{7,6},{8,9},{9,8},{10,11... | collective-permute-start | bytes 393224 | tf_op jit(solution)/shard_map/ppermute | solution.py:456
  98.1 1.5 %collective-permute-start.13 = (bf16[128,512]{1,0:T(8,128)(2,1)S(1)}, bf16[128,512]{1,0:T(8,128)(2,1)S(1)}, u32[]{:S(2)}, u32[]{:S(2)}) collective-permute-start(bf16[128,512]{1,0:T(8,128)(2,1)S(1)} %collective-permute-done.10.refs_10_.refs_6_), channel_id=1, source_target_pairs={{0,1},{1,0},{2,3},{3,2},{4,5},{5,4},{6,7},{7,6},{8,9},{9,8},{10,11... | collective-permute-start | bytes 393224 | tf_op jit(solution)/shard_map/ppermute | solution.py:456
  101.5 6.4 %collective-permute-start.18 = (bf16[256,256]{1,0:T(8,128)(2,1)S(1)}, bf16[256,256]{1,0:T(8,128)(2,1)S(1)}, u32[]{:S(2)}, u32[]{:S(2)}) collective-permute-start(bf16[256,256]{1,0:T(8,128)(2,1)S(1)} %get-tuple-element.143), channel_id=1, source_target_pairs={{0,16},{8,24},{16,0},{24,8},{1,17},{9,25},{17,1},{25,9},{2,18},{10... | collective-permute-start | bytes 393224 | tf_op jit(solution)/shard_map/ppermute | solution.py:456
  102.2 6.4 %collective-permute-start.17 = (bf16[256,256]{1,0:T(8,128)(2,1)S(1)}, bf16[256,256]{1,0:T(8,128)(2,1)S(1)}, u32[]{:S(2)}, u32[]{:S(2)}) collective-permute-start(bf16[256,256]{1,0:T(8,128)(2,1)S(1)} %get-tuple-element.142), channel_id=1, source_target_pairs={{0,8},{8,0},{16,24},{24,16},{1,9},{9,1},{17,25},{25,17},{2,10},{10... | collective-permute-start | bytes 393224 | tf_op jit(solution)/shard_map/ppermute | solution.py:456
  102.7 7.5 %collective-permute-start.16 = (bf16[256,256]{1,0:T(8,128)(2,1)S(1)}, bf16[256,256]{1,0:T(8,128)(2,1)S(1)}, u32[]{:S(2)}, u32[]{:S(2)}) collective-permute-start(bf16[256,256]{1,0:T(8,128)(2,1)S(1)} %get-tuple-element.141), channel_id=1, source_target_pairs={{0,16},{8,24},{16,0},{24,8},{1,17},{9,25},{17,1},{25,9},{2,18},{10... | collective-permute-start | bytes 393224 | tf_op jit(solution)/shard_map/ppermute | solution.py:456
  104.2 7.0 %collective-permute-start.15 = (bf16[256,256]{1,0:T(8,128)(2,1)S(1)}, bf16[256,256]{1,0:T(8,128)(2,1)S(1)}, u32[]{:S(2)}, u32[]{:S(2)}) collective-permute-start(bf16[256,256]{1,0:T(8,128)(2,1)S(1)} %get-tuple-element.140), channel_id=1, source_target_pairs={{0,8},{8,0},{16,24},{24,16},{1,9},{9,1},{17,25},{25,17},{2,10},{10... | collective-permute-start | bytes 393224 | tf_op jit(solution)/shard_map/ppermute | solution.py:456
  106.9 8.6 %copy-start.2 = (bf16[512,512]{1,0:T(8,128)(2,1)S(1)}, bf16[512,512]{1,0:T(8,128)(2,1)}, u32[]{:S(2)}) copy-start(bf16[512,512]{1,0:T(8,128)(2,1)} %refs_12_.1) | copy-start | bytes 1572868
  107.9 6.0 %collective-permute-start.22 = (bf16[128,256]{1,0:T(8,128)(2,1)S(1)}, bf16[128,256]{1,0:T(8,128)(2,1)S(1)}, u32[]{:S(2)}, u32[]{:S(2)}) collective-permute-start(bf16[128,256]{1,0:T(8,128)(2,1)S(1)} %add_convert_fusion), channel_id=1, source_target_pairs={{0,8},{8,0},{16,24},{24,16},{1,9},{9,1},{17,25},{25,17},{2,10},{10... | collective-permute-start | bytes 196616 | tf_op jit(solution)/shard_map/ppermute | solution.py:456
  108.6 5.3 %collective-permute-start.21 = (bf16[128,256]{1,0:T(8,128)(2,1)S(1)}, bf16[128,256]{1,0:T(8,128)(2,1)S(1)}, u32[]{:S(2)}, u32[]{:S(2)}) collective-permute-start(bf16[128,256]{1,0:T(8,128)(2,1)S(1)} %add_convert_fusion.1), channel_id=1, source_target_pairs={{0,16},{8,24},{16,0},{24,8},{1,17},{9,25},{17,1},{25,9},{2,18},{10... | collective-permute-start | bytes 196616 | tf_op jit(solution)/shard_map/ppermute | solution.py:456
  110.2 4.3 %collective-permute-start.20 = (bf16[128,256]{1,0:T(8,128)(2,1)S(1)}, bf16[128,256]{1,0:T(8,128)(2,1)S(1)}, u32[]{:S(2)}, u32[]{:S(2)}) collective-permute-start(bf16[128,256]{1,0:T(8,128)(2,1)S(1)} %add_convert_fusion.2), channel_id=1, source_target_pairs={{0,8},{8,0},{16,24},{24,16},{1,9},{9,1},{17,25},{25,17},{2,10},{10... | collective-permute-start | bytes 196616 | tf_op jit(solution)/shard_map/ppermute | solution.py:456
  111.2 4.3 %collective-permute-start.19 = (bf16[128,256]{1,0:T(8,128)(2,1)S(1)}, bf16[128,256]{1,0:T(8,128)(2,1)S(1)}, u32[]{:S(2)}, u32[]{:S(2)}) collective-permute-start(bf16[128,256]{1,0:T(8,128)(2,1)S(1)} %add_convert_fusion.3), channel_id=1, source_target_pairs={{0,16},{8,24},{16,0},{24,8},{1,17},{9,25},{17,1},{25,9},{2,18},{10... | collective-permute-start | bytes 196616 | tf_op jit(solution)/shard_map/ppermute | solution.py:456

commit v7 on v5

--- a/solution.py
+++ b/solution.py
@@ -12,6 +12,7 @@
 BF16 = jnp.bfloat16
 LANES = 128
 META_ROWS = 16
+HALO_ROWS = 2
 CHUNKS = 2
 MIB = 1024 * 1024
 
@@ -120,12 +121,12 @@
     at = iota((1, pieces), 1)
     part, row = at % parts, at // parts
     peer = row // count
-    whose = mark(iota((nodes, pieces), 0) == peer % nodes)
+    whose = mark(iota((nodes, pieces), 0) == peer // sects)
     place = jnp.zeros((1, pieces), F32)
     for t in range(sects):
         found = dot(sends[t].astype(F32).astype(BF16), whose)
         for c in range(count):
-            here = jnp.logical_and(peer // nodes == t, row % count == c)
+            here = jnp.logical_and(peer % sects == t, row % count == c)
             place = place + jnp.where(here, found[c : c + 1], 0.0)
     place = place + (part * block).astype(F32)
     pick_t[...] = mark(iota((parts * block, pieces), 0) == place.astype(jnp.int32))
@@ -222,23 +223,29 @@
     return dot(pick, stacked).astype(BF16)
 
 
-def join_pieces(pieces, parts):
+def piece_of(row, part, parts, sects, per):
+    count = HALO_ROWS
+    node, which = row % per // count, row % count
+    return ((node * sects + row // per) * count + which) * parts + part
+
+
+def join_pieces(pieces, parts, sects):
     count = pieces.shape[0]
     rows = count // parts
     at = iota((count, count), 0)
-    onehot = mark(iota((count, count), 1) == at % rows * parts + at // rows)
-    found = dot(onehot, pieces).astype(BF16)
+    wanted = piece_of(at % rows, at // rows, parts, sects, rows // sects)
+    found = dot(mark(iota((count, count), 1) == wanted), pieces).astype(BF16)
     return jnp.concatenate([found[i * rows : (i + 1) * rows] for i in range(parts)], axis=1)
 
 
-def cut_pieces(rows, parts):
+def cut_pieces(rows, parts, sects):
     each, count = rows.shape[0], rows.shape[0] * parts
-    at = iota((count, count), 0)
-    onehot = mark(iota((count, count), 1) == at % parts * each + at // parts)
+    at = iota((count, count), 1)
+    wanted = piece_of(at % each, at // each, parts, sects, each // sects)
     stacked = jnp.concatenate(
         [rows[:, i * LANES : (i + 1) * LANES] for i in range(parts)], axis=0
     )
-    return dot(onehot, stacked).astype(BF16)
+    return dot(mark(iota((count, count), 0) == wanted), stacked).astype(BF16)
 
 
 def add_pieces(pieces, pick_t, block, parts):
@@ -258,9 +265,9 @@
     halo[...] = halo_rows(new, pick[...], parts)
 
 
-def layer_forward(state, pieces, source, weights, parts):
+def layer_forward(state, pieces, source, weights, parts, sects):
     block = state.shape[0]
-    halo = join_pieces(pieces, parts)
+    halo = join_pieces(pieces, parts, sects)
     table = jnp.concatenate([state, halo], axis=0)
     from_src = 0.5 * dot(table, weights(0))
     to_dst = 0.5 * dot(state, weights(1))
@@ -300,12 +307,12 @@
 
 
 def first_kernel(
-    layer, parts, state, pieces, source, weights, pick, new, mixed, slopes, halo
+    layer, parts, sects, state, pieces, source, weights, pick, new, mixed, slopes, halo
 ):
     block = state.shape[0]
     own = state[...]
     used = layer_weights(weights, layer)
-    value, found = layer_forward(own, pieces[...], source, used, parts)
+    value, found = layer_forward(own, pieces[...], source, used, parts, sects)
     mixed[...] = value
     for k, part in enumerate(found):
         slopes[k * block : (k + 1) * block, :] = part
@@ -316,21 +323,22 @@
 
 
 def last_kernel(
-    layer, parts, state, pieces, source, source_t, weights, cot, out, grad_own, grad_halo
+    layer, parts, sects, state, pieces, source, source_t, weights, cot, out, grad_own, grad_halo
 ):
     own = state[...]
     used = layer_weights(weights, layer)
-    value, found = layer_forward(own, pieces[...], source, used, parts)
+    value, found = layer_forward(own, pieces[...], source, used, parts, sects)
     normed, _ = norm_parts(value)
     out[...] = (own.astype(F32) + silu(normed)).astype(BF16)
     mine, sent = layer_back(cot[...].astype(F32), value, found, source_t, used)
     grad_own[...] = mine
-    grad_halo[...] = cut_pieces(sent.astype(BF16), parts)
+    grad_halo[...] = cut_pieces(sent.astype(BF16), parts, sects)
 
 
 def back_kernel(
     layer,
     parts,
+    sects,
     mine,
     returned,
     pick_t,
@@ -348,7 +356,7 @@
     used = layer_weights(weights, layer)
     own, sent = layer_back(grad, mixed[...], found, source_t, used)
     grad_own[...] = own
-    grad_halo[...] = cut_pieces(sent.astype(BF16), parts)
+    grad_halo[...] = cut_pieces(sent.astype(BF16), parts, sects)
 
 
 def mesh_back_kernel(parts, mine, returned, pick_t, mesh_pre, weight, out):
@@ -477,7 +485,8 @@
     grid_rows, fanout = edge_len.shape
     block = mesh_init.shape[1]
     parts = width // LANES
-    both = ("sect", "node")
+    both = ("node", "sect")
+    assert halo_send.shape[-1] == HALO_ROWS
     who = jnp.stack([lax.axis_index("sect"), lax.axis_index("node")]).astype(jnp.int32)
 
     axes = [1 << i for i in range(sects.bit_length() - 1)]
@@ -608,17 +617,17 @@
     )
     assert proc_weight.shape[0] == 2
     state, mixed, slope_first, halo = call(
-        functools.partial(first_kernel, 0, parts),
+        functools.partial(first_kernel, 0, parts, sects),
         [row_low, row_high, shape((fan * block, width), BF16), halo_shape],
         [state, exchange(halo), source, proc_weight, pick],
     )
     mesh_out, grad, halo = call(
-        functools.partial(last_kernel, 1, parts),
+        functools.partial(last_kernel, 1, parts, sects),
         [row_low, row_high, halo_shape],
         [state, exchange(halo), source, source_t, proc_weight, cot[0]],
     )
     grad, halo = call(
-        functools.partial(back_kernel, 0, parts),
+        functools.partial(back_kernel, 0, parts, sects),
         [row_high, halo_shape],
         [grad, exchange(halo), pick_t, mixed, slope_first, source_t, proc_weight],
     )

time: 116 us -> 116 us (level)
  no operation moved by 1% of the time
where the time goes in v7:
time: 116 us
  blocking collectives  38.7 us (33%)
  Pallas kernels  27.5 us (24%)
  starting transfers between devices  25.9 us (22%)
  waiting for transfers between devices  22.5 us (19%)
    all_to_all x4, blocking collectives, exchange(): return lax.all_to_all(value, both, split_axis=0, concat_axis=0, tiled=True)  38.7 us
    pallas_call x17, Pallas kernels, call(): pl.pallas_call(kernel, out_shape=list(outs), in_specs=specs, out_specs=[p...  27.5 us
    ppermute x23, starting transfers between devices, swap(): return lax.ppermute(value, axis, [(i, i ^ apart) for i in range(size)])  25.9 us
    ppermute x23, waiting for transfers between devices, swap(): return lax.ppermute(value, axis, [(i, i ^ apart) for i in range(size)])  22.5 us
  transfers between devices with their start and end apart: 23, of which 14 were waited for; matrix products, arithmetic and copies ran while one was open for 0% of the time, Pallas kernels for 12%

profile of v7, /device:TPU:0, one launch (start us, length us, event | category | flops | bytes accessed | tf_op | source)
XLA Modules:
  0.0 115.9 jit_solution(11852411087517464850)
XLA Ops:
  0.6 1.1 shard_map.131
  1.7 3.0 %collective-permute-start.2 = (bf16[144,512]{1,0:T(8,128)(2,1)S(1)}, bf16[144,512]{1,0:T(8,128)(2,1)S(1)}, u32[]{:S(2)}, u32[]{:S(2)}) collective-permute-start(bf16[144,512]{1,0:T(8,128)(2,1)S(1)} %get-tuple-element.84.refs_1_), channel_id=1, source_target_pairs={{0,16},{8,24},{16,0},{24,8},{1,17},{9,25},{17,1},{25,9},{2,18},{10... | collective-permute-start | bytes 442376 | tf_op jit(solution)/shard_map/ppermute | solution.py:465
  4.7 1.5 %collective-permute-start = (bf16[144,512]{1,0:T(8,128)(2,1)S(1)}, bf16[144,512]{1,0:T(8,128)(2,1)S(1)}, u32[]{:S(2)}, u32[]{:S(2)}) collective-permute-start(bf16[144,512]{1,0:T(8,128)(2,1)S(1)} %get-tuple-element.83.refs_0_), channel_id=1, source_target_pairs={{0,8},{8,0},{16,24},{24,16},{1,9},{9,1},{17,25},{25,17},{2,10},{10... | collective-permute-start | bytes 442376 | tf_op jit(solution)/shard_map/ppermute | solution.py:465
  6.2 2.4 %collective-permute-done.2.refs_1_.refs_5_ = bf16[144,512]{1,0:T(8,128)(2,1)S(1)} collective-permute-done((bf16[144,512]{1,0:T(8,128)(2,1)S(1)}, bf16[144,512]{1,0:T(8,128)(2,1)S(1)}, u32[]{:S(2)}, u32[]{:S(2)}) %collective-permute-start.2) | collective-permute-done | bytes 147488 | tf_op jit(solution)/shard_map/ppermute | solution.py:465
  8.6 1.8 %collective-permute-start.3 = (bf16[288,512]{1,0:T(8,128)(2,1)S(1)}, bf16[288,512]{1,0:T(8,128)(2,1)S(1)}, u32[]{:S(2)}, u32[]{:S(2)}) collective-permute-start(bf16[288,512]{1,0:T(8,128)(2,1)S(1)} %pad_maximum_fusion.1), channel_id=1, source_target_pairs={{0,8},{8,0},{16,24},{24,16},{1,9},{9,1},{17,25},{25,17},{2,10},{10... | collective-permute-start | bytes 884744 | tf_op jit(solution)/shard_map/ppermute | solution.py:465
  10.4 0.0 collective-permute-done.refs_0_.refs_2_
  10.4 1.6 %collective-permute-start.1 = (bf16[288,512]{1,0:T(8,128)(2,1)S(1)}, bf16[288,512]{1,0:T(8,128)(2,1)S(1)}, u32[]{:S(2)}, u32[]{:S(2)}) collective-permute-start(bf16[288,512]{1,0:T(8,128)(2,1)S(1)} %pad_maximum_fusion), channel_id=1, source_target_pairs={{0,16},{8,24},{16,0},{24,8},{1,17},{9,25},{17,1},{25,9},{2,18},{10... | collective-permute-start | bytes 884744 | tf_op jit(solution)/shard_map/ppermute | solution.py:465
  12.0 1.5 %shard_map.132 = (bf16[256,512]{1,0:T(8,128)(2,1)S(1)}, bf16[512,256]{1,0:T(8,128)(2,1)S(1)}, bf16[1024,192]{1,0:T(8,128)(2,1)S(1)}, bf16[192,1024]{1,0:T(8,128)...) custom-call(s32[4,2,8]{2,1,0:T(2,128)} %bitcast.33, s32[8,128]{1,0:T(8,128)} %bitcast.34, ...), custom_call_target="tpu_custom_call" | custom-call | bytes 2367744 | tf_op jit(solution)/shard_map/pallas_call | solution.py:444
  13.5 0.1 pad_add_fusion.who
  13.6 1.9 %shard_map.133.refs_4_ = f32[1024,512]{1,0:T(8,128)S(1)} custom-call(s32[2]{0:T(128)S(1)} %pad_add_fusion.who, bf16[144,512]{1,0:T(8,128)(2,1)S(1)} %get-tuple-element.83.refs_0_, bf16[144,512]{1,0:T(8,128)(2,1)S(1)} %get-tuple-element.84.refs_1_, bf16[512,512]{1,0:T(8,128)(2,1)S(1)} %get-tuple-element.85.refs_2_.refs_4_.refs_8_, ...), custom_call_target="tpu_custom_call" | custom-call | bytes 2918408 | tf_op jit(solution)/shard_map/pallas_call | solution.py:444
  15.5 1.9 %shard_map.134.refs_6_.before = f32[1024,512]{1,0:T(8,128)S(1)} custom-call(s32[2]{0:T(128)S(1)} %pad_add_fusion.who, bf16[144,512]{1,0:T(8,128)(2,1)S(1)} %collective-permute-done.refs_0_.refs_2_, bf16[144,512]{1,0:T(8,128)(2,1)S(1)} %collective-permute-done.2.refs_1_.refs_5_, ...), custom_call_target="tpu_custom_call", output_to_operand_aliasing={{}: (5, {})} | custom-call | bytes 5015560 | tf_op jit(solution)/shard_map/pallas_call | solution.py:444
  17.4 0.7 collective-permute-done.1.refs_0_.refs_1_.refs_4_.refs_6_
  18.1 2.0 %shard_map.135 = (bf16[512,512]{1,0:T(8,128)(2,1)S(1)}, bf16[1024,512]{1,0:T(8,128)(2,1)S(1)}, s32[1,1024]{1,0:T(1,128)S(1)}) custom-call(s32[2]{0:T(128)S(1)} %pad_add_fusion.who, bf16[288,512]{1,0:T(8,128)(2,1)S(1)} %collective-permute-done.1.refs_0_.refs_1_.refs_4_.refs_6_, bf16[288,512]{1,0:T(8,128)(2,1)S(1)} %collective-permute-done.1.refs_0_.refs_1_.refs_4_.refs_6_, ...), custom_call_target="tpu_custom_call" | custom-call | bytes 5380104 | tf_op jit(solution)/shard_map/pallas_call | solution.py:444
  20.1 0.1 collective-permute-start.4
  20.2 0.7 shard_map.136
  20.9 1.2 %collective-permute-done.4 = bf16[512,512]{1,0:T(8,128)(2,1)S(1)} collective-permute-done((bf16[512,512]{1,0:T(8,128)(2,1)S(1)}, bf16[512,512]{1,0:T(8,128)(2,1)S(1)}, u32[]{:S(2)}, u32[]{:S(2)}) %collective-permute-start.4) | collective-permute-done | bytes 524320 | tf_op jit(solution)/shard_map/ppermute | solution.py:465
  22.1 0.2 fusion
  22.3 0.0 copy-start.1
  22.3 0.0 copy-start.3
  22.3 3.7 %collective-permute-start.5 = (bf16[128,512]{1,0:T(8,128)(2,1)S(1)}, bf16[128,512]{1,0:T(8,128)(2,1)S(1)}, u32[]{:S(2)}, u32[]{:S(2)}) collective-permute-start(bf16[128,512]{1,0:T(8,128)(2,1)S(1)} %get-tuple-element.168), channel_id=1, source_target_pairs={{0,6},{1,7},{2,4},{3,5},{4,2},{5,3},{6,0},{7,1},{8,14},{9,15},{10,... | collective-permute-start | bytes 393224 | tf_op jit(solution)/shard_map/ppermute | solution.py:465
  26.0 0.0 collective-permute-start.6
  26.0 0.8 collective-permute-start.7
  26.8 2.3 %shard_map.137 = (bf16[256,512]{1,0:T(8,128)(2,1)S(1)}, bf16[256,512]{1,0:T(8,128)(2,1)S(1)}, bf16[256,512]{1,0:T(8,128)(2,1)S(1)}, bf16[256,512]{1,0:T(8,128)(2...) custom-call(bf16[144,512]{1,0:T(8,128)(2,1)S(1)} %get-tuple-element., ...), custom_call_target="tpu_custom_call" | custom-call | bytes 4392960 | tf_op jit(solution)/shard_map/pallas_call | solution.py:444
  29.1 1.5 %collective-permute-done.5.refs_0_ = bf16[128,512]{1,0:T(8,128)(2,1)S(1)} collective-permute-done((bf16[128,512]{1,0:T(8,128)(2,1)S(1)}, bf16[128,512]{1,0:T(8,128)(2,1)S(1)}, u32[]{:S(2)}, u32[]{:S(2)}) %collective-permute-start.5) | collective-permute-done | bytes 131104 | tf_op jit(solution)/shard_map/ppermute | solution.py:465
  30.6 6.7 %collective-permute-done.6.refs_1_ = bf16[128,512]{1,0:T(8,128)(2,1)S(1)} collective-permute-done((bf16[128,512]{1,0:T(8,128)(2,1)S(1)}, bf16[128,512]{1,0:T(8,128)(2,1)S(1)}, u32[]{:S(2)}, u32[]{:S(2)}) %collective-permute-start.6) | collective-permute-done | bytes 131104 | tf_op jit(solution)/shard_map/ppermute | solution.py:465
  37.4 0.0 collective-permute-done.7.refs_2_
  37.4 0.5 shard_map.138
  37.8 11.1 %all_to_all.44 = bf16[32,8,128]{2,1,0:T(8,128)(2,1)S(1)} all-to-all(bf16[32,8,128]{2,1,0:T(8,128)(2,1)S(1)} %bitcast.29), channel_id=1, replica_groups=mesh['sect'=4,'node'=8] {'node','sect'}, dimensions={0} | all-to-all | bytes 131072 | tf_op jit(solution)/shard_map/all_to_all | solution.py:611
  49.0 1.9 %shard_map.139 = (bf16[128,512]{1,0:T(8,128)(2,1)S(1)}, f32[128,512]{1,0:T(8,128)S(1)}, bf16[1024,512]{1,0:T(8,128)(2,1)S(1)}, bf16[256,128]{1,0:T(8,128)(2,1)S(1)}) custom-call(bf16[128,512]{1,0:T(8,128)(2,1)S(1)} %get-tuple-element.102.state, bf16[256,128]{1,0:T(8,128)(2,1)S(1)} %bitcast.24, bf16[1024,192]{1,0:T(8,128)(2,1)S(1)} %get-tuple-element.104.source, ...), custom_call_target="tpu_custom_call" | custom-call | bytes 6553600 | tf_op jit(solution)/shard_map/pallas_call | solution.py:444
  50.9 9.2 %all_to_all.45 = bf16[32,8,128]{2,1,0:T(8,128)(2,1)S(1)} all-to-all(bf16[32,8,128]{2,1,0:T(8,128)(2,1)S(1)} %bitcast.30), channel_id=1, replica_groups=mesh['sect'=4,'node'=8] {'node','sect'}, dimensions={0} | all-to-all | bytes 131072 | tf_op jit(solution)/shard_map/all_to_all | solution.py:611
  60.1 3.0 %shard_map.140 = (bf16[128,512]{1,0:T(8,128)(2,1)S(1)}, f32[128,512]{1,0:T(8,128)S(1)}, bf16[256,128]{1,0:T(8,128)(2,1)S(1)}) custom-call(bf16[128,512]{1,0:T(8,128)(2,1)S(1)} %get-tuple-element.105.state, bf16[256,128]{1,0:T(8,128)(2,1)S(1)} %bitcast.25, bf16[1024,192]{1,0:T(8,128)(2,1)S(1)} %get-tuple-element.104.source, ...), custom_call_target="tpu_custom_call" | custom-call | bytes 5767168 | tf_op jit(solution)/shard_map/pallas_call | solution.py:444
  63.0 9.2 %all_to_all.46 = bf16[32,8,128]{2,1,0:T(8,128)(2,1)S(1)} all-to-all(bf16[32,8,128]{2,1,0:T(8,128)(2,1)S(1)} %bitcast.32), channel_id=1, replica_groups=mesh['sect'=4,'node'=8] {'node','sect'}, dimensions={0} | all-to-all | bytes 131072 | tf_op jit(solution)/shard_map/all_to_all | solution.py:611
  72.2 1.7 %shard_map.141 = (f32[128,512]{1,0:T(8,128)S(1)}, bf16[256,128]{1,0:T(8,128)(2,1)S(1)}) custom-call(f32[128,512]{1,0:T(8,128)S(1)} %get-tuple-element.108.mine, bf16[256,128]{1,0:T(8,128)(2,1)S(1)} %bitcast.23, bf16[512,256]{1,0:T(8,128)(2,1)S(1)} %get-tuple-element.110.pick_t, f32[128,512]{1,0:T(8,128)S(1)} %get-tuple-element.111.mixed, ...), custom_call_target="tpu_custom_call" | custom-call | bytes 6815744 | tf_op jit(solution)/shard_map/pallas_call | solution.py:444
  73.9 9.2 %all_to_all.47 = bf16[32,8,128]{2,1,0:T(8,128)(2,1)S(1)} all-to-all(bf16[32,8,128]{2,1,0:T(8,128)(2,1)S(1)} %bitcast.31), channel_id=1, replica_groups=mesh['sect'=4,'node'=8] {'node','sect'}, dimensions={0} | all-to-all | bytes 131072 | tf_op jit(solution)/shard_map/all_to_all | solution.py:611
  83.1 0.5 shard_map.142.refs_11_.refs_7_
  83.6 0.9 collective-permute-start.8
  84.5 1.3 %collective-permute-start.9 = (bf16[128,512]{1,0:T(8,128)(2,1)S(1)}, bf16[128,512]{1,0:T(8,128)(2,1)S(1)}, u32[]{:S(2)}, u32[]{:S(2)}) collective-permute-start(bf16[128,512]{1,0:T(8,128)(2,1)S(1)} %shard_map.142.refs_11_.refs_7_), channel_id=1, source_target_pairs={{0,4},{1,5},{2,6},{3,7},{4,0},{5,1},{6,2},{7,3},{8,12},{9,13},{10,... | collective-permute-start | bytes 393224 | tf_op jit(solution)/shard_map/ppermute | solution.py:465
  85.7 2.3 %collective-permute-start.10 = (bf16[128,512]{1,0:T(8,128)(2,1)S(1)}, bf16[128,512]{1,0:T(8,128)(2,1)S(1)}, u32[]{:S(2)}, u32[]{:S(2)}) collective-permute-start(bf16[128,512]{1,0:T(8,128)(2,1)S(1)} %shard_map.142.refs_11_.refs_7_), channel_id=1, source_target_pairs={{0,2},{1,3},{2,0},{3,1},{4,6},{5,7},{6,4},{7,5},{8,10},{9,11},{10,... | collective-permute-start | bytes 393224 | tf_op jit(solution)/shard_map/ppermute | solution.py:465
  88.0 0.0 collective-permute-start.14
  88.1 3.2 %shard_map.143 = (bf16[256,1024]{1,0:T(8,128)(2,1)S(1)}, bf16[256,1024]{1,0:T(8,128)(2,1)S(1)}, bf16[256,1024]{1,0:T(8,128)(2,1)S(1)}, bf16[256,1024]{1,0:T(8,12...) custom-call(s32[2]{0:T(128)S(1)} %pad_add_fusion.who, ...), custom_call_target="tpu_custom_call" | custom-call | bytes 6225928 | tf_op jit(solution)/shard_map/pallas_call | solution.py:444
  91.2 0.7 collective-permute-done.8.refs_8_.refs_4_
  91.9 0.0 collective-permute-start.11
  91.9 5.2 %collective-permute-done.9.refs_9_.refs_5_ = bf16[128,512]{1,0:T(8,128)(2,1)S(1)} collective-permute-done((bf16[128,512]{1,0:T(8,128)(2,1)S(1)}, bf16[128,512]{1,0:T(8,128)(2,1)S(1)}, u32[]{:S(2)}, u32[]{:S(2)}) %collective-permute-start.9) | collective-permute-done | bytes 131104 | tf_op jit(solution)/shard_map/ppermute | solution.py:465
  97.1 0.5 collective-permute-start.13
  97.6 0.8 collective-permute-done.12.refs_13_.refs_9_
  98.5 0.2 collective-permute-done.13.refs_14_.refs_10_
  98.6 1.8 %shard_map.144 = (bf16[256,256]{1,0:T(8,128)(2,1)S(1)}, bf16[256,256]{1,0:T(8,128)(2,1)S(1)}, bf16[256,256]{1,0:T(8,128)(2,1)S(1)}, bf16[256,256]{1,0:T(8,128)(2,1)S(1)}) custom-call(s32[2]{0:T(128)S(1)} %pad_add_fusion.who, bf16[256,1024]{1,0:T(8,128)(2,1)S(1)} %get-tuple-element.124.refs_0_, bf16[256,1024]{1,0:T(8,128)(2,1)S(1)} %get-tuple-element.125.refs_1_, ...), custom_call_target="tpu_custom_call" | custom-call | bytes 4718600 | tf_op jit(solution)/shard_map/pallas_call | solution.py:444
  100.5 0.9 collective-permute-start.18
  101.4 0.8 collective-permute-start.17
  102.2 1.4 %collective-permute-start.16 = (bf16[256,256]{1,0:T(8,128)(2,1)S(1)}, bf16[256,256]{1,0:T(8,128)(2,1)S(1)}, u32[]{:S(2)}, u32[]{:S(2)}) collective-permute-start(bf16[256,256]{1,0:T(8,128)(2,1)S(1)} %get-tuple-element.133), channel_id=1, source_target_pairs={{0,16},{8,24},{16,0},{24,8},{1,17},{9,25},{17,1},{25,9},{2,18},{10... | collective-permute-start | bytes 393224 | tf_op jit(solution)/shard_map/ppermute | solution.py:465
  103.5 1.0 collective-permute-start.15
  104.6 1.3 %shard_map.145 = (f32[128,256]{1,0:T(8,128)S(1)}, f32[128,256]{1,0:T(8,128)S(1)}, f32[128,256]{1,0:T(8,128)S(1)}, f32[128,256]{1,0:T(8,128)S(1)}) custom-call(s32[2]{0:T(128)S(1)} %pad_add_fusion.who, bf16[256,1024]{1,0:T(8,128)(2,1)S(1)} %get-tuple-element.144.refs_0_, bf16[256,1024]{1,0:T(8,128)(2,1)S(1)} %get-tuple-element.145.refs_1_, ...), custom_call_target="tpu_custom_call" | custom-call | bytes 3145736 | tf_op jit(solution)/shard_map/pallas_call | solution.py:444
  105.9 0.0 copy-start.2
  105.9 1.0 collective-permute-done.18.refs_7_
  106.9 1.0 collective-permute-start.22
  107.9 1.1 collective-permute-start.21
  109.0 0.1 collective-permute-done.16.refs_5_
  109.1 1.0 collective-permute-start.20
  110.1 0.2 collective-permute-done.15.refs_4_
  110.4 1.2 %collective-permute-start.19 = (bf16[128,256]{1,0:T(8,128)(2,1)S(1)}, bf16[128,256]{1,0:T(8,128)(2,1)S(1)}, u32[]{:S(2)}, u32[]{:S(2)}) collective-permute-start(bf16[128,256]{1,0:T(8,128)(2,1)S(1)} %add_convert_fusion.3), channel_id=1, source_target_pairs={{0,16},{8,24},{16,0},{24,8},{1,17},{9,25},{17,1},{25,9},{2,18},{10... | collective-permute-start | bytes 196616 | tf_op jit(solution)/shard_map/ppermute | solution.py:465
  111.6 1.3 %shard_map.146 = (f32[128,256]{1,0:T(8,128)S(1)}, f32[128,256]{1,0:T(8,128)S(1)}, f32[128,256]{1,0:T(8,128)S(1)}, f32[128,256]{1,0:T(8,128)S(1)}) custom-call(s32[2]{0:T(128)S(1)} %pad_add_fusion.who, bf16[256,1024]{1,0:T(8,128)(2,1)S(1)} %get-tuple-element.119.refs_0_, bf16[256,1024]{1,0:T(8,128)(2,1)S(1)} %get-tuple-element.120.refs_1_, ...), custom_call_target="tpu_custom_call" | custom-call | bytes 3145736 | tf_op jit(solution)/shard_map/pallas_call | solution.py:444
  112.9 0.5 collective-permute-done.20.refs_9_
  113.4 1.3 %collective-permute-done.19.refs_8_ = bf16[128,256]{1,0:T(8,128)(2,1)S(1)} collective-permute-done((bf16[128,256]{1,0:T(8,128)(2,1)S(1)}, bf16[128,256]{1,0:T(8,128)(2,1)S(1)}, u32[]{:S(2)}, u32[]{:S(2)}) %collective-permute-start.19) | collective-permute-done | bytes 65568 | tf_op jit(solution)/shard_map/ppermute | solution.py:465
  114.7 1.2 %shard_map.147 = bf16[256,512]{1,0:T(8,128)(2,1)} custom-call(f32[128,256]{1,0:T(8,128)S(1)} %get-tuple-element.160.refs_0_, f32[128,256]{1,0:T(8,128)S(1)} %get-tuple-element.161.refs_1_, f32[128,256]{1,0:T(8,128)S(1)} %get-tuple-element.162.refs_2_, f32[128,256]{1,0:T(8,128)S(1)} %get-tuple-element.163.refs_3_, ...), custom_call_target="tpu_custom_call" | custom-call | bytes 2097152 | tf_op jit(solution)/shard_map/pallas_call | solution.py:444
  (23 shorter events, 0.2 us)
Async XLA Ops:
  1.7 6.9 %collective-permute-start.2 = (bf16[144,512]{1,0:T(8,128)(2,1)S(1)}, bf16[144,512]{1,0:T(8,128)(2,1)S(1)}, u32[]{:S(2)}, u32[]{:S(2)}) collective-permute-start(bf16[144,512]{1,0:T(8,128)(2,1)S(1)} %get-tuple-element.84.refs_1_), channel_id=1, source_target_pairs={{0,16},{8,24},{16,0},{24,8},{1,17},{9,25},{17,1},{25,9},{2,18},{10... | collective-permute-start | bytes 442376 | tf_op jit(solution)/shard_map/ppermute | solution.py:465
  4.7 5.7 %collective-permute-start = (bf16[144,512]{1,0:T(8,128)(2,1)S(1)}, bf16[144,512]{1,0:T(8,128)(2,1)S(1)}, u32[]{:S(2)}, u32[]{:S(2)}) collective-permute-start(bf16[144,512]{1,0:T(8,128)(2,1)S(1)} %get-tuple-element.83.refs_0_), channel_id=1, source_target_pairs={{0,8},{8,0},{16,24},{24,16},{1,9},{9,1},{17,25},{25,17},{2,10},{10... | collective-permute-start | bytes 442376 | tf_op jit(solution)/shard_map/ppermute | solution.py:465
  8.6 8.8 %collective-permute-start.3 = (bf16[288,512]{1,0:T(8,128)(2,1)S(1)}, bf16[288,512]{1,0:T(8,128)(2,1)S(1)}, u32[]{:S(2)}, u32[]{:S(2)}) collective-permute-start(bf16[288,512]{1,0:T(8,128)(2,1)S(1)} %pad_maximum_fusion.1), channel_id=1, source_target_pairs={{0,8},{8,0},{16,24},{24,16},{1,9},{9,1},{17,25},{25,17},{2,10},{10... | collective-permute-start | bytes 884744 | tf_op jit(solution)/shard_map/ppermute | solution.py:465
  10.4 7.7 %collective-permute-start.1 = (bf16[288,512]{1,0:T(8,128)(2,1)S(1)}, bf16[288,512]{1,0:T(8,128)(2,1)S(1)}, u32[]{:S(2)}, u32[]{:S(2)}) collective-permute-start(bf16[288,512]{1,0:T(8,128)(2,1)S(1)} %pad_maximum_fusion), channel_id=1, source_target_pairs={{0,16},{8,24},{16,0},{24,8},{1,17},{9,25},{17,1},{25,9},{2,18},{10... | collective-permute-start | bytes 884744 | tf_op jit(solution)/shard_map/ppermute | solution.py:465
  20.1 2.0 %collective-permute-start.4 = (bf16[512,512]{1,0:T(8,128)(2,1)S(1)}, bf16[512,512]{1,0:T(8,128)(2,1)S(1)}, u32[]{:S(2)}, u32[]{:S(2)}) collective-permute-start(bf16[512,512]{1,0:T(8,128)(2,1)S(1)} %get-tuple-element.89), channel_id=1, source_target_pairs={{0,1},{1,0},{2,3},{3,2},{4,5},{5,4},{6,7},{7,6},{8,9},{9,8},{10,11... | collective-permute-start | bytes 1572872 | tf_op jit(solution)/shard_map/ppermute | solution.py:465
  22.3 15.1 %copy-start.1 = (bf16[512,512]{1,0:T(8,128)(2,1)S(1)}, bf16[512,512]{1,0:T(8,128)(2,1)}, u32[]{:S(2)}) copy-start(bf16[512,512]{1,0:T(8,128)(2,1)} %weight.1) | copy-start | bytes 1572868
  22.3 15.1 %copy-start.3 = (bf16[1,128,512]{2,1,0:T(8,128)(2,1)S(1)}, bf16[1,128,512]{2,1,0:T(8,128)(2,1)}, u32[]{:S(2)}) copy-start(bf16[1,128,512]{2,1,0:T(8,128)(2,1)} %param.18) | copy-start | bytes 393220
  22.3 8.3 %collective-permute-start.5 = (bf16[128,512]{1,0:T(8,128)(2,1)S(1)}, bf16[128,512]{1,0:T(8,128)(2,1)S(1)}, u32[]{:S(2)}, u32[]{:S(2)}) collective-permute-start(bf16[128,512]{1,0:T(8,128)(2,1)S(1)} %get-tuple-element.168), channel_id=1, source_target_pairs={{0,6},{1,7},{2,4},{3,5},{4,2},{5,3},{6,0},{7,1},{8,14},{9,15},{10,... | collective-permute-start | bytes 393224 | tf_op jit(solution)/shard_map/ppermute | solution.py:465
  26.0 11.4 %collective-permute-start.6 = (bf16[128,512]{1,0:T(8,128)(2,1)S(1)}, bf16[128,512]{1,0:T(8,128)(2,1)S(1)}, u32[]{:S(2)}, u32[]{:S(2)}) collective-permute-start(bf16[128,512]{1,0:T(8,128)(2,1)S(1)} %get-tuple-element.167), channel_id=1, source_target_pairs={{0,4},{1,5},{2,6},{3,7},{4,0},{5,1},{6,2},{7,3},{8,12},{9,13},{10,... | collective-permute-start | bytes 393224 | tf_op jit(solution)/shard_map/ppermute | solution.py:465
  26.0 23.0 %copy-start = (bf16[2,4,512,512]{3,2,1,0:T(8,128)(2,1)S(1)}, bf16[2,4,512,512]{3,2,1,0:T(8,128)(2,1)}, u32[]{:S(2)}) copy-start(bf16[2,4,512,512]{3,2,1,0:T(8,128)(2,1)} %weights.5) | copy-start | bytes 12582916
  26.0 11.4 %collective-permute-start.7 = (bf16[128,512]{1,0:T(8,128)(2,1)S(1)}, bf16[128,512]{1,0:T(8,128)(2,1)S(1)}, u32[]{:S(2)}, u32[]{:S(2)}) collective-permute-start(bf16[128,512]{1,0:T(8,128)(2,1)S(1)} %get-tuple-element.166), channel_id=1, source_target_pairs={{0,2},{1,3},{2,0},{3,1},{4,6},{5,7},{6,4},{7,5},{8,10},{9,11},{10,... | collective-permute-start | bytes 393224 | tf_op jit(solution)/shard_map/ppermute | solution.py:465
  49.0 11.1 %copy-start.4 = (bf16[1,128,512]{2,1,0:T(8,128)(2,1)S(1)}, bf16[1,128,512]{2,1,0:T(8,128)(2,1)}, u32[]{:S(2)}) copy-start(bf16[1,128,512]{2,1,0:T(8,128)(2,1)} %param.23) | copy-start | bytes 393220
  83.6 8.3 %collective-permute-start.8 = (bf16[128,512]{1,0:T(8,128)(2,1)S(1)}, bf16[128,512]{1,0:T(8,128)(2,1)S(1)}, u32[]{:S(2)}, u32[]{:S(2)}) collective-permute-start(bf16[128,512]{1,0:T(8,128)(2,1)S(1)} %shard_map.142.refs_11_.refs_7_), channel_id=1, source_target_pairs={{0,6},{1,7},{2,4},{3,5},{4,2},{5,3},{6,0},{7,1},{8,14},{9,15},{10,... | collective-permute-start | bytes 393224 | tf_op jit(solution)/shard_map/ppermute | solution.py:465
  84.5 12.6 %collective-permute-start.9 = (bf16[128,512]{1,0:T(8,128)(2,1)S(1)}, bf16[128,512]{1,0:T(8,128)(2,1)S(1)}, u32[]{:S(2)}, u32[]{:S(2)}) collective-permute-start(bf16[128,512]{1,0:T(8,128)(2,1)S(1)} %shard_map.142.refs_11_.refs_7_), channel_id=1, source_target_pairs={{0,4},{1,5},{2,6},{3,7},{4,0},{5,1},{6,2},{7,3},{8,12},{9,13},{10,... | collective-permute-start | bytes 393224 | tf_op jit(solution)/shard_map/ppermute | solution.py:465
  85.7 11.4 %collective-permute-start.10 = (bf16[128,512]{1,0:T(8,128)(2,1)S(1)}, bf16[128,512]{1,0:T(8,128)(2,1)S(1)}, u32[]{:S(2)}, u32[]{:S(2)}) collective-permute-start(bf16[128,512]{1,0:T(8,128)(2,1)S(1)} %shard_map.142.refs_11_.refs_7_), channel_id=1, source_target_pairs={{0,2},{1,3},{2,0},{3,1},{4,6},{5,7},{6,4},{7,5},{8,10},{9,11},{10,... | collective-permute-start | bytes 393224 | tf_op jit(solution)/shard_map/ppermute | solution.py:465
  88.0 9.6 %collective-permute-start.14 = (bf16[128,512]{1,0:T(8,128)(2,1)S(1)}, bf16[128,512]{1,0:T(8,128)(2,1)S(1)}, u32[]{:S(2)}, u32[]{:S(2)}) collective-permute-start(bf16[128,512]{1,0:T(8,128)(2,1)S(1)} %shard_map.142.refs_11_.refs_7_), channel_id=1, source_target_pairs={{0,1},{1,0},{2,3},{3,2},{4,5},{5,4},{6,7},{7,6},{8,9},{9,8},{10,11... | collective-permute-start | bytes 393224 | tf_op jit(solution)/shard_map/ppermute | solution.py:465
  91.9 5.7 %collective-permute-start.11 = (bf16[128,512]{1,0:T(8,128)(2,1)S(1)}, bf16[128,512]{1,0:T(8,128)(2,1)S(1)}, u32[]{:S(2)}, u32[]{:S(2)}) collective-permute-start(bf16[128,512]{1,0:T(8,128)(2,1)S(1)} %collective-permute-done.8.refs_8_.refs_4_), channel_id=1, source_target_pairs={{0,1},{1,0},{2,3},{3,2},{4,5},{5,4},{6,7},{7,6},{8,9},{9,8},{10,11... | collective-permute-start | bytes 393224 | tf_op jit(solution)/shard_map/ppermute | solution.py:465
  97.1 1.3 %collective-permute-start.12 = (bf16[128,512]{1,0:T(8,128)(2,1)S(1)}, bf16[128,512]{1,0:T(8,128)(2,1)S(1)}, u32[]{:S(2)}, u32[]{:S(2)}) collective-permute-start(bf16[128,512]{1,0:T(8,128)(2,1)S(1)} %collective-permute-done.9.refs_9_.refs_5_), channel_id=1, source_target_pairs={{0,1},{1,0},{2,3},{3,2},{4,5},{5,4},{6,7},{7,6},{8,9},{9,8},{10,11... | collective-permute-start | bytes 393224 | tf_op jit(solution)/shard_map/ppermute | solution.py:465
  97.1 1.5 %collective-permute-start.13 = (bf16[128,512]{1,0:T(8,128)(2,1)S(1)}, bf16[128,512]{1,0:T(8,128)(2,1)S(1)}, u32[]{:S(2)}, u32[]{:S(2)}) collective-permute-start(bf16[128,512]{1,0:T(8,128)(2,1)S(1)} %collective-permute-done.10.refs_10_.refs_6_), channel_id=1, source_target_pairs={{0,1},{1,0},{2,3},{3,2},{4,5},{5,4},{6,7},{7,6},{8,9},{9,8},{10,11... | collective-permute-start | bytes 393224 | tf_op jit(solution)/shard_map/ppermute | solution.py:465
  100.5 6.4 %collective-permute-start.18 = (bf16[256,256]{1,0:T(8,128)(2,1)S(1)}, bf16[256,256]{1,0:T(8,128)(2,1)S(1)}, u32[]{:S(2)}, u32[]{:S(2)}) collective-permute-start(bf16[256,256]{1,0:T(8,128)(2,1)S(1)} %get-tuple-element.135), channel_id=1, source_target_pairs={{0,16},{8,24},{16,0},{24,8},{1,17},{9,25},{17,1},{25,9},{2,18},{10... | collective-permute-start | bytes 393224 | tf_op jit(solution)/shard_map/ppermute | solution.py:465
  101.4 6.5 %collective-permute-start.17 = (bf16[256,256]{1,0:T(8,128)(2,1)S(1)}, bf16[256,256]{1,0:T(8,128)(2,1)S(1)}, u32[]{:S(2)}, u32[]{:S(2)}) collective-permute-start(bf16[256,256]{1,0:T(8,128)(2,1)S(1)} %get-tuple-element.134), channel_id=1, source_target_pairs={{0,8},{8,0},{16,24},{24,16},{1,9},{9,1},{17,25},{25,17},{2,10},{10... | collective-permute-start | bytes 393224 | tf_op jit(solution)/shard_map/ppermute | solution.py:465
  102.2 6.9 %collective-permute-start.16 = (bf16[256,256]{1,0:T(8,128)(2,1)S(1)}, bf16[256,256]{1,0:T(8,128)(2,1)S(1)}, u32[]{:S(2)}, u32[]{:S(2)}) collective-permute-start(bf16[256,256]{1,0:T(8,128)(2,1)S(1)} %get-tuple-element.133), channel_id=1, source_target_pairs={{0,16},{8,24},{16,0},{24,8},{1,17},{9,25},{17,1},{25,9},{2,18},{10... | collective-permute-start | bytes 393224 | tf_op jit(solution)/shard_map/ppermute | solution.py:465
  103.5 6.8 %collective-permute-start.15 = (bf16[256,256]{1,0:T(8,128)(2,1)S(1)}, bf16[256,256]{1,0:T(8,128)(2,1)S(1)}, u32[]{:S(2)}, u32[]{:S(2)}) collective-permute-start(bf16[256,256]{1,0:T(8,128)(2,1)S(1)} %get-tuple-element.132), channel_id=1, source_target_pairs={{0,8},{8,0},{16,24},{24,16},{1,9},{9,1},{17,25},{25,17},{2,10},{10... | collective-permute-start | bytes 393224 | tf_op jit(solution)/shard_map/ppermute | solution.py:465
  105.9 8.9 %copy-start.2 = (bf16[512,512]{1,0:T(8,128)(2,1)S(1)}, bf16[512,512]{1,0:T(8,128)(2,1)}, u32[]{:S(2)}) copy-start(bf16[512,512]{1,0:T(8,128)(2,1)} %refs_12_.1) | copy-start | bytes 1572868
  106.9 6.0 %collective-permute-start.22 = (bf16[128,256]{1,0:T(8,128)(2,1)S(1)}, bf16[128,256]{1,0:T(8,128)(2,1)S(1)}, u32[]{:S(2)}, u32[]{:S(2)}) collective-permute-start(bf16[128,256]{1,0:T(8,128)(2,1)S(1)} %add_convert_fusion), channel_id=1, source_target_pairs={{0,8},{8,0},{16,24},{24,16},{1,9},{9,1},{17,25},{25,17},{2,10},{10... | collective-permute-start | bytes 196616 | tf_op jit(solution)/shard_map/ppermute | solution.py:465
  107.9 5.0 %collective-permute-start.21 = (bf16[128,256]{1,0:T(8,128)(2,1)S(1)}, bf16[128,256]{1,0:T(8,128)(2,1)S(1)}, u32[]{:S(2)}, u32[]{:S(2)}) collective-permute-start(bf16[128,256]{1,0:T(8,128)(2,1)S(1)} %add_convert_fusion.1), channel_id=1, source_target_pairs={{0,16},{8,24},{16,0},{24,8},{1,17},{9,25},{17,1},{25,9},{2,18},{10... | collective-permute-start | bytes 196616 | tf_op jit(solution)/shard_map/ppermute | solution.py:465
  109.1 4.3 %collective-permute-start.20 = (bf16[128,256]{1,0:T(8,128)(2,1)S(1)}, bf16[128,256]{1,0:T(8,128)(2,1)S(1)}, u32[]{:S(2)}, u32[]{:S(2)}) collective-permute-start(bf16[128,256]{1,0:T(8,128)(2,1)S(1)} %add_convert_fusion.2), channel_id=1, source_target_pairs={{0,8},{8,0},{16,24},{24,16},{1,9},{9,1},{17,25},{25,17},{2,10},{10... | collective-permute-start | bytes 196616 | tf_op jit(solution)/shard_map/ppermute | solution.py:465
  110.4 4.3 %collective-permute-start.19 = (bf16[128,256]{1,0:T(8,128)(2,1)S(1)}, bf16[128,256]{1,0:T(8,128)(2,1)S(1)}, u32[]{:S(2)}, u32[]{:S(2)}) collective-permute-start(bf16[128,256]{1,0:T(8,128)(2,1)S(1)} %add_convert_fusion.3), channel_id=1, source_target_pairs={{0,16},{8,24},{16,0},{24,8},{1,17},{9,25},{17,1},{25,9},{2,18},{10... | collective-permute-start | bytes 196616 | tf_op jit(solution)/shard_map/ppermute | solution.py:465

commit v8 on v5

--- a/solution.py
+++ b/solution.py
@@ -580,9 +580,9 @@
 
     pair = keep.astype(F32) + swap(cross, "node", 1).astype(F32)
     pair = pair.reshape(half, block, width)
-    arrived = [
-        swap(pair[q].astype(BF16), "node", 2 * q) for q in reversed(range(1, half))
-    ]
+    turns = sorted(range(1, half), key=lambda q: (q.bit_length() == 1, -q))
+    turns = turns[1:2] + turns[:1] + turns[2:]
+    arrived = [swap(pair[q].astype(BF16), "node", 2 * q) for q in turns]
 
     units = [(j, p) for j in range(sects) for p in range(len(axes))]
     slopes = call(

time: 116 us -> 116 us (level)
  blocking collectives: 38.3 us -> 39.8 us
  waiting for transfers between devices: 22.9 us -> 21.6 us
    all_to_all x4, blocking collectives: 38.3 us -> 39.8 us  [exchange(): return lax.all_to_all(value, both, split_axis=0, concat_axis=0, tiled=True)]
    ppermute x23, waiting for transfers between devices: 22.9 us -> 21.6 us  [swap(): return lax.ppermute(value, axis, [(i, i ^ apart) for i in range(size)])]
where the time goes in v8:
time: 116 us
  blocking collectives  39.8 us (34%)
  Pallas kernels  27.5 us (24%)
  starting transfers between devices  25.4 us (22%)
  waiting for transfers between devices  21.6 us (19%)
    all_to_all x4, blocking collectives, exchange(): return lax.all_to_all(value, both, split_axis=0, concat_axis=0, tiled=True)  39.8 us
    pallas_call x17, Pallas kernels, call(): pl.pallas_call(kernel, out_shape=list(outs), in_specs=specs, out_specs=[p...  27.5 us
    ppermute x23, starting transfers between devices, swap(): return lax.ppermute(value, axis, [(i, i ^ apart) for i in range(size)])  25.4 us
    ppermute x23, waiting for transfers between devices, swap(): return lax.ppermute(value, axis, [(i, i ^ apart) for i in range(size)])  21.6 us
  transfers between devices with their start and end apart: 23, of which 14 were waited for; matrix products, arithmetic and copies ran while one was open for 0% of the time, Pallas kernels for 12%

profile of v8, /device:TPU:0, one launch (start us, length us, event | category | flops | bytes accessed | tf_op | source)
XLA Modules:
  0.0 115.6 jit_solution(8324570424277572764)
XLA Ops:
  0.6 1.1 shard_map.131
  1.7 3.0 %collective-permute-start.2 = (bf16[144,512]{1,0:T(8,128)(2,1)S(1)}, bf16[144,512]{1,0:T(8,128)(2,1)S(1)}, u32[]{:S(2)}, u32[]{:S(2)}) collective-permute-start(bf16[144,512]{1,0:T(8,128)(2,1)S(1)} %get-tuple-element.84.refs_1_), channel_id=1, source_target_pairs={{0,16},{8,24},{16,0},{24,8},{1,17},{9,25},{17,1},{25,9},{2,18},{10... | collective-permute-start | bytes 442376 | tf_op jit(solution)/shard_map/ppermute | solution.py:457
  4.7 1.5 %collective-permute-start = (bf16[144,512]{1,0:T(8,128)(2,1)S(1)}, bf16[144,512]{1,0:T(8,128)(2,1)S(1)}, u32[]{:S(2)}, u32[]{:S(2)}) collective-permute-start(bf16[144,512]{1,0:T(8,128)(2,1)S(1)} %get-tuple-element.83.refs_0_), channel_id=1, source_target_pairs={{0,8},{8,0},{16,24},{24,16},{1,9},{9,1},{17,25},{25,17},{2,10},{10... | collective-permute-start | bytes 442376 | tf_op jit(solution)/shard_map/ppermute | solution.py:457
  6.2 2.4 %collective-permute-done.2.refs_1_.refs_5_ = bf16[144,512]{1,0:T(8,128)(2,1)S(1)} collective-permute-done((bf16[144,512]{1,0:T(8,128)(2,1)S(1)}, bf16[144,512]{1,0:T(8,128)(2,1)S(1)}, u32[]{:S(2)}, u32[]{:S(2)}) %collective-permute-start.2) | collective-permute-done | bytes 147488 | tf_op jit(solution)/shard_map/ppermute | solution.py:457
  8.6 1.8 %collective-permute-start.3 = (bf16[288,512]{1,0:T(8,128)(2,1)S(1)}, bf16[288,512]{1,0:T(8,128)(2,1)S(1)}, u32[]{:S(2)}, u32[]{:S(2)}) collective-permute-start(bf16[288,512]{1,0:T(8,128)(2,1)S(1)} %pad_maximum_fusion.1), channel_id=1, source_target_pairs={{0,8},{8,0},{16,24},{24,16},{1,9},{9,1},{17,25},{25,17},{2,10},{10... | collective-permute-start | bytes 884744 | tf_op jit(solution)/shard_map/ppermute | solution.py:457
  10.4 1.6 %collective-permute-start.1 = (bf16[288,512]{1,0:T(8,128)(2,1)S(1)}, bf16[288,512]{1,0:T(8,128)(2,1)S(1)}, u32[]{:S(2)}, u32[]{:S(2)}) collective-permute-start(bf16[288,512]{1,0:T(8,128)(2,1)S(1)} %pad_maximum_fusion), channel_id=1, source_target_pairs={{0,16},{8,24},{16,0},{24,8},{1,17},{9,25},{17,1},{25,9},{2,18},{10... | collective-permute-start | bytes 884744 | tf_op jit(solution)/shard_map/ppermute | solution.py:457
  12.0 1.5 %shard_map.132 = (bf16[256,512]{1,0:T(8,128)(2,1)S(1)}, bf16[512,256]{1,0:T(8,128)(2,1)S(1)}, bf16[1024,192]{1,0:T(8,128)(2,1)S(1)}, bf16[192,1024]{1,0:T(8,128)...) custom-call(s32[4,2,8]{2,1,0:T(2,128)} %bitcast.33, s32[8,128]{1,0:T(8,128)} %bitcast.34, ...), custom_call_target="tpu_custom_call" | custom-call | bytes 2367744 | tf_op jit(solution)/shard_map/pallas_call | solution.py:436
  13.5 0.1 pad_add_fusion.who
  13.6 1.9 %shard_map.133.refs_4_ = f32[1024,512]{1,0:T(8,128)S(1)} custom-call(s32[2]{0:T(128)S(1)} %pad_add_fusion.who, bf16[144,512]{1,0:T(8,128)(2,1)S(1)} %get-tuple-element.83.refs_0_, bf16[144,512]{1,0:T(8,128)(2,1)S(1)} %get-tuple-element.84.refs_1_, bf16[512,512]{1,0:T(8,128)(2,1)S(1)} %get-tuple-element.85.refs_2_.refs_4_.refs_8_, ...), custom_call_target="tpu_custom_call" | custom-call | bytes 2918408 | tf_op jit(solution)/shard_map/pallas_call | solution.py:436
  15.5 1.9 %shard_map.134.refs_6_.before = f32[1024,512]{1,0:T(8,128)S(1)} custom-call(s32[2]{0:T(128)S(1)} %pad_add_fusion.who, bf16[144,512]{1,0:T(8,128)(2,1)S(1)} %collective-permute-done.refs_0_.refs_2_, bf16[144,512]{1,0:T(8,128)(2,1)S(1)} %collective-permute-done.2.refs_1_.refs_5_, ...), custom_call_target="tpu_custom_call", output_to_operand_aliasing={{}: (5, {})} | custom-call | bytes 5015560 | tf_op jit(solution)/shard_map/pallas_call | solution.py:436
  17.4 0.0 collective-permute-done.3.refs_2_.refs_3_.refs_7_
  17.4 0.7 collective-permute-done.1.refs_0_.refs_1_.refs_4_.refs_6_
  18.1 2.0 %shard_map.135 = (bf16[512,512]{1,0:T(8,128)(2,1)S(1)}, bf16[1024,512]{1,0:T(8,128)(2,1)S(1)}, s32[1,1024]{1,0:T(1,128)S(1)}) custom-call(s32[2]{0:T(128)S(1)} %pad_add_fusion.who, bf16[288,512]{1,0:T(8,128)(2,1)S(1)} %collective-permute-done.1.refs_0_.refs_1_.refs_4_.refs_6_, bf16[288,512]{1,0:T(8,128)(2,1)S(1)} %collective-permute-done.1.refs_0_.refs_1_.refs_4_.refs_6_, ...), custom_call_target="tpu_custom_call" | custom-call | bytes 5380104 | tf_op jit(solution)/shard_map/pallas_call | solution.py:436
  20.1 0.1 collective-permute-start.4
  20.2 0.7 shard_map.136
  20.9 1.2 %collective-permute-done.4 = bf16[512,512]{1,0:T(8,128)(2,1)S(1)} collective-permute-done((bf16[512,512]{1,0:T(8,128)(2,1)S(1)}, bf16[512,512]{1,0:T(8,128)(2,1)S(1)}, u32[]{:S(2)}, u32[]{:S(2)}) %collective-permute-start.4) | collective-permute-done | bytes 524320 | tf_op jit(solution)/shard_map/ppermute | solution.py:457
  22.1 0.2 fusion
  22.3 0.0 copy-start.1
  22.3 0.0 copy-start.3
  22.3 2.7 %collective-permute-start.5 = (bf16[128,512]{1,0:T(8,128)(2,1)S(1)}, bf16[128,512]{1,0:T(8,128)(2,1)S(1)}, u32[]{:S(2)}, u32[]{:S(2)}) collective-permute-start(bf16[128,512]{1,0:T(8,128)(2,1)S(1)} %get-tuple-element.168), channel_id=1, source_target_pairs={{0,4},{1,5},{2,6},{3,7},{4,0},{5,1},{6,2},{7,3},{8,12},{9,13},{10,... | collective-permute-start | bytes 393224 | tf_op jit(solution)/shard_map/ppermute | solution.py:457
  25.0 1.3 %collective-permute-start.6 = (bf16[128,512]{1,0:T(8,128)(2,1)S(1)}, bf16[128,512]{1,0:T(8,128)(2,1)S(1)}, u32[]{:S(2)}, u32[]{:S(2)}) collective-permute-start(bf16[128,512]{1,0:T(8,128)(2,1)S(1)} %get-tuple-element.167), channel_id=1, source_target_pairs={{0,6},{1,7},{2,4},{3,5},{4,2},{5,3},{6,0},{7,1},{8,14},{9,15},{10,... | collective-permute-start | bytes 393224 | tf_op jit(solution)/shard_map/ppermute | solution.py:457
  26.3 0.2 collective-permute-start.7
  26.6 2.3 %shard_map.137 = (bf16[256,512]{1,0:T(8,128)(2,1)S(1)}, bf16[256,512]{1,0:T(8,128)(2,1)S(1)}, bf16[256,512]{1,0:T(8,128)(2,1)S(1)}, bf16[256,512]{1,0:T(8,128)(2...) custom-call(bf16[144,512]{1,0:T(8,128)(2,1)S(1)} %get-tuple-element., ...), custom_call_target="tpu_custom_call" | custom-call | bytes 4392960 | tf_op jit(solution)/shard_map/pallas_call | solution.py:436
  28.9 6.4 %collective-permute-done.5.refs_0_ = bf16[128,512]{1,0:T(8,128)(2,1)S(1)} collective-permute-done((bf16[128,512]{1,0:T(8,128)(2,1)S(1)}, bf16[128,512]{1,0:T(8,128)(2,1)S(1)}, u32[]{:S(2)}, u32[]{:S(2)}) %collective-permute-start.5) | collective-permute-done | bytes 131104 | tf_op jit(solution)/shard_map/ppermute | solution.py:457
  35.3 0.0 collective-permute-done.6.refs_1_
  35.3 0.6 collective-permute-done.7.refs_2_
  35.8 0.5 shard_map.138
  36.3 12.6 %all_to_all.44 = bf16[32,8,128]{2,1,0:T(8,128)(2,1)S(1)} all-to-all(bf16[32,8,128]{2,1,0:T(8,128)(2,1)S(1)} %bitcast.29), channel_id=1, replica_groups=mesh['sect'=4,'node'=8] {'sect','node'}, dimensions={0} | all-to-all | bytes 131072 | tf_op jit(solution)/shard_map/all_to_all | solution.py:602
  48.9 1.9 %shard_map.139 = (bf16[128,512]{1,0:T(8,128)(2,1)S(1)}, f32[128,512]{1,0:T(8,128)S(1)}, bf16[1024,512]{1,0:T(8,128)(2,1)S(1)}, bf16[256,128]{1,0:T(8,128)(2,1)S(1)}) custom-call(bf16[128,512]{1,0:T(8,128)(2,1)S(1)} %get-tuple-element.102.state, bf16[256,128]{1,0:T(8,128)(2,1)S(1)} %bitcast.24, bf16[1024,192]{1,0:T(8,128)(2,1)S(1)} %get-tuple-element.104.source, ...), custom_call_target="tpu_custom_call" | custom-call | bytes 6553600 | tf_op jit(solution)/shard_map/pallas_call | solution.py:436
  50.8 9.1 %all_to_all.45 = bf16[32,8,128]{2,1,0:T(8,128)(2,1)S(1)} all-to-all(bf16[32,8,128]{2,1,0:T(8,128)(2,1)S(1)} %bitcast.30), channel_id=1, replica_groups=mesh['sect'=4,'node'=8] {'sect','node'}, dimensions={0} | all-to-all | bytes 131072 | tf_op jit(solution)/shard_map/all_to_all | solution.py:602
  59.8 3.0 %shard_map.140 = (bf16[128,512]{1,0:T(8,128)(2,1)S(1)}, f32[128,512]{1,0:T(8,128)S(1)}, bf16[256,128]{1,0:T(8,128)(2,1)S(1)}) custom-call(bf16[128,512]{1,0:T(8,128)(2,1)S(1)} %get-tuple-element.105.state, bf16[256,128]{1,0:T(8,128)(2,1)S(1)} %bitcast.25, bf16[1024,192]{1,0:T(8,128)(2,1)S(1)} %get-tuple-element.104.source, ...), custom_call_target="tpu_custom_call" | custom-call | bytes 5767168 | tf_op jit(solution)/shard_map/pallas_call | solution.py:436
  62.8 9.1 %all_to_all.46 = bf16[32,8,128]{2,1,0:T(8,128)(2,1)S(1)} all-to-all(bf16[32,8,128]{2,1,0:T(8,128)(2,1)S(1)} %bitcast.32), channel_id=1, replica_groups=mesh['sect'=4,'node'=8] {'sect','node'}, dimensions={0} | all-to-all | bytes 131072 | tf_op jit(solution)/shard_map/all_to_all | solution.py:602
  71.9 1.7 %shard_map.141 = (f32[128,512]{1,0:T(8,128)S(1)}, bf16[256,128]{1,0:T(8,128)(2,1)S(1)}) custom-call(f32[128,512]{1,0:T(8,128)S(1)} %get-tuple-element.108.mine, bf16[256,128]{1,0:T(8,128)(2,1)S(1)} %bitcast.23, bf16[512,256]{1,0:T(8,128)(2,1)S(1)} %get-tuple-element.110.pick_t, f32[128,512]{1,0:T(8,128)S(1)} %get-tuple-element.111.mixed, ...), custom_call_target="tpu_custom_call" | custom-call | bytes 6815744 | tf_op jit(solution)/shard_map/pallas_call | solution.py:436
  73.6 9.1 %all_to_all.47 = bf16[32,8,128]{2,1,0:T(8,128)(2,1)S(1)} all-to-all(bf16[32,8,128]{2,1,0:T(8,128)(2,1)S(1)} %bitcast.31), channel_id=1, replica_groups=mesh['sect'=4,'node'=8] {'sect','node'}, dimensions={0} | all-to-all | bytes 131072 | tf_op jit(solution)/shard_map/all_to_all | solution.py:602
  82.7 0.5 shard_map.142.refs_11_.refs_7_
  83.2 0.8 collective-permute-start.8
  83.9 1.2 %collective-permute-start.9 = (bf16[128,512]{1,0:T(8,128)(2,1)S(1)}, bf16[128,512]{1,0:T(8,128)(2,1)S(1)}, u32[]{:S(2)}, u32[]{:S(2)}) collective-permute-start(bf16[128,512]{1,0:T(8,128)(2,1)S(1)} %shard_map.142.refs_11_.refs_7_), channel_id=1, source_target_pairs={{0,4},{1,5},{2,6},{3,7},{4,0},{5,1},{6,2},{7,3},{8,12},{9,13},{10,... | collective-permute-start | bytes 393224 | tf_op jit(solution)/shard_map/ppermute | solution.py:457
  85.1 2.5 %collective-permute-start.10 = (bf16[128,512]{1,0:T(8,128)(2,1)S(1)}, bf16[128,512]{1,0:T(8,128)(2,1)S(1)}, u32[]{:S(2)}, u32[]{:S(2)}) collective-permute-start(bf16[128,512]{1,0:T(8,128)(2,1)S(1)} %shard_map.142.refs_11_.refs_7_), channel_id=1, source_target_pairs={{0,2},{1,3},{2,0},{3,1},{4,6},{5,7},{6,4},{7,5},{8,10},{9,11},{10,... | collective-permute-start | bytes 393224 | tf_op jit(solution)/shard_map/ppermute | solution.py:457
  87.6 3.2 %shard_map.143 = (bf16[256,1024]{1,0:T(8,128)(2,1)S(1)}, bf16[256,1024]{1,0:T(8,128)(2,1)S(1)}, bf16[256,1024]{1,0:T(8,128)(2,1)S(1)}, bf16[256,1024]{1,0:T(8,12...) custom-call(s32[2]{0:T(128)S(1)} %pad_add_fusion.who, ...), custom_call_target="tpu_custom_call" | custom-call | bytes 6225928 | tf_op jit(solution)/shard_map/pallas_call | solution.py:436
  90.8 0.7 collective-permute-done.8.refs_8_.refs_4_
  91.5 0.0 collective-permute-start.11
  91.5 5.6 %collective-permute-done.9.refs_9_.refs_5_ = bf16[128,512]{1,0:T(8,128)(2,1)S(1)} collective-permute-done((bf16[128,512]{1,0:T(8,128)(2,1)S(1)}, bf16[128,512]{1,0:T(8,128)(2,1)S(1)}, u32[]{:S(2)}, u32[]{:S(2)}) %collective-permute-start.9) | collective-permute-done | bytes 131104 | tf_op jit(solution)/shard_map/ppermute | solution.py:457
  97.1 0.0 collective-permute-start.12
  97.1 0.5 collective-permute-start.13
  97.6 0.8 collective-permute-done.12.refs_13_.refs_9_
  98.4 0.2 collective-permute-done.13.refs_14_.refs_10_
  98.6 1.8 %shard_map.144 = (bf16[256,256]{1,0:T(8,128)(2,1)S(1)}, bf16[256,256]{1,0:T(8,128)(2,1)S(1)}, bf16[256,256]{1,0:T(8,128)(2,1)S(1)}, bf16[256,256]{1,0:T(8,128)(2,1)S(1)}) custom-call(s32[2]{0:T(128)S(1)} %pad_add_fusion.who, bf16[256,1024]{1,0:T(8,128)(2,1)S(1)} %get-tuple-element.124.refs_0_, bf16[256,1024]{1,0:T(8,128)(2,1)S(1)} %get-tuple-element.125.refs_1_, ...), custom_call_target="tpu_custom_call" | custom-call | bytes 4718600 | tf_op jit(solution)/shard_map/pallas_call | solution.py:436
  100.5 0.7 collective-permute-start.18
  101.2 0.5 collective-permute-start.17
  101.7 1.5 %collective-permute-start.16 = (bf16[256,256]{1,0:T(8,128)(2,1)S(1)}, bf16[256,256]{1,0:T(8,128)(2,1)S(1)}, u32[]{:S(2)}, u32[]{:S(2)}) collective-permute-start(bf16[256,256]{1,0:T(8,128)(2,1)S(1)} %get-tuple-element.133), channel_id=1, source_target_pairs={{0,16},{8,24},{16,0},{24,8},{1,17},{9,25},{17,1},{25,9},{2,18},{10... | collective-permute-start | bytes 393224 | tf_op jit(solution)/shard_map/ppermute | solution.py:457
  103.2 1.4 %collective-permute-start.15 = (bf16[256,256]{1,0:T(8,128)(2,1)S(1)}, bf16[256,256]{1,0:T(8,128)(2,1)S(1)}, u32[]{:S(2)}, u32[]{:S(2)}) collective-permute-start(bf16[256,256]{1,0:T(8,128)(2,1)S(1)} %get-tuple-element.132), channel_id=1, source_target_pairs={{0,8},{8,0},{16,24},{24,16},{1,9},{9,1},{17,25},{25,17},{2,10},{10... | collective-permute-start | bytes 393224 | tf_op jit(solution)/shard_map/ppermute | solution.py:457
  104.6 1.3 %shard_map.145 = (f32[128,256]{1,0:T(8,128)S(1)}, f32[128,256]{1,0:T(8,128)S(1)}, f32[128,256]{1,0:T(8,128)S(1)}, f32[128,256]{1,0:T(8,128)S(1)}) custom-call(s32[2]{0:T(128)S(1)} %pad_add_fusion.who, bf16[256,1024]{1,0:T(8,128)(2,1)S(1)} %get-tuple-element.144.refs_0_, bf16[256,1024]{1,0:T(8,128)(2,1)S(1)} %get-tuple-element.145.refs_1_, ...), custom_call_target="tpu_custom_call" | custom-call | bytes 3145736 | tf_op jit(solution)/shard_map/pallas_call | solution.py:436
  105.8 0.0 copy-start.2
  105.8 1.0 collective-permute-done.18.refs_7_
  106.9 0.7 collective-permute-start.22
  107.6 1.4 %collective-permute-start.21 = (bf16[128,256]{1,0:T(8,128)(2,1)S(1)}, bf16[128,256]{1,0:T(8,128)(2,1)S(1)}, u32[]{:S(2)}, u32[]{:S(2)}) collective-permute-start(bf16[128,256]{1,0:T(8,128)(2,1)S(1)} %add_convert_fusion.1), channel_id=1, source_target_pairs={{0,16},{8,24},{16,0},{24,8},{1,17},{9,25},{17,1},{25,9},{2,18},{10... | collective-permute-start | bytes 196616 | tf_op jit(solution)/shard_map/ppermute | solution.py:457
  109.0 0.2 collective-permute-done.16.refs_5_
  109.2 0.5 collective-permute-start.20
  109.8 0.4 collective-permute-done.15.refs_4_
  110.1 1.5 %collective-permute-start.19 = (bf16[128,256]{1,0:T(8,128)(2,1)S(1)}, bf16[128,256]{1,0:T(8,128)(2,1)S(1)}, u32[]{:S(2)}, u32[]{:S(2)}) collective-permute-start(bf16[128,256]{1,0:T(8,128)(2,1)S(1)} %add_convert_fusion.3), channel_id=1, source_target_pairs={{0,16},{8,24},{16,0},{24,8},{1,17},{9,25},{17,1},{25,9},{2,18},{10... | collective-permute-start | bytes 196616 | tf_op jit(solution)/shard_map/ppermute | solution.py:457
  111.6 1.3 %shard_map.146 = (f32[128,256]{1,0:T(8,128)S(1)}, f32[128,256]{1,0:T(8,128)S(1)}, f32[128,256]{1,0:T(8,128)S(1)}, f32[128,256]{1,0:T(8,128)S(1)}) custom-call(s32[2]{0:T(128)S(1)} %pad_add_fusion.who, bf16[256,1024]{1,0:T(8,128)(2,1)S(1)} %get-tuple-element.119.refs_0_, bf16[256,1024]{1,0:T(8,128)(2,1)S(1)} %get-tuple-element.120.refs_1_, ...), custom_call_target="tpu_custom_call" | custom-call | bytes 3145736 | tf_op jit(solution)/shard_map/pallas_call | solution.py:436
  112.9 0.7 collective-permute-done.20.refs_9_
  113.6 0.9 collective-permute-done.19.refs_8_
  114.5 1.2 %shard_map.147 = bf16[256,512]{1,0:T(8,128)(2,1)} custom-call(f32[128,256]{1,0:T(8,128)S(1)} %get-tuple-element.160.refs_0_, f32[128,256]{1,0:T(8,128)S(1)} %get-tuple-element.161.refs_1_, f32[128,256]{1,0:T(8,128)S(1)} %get-tuple-element.162.refs_2_, f32[128,256]{1,0:T(8,128)S(1)} %get-tuple-element.163.refs_3_, ...), custom_call_target="tpu_custom_call" | custom-call | bytes 2097152 | tf_op jit(solution)/shard_map/pallas_call | solution.py:436
  (23 shorter events, 0.2 us)
Async XLA Ops:
  1.7 6.9 %collective-permute-start.2 = (bf16[144,512]{1,0:T(8,128)(2,1)S(1)}, bf16[144,512]{1,0:T(8,128)(2,1)S(1)}, u32[]{:S(2)}, u32[]{:S(2)}) collective-permute-start(bf16[144,512]{1,0:T(8,128)(2,1)S(1)} %get-tuple-element.84.refs_1_), channel_id=1, source_target_pairs={{0,16},{8,24},{16,0},{24,8},{1,17},{9,25},{17,1},{25,9},{2,18},{10... | collective-permute-start | bytes 442376 | tf_op jit(solution)/shard_map/ppermute | solution.py:457
  4.7 5.7 %collective-permute-start = (bf16[144,512]{1,0:T(8,128)(2,1)S(1)}, bf16[144,512]{1,0:T(8,128)(2,1)S(1)}, u32[]{:S(2)}, u32[]{:S(2)}) collective-permute-start(bf16[144,512]{1,0:T(8,128)(2,1)S(1)} %get-tuple-element.83.refs_0_), channel_id=1, source_target_pairs={{0,8},{8,0},{16,24},{24,16},{1,9},{9,1},{17,25},{25,17},{2,10},{10... | collective-permute-start | bytes 442376 | tf_op jit(solution)/shard_map/ppermute | solution.py:457
  8.6 8.8 %collective-permute-start.3 = (bf16[288,512]{1,0:T(8,128)(2,1)S(1)}, bf16[288,512]{1,0:T(8,128)(2,1)S(1)}, u32[]{:S(2)}, u32[]{:S(2)}) collective-permute-start(bf16[288,512]{1,0:T(8,128)(2,1)S(1)} %pad_maximum_fusion.1), channel_id=1, source_target_pairs={{0,8},{8,0},{16,24},{24,16},{1,9},{9,1},{17,25},{25,17},{2,10},{10... | collective-permute-start | bytes 884744 | tf_op jit(solution)/shard_map/ppermute | solution.py:457
  10.4 7.7 %collective-permute-start.1 = (bf16[288,512]{1,0:T(8,128)(2,1)S(1)}, bf16[288,512]{1,0:T(8,128)(2,1)S(1)}, u32[]{:S(2)}, u32[]{:S(2)}) collective-permute-start(bf16[288,512]{1,0:T(8,128)(2,1)S(1)} %pad_maximum_fusion), channel_id=1, source_target_pairs={{0,16},{8,24},{16,0},{24,8},{1,17},{9,25},{17,1},{25,9},{2,18},{10... | collective-permute-start | bytes 884744 | tf_op jit(solution)/shard_map/ppermute | solution.py:457
  20.1 2.0 %collective-permute-start.4 = (bf16[512,512]{1,0:T(8,128)(2,1)S(1)}, bf16[512,512]{1,0:T(8,128)(2,1)S(1)}, u32[]{:S(2)}, u32[]{:S(2)}) collective-permute-start(bf16[512,512]{1,0:T(8,128)(2,1)S(1)} %get-tuple-element.89), channel_id=1, source_target_pairs={{0,1},{1,0},{2,3},{3,2},{4,5},{5,4},{6,7},{7,6},{8,9},{9,8},{10,11... | collective-permute-start | bytes 1572872 | tf_op jit(solution)/shard_map/ppermute | solution.py:457
  22.3 13.6 %copy-start.1 = (bf16[512,512]{1,0:T(8,128)(2,1)S(1)}, bf16[512,512]{1,0:T(8,128)(2,1)}, u32[]{:S(2)}) copy-start(bf16[512,512]{1,0:T(8,128)(2,1)} %weight.1) | copy-start | bytes 1572868
  22.3 13.6 %copy-start.3 = (bf16[1,128,512]{2,1,0:T(8,128)(2,1)S(1)}, bf16[1,128,512]{2,1,0:T(8,128)(2,1)}, u32[]{:S(2)}) copy-start(bf16[1,128,512]{2,1,0:T(8,128)(2,1)} %param.18) | copy-start | bytes 393220
  22.3 13.0 %collective-permute-start.5 = (bf16[128,512]{1,0:T(8,128)(2,1)S(1)}, bf16[128,512]{1,0:T(8,128)(2,1)S(1)}, u32[]{:S(2)}, u32[]{:S(2)}) collective-permute-start(bf16[128,512]{1,0:T(8,128)(2,1)S(1)} %get-tuple-element.168), channel_id=1, source_target_pairs={{0,4},{1,5},{2,6},{3,7},{4,0},{5,1},{6,2},{7,3},{8,12},{9,13},{10,... | collective-permute-start | bytes 393224 | tf_op jit(solution)/shard_map/ppermute | solution.py:457
  25.0 10.3 %collective-permute-start.6 = (bf16[128,512]{1,0:T(8,128)(2,1)S(1)}, bf16[128,512]{1,0:T(8,128)(2,1)S(1)}, u32[]{:S(2)}, u32[]{:S(2)}) collective-permute-start(bf16[128,512]{1,0:T(8,128)(2,1)S(1)} %get-tuple-element.167), channel_id=1, source_target_pairs={{0,6},{1,7},{2,4},{3,5},{4,2},{5,3},{6,0},{7,1},{8,14},{9,15},{10,... | collective-permute-start | bytes 393224 | tf_op jit(solution)/shard_map/ppermute | solution.py:457
  26.3 22.6 %copy-start = (bf16[2,4,512,512]{3,2,1,0:T(8,128)(2,1)S(1)}, bf16[2,4,512,512]{3,2,1,0:T(8,128)(2,1)}, u32[]{:S(2)}) copy-start(bf16[2,4,512,512]{3,2,1,0:T(8,128)(2,1)} %weights.5) | copy-start | bytes 12582916
  26.3 9.5 %collective-permute-start.7 = (bf16[128,512]{1,0:T(8,128)(2,1)S(1)}, bf16[128,512]{1,0:T(8,128)(2,1)S(1)}, u32[]{:S(2)}, u32[]{:S(2)}) collective-permute-start(bf16[128,512]{1,0:T(8,128)(2,1)S(1)} %get-tuple-element.166), channel_id=1, source_target_pairs={{0,2},{1,3},{2,0},{3,1},{4,6},{5,7},{6,4},{7,5},{8,10},{9,11},{10,... | collective-permute-start | bytes 393224 | tf_op jit(solution)/shard_map/ppermute | solution.py:457
  48.9 11.0 %copy-start.4 = (bf16[1,128,512]{2,1,0:T(8,128)(2,1)S(1)}, bf16[1,128,512]{2,1,0:T(8,128)(2,1)}, u32[]{:S(2)}) copy-start(bf16[1,128,512]{2,1,0:T(8,128)(2,1)} %param.23) | copy-start | bytes 393220
  83.2 8.3 %collective-permute-start.8 = (bf16[128,512]{1,0:T(8,128)(2,1)S(1)}, bf16[128,512]{1,0:T(8,128)(2,1)S(1)}, u32[]{:S(2)}, u32[]{:S(2)}) collective-permute-start(bf16[128,512]{1,0:T(8,128)(2,1)S(1)} %shard_map.142.refs_11_.refs_7_), channel_id=1, source_target_pairs={{0,6},{1,7},{2,4},{3,5},{4,2},{5,3},{6,0},{7,1},{8,14},{9,15},{10,... | collective-permute-start | bytes 393224 | tf_op jit(solution)/shard_map/ppermute | solution.py:457
  83.9 13.2 %collective-permute-start.9 = (bf16[128,512]{1,0:T(8,128)(2,1)S(1)}, bf16[128,512]{1,0:T(8,128)(2,1)S(1)}, u32[]{:S(2)}, u32[]{:S(2)}) collective-permute-start(bf16[128,512]{1,0:T(8,128)(2,1)S(1)} %shard_map.142.refs_11_.refs_7_), channel_id=1, source_target_pairs={{0,4},{1,5},{2,6},{3,7},{4,0},{5,1},{6,2},{7,3},{8,12},{9,13},{10,... | collective-permute-start | bytes 393224 | tf_op jit(solution)/shard_map/ppermute | solution.py:457
  85.1 11.9 %collective-permute-start.10 = (bf16[128,512]{1,0:T(8,128)(2,1)S(1)}, bf16[128,512]{1,0:T(8,128)(2,1)S(1)}, u32[]{:S(2)}, u32[]{:S(2)}) collective-permute-start(bf16[128,512]{1,0:T(8,128)(2,1)S(1)} %shard_map.142.refs_11_.refs_7_), channel_id=1, source_target_pairs={{0,2},{1,3},{2,0},{3,1},{4,6},{5,7},{6,4},{7,5},{8,10},{9,11},{10,... | collective-permute-start | bytes 393224 | tf_op jit(solution)/shard_map/ppermute | solution.py:457
  87.6 10.0 %collective-permute-start.14 = (bf16[128,512]{1,0:T(8,128)(2,1)S(1)}, bf16[128,512]{1,0:T(8,128)(2,1)S(1)}, u32[]{:S(2)}, u32[]{:S(2)}) collective-permute-start(bf16[128,512]{1,0:T(8,128)(2,1)S(1)} %shard_map.142.refs_11_.refs_7_), channel_id=1, source_target_pairs={{0,1},{1,0},{2,3},{3,2},{4,5},{5,4},{6,7},{7,6},{8,9},{9,8},{10,11... | collective-permute-start | bytes 393224 | tf_op jit(solution)/shard_map/ppermute | solution.py:457
  91.5 6.1 %collective-permute-start.11 = (bf16[128,512]{1,0:T(8,128)(2,1)S(1)}, bf16[128,512]{1,0:T(8,128)(2,1)S(1)}, u32[]{:S(2)}, u32[]{:S(2)}) collective-permute-start(bf16[128,512]{1,0:T(8,128)(2,1)S(1)} %collective-permute-done.8.refs_8_.refs_4_), channel_id=1, source_target_pairs={{0,1},{1,0},{2,3},{3,2},{4,5},{5,4},{6,7},{7,6},{8,9},{9,8},{10,11... | collective-permute-start | bytes 393224 | tf_op jit(solution)/shard_map/ppermute | solution.py:457
  97.1 1.3 %collective-permute-start.12 = (bf16[128,512]{1,0:T(8,128)(2,1)S(1)}, bf16[128,512]{1,0:T(8,128)(2,1)S(1)}, u32[]{:S(2)}, u32[]{:S(2)}) collective-permute-start(bf16[128,512]{1,0:T(8,128)(2,1)S(1)} %collective-permute-done.9.refs_9_.refs_5_), channel_id=1, source_target_pairs={{0,1},{1,0},{2,3},{3,2},{4,5},{5,4},{6,7},{7,6},{8,9},{9,8},{10,11... | collective-permute-start | bytes 393224 | tf_op jit(solution)/shard_map/ppermute | solution.py:457
  97.1 1.5 %collective-permute-start.13 = (bf16[128,512]{1,0:T(8,128)(2,1)S(1)}, bf16[128,512]{1,0:T(8,128)(2,1)S(1)}, u32[]{:S(2)}, u32[]{:S(2)}) collective-permute-start(bf16[128,512]{1,0:T(8,128)(2,1)S(1)} %collective-permute-done.10.refs_10_.refs_6_), channel_id=1, source_target_pairs={{0,1},{1,0},{2,3},{3,2},{4,5},{5,4},{6,7},{7,6},{8,9},{9,8},{10,11... | collective-permute-start | bytes 393224 | tf_op jit(solution)/shard_map/ppermute | solution.py:457
  100.5 6.4 %collective-permute-start.18 = (bf16[256,256]{1,0:T(8,128)(2,1)S(1)}, bf16[256,256]{1,0:T(8,128)(2,1)S(1)}, u32[]{:S(2)}, u32[]{:S(2)}) collective-permute-start(bf16[256,256]{1,0:T(8,128)(2,1)S(1)} %get-tuple-element.135), channel_id=1, source_target_pairs={{0,16},{8,24},{16,0},{24,8},{1,17},{9,25},{17,1},{25,9},{2,18},{10... | collective-permute-start | bytes 393224 | tf_op jit(solution)/shard_map/ppermute | solution.py:457
  101.2 6.4 %collective-permute-start.17 = (bf16[256,256]{1,0:T(8,128)(2,1)S(1)}, bf16[256,256]{1,0:T(8,128)(2,1)S(1)}, u32[]{:S(2)}, u32[]{:S(2)}) collective-permute-start(bf16[256,256]{1,0:T(8,128)(2,1)S(1)} %get-tuple-element.134), channel_id=1, source_target_pairs={{0,8},{8,0},{16,24},{24,16},{1,9},{9,1},{17,25},{25,17},{2,10},{10... | collective-permute-start | bytes 393224 | tf_op jit(solution)/shard_map/ppermute | solution.py:457
  101.7 7.5 %collective-permute-start.16 = (bf16[256,256]{1,0:T(8,128)(2,1)S(1)}, bf16[256,256]{1,0:T(8,128)(2,1)S(1)}, u32[]{:S(2)}, u32[]{:S(2)}) collective-permute-start(bf16[256,256]{1,0:T(8,128)(2,1)S(1)} %get-tuple-element.133), channel_id=1, source_target_pairs={{0,16},{8,24},{16,0},{24,8},{1,17},{9,25},{17,1},{25,9},{2,18},{10... | collective-permute-start | bytes 393224 | tf_op jit(solution)/shard_map/ppermute | solution.py:457
  103.2 7.0 %collective-permute-start.15 = (bf16[256,256]{1,0:T(8,128)(2,1)S(1)}, bf16[256,256]{1,0:T(8,128)(2,1)S(1)}, u32[]{:S(2)}, u32[]{:S(2)}) collective-permute-start(bf16[256,256]{1,0:T(8,128)(2,1)S(1)} %get-tuple-element.132), channel_id=1, source_target_pairs={{0,8},{8,0},{16,24},{24,16},{1,9},{9,1},{17,25},{25,17},{2,10},{10... | collective-permute-start | bytes 393224 | tf_op jit(solution)/shard_map/ppermute | solution.py:457
  105.8 8.6 %copy-start.2 = (bf16[512,512]{1,0:T(8,128)(2,1)S(1)}, bf16[512,512]{1,0:T(8,128)(2,1)}, u32[]{:S(2)}) copy-start(bf16[512,512]{1,0:T(8,128)(2,1)} %refs_12_.1) | copy-start | bytes 1572868
  106.9 6.0 %collective-permute-start.22 = (bf16[128,256]{1,0:T(8,128)(2,1)S(1)}, bf16[128,256]{1,0:T(8,128)(2,1)S(1)}, u32[]{:S(2)}, u32[]{:S(2)}) collective-permute-start(bf16[128,256]{1,0:T(8,128)(2,1)S(1)} %add_convert_fusion), channel_id=1, source_target_pairs={{0,8},{8,0},{16,24},{24,16},{1,9},{9,1},{17,25},{25,17},{2,10},{10... | collective-permute-start | bytes 196616 | tf_op jit(solution)/shard_map/ppermute | solution.py:457
  107.6 5.3 %collective-permute-start.21 = (bf16[128,256]{1,0:T(8,128)(2,1)S(1)}, bf16[128,256]{1,0:T(8,128)(2,1)S(1)}, u32[]{:S(2)}, u32[]{:S(2)}) collective-permute-start(bf16[128,256]{1,0:T(8,128)(2,1)S(1)} %add_convert_fusion.1), channel_id=1, source_target_pairs={{0,16},{8,24},{16,0},{24,8},{1,17},{9,25},{17,1},{25,9},{2,18},{10... | collective-permute-start | bytes 196616 | tf_op jit(solution)/shard_map/ppermute | solution.py:457
  109.2 4.3 %collective-permute-start.20 = (bf16[128,256]{1,0:T(8,128)(2,1)S(1)}, bf16[128,256]{1,0:T(8,128)(2,1)S(1)}, u32[]{:S(2)}, u32[]{:S(2)}) collective-permute-start(bf16[128,256]{1,0:T(8,128)(2,1)S(1)} %add_convert_fusion.2), channel_id=1, source_target_pairs={{0,8},{8,0},{16,24},{24,16},{1,9},{9,1},{17,25},{25,17},{2,10},{10... | collective-permute-start | bytes 196616 | tf_op jit(solution)/shard_map/ppermute | solution.py:457
  110.1 4.3 %collective-permute-start.19 = (bf16[128,256]{1,0:T(8,128)(2,1)S(1)}, bf16[128,256]{1,0:T(8,128)(2,1)S(1)}, u32[]{:S(2)}, u32[]{:S(2)}) collective-permute-start(bf16[128,256]{1,0:T(8,128)(2,1)S(1)} %add_convert_fusion.3), channel_id=1, source_target_pairs={{0,16},{8,24},{16,0},{24,8},{1,17},{9,25},{17,1},{25,9},{2,18},{10... | collective-permute-start | bytes 196616 | tf_op jit(solution)/shard_map/ppermute | solution.py:457

commit v9 on v5

--- a/solution.py
+++ b/solution.py
@@ -43,9 +43,7 @@
 
 
 def back_dot(grad, weight):
-    rows = grad.shape[0]
-    both = dot_t(jnp.concatenate(halves(grad), axis=0), weight)
-    return both[:rows] + both[rows:]
+    return dot_t(grad.astype(BF16), weight)
 
 
 def mark(equal):

time: 116 us -> 116 us (level)
  no operation moved by 1% of the time
where the time goes in v9:
time: 116 us; the launch traced here: 115 us
  blocking collectives  38.3 us (33%)
  Pallas kernels  27.4 us (24%)
  starting transfers between devices  25.6 us (22%)
  waiting for transfers between devices  22.9 us (20%)
    all_to_all x4, blocking collectives, exchange(): return lax.all_to_all(value, both, split_axis=0, concat_axis=0, tiled=True)  38.3 us
    pallas_call x17, Pallas kernels, call(): pl.pallas_call(kernel, out_shape=list(outs), in_specs=specs, out_specs=[p...  27.4 us
    ppermute x23, starting transfers between devices, swap(): return lax.ppermute(value, axis, [(i, i ^ apart) for i in range(size)])  25.6 us
    ppermute x23, waiting for transfers between devices, swap(): return lax.ppermute(value, axis, [(i, i ^ apart) for i in range(size)])  22.9 us
  transfers between devices with their start and end apart: 23, of which 14 were waited for; matrix products, arithmetic and copies ran while one was open for 0% of the time, Pallas kernels for 12%

profile of v9, /device:TPU:0, one launch (start us, length us, event | category | flops | bytes accessed | tf_op | source)
XLA Modules:
  0.0 115.5 jit_solution(15640081043803597847)
XLA Ops:
  0.6 1.1 shard_map.131
  1.7 3.0 %collective-permute-start.2 = (bf16[144,512]{1,0:T(8,128)(2,1)S(1)}, bf16[144,512]{1,0:T(8,128)(2,1)S(1)}, u32[]{:S(2)}, u32[]{:S(2)}) collective-permute-start(bf16[144,512]{1,0:T(8,128)(2,1)S(1)} %get-tuple-element.84.refs_1_), channel_id=1, source_target_pairs={{0,16},{8,24},{16,0},{24,8},{1,17},{9,25},{17,1},{25,9},{2,18},{10... | collective-permute-start | bytes 442376 | tf_op jit(solution)/shard_map/ppermute | solution.py:455
  4.7 1.5 %collective-permute-start = (bf16[144,512]{1,0:T(8,128)(2,1)S(1)}, bf16[144,512]{1,0:T(8,128)(2,1)S(1)}, u32[]{:S(2)}, u32[]{:S(2)}) collective-permute-start(bf16[144,512]{1,0:T(8,128)(2,1)S(1)} %get-tuple-element.83.refs_0_), channel_id=1, source_target_pairs={{0,8},{8,0},{16,24},{24,16},{1,9},{9,1},{17,25},{25,17},{2,10},{10... | collective-permute-start | bytes 442376 | tf_op jit(solution)/shard_map/ppermute | solution.py:455
  6.2 2.4 %collective-permute-done.2.refs_1_.refs_5_ = bf16[144,512]{1,0:T(8,128)(2,1)S(1)} collective-permute-done((bf16[144,512]{1,0:T(8,128)(2,1)S(1)}, bf16[144,512]{1,0:T(8,128)(2,1)S(1)}, u32[]{:S(2)}, u32[]{:S(2)}) %collective-permute-start.2) | collective-permute-done | bytes 147488 | tf_op jit(solution)/shard_map/ppermute | solution.py:455
  8.6 1.8 %collective-permute-start.3 = (bf16[288,512]{1,0:T(8,128)(2,1)S(1)}, bf16[288,512]{1,0:T(8,128)(2,1)S(1)}, u32[]{:S(2)}, u32[]{:S(2)}) collective-permute-start(bf16[288,512]{1,0:T(8,128)(2,1)S(1)} %pad_maximum_fusion.1), channel_id=1, source_target_pairs={{0,8},{8,0},{16,24},{24,16},{1,9},{9,1},{17,25},{25,17},{2,10},{10... | collective-permute-start | bytes 884744 | tf_op jit(solution)/shard_map/ppermute | solution.py:455
  10.4 0.0 collective-permute-done.refs_0_.refs_2_
  10.4 1.6 %collective-permute-start.1 = (bf16[288,512]{1,0:T(8,128)(2,1)S(1)}, bf16[288,512]{1,0:T(8,128)(2,1)S(1)}, u32[]{:S(2)}, u32[]{:S(2)}) collective-permute-start(bf16[288,512]{1,0:T(8,128)(2,1)S(1)} %pad_maximum_fusion), channel_id=1, source_target_pairs={{0,16},{8,24},{16,0},{24,8},{1,17},{9,25},{17,1},{25,9},{2,18},{10... | collective-permute-start | bytes 884744 | tf_op jit(solution)/shard_map/ppermute | solution.py:455
  12.0 1.5 %shard_map.132 = (bf16[256,512]{1,0:T(8,128)(2,1)S(1)}, bf16[512,256]{1,0:T(8,128)(2,1)S(1)}, bf16[1024,192]{1,0:T(8,128)(2,1)S(1)}, bf16[192,1024]{1,0:T(8,128)...) custom-call(s32[4,2,8]{2,1,0:T(2,128)} %bitcast.33, s32[8,128]{1,0:T(8,128)} %bitcast.34, ...), custom_call_target="tpu_custom_call" | custom-call | bytes 2367744 | tf_op jit(solution)/shard_map/pallas_call | solution.py:434
  13.5 0.1 pad_add_fusion.who
  13.6 1.9 %shard_map.133.refs_4_ = f32[1024,512]{1,0:T(8,128)S(1)} custom-call(s32[2]{0:T(128)S(1)} %pad_add_fusion.who, bf16[144,512]{1,0:T(8,128)(2,1)S(1)} %get-tuple-element.83.refs_0_, bf16[144,512]{1,0:T(8,128)(2,1)S(1)} %get-tuple-element.84.refs_1_, bf16[512,512]{1,0:T(8,128)(2,1)S(1)} %get-tuple-element.85.refs_2_.refs_4_.refs_8_, ...), custom_call_target="tpu_custom_call" | custom-call | bytes 2918408 | tf_op jit(solution)/shard_map/pallas_call | solution.py:434
  15.5 1.9 %shard_map.134.refs_6_.before = f32[1024,512]{1,0:T(8,128)S(1)} custom-call(s32[2]{0:T(128)S(1)} %pad_add_fusion.who, bf16[144,512]{1,0:T(8,128)(2,1)S(1)} %collective-permute-done.refs_0_.refs_2_, bf16[144,512]{1,0:T(8,128)(2,1)S(1)} %collective-permute-done.2.refs_1_.refs_5_, ...), custom_call_target="tpu_custom_call", output_to_operand_aliasing={{}: (5, {})} | custom-call | bytes 5015560 | tf_op jit(solution)/shard_map/pallas_call | solution.py:434
  17.4 0.0 collective-permute-done.3.refs_2_.refs_3_.refs_7_
  17.4 0.7 collective-permute-done.1.refs_0_.refs_1_.refs_4_.refs_6_
  18.1 2.0 %shard_map.135 = (bf16[512,512]{1,0:T(8,128)(2,1)S(1)}, bf16[1024,512]{1,0:T(8,128)(2,1)S(1)}, s32[1,1024]{1,0:T(1,128)S(1)}) custom-call(s32[2]{0:T(128)S(1)} %pad_add_fusion.who, bf16[288,512]{1,0:T(8,128)(2,1)S(1)} %collective-permute-done.1.refs_0_.refs_1_.refs_4_.refs_6_, bf16[288,512]{1,0:T(8,128)(2,1)S(1)} %collective-permute-done.1.refs_0_.refs_1_.refs_4_.refs_6_, ...), custom_call_target="tpu_custom_call" | custom-call | bytes 5380104 | tf_op jit(solution)/shard_map/pallas_call | solution.py:434
  20.1 0.1 collective-permute-start.4
  20.2 0.7 shard_map.136
  20.9 1.2 %collective-permute-done.4 = bf16[512,512]{1,0:T(8,128)(2,1)S(1)} collective-permute-done((bf16[512,512]{1,0:T(8,128)(2,1)S(1)}, bf16[512,512]{1,0:T(8,128)(2,1)S(1)}, u32[]{:S(2)}, u32[]{:S(2)}) %collective-permute-start.4) | collective-permute-done | bytes 524320 | tf_op jit(solution)/shard_map/ppermute | solution.py:455
  22.1 0.2 fusion
  22.3 0.0 copy-start.1
  22.3 0.0 copy-start.3
  22.3 3.7 %collective-permute-start.5 = (bf16[128,512]{1,0:T(8,128)(2,1)S(1)}, bf16[128,512]{1,0:T(8,128)(2,1)S(1)}, u32[]{:S(2)}, u32[]{:S(2)}) collective-permute-start(bf16[128,512]{1,0:T(8,128)(2,1)S(1)} %get-tuple-element.168), channel_id=1, source_target_pairs={{0,6},{1,7},{2,4},{3,5},{4,2},{5,3},{6,0},{7,1},{8,14},{9,15},{10,... | collective-permute-start | bytes 393224 | tf_op jit(solution)/shard_map/ppermute | solution.py:455
  26.0 0.8 collective-permute-start.7
  26.8 2.3 %shard_map.137 = (bf16[256,512]{1,0:T(8,128)(2,1)S(1)}, bf16[256,512]{1,0:T(8,128)(2,1)S(1)}, bf16[256,512]{1,0:T(8,128)(2,1)S(1)}, bf16[256,512]{1,0:T(8,128)(2...) custom-call(bf16[144,512]{1,0:T(8,128)(2,1)S(1)} %get-tuple-element., ...), custom_call_target="tpu_custom_call" | custom-call | bytes 4392960 | tf_op jit(solution)/shard_map/pallas_call | solution.py:434
  29.1 1.5 %collective-permute-done.5.refs_0_ = bf16[128,512]{1,0:T(8,128)(2,1)S(1)} collective-permute-done((bf16[128,512]{1,0:T(8,128)(2,1)S(1)}, bf16[128,512]{1,0:T(8,128)(2,1)S(1)}, u32[]{:S(2)}, u32[]{:S(2)}) %collective-permute-start.5) | collective-permute-done | bytes 131104 | tf_op jit(solution)/shard_map/ppermute | solution.py:455
  30.6 6.7 %collective-permute-done.6.refs_1_ = bf16[128,512]{1,0:T(8,128)(2,1)S(1)} collective-permute-done((bf16[128,512]{1,0:T(8,128)(2,1)S(1)}, bf16[128,512]{1,0:T(8,128)(2,1)S(1)}, u32[]{:S(2)}, u32[]{:S(2)}) %collective-permute-start.6) | collective-permute-done | bytes 131104 | tf_op jit(solution)/shard_map/ppermute | solution.py:455
  37.4 0.0 collective-permute-done.7.refs_2_
  37.4 0.5 shard_map.138
  37.8 11.0 %all_to_all.44 = bf16[32,8,128]{2,1,0:T(8,128)(2,1)S(1)} all-to-all(bf16[32,8,128]{2,1,0:T(8,128)(2,1)S(1)} %bitcast.29), channel_id=1, replica_groups=mesh['sect'=4,'node'=8] {'sect','node'}, dimensions={0} | all-to-all | bytes 131072 | tf_op jit(solution)/shard_map/all_to_all | solution.py:600
  48.9 1.9 %shard_map.139 = (bf16[128,512]{1,0:T(8,128)(2,1)S(1)}, f32[128,512]{1,0:T(8,128)S(1)}, bf16[1024,512]{1,0:T(8,128)(2,1)S(1)}, bf16[256,128]{1,0:T(8,128)(2,1)S(1)}) custom-call(bf16[128,512]{1,0:T(8,128)(2,1)S(1)} %get-tuple-element.102.state, bf16[256,128]{1,0:T(8,128)(2,1)S(1)} %bitcast.24, bf16[1024,192]{1,0:T(8,128)(2,1)S(1)} %get-tuple-element.104.source, ...), custom_call_target="tpu_custom_call" | custom-call | bytes 6553600 | tf_op jit(solution)/shard_map/pallas_call | solution.py:434
  50.7 9.1 %all_to_all.45 = bf16[32,8,128]{2,1,0:T(8,128)(2,1)S(1)} all-to-all(bf16[32,8,128]{2,1,0:T(8,128)(2,1)S(1)} %bitcast.30), channel_id=1, replica_groups=mesh['sect'=4,'node'=8] {'sect','node'}, dimensions={0} | all-to-all | bytes 131072 | tf_op jit(solution)/shard_map/all_to_all | solution.py:600
  59.8 3.0 %shard_map.140 = (bf16[128,512]{1,0:T(8,128)(2,1)S(1)}, f32[128,512]{1,0:T(8,128)S(1)}, bf16[256,128]{1,0:T(8,128)(2,1)S(1)}) custom-call(bf16[128,512]{1,0:T(8,128)(2,1)S(1)} %get-tuple-element.105.state, bf16[256,128]{1,0:T(8,128)(2,1)S(1)} %bitcast.25, bf16[1024,192]{1,0:T(8,128)(2,1)S(1)} %get-tuple-element.104.source, ...), custom_call_target="tpu_custom_call" | custom-call | bytes 5767168 | tf_op jit(solution)/shard_map/pallas_call | solution.py:434
  62.8 9.1 %all_to_all.46 = bf16[32,8,128]{2,1,0:T(8,128)(2,1)S(1)} all-to-all(bf16[32,8,128]{2,1,0:T(8,128)(2,1)S(1)} %bitcast.32), channel_id=1, replica_groups=mesh['sect'=4,'node'=8] {'sect','node'}, dimensions={0} | all-to-all | bytes 131072 | tf_op jit(solution)/shard_map/all_to_all | solution.py:600
  71.9 1.7 %shard_map.141 = (f32[128,512]{1,0:T(8,128)S(1)}, bf16[256,128]{1,0:T(8,128)(2,1)S(1)}) custom-call(f32[128,512]{1,0:T(8,128)S(1)} %get-tuple-element.108.mine, bf16[256,128]{1,0:T(8,128)(2,1)S(1)} %bitcast.23, bf16[512,256]{1,0:T(8,128)(2,1)S(1)} %get-tuple-element.110.pick_t, f32[128,512]{1,0:T(8,128)S(1)} %get-tuple-element.111.mixed, ...), custom_call_target="tpu_custom_call" | custom-call | bytes 6815744 | tf_op jit(solution)/shard_map/pallas_call | solution.py:434
  73.6 9.1 %all_to_all.47 = bf16[32,8,128]{2,1,0:T(8,128)(2,1)S(1)} all-to-all(bf16[32,8,128]{2,1,0:T(8,128)(2,1)S(1)} %bitcast.31), channel_id=1, replica_groups=mesh['sect'=4,'node'=8] {'sect','node'}, dimensions={0} | all-to-all | bytes 131072 | tf_op jit(solution)/shard_map/all_to_all | solution.py:600
  82.7 0.4 shard_map.142.refs_11_.refs_7_
  83.1 0.8 collective-permute-start.8
  83.9 1.2 %collective-permute-start.9 = (bf16[128,512]{1,0:T(8,128)(2,1)S(1)}, bf16[128,512]{1,0:T(8,128)(2,1)S(1)}, u32[]{:S(2)}, u32[]{:S(2)}) collective-permute-start(bf16[128,512]{1,0:T(8,128)(2,1)S(1)} %shard_map.142.refs_11_.refs_7_), channel_id=1, source_target_pairs={{0,4},{1,5},{2,6},{3,7},{4,0},{5,1},{6,2},{7,3},{8,12},{9,13},{10,... | collective-permute-start | bytes 393224 | tf_op jit(solution)/shard_map/ppermute | solution.py:455
  85.1 2.5 %collective-permute-start.10 = (bf16[128,512]{1,0:T(8,128)(2,1)S(1)}, bf16[128,512]{1,0:T(8,128)(2,1)S(1)}, u32[]{:S(2)}, u32[]{:S(2)}) collective-permute-start(bf16[128,512]{1,0:T(8,128)(2,1)S(1)} %shard_map.142.refs_11_.refs_7_), channel_id=1, source_target_pairs={{0,2},{1,3},{2,0},{3,1},{4,6},{5,7},{6,4},{7,5},{8,10},{9,11},{10,... | collective-permute-start | bytes 393224 | tf_op jit(solution)/shard_map/ppermute | solution.py:455
  87.6 0.0 collective-permute-start.14
  87.6 3.2 %shard_map.143 = (bf16[256,1024]{1,0:T(8,128)(2,1)S(1)}, bf16[256,1024]{1,0:T(8,128)(2,1)S(1)}, bf16[256,1024]{1,0:T(8,128)(2,1)S(1)}, bf16[256,1024]{1,0:T(8,12...) custom-call(s32[2]{0:T(128)S(1)} %pad_add_fusion.who, ...), custom_call_target="tpu_custom_call" | custom-call | bytes 6225928 | tf_op jit(solution)/shard_map/pallas_call | solution.py:434
  90.8 0.7 collective-permute-done.8.refs_8_.refs_4_
  91.5 5.6 %collective-permute-done.9.refs_9_.refs_5_ = bf16[128,512]{1,0:T(8,128)(2,1)S(1)} collective-permute-done((bf16[128,512]{1,0:T(8,128)(2,1)S(1)}, bf16[128,512]{1,0:T(8,128)(2,1)S(1)}, u32[]{:S(2)}, u32[]{:S(2)}) %collective-permute-start.9) | collective-permute-done | bytes 131104 | tf_op jit(solution)/shard_map/ppermute | solution.py:455
  97.0 0.5 collective-permute-start.13
  97.6 0.8 collective-permute-done.12.refs_13_.refs_9_
  98.4 0.2 collective-permute-done.13.refs_14_.refs_10_
  98.6 1.8 %shard_map.144 = (bf16[256,256]{1,0:T(8,128)(2,1)S(1)}, bf16[256,256]{1,0:T(8,128)(2,1)S(1)}, bf16[256,256]{1,0:T(8,128)(2,1)S(1)}, bf16[256,256]{1,0:T(8,128)(2,1)S(1)}) custom-call(s32[2]{0:T(128)S(1)} %pad_add_fusion.who, bf16[256,1024]{1,0:T(8,128)(2,1)S(1)} %get-tuple-element.124.refs_0_, bf16[256,1024]{1,0:T(8,128)(2,1)S(1)} %get-tuple-element.125.refs_1_, ...), custom_call_target="tpu_custom_call" | custom-call | bytes 4718600 | tf_op jit(solution)/shard_map/pallas_call | solution.py:434
  100.4 0.7 collective-permute-start.18
  101.1 0.5 collective-permute-start.17
  101.6 1.5 %collective-permute-start.16 = (bf16[256,256]{1,0:T(8,128)(2,1)S(1)}, bf16[256,256]{1,0:T(8,128)(2,1)S(1)}, u32[]{:S(2)}, u32[]{:S(2)}) collective-permute-start(bf16[256,256]{1,0:T(8,128)(2,1)S(1)} %get-tuple-element.133), channel_id=1, source_target_pairs={{0,16},{8,24},{16,0},{24,8},{1,17},{9,25},{17,1},{25,9},{2,18},{10... | collective-permute-start | bytes 393224 | tf_op jit(solution)/shard_map/ppermute | solution.py:455
  103.1 1.4 %collective-permute-start.15 = (bf16[256,256]{1,0:T(8,128)(2,1)S(1)}, bf16[256,256]{1,0:T(8,128)(2,1)S(1)}, u32[]{:S(2)}, u32[]{:S(2)}) collective-permute-start(bf16[256,256]{1,0:T(8,128)(2,1)S(1)} %get-tuple-element.132), channel_id=1, source_target_pairs={{0,8},{8,0},{16,24},{24,16},{1,9},{9,1},{17,25},{25,17},{2,10},{10... | collective-permute-start | bytes 393224 | tf_op jit(solution)/shard_map/ppermute | solution.py:455
  104.5 1.3 %shard_map.145 = (f32[128,256]{1,0:T(8,128)S(1)}, f32[128,256]{1,0:T(8,128)S(1)}, f32[128,256]{1,0:T(8,128)S(1)}, f32[128,256]{1,0:T(8,128)S(1)}) custom-call(s32[2]{0:T(128)S(1)} %pad_add_fusion.who, bf16[256,1024]{1,0:T(8,128)(2,1)S(1)} %get-tuple-element.144.refs_0_, bf16[256,1024]{1,0:T(8,128)(2,1)S(1)} %get-tuple-element.145.refs_1_, ...), custom_call_target="tpu_custom_call" | custom-call | bytes 3145736 | tf_op jit(solution)/shard_map/pallas_call | solution.py:434
  105.8 0.0 copy-start.2
  105.8 1.0 collective-permute-done.18.refs_7_
  106.8 0.7 collective-permute-start.22
  107.5 1.5 %collective-permute-start.21 = (bf16[128,256]{1,0:T(8,128)(2,1)S(1)}, bf16[128,256]{1,0:T(8,128)(2,1)S(1)}, u32[]{:S(2)}, u32[]{:S(2)}) collective-permute-start(bf16[128,256]{1,0:T(8,128)(2,1)S(1)} %add_convert_fusion.1), channel_id=1, source_target_pairs={{0,16},{8,24},{16,0},{24,8},{1,17},{9,25},{17,1},{25,9},{2,18},{10... | collective-permute-start | bytes 196616 | tf_op jit(solution)/shard_map/ppermute | solution.py:455
  109.0 0.2 collective-permute-done.16.refs_5_
  109.2 0.6 collective-permute-start.20
  109.7 0.4 collective-permute-done.15.refs_4_
  110.1 1.5 %collective-permute-start.19 = (bf16[128,256]{1,0:T(8,128)(2,1)S(1)}, bf16[128,256]{1,0:T(8,128)(2,1)S(1)}, u32[]{:S(2)}, u32[]{:S(2)}) collective-permute-start(bf16[128,256]{1,0:T(8,128)(2,1)S(1)} %add_convert_fusion.3), channel_id=1, source_target_pairs={{0,16},{8,24},{16,0},{24,8},{1,17},{9,25},{17,1},{25,9},{2,18},{10... | collective-permute-start | bytes 196616 | tf_op jit(solution)/shard_map/ppermute | solution.py:455
  111.5 1.3 %shard_map.146 = (f32[128,256]{1,0:T(8,128)S(1)}, f32[128,256]{1,0:T(8,128)S(1)}, f32[128,256]{1,0:T(8,128)S(1)}, f32[128,256]{1,0:T(8,128)S(1)}) custom-call(s32[2]{0:T(128)S(1)} %pad_add_fusion.who, bf16[256,1024]{1,0:T(8,128)(2,1)S(1)} %get-tuple-element.119.refs_0_, bf16[256,1024]{1,0:T(8,128)(2,1)S(1)} %get-tuple-element.120.refs_1_, ...), custom_call_target="tpu_custom_call" | custom-call | bytes 3145736 | tf_op jit(solution)/shard_map/pallas_call | solution.py:434
  112.8 0.0 collective-permute-done.21.refs_10_
  112.8 0.7 collective-permute-done.20.refs_9_
  113.5 0.9 collective-permute-done.19.refs_8_
  114.4 1.0 shard_map.147
  (23 shorter events, 0.2 us)
Async XLA Ops:
  1.7 6.9 %collective-permute-start.2 = (bf16[144,512]{1,0:T(8,128)(2,1)S(1)}, bf16[144,512]{1,0:T(8,128)(2,1)S(1)}, u32[]{:S(2)}, u32[]{:S(2)}) collective-permute-start(bf16[144,512]{1,0:T(8,128)(2,1)S(1)} %get-tuple-element.84.refs_1_), channel_id=1, source_target_pairs={{0,16},{8,24},{16,0},{24,8},{1,17},{9,25},{17,1},{25,9},{2,18},{10... | collective-permute-start | bytes 442376 | tf_op jit(solution)/shard_map/ppermute | solution.py:455
  4.7 5.7 %collective-permute-start = (bf16[144,512]{1,0:T(8,128)(2,1)S(1)}, bf16[144,512]{1,0:T(8,128)(2,1)S(1)}, u32[]{:S(2)}, u32[]{:S(2)}) collective-permute-start(bf16[144,512]{1,0:T(8,128)(2,1)S(1)} %get-tuple-element.83.refs_0_), channel_id=1, source_target_pairs={{0,8},{8,0},{16,24},{24,16},{1,9},{9,1},{17,25},{25,17},{2,10},{10... | collective-permute-start | bytes 442376 | tf_op jit(solution)/shard_map/ppermute | solution.py:455
  8.6 8.8 %collective-permute-start.3 = (bf16[288,512]{1,0:T(8,128)(2,1)S(1)}, bf16[288,512]{1,0:T(8,128)(2,1)S(1)}, u32[]{:S(2)}, u32[]{:S(2)}) collective-permute-start(bf16[288,512]{1,0:T(8,128)(2,1)S(1)} %pad_maximum_fusion.1), channel_id=1, source_target_pairs={{0,8},{8,0},{16,24},{24,16},{1,9},{9,1},{17,25},{25,17},{2,10},{10... | collective-permute-start | bytes 884744 | tf_op jit(solution)/shard_map/ppermute | solution.py:455
  10.4 7.7 %collective-permute-start.1 = (bf16[288,512]{1,0:T(8,128)(2,1)S(1)}, bf16[288,512]{1,0:T(8,128)(2,1)S(1)}, u32[]{:S(2)}, u32[]{:S(2)}) collective-permute-start(bf16[288,512]{1,0:T(8,128)(2,1)S(1)} %pad_maximum_fusion), channel_id=1, source_target_pairs={{0,16},{8,24},{16,0},{24,8},{1,17},{9,25},{17,1},{25,9},{2,18},{10... | collective-permute-start | bytes 884744 | tf_op jit(solution)/shard_map/ppermute | solution.py:455
  20.1 2.0 %collective-permute-start.4 = (bf16[512,512]{1,0:T(8,128)(2,1)S(1)}, bf16[512,512]{1,0:T(8,128)(2,1)S(1)}, u32[]{:S(2)}, u32[]{:S(2)}) collective-permute-start(bf16[512,512]{1,0:T(8,128)(2,1)S(1)} %get-tuple-element.89), channel_id=1, source_target_pairs={{0,1},{1,0},{2,3},{3,2},{4,5},{5,4},{6,7},{7,6},{8,9},{9,8},{10,11... | collective-permute-start | bytes 1572872 | tf_op jit(solution)/shard_map/ppermute | solution.py:455
  22.3 15.1 %copy-start.1 = (bf16[512,512]{1,0:T(8,128)(2,1)S(1)}, bf16[512,512]{1,0:T(8,128)(2,1)}, u32[]{:S(2)}) copy-start(bf16[512,512]{1,0:T(8,128)(2,1)} %weight.1) | copy-start | bytes 1572868
  22.3 15.1 %copy-start.3 = (bf16[1,128,512]{2,1,0:T(8,128)(2,1)S(1)}, bf16[1,128,512]{2,1,0:T(8,128)(2,1)}, u32[]{:S(2)}) copy-start(bf16[1,128,512]{2,1,0:T(8,128)(2,1)} %param.18) | copy-start | bytes 393220
  22.3 8.3 %collective-permute-start.5 = (bf16[128,512]{1,0:T(8,128)(2,1)S(1)}, bf16[128,512]{1,0:T(8,128)(2,1)S(1)}, u32[]{:S(2)}, u32[]{:S(2)}) collective-permute-start(bf16[128,512]{1,0:T(8,128)(2,1)S(1)} %get-tuple-element.168), channel_id=1, source_target_pairs={{0,6},{1,7},{2,4},{3,5},{4,2},{5,3},{6,0},{7,1},{8,14},{9,15},{10,... | collective-permute-start | bytes 393224 | tf_op jit(solution)/shard_map/ppermute | solution.py:455
  26.0 11.4 %collective-permute-start.6 = (bf16[128,512]{1,0:T(8,128)(2,1)S(1)}, bf16[128,512]{1,0:T(8,128)(2,1)S(1)}, u32[]{:S(2)}, u32[]{:S(2)}) collective-permute-start(bf16[128,512]{1,0:T(8,128)(2,1)S(1)} %get-tuple-element.167), channel_id=1, source_target_pairs={{0,4},{1,5},{2,6},{3,7},{4,0},{5,1},{6,2},{7,3},{8,12},{9,13},{10,... | collective-permute-start | bytes 393224 | tf_op jit(solution)/shard_map/ppermute | solution.py:455
  26.0 22.9 %copy-start = (bf16[2,4,512,512]{3,2,1,0:T(8,128)(2,1)S(1)}, bf16[2,4,512,512]{3,2,1,0:T(8,128)(2,1)}, u32[]{:S(2)}) copy-start(bf16[2,4,512,512]{3,2,1,0:T(8,128)(2,1)} %weights.5) | copy-start | bytes 12582916
  26.0 11.4 %collective-permute-start.7 = (bf16[128,512]{1,0:T(8,128)(2,1)S(1)}, bf16[128,512]{1,0:T(8,128)(2,1)S(1)}, u32[]{:S(2)}, u32[]{:S(2)}) collective-permute-start(bf16[128,512]{1,0:T(8,128)(2,1)S(1)} %get-tuple-element.166), channel_id=1, source_target_pairs={{0,2},{1,3},{2,0},{3,1},{4,6},{5,7},{6,4},{7,5},{8,10},{9,11},{10,... | collective-permute-start | bytes 393224 | tf_op jit(solution)/shard_map/ppermute | solution.py:455
  48.9 11.0 %copy-start.4 = (bf16[1,128,512]{2,1,0:T(8,128)(2,1)S(1)}, bf16[1,128,512]{2,1,0:T(8,128)(2,1)}, u32[]{:S(2)}) copy-start(bf16[1,128,512]{2,1,0:T(8,128)(2,1)} %param.23) | copy-start | bytes 393220
  83.1 8.3 %collective-permute-start.8 = (bf16[128,512]{1,0:T(8,128)(2,1)S(1)}, bf16[128,512]{1,0:T(8,128)(2,1)S(1)}, u32[]{:S(2)}, u32[]{:S(2)}) collective-permute-start(bf16[128,512]{1,0:T(8,128)(2,1)S(1)} %shard_map.142.refs_11_.refs_7_), channel_id=1, source_target_pairs={{0,6},{1,7},{2,4},{3,5},{4,2},{5,3},{6,0},{7,1},{8,14},{9,15},{10,... | collective-permute-start | bytes 393224 | tf_op jit(solution)/shard_map/ppermute | solution.py:455
  83.9 13.2 %collective-permute-start.9 = (bf16[128,512]{1,0:T(8,128)(2,1)S(1)}, bf16[128,512]{1,0:T(8,128)(2,1)S(1)}, u32[]{:S(2)}, u32[]{:S(2)}) collective-permute-start(bf16[128,512]{1,0:T(8,128)(2,1)S(1)} %shard_map.142.refs_11_.refs_7_), channel_id=1, source_target_pairs={{0,4},{1,5},{2,6},{3,7},{4,0},{5,1},{6,2},{7,3},{8,12},{9,13},{10,... | collective-permute-start | bytes 393224 | tf_op jit(solution)/shard_map/ppermute | solution.py:455
  85.1 11.9 %collective-permute-start.10 = (bf16[128,512]{1,0:T(8,128)(2,1)S(1)}, bf16[128,512]{1,0:T(8,128)(2,1)S(1)}, u32[]{:S(2)}, u32[]{:S(2)}) collective-permute-start(bf16[128,512]{1,0:T(8,128)(2,1)S(1)} %shard_map.142.refs_11_.refs_7_), channel_id=1, source_target_pairs={{0,2},{1,3},{2,0},{3,1},{4,6},{5,7},{6,4},{7,5},{8,10},{9,11},{10,... | collective-permute-start | bytes 393224 | tf_op jit(solution)/shard_map/ppermute | solution.py:455
  87.6 10.0 %collective-permute-start.14 = (bf16[128,512]{1,0:T(8,128)(2,1)S(1)}, bf16[128,512]{1,0:T(8,128)(2,1)S(1)}, u32[]{:S(2)}, u32[]{:S(2)}) collective-permute-start(bf16[128,512]{1,0:T(8,128)(2,1)S(1)} %shard_map.142.refs_11_.refs_7_), channel_id=1, source_target_pairs={{0,1},{1,0},{2,3},{3,2},{4,5},{5,4},{6,7},{7,6},{8,9},{9,8},{10,11... | collective-permute-start | bytes 393224 | tf_op jit(solution)/shard_map/ppermute | solution.py:455
  91.5 6.1 %collective-permute-start.11 = (bf16[128,512]{1,0:T(8,128)(2,1)S(1)}, bf16[128,512]{1,0:T(8,128)(2,1)S(1)}, u32[]{:S(2)}, u32[]{:S(2)}) collective-permute-start(bf16[128,512]{1,0:T(8,128)(2,1)S(1)} %collective-permute-done.8.refs_8_.refs_4_), channel_id=1, source_target_pairs={{0,1},{1,0},{2,3},{3,2},{4,5},{5,4},{6,7},{7,6},{8,9},{9,8},{10,11... | collective-permute-start | bytes 393224 | tf_op jit(solution)/shard_map/ppermute | solution.py:455
  97.0 1.3 %collective-permute-start.12 = (bf16[128,512]{1,0:T(8,128)(2,1)S(1)}, bf16[128,512]{1,0:T(8,128)(2,1)S(1)}, u32[]{:S(2)}, u32[]{:S(2)}) collective-permute-start(bf16[128,512]{1,0:T(8,128)(2,1)S(1)} %collective-permute-done.9.refs_9_.refs_5_), channel_id=1, source_target_pairs={{0,1},{1,0},{2,3},{3,2},{4,5},{5,4},{6,7},{7,6},{8,9},{9,8},{10,11... | collective-permute-start | bytes 393224 | tf_op jit(solution)/shard_map/ppermute | solution.py:455
  97.0 1.5 %collective-permute-start.13 = (bf16[128,512]{1,0:T(8,128)(2,1)S(1)}, bf16[128,512]{1,0:T(8,128)(2,1)S(1)}, u32[]{:S(2)}, u32[]{:S(2)}) collective-permute-start(bf16[128,512]{1,0:T(8,128)(2,1)S(1)} %collective-permute-done.10.refs_10_.refs_6_), channel_id=1, source_target_pairs={{0,1},{1,0},{2,3},{3,2},{4,5},{5,4},{6,7},{7,6},{8,9},{9,8},{10,11... | collective-permute-start | bytes 393224 | tf_op jit(solution)/shard_map/ppermute | solution.py:455
  100.4 6.4 %collective-permute-start.18 = (bf16[256,256]{1,0:T(8,128)(2,1)S(1)}, bf16[256,256]{1,0:T(8,128)(2,1)S(1)}, u32[]{:S(2)}, u32[]{:S(2)}) collective-permute-start(bf16[256,256]{1,0:T(8,128)(2,1)S(1)} %get-tuple-element.135), channel_id=1, source_target_pairs={{0,16},{8,24},{16,0},{24,8},{1,17},{9,25},{17,1},{25,9},{2,18},{10... | collective-permute-start | bytes 393224 | tf_op jit(solution)/shard_map/ppermute | solution.py:455
  101.1 6.4 %collective-permute-start.17 = (bf16[256,256]{1,0:T(8,128)(2,1)S(1)}, bf16[256,256]{1,0:T(8,128)(2,1)S(1)}, u32[]{:S(2)}, u32[]{:S(2)}) collective-permute-start(bf16[256,256]{1,0:T(8,128)(2,1)S(1)} %get-tuple-element.134), channel_id=1, source_target_pairs={{0,8},{8,0},{16,24},{24,16},{1,9},{9,1},{17,25},{25,17},{2,10},{10... | collective-permute-start | bytes 393224 | tf_op jit(solution)/shard_map/ppermute | solution.py:455
  101.6 7.5 %collective-permute-start.16 = (bf16[256,256]{1,0:T(8,128)(2,1)S(1)}, bf16[256,256]{1,0:T(8,128)(2,1)S(1)}, u32[]{:S(2)}, u32[]{:S(2)}) collective-permute-start(bf16[256,256]{1,0:T(8,128)(2,1)S(1)} %get-tuple-element.133), channel_id=1, source_target_pairs={{0,16},{8,24},{16,0},{24,8},{1,17},{9,25},{17,1},{25,9},{2,18},{10... | collective-permute-start | bytes 393224 | tf_op jit(solution)/shard_map/ppermute | solution.py:455
  103.1 7.0 %collective-permute-start.15 = (bf16[256,256]{1,0:T(8,128)(2,1)S(1)}, bf16[256,256]{1,0:T(8,128)(2,1)S(1)}, u32[]{:S(2)}, u32[]{:S(2)}) collective-permute-start(bf16[256,256]{1,0:T(8,128)(2,1)S(1)} %get-tuple-element.132), channel_id=1, source_target_pairs={{0,8},{8,0},{16,24},{24,16},{1,9},{9,1},{17,25},{25,17},{2,10},{10... | collective-permute-start | bytes 393224 | tf_op jit(solution)/shard_map/ppermute | solution.py:455
  105.8 8.6 %copy-start.2 = (bf16[512,512]{1,0:T(8,128)(2,1)S(1)}, bf16[512,512]{1,0:T(8,128)(2,1)}, u32[]{:S(2)}) copy-start(bf16[512,512]{1,0:T(8,128)(2,1)} %refs_12_.1) | copy-start | bytes 1572868
  106.8 6.0 %collective-permute-start.22 = (bf16[128,256]{1,0:T(8,128)(2,1)S(1)}, bf16[128,256]{1,0:T(8,128)(2,1)S(1)}, u32[]{:S(2)}, u32[]{:S(2)}) collective-permute-start(bf16[128,256]{1,0:T(8,128)(2,1)S(1)} %add_convert_fusion), channel_id=1, source_target_pairs={{0,8},{8,0},{16,24},{24,16},{1,9},{9,1},{17,25},{25,17},{2,10},{10... | collective-permute-start | bytes 196616 | tf_op jit(solution)/shard_map/ppermute | solution.py:455
  107.5 5.3 %collective-permute-start.21 = (bf16[128,256]{1,0:T(8,128)(2,1)S(1)}, bf16[128,256]{1,0:T(8,128)(2,1)S(1)}, u32[]{:S(2)}, u32[]{:S(2)}) collective-permute-start(bf16[128,256]{1,0:T(8,128)(2,1)S(1)} %add_convert_fusion.1), channel_id=1, source_target_pairs={{0,16},{8,24},{16,0},{24,8},{1,17},{9,25},{17,1},{25,9},{2,18},{10... | collective-permute-start | bytes 196616 | tf_op jit(solution)/shard_map/ppermute | solution.py:455
  109.2 4.3 %collective-permute-start.20 = (bf16[128,256]{1,0:T(8,128)(2,1)S(1)}, bf16[128,256]{1,0:T(8,128)(2,1)S(1)}, u32[]{:S(2)}, u32[]{:S(2)}) collective-permute-start(bf16[128,256]{1,0:T(8,128)(2,1)S(1)} %add_convert_fusion.2), channel_id=1, source_target_pairs={{0,8},{8,0},{16,24},{24,16},{1,9},{9,1},{17,25},{25,17},{2,10},{10... | collective-permute-start | bytes 196616 | tf_op jit(solution)/shard_map/ppermute | solution.py:455
  110.1 4.3 %collective-permute-start.19 = (bf16[128,256]{1,0:T(8,128)(2,1)S(1)}, bf16[128,256]{1,0:T(8,128)(2,1)S(1)}, u32[]{:S(2)}, u32[]{:S(2)}) collective-permute-start(bf16[128,256]{1,0:T(8,128)(2,1)S(1)} %add_convert_fusion.3), channel_id=1, source_target_pairs={{0,16},{8,24},{16,0},{24,8},{1,17},{9,25},{17,1},{25,9},{2,18},{10... | collective-permute-start | bytes 196616 | tf_op jit(solution)/shard_map/ppermute | solution.py:455
